TPU v7x, 32 devices: a whole 2x2x4 slice. The times are simulated.
32 devices in a mesh: dp: 16 (over z, y, x), mp: 2 (over core).
Axes of the slice: x: 2, y: 2, z: 4, core: 2. Of those that a mesh axis runs over, the one named last changes fastest.
Arguments:
- activations: bfloat16 [4096, 4096], P('dp', 'mp'), may hold values from -6 to 6
- out_grad: bfloat16 [4096, 14336], P('dp', 'mp'), may hold values from -6 to 6
- row_blocks: int32 [112, 8], P('mp'), may hold values from 0 to 31, as said below
- doc_lengths: int32 [16, 4], P('dp'), may hold values from 0 to 256, as said below
Outputs:
- weight_grad: float32 [112, 1024, 128], P('mp', 'dp')
Inputs may be any that keep to these rules, and one draw needn't show every extreme that they name: `row_blocks`: each row holds 8 distinct row-block indices. `doc_lengths`: the lengths of one index of dp sum to at most 256; at some index one document fills all 256 slots.
All inputs are finite; a program needn't handle non-finite values.
Results may differ from a plain program's by a relative error of at most 0.0003.
Values may be sent and summed in bfloat16 or wider, within the bound.
No kernel may reach another device: no remote copies, remote signals or barrier semaphores. Data moves between devices by JAX's collectives and lax.ppermute only.
A program may use at most 128 MiB of HBM per device.

v0:
```python
import jax
import jax.numpy as jnp
from jax import lax
from jax.sharding import PartitionSpec as P

BLOCK = 128


def block_sums(features, grads, row_blocks, width):
    slot_count = features.shape[0]
    blocked = features.reshape(slot_count, features.shape[1] // width, width)
    column_count = grads.shape[1] // width

    def one_column(column):
        chosen = jnp.take(blocked, row_blocks[column], axis=1).reshape(slot_count, -1)
        piece = lax.dynamic_slice_in_dim(grads, column * width, width, 1)
        return lax.dot_general(
            chosen, piece, (((0,), (0,)), ((), ())), preferred_element_type=jnp.float32
        )

    return lax.map(one_column, jnp.arange(column_count, dtype=jnp.int32))


def shards(activations, out_grad, row_blocks, doc_lengths):
    features = lax.all_gather(activations, "mp", axis=1, tiled=True)
    slot_count = features.shape[0]
    width = BLOCK
    live = jnp.sum(doc_lengths)
    slots = jnp.arange(slot_count, dtype=jnp.int32)
    masked = jnp.where((slots < live)[:, None], out_grad, jnp.zeros_like(out_grad))
    partial_sums = block_sums(features, masked, row_blocks, width)
    total_slots = slot_count * lax.axis_size("dp")
    partial_sums = partial_sums * (jnp.float32(1.0) / jnp.sqrt(jnp.float32(total_slots)))
    owners = lax.axis_size("dp")
    column_count = partial_sums.shape[0]
    stacked = partial_sums.shape[1]
    pieces = partial_sums.reshape(column_count, owners, stacked // owners, width)
    received = lax.all_to_all(pieces, "dp", split_axis=1, concat_axis=1, tiled=True)
    return jnp.sum(received, axis=1)


def solution(mesh):
    in_specs = (P("dp", "mp"), P("dp", "mp"), P("mp", None), P("dp", None))
    out_specs = P("mp", "dp", None)
    return jax.shard_map(shards, mesh=mesh, in_specs=in_specs, out_specs=out_specs, check_vma=False)
```

profile of v0, /device:TPU:0, one launch (start us, length us, event | category | flops | bytes accessed | tf_op | source)
XLA Modules:
  0.0 1061.7 jit_solution(16066906324142382860)
XLA Ops:
  6.5 2.3 copy.16
  11.6 4.2 broadcast_select_fusion
  15.8 6.5 all-gather.2.cloned.1.call-done
  22.3 3.2 copy.18
  25.5 355.6 %while.10 = (s32[]{:T(128)}, f32[56,1024,128]{2,1,0:T(8,128)}, s32[56]{0:T(128)S(1)}, s32[56,8]{1,0:T(8,128)S(1)}, bf16[256,32,128]{2,0,1:T(8,128)(2,1)S(1)}, /*...) while((s32[]{:T(128)}, f32[56,1024,128]{2,1,0:T(8,128)}, ...), condition=%wide.region_2.3_spmd, body=%wide.region_1.2_spmd.sunk | while | flops 67372112 | bytes 4266885 | solution.py:21
  29.9 1.9 fusion.12
  36.2 2.0 fusion.12
  42.6 2.0 fusion.12
  48.9 2.0 fusion.12
  55.3 1.9 fusion.12
  61.6 2.0 fusion.12
  68.0 1.9 fusion.12
  74.3 2.0 fusion.12
  80.7 1.9 fusion.12
  87.0 2.0 fusion.12
  93.4 1.9 fusion.12
  99.7 1.9 fusion.12
  106.1 2.0 fusion.12
  112.4 2.0 fusion.12
  118.8 1.9 fusion.12
  125.1 1.9 fusion.12
  131.4 2.0 fusion.12
  137.8 2.0 fusion.12
  144.2 1.9 fusion.12
  150.6 1.9 fusion.12
  156.9 2.0 fusion.12
  163.3 1.9 fusion.12
  169.6 1.9 fusion.12
  176.0 1.9 fusion.12
  182.3 2.0 fusion.12
  188.7 2.0 fusion.12
  201.4 1.9 fusion.12
  207.7 2.0 fusion.12
  214.1 2.0 fusion.12
  220.4 1.9 fusion.12
  226.7 1.9 fusion.12
  233.1 1.9 fusion.12
  239.4 2.0 fusion.12
  245.8 2.0 fusion.12
  252.1 2.0 fusion.12
  258.5 1.9 fusion.12
  264.8 2.0 fusion.12
  271.2 1.9 fusion.12
  277.5 2.0 fusion.12
  283.8 1.9 fusion.12
  290.2 2.0 fusion.12
  296.6 1.9 fusion.12
  302.9 2.0 fusion.12
  309.3 2.0 fusion.12
  315.6 2.0 fusion.12
  322.0 1.9 fusion.12
  328.3 2.0 fusion.12
  334.6 2.0 fusion.12
  341.0 2.0 fusion.12
  347.4 1.9 fusion.12
  353.8 1.9 fusion.12
  360.1 2.0 fusion.12
  366.5 2.0 fusion.12
  372.8 1.9 fusion.12
  379.1 2.0 fusion.12
  381.1 10.8 %broadcast_multiply_fusion = f32[56,1024,128]{2,1,0:T(8,128)S(1)} fusion(f32[56,1024,128]{2,1,0:T(8,128)} %get-tuple-element.37), kind=kLoop, calls=%fused_computation.13 | loop fusion | flops 7340032 | bytes 58720256 | tf_op jit(solution)/shard_map/mul | solution.py:33
  391.9 10.0 copy.19
  401.9 640.9 %all_to_all.5 = f32[56,16,64,128]{3,2,0,1:T(8,128)} all-to-all(f32[56,16,64,128]{3,2,0,1:T(8,128)} %copy.19), channel_id=1, replica_groups=mesh['dp'=16,'mp'=2] {'dp'}, dimensions={1} | all-to-all | bytes 58720256 | tf_op jit(solution)/shard_map/all_to_all | solution.py:38
  1042.8 12.0 %reduce_sum.19 = f32[56,64,128]{2,1,0:T(8,128)} reduce(f32[56,16,64,128]{3,2,0,1:T(8,128)} %all_to_all.5, f32[]{:T(128)} %constant.29.clone.1), dimensions={1}, to_apply=%region_3.4 | reduce | flops 6881280 | bytes 31195140 | tf_op jit(solution)/shard_map/reduce_sum | solution.py:39
  (456 shorter events, 103.1 us)
Async XLA Ops:
  6.5 15.7 %all-gather.2.cloned.1.call-start = ((), (), s32[]{:S(2)}) async-start(), calls=%async_computation.1 | async-start | bytes 3145728 | tf_op jit(solution)/shard_map/all_gather | solution.py:25
Sparse Core Ops, SparseCore 0:
  8.9 13.2 all-gather.1
where the time goes:
time: 1070 us; the launch traced here: 1060 us
  blocking collectives  641 us (60%)
  loops' own time  148 us (14%)
  matrix products  109 us (10%)
  local copies, waits for them, and re-layouts  101 us (9%)
  other arithmetic  42.4 us (4%)
  between operations  13.4 us (1%)
    all_to_all x1, blocking collectives, shards(): lax.all_to_all(pieces, 'dp', split_axis=1, concat_axis=1, tiled=True)  641 us
    another operation x1, loops' own time, block_sums(): return lax.map(one_column, jnp.arange(column_count, dtype=jnp.int32))  148 us
    dot_general x56, matrix products, one_column(): lax.dot_general(chosen, piece, (((0,), (0,)), ((), ())), preferred_elemen...  109 us
    gather x112, local copies, waits for them, and re-layouts, one_column(): jnp.take(blocked, row_blocks[column], axis=1).reshape(slot_count, -1)  48.2 us
    dynamic_slice x56, local copies, waits for them, and re-layouts, block_sums(): return lax.map(one_column, jnp.arange(column_count, dtype=jnp.int32))  32.6 us
  transfers between devices with their start and end apart: 1, of which 1 were waited for; matrix products, arithmetic and copies ran while one was open for 1% of the time, Pallas kernels for 0%

commit v1 on v0

v1 whole, which is shorter than its diff:
```python
import functools

import jax
import jax.numpy as jnp
from jax import lax
from jax.experimental import pallas as pl
from jax.experimental.pallas import tpu as pltpu
from jax.sharding import PartitionSpec as P

BLOCK = 128
LEVELS = 32700.0
STEPS = 128.0
SMALLEST = 2.0**-110
VMEM_LIMIT = 16 * 1024 * 1024


def pad16(rows):
    return -(-rows // 16) * 16


def params():
    return pltpu.CompilerParams(vmem_limit_bytes=VMEM_LIMIT)


def encode(values):
    largest = jnp.max(jnp.abs(values), axis=0, keepdims=True)
    power = jnp.ceil(jnp.log2(jnp.maximum(largest, SMALLEST)) * STEPS)
    codes = jnp.round(values * (jnp.exp2(power * (-1.0 / STEPS)) * LEVELS))
    return codes.astype(jnp.int32).astype(jnp.int16), power


def send_powers(sent, powers, body):
    sent[pl.ds(body, powers.shape[0]), :] = powers[...].astype(jnp.int32).astype(jnp.int16)


def read_scales(got, scales, body):
    coded = got[pl.ds(body, scales.shape[0]), :].astype(jnp.int32).astype(jnp.float32)
    scales[...] = jnp.exp2(coded * (1.0 / STEPS)) * (1.0 / LEVELS)


def multiply_kernel(width, rows, height, order, me, picks, turned, own_g, near_g, _, keep, sent, powers):
    half = len(order) // 2
    slots = own_g.shape[0]
    per_block = height // rows

    def column(c, _):
        lanes = pl.ds(pl.multiple_of(c * BLOCK, BLOCK), BLOCK)

        def product(masks):
            starts = []
            for mask in masks:
                piece = me[0] ^ mask
                entry, part = piece // per_block, piece % per_block
                starts.append(pl.multiple_of(picks[c, entry] * height + part * rows, rows))
            left = jnp.concatenate([turned[pl.ds(s, rows), :] for s in starts], axis=0)
            return jnp.dot(left[:, :slots], own_g[:, lanes], preferred_element_type=jnp.float32) + jnp.dot(
                left[:, slots:], near_g[:, lanes], preferred_element_type=jnp.float32
            )

        at = pl.ds(pl.multiple_of(c * (half * rows), half * rows), half * rows)
        away = product(order[half:])
        for j in range(half):
            codes, power = encode(away[j * rows : (j + 1) * rows])
            sent[pl.ds(pl.multiple_of((c * half + j) * rows, rows), rows), :] = codes
            powers[pl.ds(c * half + j, 1), :] = power
        keep[at, :] = product(order[:half])
        return 0

    lax.fori_loop(0, width, column, 0)
    send_powers(sent, powers, width * half * rows)


def combine_kernel(width, rows, pieces, factor, keep, got, _, *rest):
    if pieces > 1:
        mine, sent, scales, powers = rest
    else:
        mine, scales = rest
    half = pieces // 2
    read_scales(got, scales, width * pieces * rows)

    def column(c, _):
        def summed(j):
            at = pl.ds(pl.multiple_of((c * pieces + j) * rows, rows), rows)
            return keep[at, :] + got[at, :].astype(jnp.int32).astype(jnp.float32) * scales[pl.ds(c * pieces + j, 1), :]

        for j in range(half):
            to = pl.ds(pl.multiple_of((c * half + j) * rows, rows), rows)
            codes, power = encode(summed(half + j))
            sent[to, :] = codes
            powers[pl.ds(c * half + j, 1), :] = power
            mine[to, :] = summed(j)
        if pieces == 1:
            mine[c] = summed(0) * factor
        return 0

    lax.fori_loop(0, width, column, 0)
    if pieces > 1:
        send_powers(sent, powers, width * half * rows)


def widths_of(columns):
    if columns <= 12:
        return [columns]
    middle = columns - 8
    parts = -(-middle // 8)
    cuts = [middle * i // parts for i in range(parts + 1)]
    return [4] + [b - a for a, b in zip(cuts, cuts[1:])] + [4]


def masks_of(bits):
    masks = [0]
    for bit in reversed(bits):
        masks = masks + [m | 1 << bit for m in masks]
    return masks


def shards(owners, groups, activations, out_grad, row_blocks, doc_lengths):
    slots, features = activations.shape
    columns, entries = row_blocks.shape
    rows = entries * BLOCK // owners
    per_block = BLOCK // rows
    height = BLOCK // 2
    factor = 1.0 / float(slots * owners) ** 0.5
    pieces = owners // 2
    bits = list(range(pieces.bit_length() - 1))
    widths = widths_of(columns)
    count = len(widths)
    starts = [sum(widths[:i]) for i in range(count)]

    me = lax.axis_index("dp")
    half, place = me % 2, (me // 2).astype(jnp.int32).reshape(1)
    beside = [(i, i ^ 1) for i in range(owners)]

    def cut(i):
        return out_grad[:, starts[i] * BLOCK : (starts[i] + widths[i]) * BLOCK]

    def fetch(piece, after):
        piece, after = lax.optimization_barrier((piece, after))
        return lax.ppermute(piece, "dp", beside), after

    own_g = [cut(i) for i in range(count)]
    near_g = {0: lax.ppermute(own_g[0], "dp", beside)}

    live = jnp.sum(doc_lengths)
    keep = jnp.arange(slots, dtype=jnp.int32) < live
    masked = jnp.where(keep[:, None], activations, jnp.zeros_like(activations))
    split = masked.T.reshape(features // BLOCK, per_block // 2, 2, rows, slots)
    halves = [
        lax.dynamic_index_in_dim(split, h, 2, keepdims=False).reshape(features // 2, slots) for h in (half, 1 - half)
    ]
    near_half = lax.ppermute(halves[1], "dp", beside)
    near_half, near_g[0] = lax.optimization_barrier((near_half, near_g[0]))
    if count > 1:
        near_g[1], halves[0] = fetch(own_g[1], halves[0])

    def spread(part):
        return [part] + [
            lax.ppermute(part, "mp", [(g, (g + s) % groups) for g in range(groups)]) for s in range(1, groups)
        ]

    own_t, near_t = spread(halves[0]), spread(near_half)
    turned = jnp.concatenate([jnp.concatenate(own_t, axis=0), jnp.concatenate(near_t, axis=0)], axis=1)
    blocks = features // BLOCK
    picks = (lax.axis_index("mp") - row_blocks // blocks) % groups * blocks + row_blocks % blocks

    vmem = pl.BlockSpec(memory_space=pltpu.VMEM)
    smem = pl.BlockSpec(memory_space=pltpu.SMEM)

    def coded(width, n):
        return jax.ShapeDtypeStruct((width * n * rows + pad16(width * n), BLOCK), jnp.int16)

    def sums(width, n):
        return jax.ShapeDtypeStruct((width * n * rows, BLOCK), jnp.float32)

    def scale(width, n):
        return pltpu.VMEM((pad16(width * n), BLOCK), jnp.float32)

    small = pl.CostEstimate(flops=1024, bytes_accessed=1024, transcendentals=0)
    anywhere = pl.BlockSpec(memory_space=pl.ANY)

    def multiply(i, order, last):
        width, n = widths[i], pieces // 2
        chosen = picks[starts[i] : starts[i] + width]
        return pl.pallas_call(
            functools.partial(multiply_kernel, width, rows, height, order),
            out_shape=[sums(width, n), coded(width, n)],
            in_specs=[smem, smem, vmem, vmem, vmem, anywhere],
            out_specs=[vmem, vmem],
            scratch_shapes=[scale(width, n)],
            compiler_params=params(),
            cost_estimate=small,
            name="multiply",
        )(place, chosen, turned, own_g[i], near_g[i], last)

    def combine(i, n, kept, got, last):
        width = widths[i]
        if n > 1:
            outs = [sums(width, n // 2), coded(width, n // 2)]
            scratch = [scale(width, n), scale(width, n // 2)]
        else:
            outs = [jax.ShapeDtypeStruct((width, rows, BLOCK), jnp.float32)]
            scratch = [scale(width, n)]
        return pl.pallas_call(
            functools.partial(combine_kernel, width, rows, n, factor),
            out_shape=outs,
            in_specs=[vmem, vmem, anywhere],
            out_specs=[vmem] * len(outs),
            scratch_shapes=scratch,
            compiler_params=params(),
            cost_estimate=small,
            name="combine",
        )(kept, got, last)

    def swap(sent, bit):
        return lax.ppermute(sent, "dp", [(o, o ^ (2 << bit)) for o in range(owners)])

    depth = len(bits)
    held, outputs, last = {}, [None] * count, place
    for tick in range(count + depth):
        if tick < count:
            kept, sent = multiply(tick, masks_of(bits), last)
            last = kept
            if tick + 2 < count:
                near_g[tick + 2], kept = fetch(own_g[tick + 2], kept)
            held[tick] = (pieces // 2, kept, swap(sent, bits[0]))
        for step in range(1, depth + 1):
            i = tick - step
            if 0 <= i < count:
                n, kept, got = held[i]
                result = combine(i, n, kept, got, last)
                last = result[0]
                if n > 1:
                    held[i] = (n // 2, result[0], swap(result[1], bits[step]))
                else:
                    outputs[i] = result[0]
    return jnp.concatenate(outputs, axis=0)


def solution(mesh):
    in_specs = (P("dp", "mp"), P("dp", "mp"), P("mp", None), P("dp", None))
    out_specs = P("mp", "dp", None)
    body = functools.partial(shards, mesh.shape["dp"], mesh.shape["mp"])
    return jax.shard_map(body, mesh=mesh, in_specs=in_specs, out_specs=out_specs, check_vma=False)
```

time: 1070 us -> 142 us (0.13)
  blocking collectives: 641 us -> 0 us
  loops' own time: 148 us -> 0 us
  matrix products: 109 us -> 0 us
  local copies, waits for them, and re-layouts: 101 us -> 4.36 us
  starting transfers between devices: 0.01 us -> 49.8 us
  waiting for transfers between devices: 6.48 us -> 56.1 us
  other arithmetic: 42.4 us -> 3.07 us
  Pallas kernels: 0 us -> 28.3 us
  between operations: 13.4 us -> 0.57 us
    all_to_all x1 -> x0, blocking collectives: 641 us -> none  [shards(): lax.all_to_all(pieces, 'dp', split_axis=1, concat_axis=1, tiled=True)]
    another operation x1 -> x0, loops' own time: 148 us -> none  [block_sums(): return lax.map(one_column, jnp.arange(column_count, dtype=jnp.int32))]
    dot_general x56 -> x0, matrix products: 109 us -> none  [one_column(): lax.dot_general(chosen, piece, (((0,), (0,)), ((), ())), preferred_elemen...]
    ppermute x0 -> x35, waiting for transfers between devices: none -> 56.1 us  [the longest x24 30.1 us: swap(): return lax.ppermute(sent, 'dp', [(o, o ^ 2 << bit) for o in range(owners)])]
    ppermute x0 -> x35, starting transfers between devices: none -> 49.8 us  [the longest x24 34.6 us: swap(): return lax.ppermute(sent, 'dp', [(o, o ^ 2 << bit) for o in range(owners)])]
    gather x112 -> x0, local copies, waits for them, and re-layouts: 48.2 us -> none  [one_column(): jnp.take(blocked, row_blocks[column], axis=1).reshape(slot_count, -1)]
    dynamic_slice x56 -> x1, local copies, waits for them, and re-layouts: 32.6 us -> 0.89 us  [shards(): lax.dynamic_index_in_dim(split, h, 2, keepdims=False)]
    pallas_call x0 -> x32, Pallas kernels: none -> 28.3 us  [the longest x8 22 us: multiply(): pl.pallas_call(functools.partial(multiply_kernel, width, rows, height, or...]
  transfers between devices with their start and end apart: 1 -> 35, of which waited for: 1 -> 15; matrix products, arithmetic and copies ran while one was open for 1% -> 2% of each run, Pallas kernels for 0% -> 20%
where the time goes in v1:
time: 142 us
  waiting for transfers between devices  56.1 us (40%)
  starting transfers between devices  49.8 us (35%)
  Pallas kernels  28.3 us (20%)
  local copies, waits for them, and re-layouts  4.36 us (3%)
  other arithmetic  3.07 us (2%)
    ppermute x24, starting transfers between devices, swap(): return lax.ppermute(sent, 'dp', [(o, o ^ 2 << bit) for o in range(owners)])  34.6 us
    ppermute x24, waiting for transfers between devices, swap(): return lax.ppermute(sent, 'dp', [(o, o ^ 2 << bit) for o in range(owners)])  30.1 us
    pallas_call x8, Pallas kernels, multiply(): pl.pallas_call(functools.partial(multiply_kernel, width, rows, height, or...  22 us
    ppermute x1, waiting for transfers between devices, shards(): near_g = {0: lax.ppermute(own_g[0], 'dp', beside)}  15.7 us
    ppermute x7, starting transfers between devices, fetch(): return (lax.ppermute(piece, 'dp', beside), after)  10.9 us
    ppermute x7, waiting for transfers between devices, fetch(): return (lax.ppermute(piece, 'dp', beside), after)  9.92 us
    pallas_call x24, Pallas kernels, combine(): pl.pallas_call(functools.partial(combine_kernel, width, rows, n, factor),...  6.24 us
    ppermute x1, starting transfers between devices, shards(): near_half = lax.ppermute(halves[1], 'dp', beside)  2.94 us
  transfers between devices with their start and end apart: 35, of which 15 were waited for; matrix products, arithmetic and copies ran while one was open for 2% of the time, Pallas kernels for 20%

profile of v1, /device:TPU:0, one launch (start us, length us, event | category | flops | bytes accessed | tf_op | source)
XLA Modules:
  0.0 142.2 jit_solution(5093812357326645677)
XLA Ops:
  0.0 1.5 %copy.15 = bf16[256,2048]{0,1:T(8,128)(2,1)S(1)} copy(bf16[256,2048]{1,0:T(8,128)(2,1)} %param.4) | data formatting | bytes 2097152 | tf_op args[0]
  1.5 0.6 reduce_sum.9
  2.1 0.6 iota_compare_fusion
  2.9 0.9 constant_dynamic-slice_fusion.1
  3.8 2.9 %collective-permute-start.1 = (bf16[1024,256]{1,0:T(8,128)(2,1)S(1)}, bf16[1024,256]{1,0:T(8,128)(2,1)}, u32[]{:S(2)}, u32[]{:S(2)}) collective-permute-start(bf16[1024,256]{1,0:T(8,128)(2,1)S(1)} %bitcast.7), channel_id=1, source_target_pairs={{0,2},{2,0},{4,6},{6,4},{8,10},{10,8},{12,14},{14,12},{16,18},{18,... | collective-permute-start | bytes 1572872 | tf_op jit(solution)/shard_map/ppermute | solution.py:151
  6.8 1.3 collective-permute-start.2
  8.5 15.7 %collective-permute-done.2.near_g = bf16[256,512]{1,0:T(8,128)(2,1)S(1)} collective-permute-done((bf16[256,512]{1,0:T(8,128)(2,1)S(1)}, bf16[256,512]{1,0:T(8,128)(2,1)S(1)}, u32[]{:S(2)}, u32[]{:S(2)}) %collective-permute-start.2) | collective-permute-done | bytes 262176 | tf_op jit(solution)/shard_map/ppermute | solution.py:142
  24.3 0.7 copy-done.2
  25.0 1.7 %collective-permute-start.5 = (bf16[256,1024]{1,0:T(8,128)(2,1)S(1)}, bf16[256,1024]{1,0:T(8,128)(2,1)}, u32[]{:S(2)}, u32[]{:S(2)}) collective-permute-start(bf16[256,1024]{1,0:T(8,128)(2,1)S(1)} %get-tuple-element.75.own_g), channel_id=1, source_target_pairs={{0,2},{2,0},{4,6},{6,4},{8,10},{10,8},{12,14},{14,12},{16,18},{18,... | collective-permute-start | bytes 1572872 | tf_op jit(solution)/shard_map/ppermute | solution.py:139
  27.2 1.7 %maximum_maximum_fusion.turned = bf16[2048,512]{1,0:T(8,128)(2,1)S(1)} fusion(bf16[1024,256]{1,0:T(8,128)(2,1)} %collective-permute-done.3, bf16[1024,256]{1,0:T(8,128)(2,1)} %collective-permute-done.1, bf16[1024,256]{1,0:T(8,128)(2,1)} %collective-permute-done, bf16[1024,256]{1,0:T(8,128)(2,1)} %bitcast.3), kind=kLoop, calls=%fused_computation | loop fusion | flops 8388608 | bytes 4194304 | tf_op jit(solution)/shard_map/concatenate | solution.py:162
  28.9 1.7 %multiply.8 = (f32[1024,128]{1,0:T(8,128)S(1)}, s16[1040,128]{1,0:T(8,128)(2,1)S(1)}) custom-call(s32[1]{0:T(128)} %bitcast.me._, s32[4,8]{1,0:T(4,128)S(1)} %get-tuple-element.144.picks, bf16[2048,512]{1,0:T(8,128)(2,1)S(1)} %maximum_maximum_fusion.turned, bf16[256,512]{1,0:T(8,128)(2,1)S(1)} %copy-done.1, bf16[256,512]{1,0:T(8,128)(2,1)S(1)} %copy-done.3, ...), custom_call_target="tpu_custom_call" | custom-call | flops 1024 | bytes 1024 | tf_op jit(solution)/shard_map/multiply/pallas_call | solution.py:184
  30.7 1.8 %collective-permute-start.8 = (bf16[256,1024]{1,0:T(8,128)(2,1)S(1)}, bf16[256,1024]{1,0:T(8,128)(2,1)S(1)}, u32[]{:S(2)}, u32[]{:S(2)}) collective-permute-start(bf16[256,1024]{1,0:T(8,128)(2,1)S(1)} %get-tuple-element.81.own_g), channel_id=1, source_target_pairs={{0,2},{2,0},{4,6},{6,4},{8,10},{10,8},{12,14},{14,12},{16,18},{18,... | collective-permute-start | bytes 1572872 | tf_op jit(solution)/shard_map/ppermute | solution.py:139
  32.5 1.5 %collective-permute-start.4 = (s16[1040,128]{1,0:T(8,128)(2,1)S(1)}, s16[1040,128]{1,0:T(8,128)(2,1)S(1)}, u32[]{:S(2)}, u32[]{:S(2)}) collective-permute-start(s16[1040,128]{1,0:T(8,128)(2,1)S(1)} %get-tuple-element.74), channel_id=1, source_target_pairs={{0,4},{2,6},{4,0},{6,2},{8,12},{10,14},{12,8},{14,10},{16,20},{18,... | collective-permute-start | bytes 798728 | tf_op jit(solution)/shard_map/ppermute | solution.py:215
  34.0 5.8 %collective-permute-done.5.near_g = bf16[256,1024]{1,0:T(8,128)(2,1)} collective-permute-done((bf16[256,1024]{1,0:T(8,128)(2,1)S(1)}, bf16[256,1024]{1,0:T(8,128)(2,1)}, u32[]{:S(2)}, u32[]{:S(2)}) %collective-permute-start.5) | collective-permute-done | bytes 524320 | tf_op jit(solution)/shard_map/ppermute | solution.py:139
  39.8 3.5 %multiply.9 = (f32[2048,128]{1,0:T(8,128)S(1)}, s16[2080,128]{1,0:T(8,128)(2,1)S(1)}) custom-call(s32[1]{0:T(128)} %bitcast.me._, s32[8,8]{1,0:T(8,128)S(1)} %get-tuple-element.150.picks, bf16[2048,512]{1,0:T(8,128)(2,1)S(1)} %maximum_maximum_fusion.turned, bf16[256,1024]{1,0:T(8,128)(2,1)S(1)} %get-tuple-element.75.own_g, ...), custom_call_target="tpu_custom_call" | custom-call | flops 1024 | bytes 1024 | tf_op jit(solution)/shard_map/multiply/pallas_call | solution.py:184
  43.3 1.8 %collective-permute-start.7 = (s16[2080,128]{1,0:T(8,128)(2,1)S(1)}, s16[2080,128]{1,0:T(8,128)(2,1)S(1)}, u32[]{:S(2)}, u32[]{:S(2)}) collective-permute-start(s16[2080,128]{1,0:T(8,128)(2,1)S(1)} %get-tuple-element.80), channel_id=1, source_target_pairs={{0,4},{2,6},{4,0},{6,2},{8,12},{10,14},{12,8},{14,10},{16,20},{18,... | collective-permute-start | bytes 1597448 | tf_op jit(solution)/shard_map/ppermute | solution.py:215
  45.1 1.5 %collective-permute-start.12 = (bf16[256,1024]{1,0:T(8,128)(2,1)S(1)}, bf16[256,1024]{1,0:T(8,128)(2,1)S(1)}, u32[]{:S(2)}, u32[]{:S(2)}) collective-permute-start(bf16[256,1024]{1,0:T(8,128)(2,1)S(1)} %get-tuple-element.89.own_g), channel_id=1, source_target_pairs={{0,2},{2,0},{4,6},{6,4},{8,10},{10,8},{12,14},{14,12},{16,18},{18,... | collective-permute-start | bytes 1572872 | tf_op jit(solution)/shard_map/ppermute | solution.py:139
  46.8 4.1 %collective-permute-done.8.near_g = bf16[256,1024]{1,0:T(8,128)(2,1)S(1)} collective-permute-done((bf16[256,1024]{1,0:T(8,128)(2,1)S(1)}, bf16[256,1024]{1,0:T(8,128)(2,1)S(1)}, u32[]{:S(2)}, u32[]{:S(2)}) %collective-permute-start.8) | collective-permute-done | bytes 524320 | tf_op jit(solution)/shard_map/ppermute | solution.py:139
  50.9 3.0 %multiply.10 = (f32[2048,128]{1,0:T(8,128)S(1)}, s16[2080,128]{1,0:T(8,128)(2,1)S(1)}) custom-call(s32[1]{0:T(128)} %bitcast.me._, s32[8,8]{1,0:T(8,128)S(1)} %get-tuple-element.149.picks, bf16[2048,512]{1,0:T(8,128)(2,1)S(1)} %maximum_maximum_fusion.turned, bf16[256,1024]{1,0:T(8,128)(2,1)S(1)} %get-tuple-element.81.own_g, ...), custom_call_target="tpu_custom_call" | custom-call | flops 1024 | bytes 1024 | tf_op jit(solution)/shard_map/multiply/pallas_call | solution.py:184
  54.0 1.8 %collective-permute-start.11 = (s16[2080,128]{1,0:T(8,128)(2,1)S(1)}, s16[2080,128]{1,0:T(8,128)(2,1)S(1)}, u32[]{:S(2)}, u32[]{:S(2)}) collective-permute-start(s16[2080,128]{1,0:T(8,128)(2,1)S(1)} %get-tuple-element.88), channel_id=1, source_target_pairs={{0,4},{2,6},{4,0},{6,2},{8,12},{10,14},{12,8},{14,10},{16,20},{18,... | collective-permute-start | bytes 1597448 | tf_op jit(solution)/shard_map/ppermute | solution.py:215
  55.8 1.5 %collective-permute-start.16 = (bf16[256,1024]{1,0:T(8,128)(2,1)S(1)}, bf16[256,1024]{1,0:T(8,128)(2,1)S(1)}, u32[]{:S(2)}, u32[]{:S(2)}) collective-permute-start(bf16[256,1024]{1,0:T(8,128)(2,1)S(1)} %get-tuple-element.97.own_g), channel_id=1, source_target_pairs={{0,2},{2,0},{4,6},{6,4},{8,10},{10,8},{12,14},{14,12},{16,18},{18,... | collective-permute-start | bytes 1572872 | tf_op jit(solution)/shard_map/ppermute | solution.py:139
  57.3 1.6 %collective-permute-start.6 = (s16[528,128]{1,0:T(8,128)(2,1)S(1)}, s16[528,128]{1,0:T(8,128)(2,1)S(1)}, u32[]{:S(2)}, u32[]{:S(2)}) collective-permute-start(s16[528,128]{1,0:T(8,128)(2,1)S(1)} %get-tuple-element.78), channel_id=1, source_target_pairs={{0,8},{2,10},{4,12},{6,14},{8,0},{10,2},{12,4},{14,6},{16,24},{18,... | collective-permute-start | bytes 405512 | tf_op jit(solution)/shard_map/ppermute | solution.py:215
  58.9 0.5 combine.25
  59.3 3.0 %collective-permute-done.6.got = s16[528,128]{1,0:T(8,128)(2,1)S(1)} collective-permute-done((s16[528,128]{1,0:T(8,128)(2,1)S(1)}, s16[528,128]{1,0:T(8,128)(2,1)S(1)}, u32[]{:S(2)}, u32[]{:S(2)}) %collective-permute-start.6) | collective-permute-done | bytes 135200 | tf_op jit(solution)/shard_map/ppermute | solution.py:215
  62.5 3.0 %multiply.11 = (f32[2048,128]{1,0:T(8,128)S(1)}, s16[2080,128]{1,0:T(8,128)(2,1)S(1)}) custom-call(s32[1]{0:T(128)} %bitcast.me._, s32[8,8]{1,0:T(8,128)S(1)} %get-tuple-element.148.picks, bf16[2048,512]{1,0:T(8,128)(2,1)S(1)} %maximum_maximum_fusion.turned, bf16[256,1024]{1,0:T(8,128)(2,1)S(1)} %get-tuple-element.89.own_g, ...), custom_call_target="tpu_custom_call" | custom-call | flops 1024 | bytes 1024 | tf_op jit(solution)/shard_map/multiply/pallas_call | solution.py:184
  65.5 1.5 %collective-permute-start.15 = (s16[2080,128]{1,0:T(8,128)(2,1)S(1)}, s16[2080,128]{1,0:T(8,128)(2,1)S(1)}, u32[]{:S(2)}, u32[]{:S(2)}) collective-permute-start(s16[2080,128]{1,0:T(8,128)(2,1)S(1)} %get-tuple-element.96), channel_id=1, source_target_pairs={{0,4},{2,6},{4,0},{6,2},{8,12},{10,14},{12,8},{14,10},{16,20},{18,... | collective-permute-start | bytes 1597448 | tf_op jit(solution)/shard_map/ppermute | solution.py:215
  67.0 1.6 %collective-permute-start.10 = (s16[1040,128]{1,0:T(8,128)(2,1)S(1)}, s16[1040,128]{1,0:T(8,128)(2,1)S(1)}, u32[]{:S(2)}, u32[]{:S(2)}) collective-permute-start(s16[1040,128]{1,0:T(8,128)(2,1)S(1)} %get-tuple-element.86), channel_id=1, source_target_pairs={{0,8},{2,10},{4,12},{6,14},{8,0},{10,2},{12,4},{14,6},{16,24},{18,... | collective-permute-start | bytes 798728 | tf_op jit(solution)/shard_map/ppermute | solution.py:215
  68.6 1.5 %collective-permute-start.20 = (bf16[256,1024]{1,0:T(8,128)(2,1)S(1)}, bf16[256,1024]{1,0:T(8,128)(2,1)S(1)}, u32[]{:S(2)}, u32[]{:S(2)}) collective-permute-start(bf16[256,1024]{1,0:T(8,128)(2,1)S(1)} %get-tuple-element.105.own_g), channel_id=1, source_target_pairs={{0,2},{2,0},{4,6},{6,4},{8,10},{10,8},{12,14},{14,12},{16,18},{18,... | collective-permute-start | bytes 1572872 | tf_op jit(solution)/shard_map/ppermute | solution.py:139
  70.1 2.6 %collective-permute-start.9 = (s16[272,128]{1,0:T(8,128)(2,1)S(1)}, s16[272,128]{1,0:T(8,128)(2,1)S(1)}, u32[]{:S(2)}, u32[]{:S(2)}) collective-permute-start(s16[272,128]{1,0:T(8,128)(2,1)S(1)} %get-tuple-element.85), channel_id=1, source_target_pairs={{0,16},{2,18},{4,20},{6,22},{8,24},{10,26},{12,28},{14,30},{16,0},... | collective-permute-start | bytes 208904 | tf_op jit(solution)/shard_map/ppermute | solution.py:215
  72.7 0.5 combine.27
  73.1 2.6 %collective-permute-done.10.got = s16[1040,128]{1,0:T(8,128)(2,1)S(1)} collective-permute-done((s16[1040,128]{1,0:T(8,128)(2,1)S(1)}, s16[1040,128]{1,0:T(8,128)(2,1)S(1)}, u32[]{:S(2)}, u32[]{:S(2)}) %collective-permute-start.10) | collective-permute-done | bytes 266272 | tf_op jit(solution)/shard_map/ppermute | solution.py:215
  76.1 3.0 %multiply.12 = (f32[2048,128]{1,0:T(8,128)S(1)}, s16[2080,128]{1,0:T(8,128)(2,1)S(1)}) custom-call(s32[1]{0:T(128)} %bitcast.me._, s32[8,8]{1,0:T(8,128)S(1)} %get-tuple-element.147.picks, bf16[2048,512]{1,0:T(8,128)(2,1)S(1)} %maximum_maximum_fusion.turned, bf16[256,1024]{1,0:T(8,128)(2,1)S(1)} %get-tuple-element.97.own_g, ...), custom_call_target="tpu_custom_call" | custom-call | flops 1024 | bytes 1024 | tf_op jit(solution)/shard_map/multiply/pallas_call | solution.py:184
  79.2 0.5 collective-permute-start.19
  79.7 2.5 %collective-permute-start.14 = (s16[1040,128]{1,0:T(8,128)(2,1)S(1)}, s16[1040,128]{1,0:T(8,128)(2,1)S(1)}, u32[]{:S(2)}, u32[]{:S(2)}) collective-permute-start(s16[1040,128]{1,0:T(8,128)(2,1)S(1)} %get-tuple-element.94), channel_id=1, source_target_pairs={{0,8},{2,10},{4,12},{6,14},{8,0},{10,2},{12,4},{14,6},{16,24},{18,... | collective-permute-start | bytes 798728 | tf_op jit(solution)/shard_map/ppermute | solution.py:215
  82.1 1.5 %collective-permute-start.24 = (bf16[256,1024]{1,0:T(8,128)(2,1)S(1)}, bf16[256,1024]{1,0:T(8,128)(2,1)S(1)}, u32[]{:S(2)}, u32[]{:S(2)}) collective-permute-start(bf16[256,1024]{1,0:T(8,128)(2,1)S(1)} %get-tuple-element.113.own_g), channel_id=1, source_target_pairs={{0,2},{2,0},{4,6},{6,4},{8,10},{10,8},{12,14},{14,12},{16,18},{18,... | collective-permute-start | bytes 1572872 | tf_op jit(solution)/shard_map/ppermute | solution.py:139
  83.6 1.9 %collective-permute-start.13 = (s16[528,128]{1,0:T(8,128)(2,1)S(1)}, s16[528,128]{1,0:T(8,128)(2,1)S(1)}, u32[]{:S(2)}, u32[]{:S(2)}) collective-permute-start(s16[528,128]{1,0:T(8,128)(2,1)S(1)} %get-tuple-element.93), channel_id=1, source_target_pairs={{0,16},{2,18},{4,20},{6,22},{8,24},{10,26},{12,28},{14,30},{16,0},... | collective-permute-start | bytes 405512 | tf_op jit(solution)/shard_map/ppermute | solution.py:215
  85.5 0.4 combine.30
  85.9 5.8 %collective-permute-done.14.got = s16[1040,128]{1,0:T(8,128)(2,1)S(1)} collective-permute-done((s16[1040,128]{1,0:T(8,128)(2,1)S(1)}, s16[1040,128]{1,0:T(8,128)(2,1)S(1)}, u32[]{:S(2)}, u32[]{:S(2)}) %collective-permute-start.14) | collective-permute-done | bytes 266272 | tf_op jit(solution)/shard_map/ppermute | solution.py:215
  92.1 3.2 %collective-permute-start.17 = (s16[528,128]{1,0:T(8,128)(2,1)S(1)}, s16[528,128]{1,0:T(8,128)(2,1)S(1)}, u32[]{:S(2)}, u32[]{:S(2)}) collective-permute-start(s16[528,128]{1,0:T(8,128)(2,1)S(1)} %get-tuple-element.101), channel_id=1, source_target_pairs={{0,16},{2,18},{4,20},{6,22},{8,24},{10,26},{12,28},{14,30},{16,0},... | collective-permute-start | bytes 405512 | tf_op jit(solution)/shard_map/ppermute | solution.py:215
  95.4 3.0 %multiply.13 = (f32[2048,128]{1,0:T(8,128)S(1)}, s16[2080,128]{1,0:T(8,128)(2,1)S(1)}) custom-call(s32[1]{0:T(128)} %bitcast.me._, s32[8,8]{1,0:T(8,128)S(1)} %get-tuple-element.146.picks, bf16[2048,512]{1,0:T(8,128)(2,1)S(1)} %maximum_maximum_fusion.turned, bf16[256,1024]{1,0:T(8,128)(2,1)S(1)} %get-tuple-element.105.own_g, ...), custom_call_target="tpu_custom_call" | custom-call | flops 1024 | bytes 1024 | tf_op jit(solution)/shard_map/multiply/pallas_call | solution.py:184
  98.4 2.2 %collective-permute-start.23 = (s16[2080,128]{1,0:T(8,128)(2,1)S(1)}, s16[2080,128]{1,0:T(8,128)(2,1)S(1)}, u32[]{:S(2)}, u32[]{:S(2)}) collective-permute-start(s16[2080,128]{1,0:T(8,128)(2,1)S(1)} %get-tuple-element.112), channel_id=1, source_target_pairs={{0,4},{2,6},{4,0},{6,2},{8,12},{10,14},{12,8},{14,10},{16,20},{18,... | collective-permute-start | bytes 1597448 | tf_op jit(solution)/shard_map/ppermute | solution.py:215
  100.6 0.4 combine.33
  101.6 3.0 %multiply.14 = (f32[2048,128]{1,0:T(8,128)S(1)}, s16[2080,128]{1,0:T(8,128)(2,1)S(1)}) custom-call(s32[1]{0:T(128)} %bitcast.me._, s32[8,8]{1,0:T(8,128)S(1)} %get-tuple-element.145.picks, bf16[2048,512]{1,0:T(8,128)(2,1)S(1)} %maximum_maximum_fusion.turned, bf16[256,1024]{1,0:T(8,128)(2,1)S(1)} %get-tuple-element.113.own_g, ...), custom_call_target="tpu_custom_call" | custom-call | flops 1024 | bytes 1024 | tf_op jit(solution)/shard_map/multiply/pallas_call | solution.py:184
  104.7 1.4 collective-permute-start.22
  106.0 1.4 collective-permute-start.28
  107.4 2.4 %collective-permute-start.21 = (s16[528,128]{1,0:T(8,128)(2,1)S(1)}, s16[528,128]{1,0:T(8,128)(2,1)S(1)}, u32[]{:S(2)}, u32[]{:S(2)}) collective-permute-start(s16[528,128]{1,0:T(8,128)(2,1)S(1)} %get-tuple-element.109), channel_id=1, source_target_pairs={{0,16},{2,18},{4,20},{6,22},{8,24},{10,26},{12,28},{14,30},{16,0},... | collective-permute-start | bytes 405512 | tf_op jit(solution)/shard_map/ppermute | solution.py:215
  109.8 1.8 %collective-permute-done.23.got = s16[2080,128]{1,0:T(8,128)(2,1)S(1)} collective-permute-done((s16[2080,128]{1,0:T(8,128)(2,1)S(1)}, s16[2080,128]{1,0:T(8,128)(2,1)S(1)}, u32[]{:S(2)}, u32[]{:S(2)}) %collective-permute-start.23) | collective-permute-done | bytes 532512 | tf_op jit(solution)/shard_map/ppermute | solution.py:215
  111.6 0.5 combine.36
  112.1 1.5 %collective-permute-start.26 = (s16[1040,128]{1,0:T(8,128)(2,1)S(1)}, s16[1040,128]{1,0:T(8,128)(2,1)S(1)}, u32[]{:S(2)}, u32[]{:S(2)}) collective-permute-start(s16[1040,128]{1,0:T(8,128)(2,1)S(1)} %get-tuple-element.118), channel_id=1, source_target_pairs={{0,8},{2,10},{4,12},{6,14},{8,0},{10,2},{12,4},{14,6},{16,24},{18,... | collective-permute-start | bytes 798728 | tf_op jit(solution)/shard_map/ppermute | solution.py:215
  113.7 1.4 collective-permute-done.22.got
  115.6 1.7 %multiply.15 = (f32[1024,128]{1,0:T(8,128)S(1)}, s16[1040,128]{1,0:T(8,128)(2,1)S(1)}) custom-call(s32[1]{0:T(128)} %bitcast.me._, s32[4,8]{1,0:T(4,128)S(1)} %get-tuple-element.143.picks, bf16[2048,512]{1,0:T(8,128)(2,1)S(1)} %maximum_maximum_fusion.turned, bf16[256,512]{1,0:T(8,128)(2,1)S(1)} %get-tuple-element.120.own_g, ...), custom_call_target="tpu_custom_call" | custom-call | flops 1024 | bytes 1024 | tf_op jit(solution)/shard_map/multiply/pallas_call | solution.py:184
  117.3 1.1 collective-permute-start.31
  118.4 2.2 %collective-permute-start.25 = (s16[528,128]{1,0:T(8,128)(2,1)S(1)}, s16[528,128]{1,0:T(8,128)(2,1)S(1)}, u32[]{:S(2)}, u32[]{:S(2)}) collective-permute-start(s16[528,128]{1,0:T(8,128)(2,1)S(1)} %get-tuple-element.117), channel_id=1, source_target_pairs={{0,16},{2,18},{4,20},{6,22},{8,24},{10,26},{12,28},{14,30},{16,0},... | collective-permute-start | bytes 405512 | tf_op jit(solution)/shard_map/ppermute | solution.py:215
  120.6 0.4 combine.39
  121.0 1.6 %collective-permute-start.30 = (s16[1040,128]{1,0:T(8,128)(2,1)S(1)}, s16[1040,128]{1,0:T(8,128)(2,1)S(1)}, u32[]{:S(2)}, u32[]{:S(2)}) collective-permute-start(s16[1040,128]{1,0:T(8,128)(2,1)S(1)} %get-tuple-element.125), channel_id=1, source_target_pairs={{0,8},{2,10},{4,12},{6,14},{8,0},{10,2},{12,4},{14,6},{16,24},{18,... | collective-permute-start | bytes 798728 | tf_op jit(solution)/shard_map/ppermute | solution.py:215
  122.7 1.6 %collective-permute-done.26.got = s16[1040,128]{1,0:T(8,128)(2,1)S(1)} collective-permute-done((s16[1040,128]{1,0:T(8,128)(2,1)S(1)}, s16[1040,128]{1,0:T(8,128)(2,1)S(1)}, u32[]{:S(2)}, u32[]{:S(2)}) %collective-permute-start.26) | collective-permute-done | bytes 266272 | tf_op jit(solution)/shard_map/ppermute | solution.py:215
  124.9 2.5 %collective-permute-done.25.got = s16[528,128]{1,0:T(8,128)(2,1)S(1)} collective-permute-done((s16[528,128]{1,0:T(8,128)(2,1)S(1)}, s16[528,128]{1,0:T(8,128)(2,1)S(1)}, u32[]{:S(2)}, u32[]{:S(2)}) %collective-permute-start.25) | collective-permute-done | bytes 135200 | tf_op jit(solution)/shard_map/ppermute | solution.py:215
  127.8 4.3 %collective-permute-done.30.got = s16[1040,128]{1,0:T(8,128)(2,1)S(1)} collective-permute-done((s16[1040,128]{1,0:T(8,128)(2,1)S(1)}, s16[1040,128]{1,0:T(8,128)(2,1)S(1)}, u32[]{:S(2)}, u32[]{:S(2)}) %collective-permute-start.30) | collective-permute-done | bytes 266272 | tf_op jit(solution)/shard_map/ppermute | solution.py:215
  132.5 0.8 collective-permute-start.32
  133.2 1.9 %collective-permute-done.29.got = s16[528,128]{1,0:T(8,128)(2,1)S(1)} collective-permute-done((s16[528,128]{1,0:T(8,128)(2,1)S(1)}, s16[528,128]{1,0:T(8,128)(2,1)S(1)}, u32[]{:S(2)}, u32[]{:S(2)}) %collective-permute-start.29) | collective-permute-done | bytes 135200 | tf_op jit(solution)/shard_map/ppermute | solution.py:215
  135.5 0.7 collective-permute-start.34
  136.2 3.6 %collective-permute-done.32.got = s16[528,128]{1,0:T(8,128)(2,1)S(1)} collective-permute-done((s16[528,128]{1,0:T(8,128)(2,1)S(1)}, s16[528,128]{1,0:T(8,128)(2,1)S(1)}, u32[]{:S(2)}, u32[]{:S(2)}) %collective-permute-start.32) | collective-permute-done | bytes 135200 | tf_op jit(solution)/shard_map/ppermute | solution.py:215
  139.9 1.6 %collective-permute-done.34.got = s16[272,128]{1,0:T(8,128)(2,1)S(1)} collective-permute-done((s16[272,128]{1,0:T(8,128)(2,1)S(1)}, s16[272,128]{1,0:T(8,128)(2,1)S(1)}, u32[]{:S(2)}, u32[]{:S(2)}) %collective-permute-start.34) | collective-permute-done | bytes 69664 | tf_op jit(solution)/shard_map/ppermute | solution.py:215
  141.5 0.7 constant_dynamic-update-slice_fusion
  (74 shorter events, 5.1 us)
Async XLA Ops:
  0.0 1.5 %copy-start.7 = (s32[1,4]{1,0:T(1,128)S(1)}, s32[1,4]{1,0:T(1,128)}, u32[]{:S(2)}) copy-start(s32[1,4]{1,0:T(1,128)} %param.7) | copy-start | bytes 52
  2.8 3.9 %copy-start.4 = (bf16[256,7168]{1,0:T(8,128)(2,1)S(1)}, bf16[256,7168]{1,0:T(8,128)(2,1)}, u32[]{:S(2)}) copy-start(bf16[256,7168]{1,0:T(8,128)(2,1)} %param.5) | copy-start | bytes 11010052
  3.8 21.2 %collective-permute-start.1 = (bf16[1024,256]{1,0:T(8,128)(2,1)S(1)}, bf16[1024,256]{1,0:T(8,128)(2,1)}, u32[]{:S(2)}, u32[]{:S(2)}) collective-permute-start(bf16[1024,256]{1,0:T(8,128)(2,1)S(1)} %bitcast.7), channel_id=1, source_target_pairs={{0,2},{2,0},{4,6},{6,4},{8,10},{10,8},{12,14},{14,12},{16,18},{18,... | collective-permute-start | bytes 1572872 | tf_op jit(solution)/shard_map/ppermute | solution.py:151
  6.8 1.7 %copy-start = (bf16[256,512]{1,0:T(8,128)(2,1)}, bf16[256,512]{1,0:T(8,128)(2,1)S(1)}, u32[]{:S(2)}) copy-start(bf16[256,512]{1,0:T(8,128)(2,1)S(1)} %get-tuple-element.134.own_g) | copy-start | bytes 786436
  6.8 19.9 %copy-start.6 = (s32[56,8]{0,1:T(8,128)S(1)}, s32[56,8]{0,1:T(8,128)}, u32[]{:S(2)}) copy-start(s32[56,8]{0,1:T(8,128)} %param.6) | copy-start | bytes 5380
  6.8 17.5 %collective-permute-start.2 = (bf16[256,512]{1,0:T(8,128)(2,1)S(1)}, bf16[256,512]{1,0:T(8,128)(2,1)S(1)}, u32[]{:S(2)}, u32[]{:S(2)}) collective-permute-start(bf16[256,512]{1,0:T(8,128)(2,1)S(1)} %get-tuple-element.134.own_g), channel_id=1, source_target_pairs={{0,2},{2,0},{4,6},{6,4},{8,10},{10,8},{12,14},{14,12},{16,18},{18,... | collective-permute-start | bytes 786440 | tf_op jit(solution)/shard_map/ppermute | solution.py:142
  8.5 18.4 %collective-permute-start = (bf16[1024,256]{1,0:T(8,128)(2,1)}, bf16[1024,256]{1,0:T(8,128)(2,1)}, u32[]{:S(2)}, u32[]{:S(2)}) collective-permute-start(bf16[1024,256]{1,0:T(8,128)(2,1)} %bitcast.3), channel_id=1, source_target_pairs={{0,1},{1,0},{2,3},{3,2},{4,5},{5,4},{6,7},{7,6},{8,9},{9,8},{10,11... | collective-permute-start | bytes 1572872 | tf_op jit(solution)/shard_map/ppermute | solution.py:158
  24.3 0.7 copy-start.2
  25.0 2.3 %collective-permute-start.3 = (bf16[1024,256]{1,0:T(8,128)(2,1)}, bf16[1024,256]{1,0:T(8,128)(2,1)}, u32[]{:S(2)}, u32[]{:S(2)}) collective-permute-start(bf16[1024,256]{1,0:T(8,128)(2,1)} %collective-permute-done.1), channel_id=1, source_target_pairs={{0,1},{1,0},{2,3},{3,2},{4,5},{5,4},{6,7},{7,6},{8,9},{9,8},{10,11... | collective-permute-start | bytes 1572872 | tf_op jit(solution)/shard_map/ppermute | solution.py:158
  25.0 14.8 %collective-permute-start.5 = (bf16[256,1024]{1,0:T(8,128)(2,1)S(1)}, bf16[256,1024]{1,0:T(8,128)(2,1)}, u32[]{:S(2)}, u32[]{:S(2)}) collective-permute-start(bf16[256,1024]{1,0:T(8,128)(2,1)S(1)} %get-tuple-element.75.own_g), channel_id=1, source_target_pairs={{0,2},{2,0},{4,6},{6,4},{8,10},{10,8},{12,14},{14,12},{16,18},{18,... | collective-permute-start | bytes 1572872 | tf_op jit(solution)/shard_map/ppermute | solution.py:139
  26.9 2.0 %copy-start.1 = (bf16[256,512]{1,0:T(8,128)(2,1)S(1)}, bf16[256,512]{1,0:T(8,128)(2,1)}, u32[]{:S(2)}) copy-start(bf16[256,512]{1,0:T(8,128)(2,1)} %copy-done) | copy-start | bytes 786436
  26.9 2.0 %copy-start.3 = (bf16[256,512]{1,0:T(8,128)(2,1)S(1)}, bf16[256,512]{1,0:T(8,128)(2,1)}, u32[]{:S(2)}) copy-start(bf16[256,512]{1,0:T(8,128)(2,1)} %copy-done.2) | copy-start | bytes 786436
  30.7 20.3 %collective-permute-start.8 = (bf16[256,1024]{1,0:T(8,128)(2,1)S(1)}, bf16[256,1024]{1,0:T(8,128)(2,1)S(1)}, u32[]{:S(2)}, u32[]{:S(2)}) collective-permute-start(bf16[256,1024]{1,0:T(8,128)(2,1)S(1)} %get-tuple-element.81.own_g), channel_id=1, source_target_pairs={{0,2},{2,0},{4,6},{6,4},{8,10},{10,8},{12,14},{14,12},{16,18},{18,... | collective-permute-start | bytes 1572872 | tf_op jit(solution)/shard_map/ppermute | solution.py:139
  32.5 14.1 %collective-permute-start.4 = (s16[1040,128]{1,0:T(8,128)(2,1)S(1)}, s16[1040,128]{1,0:T(8,128)(2,1)S(1)}, u32[]{:S(2)}, u32[]{:S(2)}) collective-permute-start(s16[1040,128]{1,0:T(8,128)(2,1)S(1)} %get-tuple-element.74), channel_id=1, source_target_pairs={{0,4},{2,6},{4,0},{6,2},{8,12},{10,14},{12,8},{14,10},{16,20},{18,... | collective-permute-start | bytes 798728 | tf_op jit(solution)/shard_map/ppermute | solution.py:215
  43.3 15.6 %collective-permute-start.7 = (s16[2080,128]{1,0:T(8,128)(2,1)S(1)}, s16[2080,128]{1,0:T(8,128)(2,1)S(1)}, u32[]{:S(2)}, u32[]{:S(2)}) collective-permute-start(s16[2080,128]{1,0:T(8,128)(2,1)S(1)} %get-tuple-element.80), channel_id=1, source_target_pairs={{0,4},{2,6},{4,0},{6,2},{8,12},{10,14},{12,8},{14,10},{16,20},{18,... | collective-permute-start | bytes 1597448 | tf_op jit(solution)/shard_map/ppermute | solution.py:215
  45.1 17.4 %collective-permute-start.12 = (bf16[256,1024]{1,0:T(8,128)(2,1)S(1)}, bf16[256,1024]{1,0:T(8,128)(2,1)S(1)}, u32[]{:S(2)}, u32[]{:S(2)}) collective-permute-start(bf16[256,1024]{1,0:T(8,128)(2,1)S(1)} %get-tuple-element.89.own_g), channel_id=1, source_target_pairs={{0,2},{2,0},{4,6},{6,4},{8,10},{10,8},{12,14},{14,12},{16,18},{18,... | collective-permute-start | bytes 1572872 | tf_op jit(solution)/shard_map/ppermute | solution.py:139
  54.0 16.1 %collective-permute-start.11 = (s16[2080,128]{1,0:T(8,128)(2,1)S(1)}, s16[2080,128]{1,0:T(8,128)(2,1)S(1)}, u32[]{:S(2)}, u32[]{:S(2)}) collective-permute-start(s16[2080,128]{1,0:T(8,128)(2,1)S(1)} %get-tuple-element.88), channel_id=1, source_target_pairs={{0,4},{2,6},{4,0},{6,2},{8,12},{10,14},{12,8},{14,10},{16,20},{18,... | collective-permute-start | bytes 1597448 | tf_op jit(solution)/shard_map/ppermute | solution.py:215
  55.8 20.3 %collective-permute-start.16 = (bf16[256,1024]{1,0:T(8,128)(2,1)S(1)}, bf16[256,1024]{1,0:T(8,128)(2,1)S(1)}, u32[]{:S(2)}, u32[]{:S(2)}) collective-permute-start(bf16[256,1024]{1,0:T(8,128)(2,1)S(1)} %get-tuple-element.97.own_g), channel_id=1, source_target_pairs={{0,2},{2,0},{4,6},{6,4},{8,10},{10,8},{12,14},{14,12},{16,18},{18,... | collective-permute-start | bytes 1572872 | tf_op jit(solution)/shard_map/ppermute | solution.py:139
  57.3 5.0 %collective-permute-start.6 = (s16[528,128]{1,0:T(8,128)(2,1)S(1)}, s16[528,128]{1,0:T(8,128)(2,1)S(1)}, u32[]{:S(2)}, u32[]{:S(2)}) collective-permute-start(s16[528,128]{1,0:T(8,128)(2,1)S(1)} %get-tuple-element.78), channel_id=1, source_target_pairs={{0,8},{2,10},{4,12},{6,14},{8,0},{10,2},{12,4},{14,6},{16,24},{18,... | collective-permute-start | bytes 405512 | tf_op jit(solution)/shard_map/ppermute | solution.py:215
  65.5 18.1 %collective-permute-start.15 = (s16[2080,128]{1,0:T(8,128)(2,1)S(1)}, s16[2080,128]{1,0:T(8,128)(2,1)S(1)}, u32[]{:S(2)}, u32[]{:S(2)}) collective-permute-start(s16[2080,128]{1,0:T(8,128)(2,1)S(1)} %get-tuple-element.96), channel_id=1, source_target_pairs={{0,4},{2,6},{4,0},{6,2},{8,12},{10,14},{12,8},{14,10},{16,20},{18,... | collective-permute-start | bytes 1597448 | tf_op jit(solution)/shard_map/ppermute | solution.py:215
  67.0 8.7 %collective-permute-start.10 = (s16[1040,128]{1,0:T(8,128)(2,1)S(1)}, s16[1040,128]{1,0:T(8,128)(2,1)S(1)}, u32[]{:S(2)}, u32[]{:S(2)}) collective-permute-start(s16[1040,128]{1,0:T(8,128)(2,1)S(1)} %get-tuple-element.86), channel_id=1, source_target_pairs={{0,8},{2,10},{4,12},{6,14},{8,0},{10,2},{12,4},{14,6},{16,24},{18,... | collective-permute-start | bytes 798728 | tf_op jit(solution)/shard_map/ppermute | solution.py:215
  68.6 26.8 %collective-permute-start.20 = (bf16[256,1024]{1,0:T(8,128)(2,1)S(1)}, bf16[256,1024]{1,0:T(8,128)(2,1)S(1)}, u32[]{:S(2)}, u32[]{:S(2)}) collective-permute-start(bf16[256,1024]{1,0:T(8,128)(2,1)S(1)} %get-tuple-element.105.own_g), channel_id=1, source_target_pairs={{0,2},{2,0},{4,6},{6,4},{8,10},{10,8},{12,14},{14,12},{16,18},{18,... | collective-permute-start | bytes 1572872 | tf_op jit(solution)/shard_map/ppermute | solution.py:139
  70.1 6.0 %collective-permute-start.9 = (s16[272,128]{1,0:T(8,128)(2,1)S(1)}, s16[272,128]{1,0:T(8,128)(2,1)S(1)}, u32[]{:S(2)}, u32[]{:S(2)}) collective-permute-start(s16[272,128]{1,0:T(8,128)(2,1)S(1)} %get-tuple-element.85), channel_id=1, source_target_pairs={{0,16},{2,18},{4,20},{6,22},{8,24},{10,26},{12,28},{14,30},{16,0},... | collective-permute-start | bytes 208904 | tf_op jit(solution)/shard_map/ppermute | solution.py:215
  79.2 21.5 %collective-permute-start.19 = (s16[2080,128]{1,0:T(8,128)(2,1)S(1)}, s16[2080,128]{1,0:T(8,128)(2,1)S(1)}, u32[]{:S(2)}, u32[]{:S(2)}) collective-permute-start(s16[2080,128]{1,0:T(8,128)(2,1)S(1)} %get-tuple-element.104), channel_id=1, source_target_pairs={{0,4},{2,6},{4,0},{6,2},{8,12},{10,14},{12,8},{14,10},{16,20},{18,... | collective-permute-start | bytes 1597448 | tf_op jit(solution)/shard_map/ppermute | solution.py:215
  79.7 12.1 %collective-permute-start.14 = (s16[1040,128]{1,0:T(8,128)(2,1)S(1)}, s16[1040,128]{1,0:T(8,128)(2,1)S(1)}, u32[]{:S(2)}, u32[]{:S(2)}) collective-permute-start(s16[1040,128]{1,0:T(8,128)(2,1)S(1)} %get-tuple-element.94), channel_id=1, source_target_pairs={{0,8},{2,10},{4,12},{6,14},{8,0},{10,2},{12,4},{14,6},{16,24},{18,... | collective-permute-start | bytes 798728 | tf_op jit(solution)/shard_map/ppermute | solution.py:215
  82.1 19.4 %collective-permute-start.24 = (bf16[256,1024]{1,0:T(8,128)(2,1)S(1)}, bf16[256,1024]{1,0:T(8,128)(2,1)S(1)}, u32[]{:S(2)}, u32[]{:S(2)}) collective-permute-start(bf16[256,1024]{1,0:T(8,128)(2,1)S(1)} %get-tuple-element.113.own_g), channel_id=1, source_target_pairs={{0,2},{2,0},{4,6},{6,4},{8,10},{10,8},{12,14},{14,12},{16,18},{18,... | collective-permute-start | bytes 1572872 | tf_op jit(solution)/shard_map/ppermute | solution.py:139
  83.6 8.5 %collective-permute-start.13 = (s16[528,128]{1,0:T(8,128)(2,1)S(1)}, s16[528,128]{1,0:T(8,128)(2,1)S(1)}, u32[]{:S(2)}, u32[]{:S(2)}) collective-permute-start(s16[528,128]{1,0:T(8,128)(2,1)S(1)} %get-tuple-element.93), channel_id=1, source_target_pairs={{0,16},{2,18},{4,20},{6,22},{8,24},{10,26},{12,28},{14,30},{16,0},... | collective-permute-start | bytes 405512 | tf_op jit(solution)/shard_map/ppermute | solution.py:215
  91.8 9.3 %collective-permute-start.18 = (s16[1040,128]{1,0:T(8,128)(2,1)S(1)}, s16[1040,128]{1,0:T(8,128)(2,1)S(1)}, u32[]{:S(2)}, u32[]{:S(2)}) collective-permute-start(s16[1040,128]{1,0:T(8,128)(2,1)S(1)} %get-tuple-element.102), channel_id=1, source_target_pairs={{0,8},{2,10},{4,12},{6,14},{8,0},{10,2},{12,4},{14,6},{16,24},{18,... | collective-permute-start | bytes 798728 | tf_op jit(solution)/shard_map/ppermute | solution.py:215
  92.1 9.3 %collective-permute-start.17 = (s16[528,128]{1,0:T(8,128)(2,1)S(1)}, s16[528,128]{1,0:T(8,128)(2,1)S(1)}, u32[]{:S(2)}, u32[]{:S(2)}) collective-permute-start(s16[528,128]{1,0:T(8,128)(2,1)S(1)} %get-tuple-element.101), channel_id=1, source_target_pairs={{0,16},{2,18},{4,20},{6,22},{8,24},{10,26},{12,28},{14,30},{16,0},... | collective-permute-start | bytes 405512 | tf_op jit(solution)/shard_map/ppermute | solution.py:215
  98.4 13.2 %collective-permute-start.23 = (s16[2080,128]{1,0:T(8,128)(2,1)S(1)}, s16[2080,128]{1,0:T(8,128)(2,1)S(1)}, u32[]{:S(2)}, u32[]{:S(2)}) collective-permute-start(s16[2080,128]{1,0:T(8,128)(2,1)S(1)} %get-tuple-element.112), channel_id=1, source_target_pairs={{0,4},{2,6},{4,0},{6,2},{8,12},{10,14},{12,8},{14,10},{16,20},{18,... | collective-permute-start | bytes 1597448 | tf_op jit(solution)/shard_map/ppermute | solution.py:215
  104.6 16.0 %collective-permute-start.27 = (s16[2080,128]{1,0:T(8,128)(2,1)S(1)}, s16[2080,128]{1,0:T(8,128)(2,1)S(1)}, u32[]{:S(2)}, u32[]{:S(2)}) collective-permute-start(s16[2080,128]{1,0:T(8,128)(2,1)S(1)} %get-tuple-element.119), channel_id=1, source_target_pairs={{0,4},{2,6},{4,0},{6,2},{8,12},{10,14},{12,8},{14,10},{16,20},{18,... | collective-permute-start | bytes 1597448 | tf_op jit(solution)/shard_map/ppermute | solution.py:215
  104.7 10.4 %collective-permute-start.22 = (s16[1040,128]{1,0:T(8,128)(2,1)S(1)}, s16[1040,128]{1,0:T(8,128)(2,1)S(1)}, u32[]{:S(2)}, u32[]{:S(2)}) collective-permute-start(s16[1040,128]{1,0:T(8,128)(2,1)S(1)} %get-tuple-element.110), channel_id=1, source_target_pairs={{0,8},{2,10},{4,12},{6,14},{8,0},{10,2},{12,4},{14,6},{16,24},{18,... | collective-permute-start | bytes 798728 | tf_op jit(solution)/shard_map/ppermute | solution.py:215
  106.0 9.5 %collective-permute-start.28 = (bf16[256,512]{1,0:T(8,128)(2,1)S(1)}, bf16[256,512]{1,0:T(8,128)(2,1)S(1)}, u32[]{:S(2)}, u32[]{:S(2)}) collective-permute-start(bf16[256,512]{1,0:T(8,128)(2,1)S(1)} %get-tuple-element.120.own_g), channel_id=1, source_target_pairs={{0,2},{2,0},{4,6},{6,4},{8,10},{10,8},{12,14},{14,12},{16,18},{18,... | collective-permute-start | bytes 786440 | tf_op jit(solution)/shard_map/ppermute | solution.py:139
  107.4 8.0 %collective-permute-start.21 = (s16[528,128]{1,0:T(8,128)(2,1)S(1)}, s16[528,128]{1,0:T(8,128)(2,1)S(1)}, u32[]{:S(2)}, u32[]{:S(2)}) collective-permute-start(s16[528,128]{1,0:T(8,128)(2,1)S(1)} %get-tuple-element.109), channel_id=1, source_target_pairs={{0,16},{2,18},{4,20},{6,22},{8,24},{10,26},{12,28},{14,30},{16,0},... | collective-permute-start | bytes 405512 | tf_op jit(solution)/shard_map/ppermute | solution.py:215
  112.1 12.2 %collective-permute-start.26 = (s16[1040,128]{1,0:T(8,128)(2,1)S(1)}, s16[1040,128]{1,0:T(8,128)(2,1)S(1)}, u32[]{:S(2)}, u32[]{:S(2)}) collective-permute-start(s16[1040,128]{1,0:T(8,128)(2,1)S(1)} %get-tuple-element.118), channel_id=1, source_target_pairs={{0,8},{2,10},{4,12},{6,14},{8,0},{10,2},{12,4},{14,6},{16,24},{18,... | collective-permute-start | bytes 798728 | tf_op jit(solution)/shard_map/ppermute | solution.py:215
  117.3 10.2 %collective-permute-start.31 = (s16[1040,128]{1,0:T(8,128)(2,1)S(1)}, s16[1040,128]{1,0:T(8,128)(2,1)S(1)}, u32[]{:S(2)}, u32[]{:S(2)}) collective-permute-start(s16[1040,128]{1,0:T(8,128)(2,1)S(1)} %get-tuple-element.126), channel_id=1, source_target_pairs={{0,4},{2,6},{4,0},{6,2},{8,12},{10,14},{12,8},{14,10},{16,20},{18,... | collective-permute-start | bytes 798728 | tf_op jit(solution)/shard_map/ppermute | solution.py:215
  118.4 9.0 %collective-permute-start.25 = (s16[528,128]{1,0:T(8,128)(2,1)S(1)}, s16[528,128]{1,0:T(8,128)(2,1)S(1)}, u32[]{:S(2)}, u32[]{:S(2)}) collective-permute-start(s16[528,128]{1,0:T(8,128)(2,1)S(1)} %get-tuple-element.117), channel_id=1, source_target_pairs={{0,16},{2,18},{4,20},{6,22},{8,24},{10,26},{12,28},{14,30},{16,0},... | collective-permute-start | bytes 405512 | tf_op jit(solution)/shard_map/ppermute | solution.py:215
  121.0 11.1 %collective-permute-start.30 = (s16[1040,128]{1,0:T(8,128)(2,1)S(1)}, s16[1040,128]{1,0:T(8,128)(2,1)S(1)}, u32[]{:S(2)}, u32[]{:S(2)}) collective-permute-start(s16[1040,128]{1,0:T(8,128)(2,1)S(1)} %get-tuple-element.125), channel_id=1, source_target_pairs={{0,8},{2,10},{4,12},{6,14},{8,0},{10,2},{12,4},{14,6},{16,24},{18,... | collective-permute-start | bytes 798728 | tf_op jit(solution)/shard_map/ppermute | solution.py:215
  124.7 10.5 %collective-permute-start.29 = (s16[528,128]{1,0:T(8,128)(2,1)S(1)}, s16[528,128]{1,0:T(8,128)(2,1)S(1)}, u32[]{:S(2)}, u32[]{:S(2)}) collective-permute-start(s16[528,128]{1,0:T(8,128)(2,1)S(1)} %get-tuple-element.124), channel_id=1, source_target_pairs={{0,16},{2,18},{4,20},{6,22},{8,24},{10,26},{12,28},{14,30},{16,0},... | collective-permute-start | bytes 405512 | tf_op jit(solution)/shard_map/ppermute | solution.py:215
  127.7 7.5 %collective-permute-start.33 = (s16[528,128]{1,0:T(8,128)(2,1)S(1)}, s16[528,128]{1,0:T(8,128)(2,1)S(1)}, u32[]{:S(2)}, u32[]{:S(2)}) collective-permute-start(s16[528,128]{1,0:T(8,128)(2,1)S(1)} %get-tuple-element.130), channel_id=1, source_target_pairs={{0,8},{2,10},{4,12},{6,14},{8,0},{10,2},{12,4},{14,6},{16,24},{18,... | collective-permute-start | bytes 405512 | tf_op jit(solution)/shard_map/ppermute | solution.py:215
  132.5 7.3 %collective-permute-start.32 = (s16[528,128]{1,0:T(8,128)(2,1)S(1)}, s16[528,128]{1,0:T(8,128)(2,1)S(1)}, u32[]{:S(2)}, u32[]{:S(2)}) collective-permute-start(s16[528,128]{1,0:T(8,128)(2,1)S(1)} %get-tuple-element.129), channel_id=1, source_target_pairs={{0,16},{2,18},{4,20},{6,22},{8,24},{10,26},{12,28},{14,30},{16,0},... | collective-permute-start | bytes 405512 | tf_op jit(solution)/shard_map/ppermute | solution.py:215
  135.5 6.0 %collective-permute-start.34 = (s16[272,128]{1,0:T(8,128)(2,1)S(1)}, s16[272,128]{1,0:T(8,128)(2,1)S(1)}, u32[]{:S(2)}, u32[]{:S(2)}) collective-permute-start(s16[272,128]{1,0:T(8,128)(2,1)S(1)} %get-tuple-element.132), channel_id=1, source_target_pairs={{0,16},{2,18},{4,20},{6,22},{8,24},{10,26},{12,28},{14,30},{16,0},... | collective-permute-start | bytes 208904 | tf_op jit(solution)/shard_map/ppermute | solution.py:215
  139.9 1.6 %copy-start.5 = (f32[56,64,128]{2,1,0:T(8,128)}, f32[56,64,128]{2,1,0:T(8,128)S(1)}, u32[]{:S(2)}) copy-start(f32[56,64,128]{2,1,0:T(8,128)S(1)} %constant_dynamic-update-slice_fusion.1) | copy-start | bytes 5505028

commit v2 on v1

--- a/solution.py
+++ b/solution.py
@@ -54,7 +54,7 @@
                 starts.append(pl.multiple_of(picks[c, entry] * height + part * rows, rows))
             left = jnp.concatenate([turned[pl.ds(s, rows), :] for s in starts], axis=0)
             return jnp.dot(left[:, :slots], own_g[:, lanes], preferred_element_type=jnp.float32) + jnp.dot(
-                left[:, slots:], near_g[:, lanes], preferred_element_type=jnp.float32
+                left[:, slots:], near_g[1 - me[1], :, lanes], preferred_element_type=jnp.float32
             )
 
         at = pl.ds(pl.multiple_of(c * (half * rows), half * rows), half * rows)
@@ -128,7 +128,7 @@
     starts = [sum(widths[:i]) for i in range(count)]
 
     me = lax.axis_index("dp")
-    half, place = me % 2, (me // 2).astype(jnp.int32).reshape(1)
+    half, place = me % 2, jnp.stack([me // 2, me % 2]).astype(jnp.int32)
     beside = [(i, i ^ 1) for i in range(owners)]
 
     def cut(i):
@@ -136,10 +136,15 @@
 
     def fetch(piece, after):
         piece, after = lax.optimization_barrier((piece, after))
-        return lax.ppermute(piece, "dp", beside), after
+        return both(piece), after
+
+    pairs = [[i, i + 1] for i in range(0, owners, 2)]
+
+    def both(piece):
+        return lax.all_gather(piece, "dp", axis_index_groups=pairs)
 
     own_g = [cut(i) for i in range(count)]
-    near_g = {0: lax.ppermute(own_g[0], "dp", beside)}
+    near_g = {0: both(own_g[0])}
 
     live = jnp.sum(doc_lengths)
     keep = jnp.arange(slots, dtype=jnp.int32) < live

time: 142 us -> 220 us (1.55)
  local copies, waits for them, and re-layouts: 4.36 us -> 43.3 us
  blocking collectives: 0 us -> 27.4 us
  between operations: 0.57 us -> 14.2 us
  starting transfers between devices: 49.8 us -> 37.7 us
  Pallas kernels: 28.3 us -> 34.2 us
  waiting for transfers between devices: 56.1 us -> 59 us
    unnamed x25 -> x147, local copies, waits for them, and re-layouts: 2.42 us -> 38.5 us
    all_gather x0 -> x2, blocking collectives: none -> 27.4 us  [both(): return lax.all_gather(piece, 'dp', axis_index_groups=pairs)]
    ppermute x8 -> x0, waiting for transfers between devices: 25.7 us -> none  [the longest x1 15.7 us: shards(): near_g = {0: lax.ppermute(own_g[0], 'dp', beside)}]
    ppermute x24, waiting for transfers between devices: 30.1 us -> 54.2 us  [swap(): return lax.ppermute(sent, 'dp', [(o, o ^ 2 << bit) for o in range(owners)])]
    ppermute x8 -> x0, starting transfers between devices: 12.2 us -> none  [the longest x7 10.9 us: fetch(): return (lax.ppermute(piece, 'dp', beside), after)]
    pallas_call x24, Pallas kernels: 6.24 us -> 11.6 us  [combine(): pl.pallas_call(functools.partial(combine_kernel, width, rows, n, factor),...]
    all_gather x0 -> x6, waiting for transfers between devices: none -> 4.42 us  [both(): return lax.all_gather(piece, 'dp', axis_index_groups=pairs)]
    slice x2, local copies, waits for them, and re-layouts: 0.37 us -> 2.8 us  [cut(): return out_grad[:, starts[i] * BLOCK:(starts[i] + widths[i]) * BLOCK]]
  transfers between devices with their start and end apart: 35 -> 33, of which waited for: 15 -> 12; matrix products, arithmetic and copies ran while one was open for 2% -> 3% of each run, Pallas kernels for 20% -> 16%
where the time goes in v2:
time: 220 us; the launch traced here: 219 us
  waiting for transfers between devices  59 us (27%)
  local copies, waits for them, and re-layouts  43.3 us (20%)
  starting transfers between devices  37.7 us (17%)
  Pallas kernels  34.2 us (16%)
  blocking collectives  27.4 us (12%)
  between operations  14.2 us (6%)
  other arithmetic  2.83 us (1%)
    ppermute x24, waiting for transfers between devices, swap(): return lax.ppermute(sent, 'dp', [(o, o ^ 2 << bit) for o in range(owners)])  54.2 us
    unnamed x147, local copies, waits for them, and re-layouts  38.5 us
    ppermute x24, starting transfers between devices, swap(): return lax.ppermute(sent, 'dp', [(o, o ^ 2 << bit) for o in range(owners)])  34.5 us
    all_gather x2, blocking collectives, both(): return lax.all_gather(piece, 'dp', axis_index_groups=pairs)  27.4 us
    pallas_call x8, Pallas kernels, multiply(): pl.pallas_call(functools.partial(multiply_kernel, width, rows, height, or...  22.6 us
    pallas_call x24, Pallas kernels, combine(): pl.pallas_call(functools.partial(combine_kernel, width, rows, n, factor),...  11.6 us
    all_gather x6, waiting for transfers between devices, both(): return lax.all_gather(piece, 'dp', axis_index_groups=pairs)  4.42 us
  transfers between devices with their start and end apart: 33, of which 12 were waited for; matrix products, arithmetic and copies ran while one was open for 3% of the time, Pallas kernels for 16%

profile of v2, /device:TPU:0, one launch (start us, length us, event | category | flops | bytes accessed | tf_op | source)
XLA Modules:
  0.0 218.7 jit_solution(16396856206677125488)
XLA Ops:
  6.5 1.5 copy.15
  9.6 3.0 %collective-permute-start.1 = (bf16[1024,256]{1,0:T(8,128)(2,1)S(1)}, bf16[1024,256]{1,0:T(8,128)(2,1)S(1)}, u32[]{:S(2)}, u32[]{:S(2)}) collective-permute-start(bf16[1024,256]{1,0:T(8,128)(2,1)S(1)} %bitcast.26), channel_id=1, source_target_pairs={{0,2},{2,0},{4,6},{6,4},{8,10},{10,8},{12,14},{14,12},{16,18},{18,... | collective-permute-start | bytes 1572872 | tf_op jit(solution)/shard_map/ppermute | solution.py:156
  12.6 1.7 fusion.6
  14.4 1.1 fusion.5
  15.6 20.4 %all-gather = bf16[512,512]{1,0:T(8,128)(2,1)S(1)} all-gather(bf16[256,512]{1,0:T(8,128)(2,1)S(1)} %get-tuple-element.134.own_g), channel_id=2, replica_groups={{0,2},{4,6},{8,10},{12,14},{16,18},{20,22},{24,26},{28,30},{1,3},{5,7},..., dimensions={0}, use_global_device_ids=true | all-gather | bytes 786432 | tf_op jit(solution)/shard_map/all_gather | solution.py:144
  37.9 1.4 maximum_maximum_fusion.turned
  39.2 1.7 multiply.8
  43.2 1.0 copy-done.21
  44.2 1.2 copy-done.32
  45.5 3.0 %multiply.9 = (f32[2048,128]{1,0:T(8,128)S(1)}, s16[2080,128]{1,0:T(8,128)(2,1)S(1)}) custom-call(s32[2]{0:T(128)S(1)} %pad_add_fusion.me._, s32[8,8]{1,0:T(8,128)S(1)} %get-tuple-element.150.picks, bf16[2048,512]{1,0:T(8,128)(2,1)S(1)} %maximum_maximum_fusion.turned, bf16[256,1024]{1,0:T(8,128)(2,1)S(1)} %copy-done.5, bf16[2,256,1024]{2,1,0:T(8,128)(2,1)S(1)} %bitcast.20, ...), custom_call_target="tpu_custom_call" | custom-call | flops 1024 | bytes 1024 | tf_op jit(solution)/shard_map/multiply/pallas_call | solution.py:189
  48.5 1.0 copy-done.6
  50.4 1.4 collective-permute-start.3
  51.8 7.3 %collective-permute-done.3.got = s16[1040,128]{1,0:T(8,128)(2,1)S(1)} collective-permute-done((s16[1040,128]{1,0:T(8,128)(2,1)}, s16[1040,128]{1,0:T(8,128)(2,1)S(1)}, u32[]{:S(2)}, u32[]{:S(2)}) %collective-permute-start.3) | collective-permute-done | bytes 266272 | tf_op jit(solution)/shard_map/ppermute | solution.py:220
  59.1 1.2 copy-done.7
  61.9 4.4 %all-gather.17.cloned.1.call-done = bf16[512,1024]{1,0:T(8,128)(2,1)} async-done(((bf16[256,1024]{1,0:T(8,128)(2,1)}), bf16[512,1024]{1,0:T(8,128)(2,1)}) %all-gather.17.cloned.1.call-update) | async-done | bytes 1048592 | tf_op jit(solution)/shard_map/all_gather | solution.py:144
  66.3 1.2 copy-done.34
  68.5 3.0 %multiply.10 = (f32[2048,128]{1,0:T(8,128)S(1)}, s16[2080,128]{1,0:T(8,128)(2,1)S(1)}) custom-call(s32[2]{0:T(128)S(1)} %pad_add_fusion.me._, s32[8,8]{1,0:T(8,128)S(1)} %get-tuple-element.149.picks, bf16[2048,512]{1,0:T(8,128)(2,1)S(1)} %maximum_maximum_fusion.turned, bf16[256,1024]{1,0:T(8,128)(2,1)S(1)} %copy-done.4, bf16[2,256,1024]{2,1,0:T(8,128)(2,1)S(1)} %bitcast.22, ...), custom_call_target="tpu_custom_call" | custom-call | flops 1024 | bytes 1024 | tf_op jit(solution)/shard_map/multiply/pallas_call | solution.py:189
  71.6 1.0 copy-done.15
  73.5 1.5 collective-permute-start.5
  75.1 1.5 collective-permute-start.4
  76.6 11.1 %collective-permute-done.5.got = s16[2080,128]{1,0:T(8,128)(2,1)S(1)} collective-permute-done((s16[2080,128]{1,0:T(8,128)(2,1)}, s16[2080,128]{1,0:T(8,128)(2,1)S(1)}, u32[]{:S(2)}, u32[]{:S(2)}) %collective-permute-start.5) | collective-permute-done | bytes 532512 | tf_op jit(solution)/shard_map/ppermute | solution.py:220
  87.7 1.2 copy-done.8
  88.9 1.2 copy-done.16
  93.1 1.3 copy-done.33
  95.0 3.0 %multiply.11 = (f32[2048,128]{1,0:T(8,128)S(1)}, s16[2080,128]{1,0:T(8,128)(2,1)S(1)}) custom-call(s32[2]{0:T(128)S(1)} %pad_add_fusion.me._, s32[8,8]{1,0:T(8,128)S(1)} %copy-done.48, bf16[2048,512]{1,0:T(8,128)(2,1)S(1)} %maximum_maximum_fusion.turned, bf16[256,1024]{1,0:T(8,128)(2,1)S(1)} %copy-done.3, bf16[2,256,1024]{2,1,0:T(8,128)(2,1)S(1)} %bitcast.21, ...), custom_call_target="tpu_custom_call" | custom-call | flops 1024 | bytes 1024 | tf_op jit(solution)/shard_map/multiply/pallas_call | solution.py:189
  98.1 1.0 copy-done.9
  99.9 1.5 collective-permute-start.8
  101.4 1.5 collective-permute-start.7
  102.9 2.4 %collective-permute-start.6 = (s16[272,128]{1,0:T(8,128)(2,1)}, s16[272,128]{1,0:T(8,128)(2,1)S(1)}, u32[]{:S(2)}, u32[]{:S(2)}) collective-permute-start(s16[272,128]{1,0:T(8,128)(2,1)} %copy-done.62), channel_id=1, source_target_pairs={{0,16},{2,18},{4,20},{6,22},{8,24},{10,26},{12,28},{14,30},{16,0},... | collective-permute-start | bytes 208904 | tf_op jit(solution)/shard_map/ppermute | solution.py:220
  105.3 7.9 %collective-permute-done.8.got = s16[2080,128]{1,0:T(8,128)(2,1)S(1)} collective-permute-done((s16[2080,128]{1,0:T(8,128)(2,1)}, s16[2080,128]{1,0:T(8,128)(2,1)S(1)}, u32[]{:S(2)}, u32[]{:S(2)}) %collective-permute-start.8) | collective-permute-done | bytes 532512 | tf_op jit(solution)/shard_map/ppermute | solution.py:220
  113.3 1.2 copy-done.10
  114.5 1.2 copy-done.17
  118.4 1.3 copy-done.31
  119.7 3.0 %multiply.12 = (f32[2048,128]{1,0:T(8,128)S(1)}, s16[2080,128]{1,0:T(8,128)(2,1)S(1)}) custom-call(s32[2]{0:T(128)S(1)} %pad_add_fusion.me._, s32[8,8]{1,0:T(8,128)S(1)} %get-tuple-element.147.picks, bf16[2048,512]{1,0:T(8,128)(2,1)S(1)} %maximum_maximum_fusion.turned, bf16[256,1024]{1,0:T(8,128)(2,1)S(1)} %copy-done.2, bf16[2,256,1024]{2,1,0:T(8,128)(2,1)S(1)} %bitcast.19, ...), custom_call_target="tpu_custom_call" | custom-call | flops 1024 | bytes 1024 | tf_op jit(solution)/shard_map/multiply/pallas_call | solution.py:189
  122.8 1.0 copy-done.12
  124.6 1.5 collective-permute-start.11
  126.7 1.5 collective-permute-start.10
  128.2 11.8 %collective-permute-done.11.got = s16[2080,128]{1,0:T(8,128)(2,1)S(1)} collective-permute-done((s16[2080,128]{1,0:T(8,128)(2,1)}, s16[2080,128]{1,0:T(8,128)(2,1)S(1)}, u32[]{:S(2)}, u32[]{:S(2)}) %collective-permute-start.11) | collective-permute-done | bytes 532512 | tf_op jit(solution)/shard_map/ppermute | solution.py:220
  139.9 1.2 copy-done.11
  141.2 1.3 copy-done.13
  142.4 1.1 combine.30
  143.6 1.4 collective-permute-start.13
  145.0 2.4 %collective-permute-start.9 = (s16[528,128]{1,0:T(8,128)(2,1)}, s16[528,128]{1,0:T(8,128)(2,1)S(1)}, u32[]{:S(2)}, u32[]{:S(2)}) collective-permute-start(s16[528,128]{1,0:T(8,128)(2,1)} %copy-done.59), channel_id=1, source_target_pairs={{0,16},{2,18},{4,20},{6,22},{8,24},{10,26},{12,28},{14,30},{16,0},... | collective-permute-start | bytes 405512 | tf_op jit(solution)/shard_map/ppermute | solution.py:220
  147.4 1.0 combine.31
  149.0 2.5 %collective-permute-done.9.got = s16[528,128]{1,0:T(8,128)(2,1)S(1)} collective-permute-done((s16[528,128]{1,0:T(8,128)(2,1)}, s16[528,128]{1,0:T(8,128)(2,1)S(1)}, u32[]{:S(2)}, u32[]{:S(2)}) %collective-permute-start.9) | collective-permute-done | bytes 135200 | tf_op jit(solution)/shard_map/ppermute | solution.py:220
  152.3 1.2 copy-done.29
  153.5 3.8 %multiply.13 = (f32[2048,128]{1,0:T(8,128)S(1)}, s16[2080,128]{1,0:T(8,128)(2,1)}) custom-call(s32[2]{0:T(128)S(1)} %pad_add_fusion.me._, s32[8,8]{1,0:T(8,128)S(1)} %get-tuple-element.146.picks, bf16[2048,512]{1,0:T(8,128)(2,1)S(1)} %maximum_maximum_fusion.turned, bf16[256,1024]{1,0:T(8,128)(2,1)S(1)} %copy-done.1, bf16[2,256,1024]{2,1,0:T(8,128)(2,1)S(1)} %bitcast.17, ...), custom_call_target="tpu_custom_call" | custom-call | flops 1024 | bytes 1024 | tf_op jit(solution)/shard_map/multiply/pallas_call | solution.py:189
  157.4 1.5 collective-permute-start.17
  158.9 1.6 combine.33
  160.5 1.5 combine.34
  165.1 1.2 copy-done.30
  166.3 3.0 %multiply.14 = (f32[2048,128]{1,0:T(8,128)S(1)}, s16[2080,128]{1,0:T(8,128)(2,1)S(1)}) custom-call(s32[2]{0:T(128)S(1)} %pad_add_fusion.me._, s32[8,8]{1,0:T(8,128)S(1)} %get-tuple-element.145.picks, bf16[2048,512]{1,0:T(8,128)(2,1)S(1)} %maximum_maximum_fusion.turned, bf16[256,1024]{1,0:T(8,128)(2,1)S(1)} %copy-done, bf16[2,256,1024]{2,1,0:T(8,128)(2,1)S(1)} %bitcast.18, ...), custom_call_target="tpu_custom_call" | custom-call | flops 1024 | bytes 1024 | tf_op jit(solution)/shard_map/multiply/pallas_call | solution.py:189
  169.9 2.6 %collective-permute-start.16 = (s16[1040,128]{1,0:T(8,128)(2,1)S(1)}, s16[1040,128]{1,0:T(8,128)(2,1)S(1)}, u32[]{:S(2)}, u32[]{:S(2)}) collective-permute-start(s16[1040,128]{1,0:T(8,128)(2,1)S(1)} %copy-done.56), channel_id=1, source_target_pairs={{0,8},{2,10},{4,12},{6,14},{8,0},{10,2},{12,4},{14,6},{16,24},{18,... | collective-permute-start | bytes 798728 | tf_op jit(solution)/shard_map/ppermute | solution.py:220
  172.5 3.0 %collective-permute-start.15 = (s16[528,128]{1,0:T(8,128)(2,1)S(1)}, s16[528,128]{1,0:T(8,128)(2,1)S(1)}, u32[]{:S(2)}, u32[]{:S(2)}) collective-permute-start(s16[528,128]{1,0:T(8,128)(2,1)S(1)} %copy-done.61), channel_id=1, source_target_pairs={{0,16},{2,18},{4,20},{6,22},{8,24},{10,26},{12,28},{14,30},{16,0},... | collective-permute-start | bytes 405512 | tf_op jit(solution)/shard_map/ppermute | solution.py:220
  175.5 7.0 %all-gather.7 = bf16[512,512]{1,0:T(8,128)(2,1)S(1)} all-gather(bf16[256,512]{1,0:T(8,128)(2,1)S(1)} %get-tuple-element.120.own_g), channel_id=9, replica_groups={{0,2},{4,6},{8,10},{12,14},{16,18},{20,22},{24,26},{28,30},{1,3},{5,7},..., dimensions={0}, use_global_device_ids=true | all-gather | bytes 786432 | tf_op jit(solution)/shard_map/all_gather | solution.py:144
  182.5 1.5 combine.36
  184.7 1.7 multiply.15
  186.5 1.5 collective-permute-start.23
  188.9 2.6 %collective-permute-start.22 = (s16[1040,128]{1,0:T(8,128)(2,1)S(1)}, s16[1040,128]{1,0:T(8,128)(2,1)S(1)}, u32[]{:S(2)}, u32[]{:S(2)}) collective-permute-start(s16[1040,128]{1,0:T(8,128)(2,1)S(1)} %get-tuple-element.125), channel_id=1, source_target_pairs={{0,8},{2,10},{4,12},{6,14},{8,0},{10,2},{12,4},{14,6},{16,24},{18,... | collective-permute-start | bytes 798728 | tf_op jit(solution)/shard_map/ppermute | solution.py:220
  192.4 1.6 collective-permute-start.21
  194.0 4.3 %collective-permute-done.18.got = s16[528,128]{1,0:T(8,128)(2,1)S(1)} collective-permute-done((s16[528,128]{1,0:T(8,128)(2,1)S(1)}, s16[528,128]{1,0:T(8,128)(2,1)S(1)}, u32[]{:S(2)}, u32[]{:S(2)}) %collective-permute-start.18) | collective-permute-done | bytes 135200 | tf_op jit(solution)/shard_map/ppermute | solution.py:220
  199.1 2.7 %collective-permute-start.24 = (s16[528,128]{1,0:T(8,128)(2,1)S(1)}, s16[528,128]{1,0:T(8,128)(2,1)S(1)}, u32[]{:S(2)}, u32[]{:S(2)}) collective-permute-start(s16[528,128]{1,0:T(8,128)(2,1)S(1)} %get-tuple-element.129), channel_id=1, source_target_pairs={{0,16},{2,18},{4,20},{6,22},{8,24},{10,26},{12,28},{14,30},{16,0},... | collective-permute-start | bytes 405512 | tf_op jit(solution)/shard_map/ppermute | solution.py:220
  202.9 2.8 %collective-permute-done.25.got = s16[528,128]{1,0:T(8,128)(2,1)S(1)} collective-permute-done((s16[528,128]{1,0:T(8,128)(2,1)S(1)}, s16[528,128]{1,0:T(8,128)(2,1)S(1)}, u32[]{:S(2)}, u32[]{:S(2)}) %collective-permute-start.25) | collective-permute-done | bytes 135200 | tf_op jit(solution)/shard_map/ppermute | solution.py:220
  206.1 5.0 %collective-permute-done.26.got = s16[272,128]{1,0:T(8,128)(2,1)S(1)} collective-permute-done((s16[272,128]{1,0:T(8,128)(2,1)S(1)}, s16[272,128]{1,0:T(8,128)(2,1)S(1)}, u32[]{:S(2)}, u32[]{:S(2)}) %collective-permute-start.26) | collective-permute-done | bytes 69664 | tf_op jit(solution)/shard_map/ppermute | solution.py:220
  (201 shorter events, 28.9 us)
Async XLA Ops:
  6.5 1.5 copy-start.68
  6.5 36.7 %all-gather.15.cloned.1.call-start = ((), (), s32[]{:S(2)}) async-start(), calls=%async_computation | async-start | bytes 1572864 | tf_op jit(solution)/shard_map/all_gather | solution.py:144
  9.3 3.2 %copy-start.63 = (bf16[256,7168]{1,0:T(8,128)(2,1)S(1)}, bf16[256,7168]{1,0:T(8,128)(2,1)}, u32[]{:S(2)}) copy-start(bf16[256,7168]{1,0:T(8,128)(2,1)} %param.5) | copy-start | bytes 11010052
  9.6 5.9 %copy-start.67 = (s32[56,8]{0,1:T(8,128)S(1)}, s32[56,8]{0,1:T(8,128)}, u32[]{:S(2)}) copy-start(s32[56,8]{0,1:T(8,128)} %param.6) | copy-start | bytes 5380
  9.6 26.4 %collective-permute-start.1 = (bf16[1024,256]{1,0:T(8,128)(2,1)S(1)}, bf16[1024,256]{1,0:T(8,128)(2,1)S(1)}, u32[]{:S(2)}, u32[]{:S(2)}) collective-permute-start(bf16[1024,256]{1,0:T(8,128)(2,1)S(1)} %bitcast.26), channel_id=1, source_target_pairs={{0,2},{2,0},{4,6},{6,4},{8,10},{10,8},{12,14},{14,12},{16,18},{18,... | collective-permute-start | bytes 1572872 | tf_op jit(solution)/shard_map/ppermute | solution.py:156
  14.3 22.4 %collective-permute-start = (bf16[1024,256]{1,0:T(8,128)(2,1)S(1)}, bf16[1024,256]{1,0:T(8,128)(2,1)S(1)}, u32[]{:S(2)}, u32[]{:S(2)}) collective-permute-start(bf16[1024,256]{1,0:T(8,128)(2,1)S(1)} %bitcast.24), channel_id=1, source_target_pairs={{0,1},{1,0},{2,3},{3,2},{4,5},{5,4},{6,7},{7,6},{8,9},{9,8},{10,11... | collective-permute-start | bytes 1572872 | tf_op jit(solution)/shard_map/ppermute | solution.py:163
  14.3 52.0 %all-gather.17.cloned.1.call-start = ((), (), s32[]{:S(2)}) async-start(), calls=%async_computation.1 | async-start | bytes 1572864 | tf_op jit(solution)/shard_map/all_gather | solution.py:144
  36.0 1.9 collective-permute-start.2
  39.2 4.0 %copy-start.5 = (bf16[256,1024]{1,0:T(8,128)(2,1)S(1)}, bf16[256,1024]{1,0:T(8,128)(2,1)}, u32[]{:S(2)}) copy-start(bf16[256,1024]{1,0:T(8,128)(2,1)} %get-tuple-element.75.own_g) | copy-start | bytes 1572868
  42.6 50.5 %all-gather.19.cloned.1.call-start = ((), (), s32[]{:S(2)}) async-start(), calls=%async_computation.2 | async-start | bytes 1572864 | tf_op jit(solution)/shard_map/all_gather | solution.py:144
  45.5 13.6 %copy-start.22 = (f32[1024,128]{1,0:T(8,128)S(1)}, f32[1024,128]{1,0:T(8,128)}, u32[]{:S(2)}) copy-start(f32[1024,128]{1,0:T(8,128)} %copy-done.20) | copy-start | bytes 1572868
  50.3 16.1 %copy-start.4 = (bf16[256,1024]{1,0:T(8,128)(2,1)S(1)}, bf16[256,1024]{1,0:T(8,128)(2,1)}, u32[]{:S(2)}) copy-start(bf16[256,1024]{1,0:T(8,128)(2,1)} %get-tuple-element.81.own_g) | copy-start | bytes 1572868
  50.3 68.1 %all-gather.21.cloned.1.call-start = ((), (), s32[]{:S(2)}) async-start(), calls=%async_computation.3 | async-start | bytes 1572864 | tf_op jit(solution)/shard_map/all_gather | solution.py:144
  50.4 8.7 %collective-permute-start.3 = (s16[1040,128]{1,0:T(8,128)(2,1)}, s16[1040,128]{1,0:T(8,128)(2,1)S(1)}, u32[]{:S(2)}, u32[]{:S(2)}) collective-permute-start(s16[1040,128]{1,0:T(8,128)(2,1)} %copy-done.58), channel_id=1, source_target_pairs={{0,4},{2,6},{4,0},{6,2},{8,12},{10,14},{12,8},{14,10},{16,20},{18,... | collective-permute-start | bytes 798728 | tf_op jit(solution)/shard_map/ppermute | solution.py:220
  73.5 19.6 %copy-start.3 = (bf16[256,1024]{1,0:T(8,128)(2,1)S(1)}, bf16[256,1024]{1,0:T(8,128)(2,1)}, u32[]{:S(2)}) copy-start(bf16[256,1024]{1,0:T(8,128)(2,1)} %get-tuple-element.89.own_g) | copy-start | bytes 1572868
  73.5 78.8 %all-gather.23.cloned.1.call-start = ((), (), s32[]{:S(2)}) async-start(), calls=%async_computation.4 | async-start | bytes 1572864 | tf_op jit(solution)/shard_map/all_gather | solution.py:144
  73.5 14.1 %collective-permute-start.5 = (s16[2080,128]{1,0:T(8,128)(2,1)}, s16[2080,128]{1,0:T(8,128)(2,1)S(1)}, u32[]{:S(2)}, u32[]{:S(2)}) collective-permute-start(s16[2080,128]{1,0:T(8,128)(2,1)} %copy-done.53), channel_id=1, source_target_pairs={{0,4},{2,6},{4,0},{6,2},{8,12},{10,14},{12,8},{14,10},{16,20},{18,... | collective-permute-start | bytes 1597448 | tf_op jit(solution)/shard_map/ppermute | solution.py:220
  75.1 16.2 %collective-permute-start.4 = (s16[528,128]{1,0:T(8,128)(2,1)}, s16[528,128]{1,0:T(8,128)(2,1)S(1)}, u32[]{:S(2)}, u32[]{:S(2)}) collective-permute-start(s16[528,128]{1,0:T(8,128)(2,1)} %get-tuple-element.78), channel_id=1, source_target_pairs={{0,8},{2,10},{4,12},{6,14},{8,0},{10,2},{12,4},{14,6},{16,24},{18,... | collective-permute-start | bytes 405512 | tf_op jit(solution)/shard_map/ppermute | solution.py:220
  93.1 5.0 %copy-start.44 = (f32[256,128]{1,0:T(8,128)}, f32[256,128]{1,0:T(8,128)S(1)}, u32[]{:S(2)}) copy-start(f32[256,128]{1,0:T(8,128)S(1)} %get-tuple-element.84._.keep) | copy-start | bytes 393220
  99.9 65.2 %all-gather.25.cloned.1.call-start = ((), (), s32[]{:S(2)}) async-start(), calls=%async_computation.5 | async-start | bytes 1572864 | tf_op jit(solution)/shard_map/all_gather | solution.py:144
  99.9 13.3 %collective-permute-start.8 = (s16[2080,128]{1,0:T(8,128)(2,1)}, s16[2080,128]{1,0:T(8,128)(2,1)S(1)}, u32[]{:S(2)}, u32[]{:S(2)}) collective-permute-start(s16[2080,128]{1,0:T(8,128)(2,1)} %copy-done.52), channel_id=1, source_target_pairs={{0,4},{2,6},{4,0},{6,2},{8,12},{10,14},{12,8},{14,10},{16,20},{18,... | collective-permute-start | bytes 1597448 | tf_op jit(solution)/shard_map/ppermute | solution.py:220
  101.4 14.7 %collective-permute-start.7 = (s16[1040,128]{1,0:T(8,128)(2,1)}, s16[1040,128]{1,0:T(8,128)(2,1)S(1)}, u32[]{:S(2)}, u32[]{:S(2)}) collective-permute-start(s16[1040,128]{1,0:T(8,128)(2,1)} %copy-done.57), channel_id=1, source_target_pairs={{0,8},{2,10},{4,12},{6,14},{8,0},{10,2},{12,4},{14,6},{16,24},{18,... | collective-permute-start | bytes 798728 | tf_op jit(solution)/shard_map/ppermute | solution.py:220
  102.9 15.5 %copy-start.2 = (bf16[256,1024]{1,0:T(8,128)(2,1)S(1)}, bf16[256,1024]{1,0:T(8,128)(2,1)}, u32[]{:S(2)}) copy-start(bf16[256,1024]{1,0:T(8,128)(2,1)} %get-tuple-element.97.own_g) | copy-start | bytes 1572868
  102.9 14.7 %collective-permute-start.6 = (s16[272,128]{1,0:T(8,128)(2,1)}, s16[272,128]{1,0:T(8,128)(2,1)S(1)}, u32[]{:S(2)}, u32[]{:S(2)}) collective-permute-start(s16[272,128]{1,0:T(8,128)(2,1)} %copy-done.62), channel_id=1, source_target_pairs={{0,16},{2,18},{4,20},{6,22},{8,24},{10,26},{12,28},{14,30},{16,0},... | collective-permute-start | bytes 208904 | tf_op jit(solution)/shard_map/ppermute | solution.py:220
  115.7 1.9 copy-start.45
  116.2 1.5 copy-start.54
  118.4 1.3 copy-start.31
  124.6 22.8 %copy-start.24 = (f32[1024,128]{1,0:T(8,128)S(1)}, f32[1024,128]{1,0:T(8,128)}, u32[]{:S(2)}) copy-start(f32[1024,128]{1,0:T(8,128)} %copy-done.23) | copy-start | bytes 1572868
  124.6 15.3 %collective-permute-start.11 = (s16[2080,128]{1,0:T(8,128)(2,1)}, s16[2080,128]{1,0:T(8,128)(2,1)S(1)}, u32[]{:S(2)}, u32[]{:S(2)}) collective-permute-start(s16[2080,128]{1,0:T(8,128)(2,1)} %copy-done.50), channel_id=1, source_target_pairs={{0,4},{2,6},{4,0},{6,2},{8,12},{10,14},{12,8},{14,10},{16,20},{18,... | collective-permute-start | bytes 1597448 | tf_op jit(solution)/shard_map/ppermute | solution.py:220
  126.1 32.7 %collective-permute-start.14 = (s16[2080,128]{1,0:T(8,128)(2,1)}, s16[2080,128]{1,0:T(8,128)(2,1)}, u32[]{:S(2)}, u32[]{:S(2)}) collective-permute-start(s16[2080,128]{1,0:T(8,128)(2,1)} %copy-done.51), channel_id=1, source_target_pairs={{0,4},{2,6},{4,0},{6,2},{8,12},{10,14},{12,8},{14,10},{16,20},{18,... | collective-permute-start | bytes 1597448 | tf_op jit(solution)/shard_map/ppermute | solution.py:220
  126.7 25.6 %copy-start.1 = (bf16[256,1024]{1,0:T(8,128)(2,1)S(1)}, bf16[256,1024]{1,0:T(8,128)(2,1)}, u32[]{:S(2)}) copy-start(bf16[256,1024]{1,0:T(8,128)(2,1)} %get-tuple-element.105.own_g) | copy-start | bytes 1572868
  126.7 20.7 %collective-permute-start.10 = (s16[1040,128]{1,0:T(8,128)(2,1)}, s16[1040,128]{1,0:T(8,128)(2,1)S(1)}, u32[]{:S(2)}, u32[]{:S(2)}) collective-permute-start(s16[1040,128]{1,0:T(8,128)(2,1)} %copy-done.54), channel_id=1, source_target_pairs={{0,8},{2,10},{4,12},{6,14},{8,0},{10,2},{12,4},{14,6},{16,24},{18,... | collective-permute-start | bytes 798728 | tf_op jit(solution)/shard_map/ppermute | solution.py:220
  141.2 1.3 copy-start.13
  142.4 9.0 %copy-start.43 = (f32[512,128]{1,0:T(8,128)S(1)}, f32[512,128]{1,0:T(8,128)}, u32[]{:S(2)}) copy-start(f32[512,128]{1,0:T(8,128)} %copy-done.42) | copy-start | bytes 786436
  143.6 7.9 %copy-start.27 = (f32[1024,128]{1,0:T(8,128)}, f32[1024,128]{1,0:T(8,128)S(1)}, u32[]{:S(2)}) copy-start(f32[1024,128]{1,0:T(8,128)S(1)} %get-tuple-element.99._.keep) | copy-start | bytes 1572868
  143.6 16.9 %collective-permute-start.13 = (s16[1040,128]{1,0:T(8,128)(2,1)}, s16[1040,128]{1,0:T(8,128)(2,1)}, u32[]{:S(2)}, u32[]{:S(2)}) collective-permute-start(s16[1040,128]{1,0:T(8,128)(2,1)} %get-tuple-element.102), channel_id=1, source_target_pairs={{0,8},{2,10},{4,12},{6,14},{8,0},{10,2},{12,4},{14,6},{16,24},{18,... | collective-permute-start | bytes 798728 | tf_op jit(solution)/shard_map/ppermute | solution.py:220
  145.0 6.5 %collective-permute-start.9 = (s16[528,128]{1,0:T(8,128)(2,1)}, s16[528,128]{1,0:T(8,128)(2,1)S(1)}, u32[]{:S(2)}, u32[]{:S(2)}) collective-permute-start(s16[528,128]{1,0:T(8,128)(2,1)} %copy-done.59), channel_id=1, source_target_pairs={{0,16},{2,18},{4,20},{6,22},{8,24},{10,26},{12,28},{14,30},{16,0},... | collective-permute-start | bytes 405512 | tf_op jit(solution)/shard_map/ppermute | solution.py:220
  148.4 14.2 %collective-permute-start.12 = (s16[528,128]{1,0:T(8,128)(2,1)}, s16[528,128]{1,0:T(8,128)(2,1)S(1)}, u32[]{:S(2)}, u32[]{:S(2)}) collective-permute-start(s16[528,128]{1,0:T(8,128)(2,1)} %get-tuple-element.101), channel_id=1, source_target_pairs={{0,16},{2,18},{4,20},{6,22},{8,24},{10,26},{12,28},{14,30},{16,0},... | collective-permute-start | bytes 405512 | tf_op jit(solution)/shard_map/ppermute | solution.py:220
  153.5 5.4 %copy-start.14 = (f32[2048,128]{1,0:T(8,128)S(1)}, f32[2048,128]{1,0:T(8,128)}, u32[]{:S(2)}) copy-start(f32[2048,128]{1,0:T(8,128)} %copy-done.12) | copy-start | bytes 3145732
  157.4 4.6 %copy-start.18 = (f32[2048,128]{1,0:T(8,128)}, f32[2048,128]{1,0:T(8,128)S(1)}, u32[]{:S(2)}) copy-start(f32[2048,128]{1,0:T(8,128)S(1)} %get-tuple-element.111._.keep) | copy-start | bytes 3145732
  157.4 3.1 %copy-start.28 = (f32[1024,128]{1,0:T(8,128)S(1)}, f32[1024,128]{1,0:T(8,128)}, u32[]{:S(2)}) copy-start(f32[1024,128]{1,0:T(8,128)} %copy-done.27) | copy-start | bytes 1572868
  157.4 25.2 %collective-permute-start.17 = (s16[2080,128]{1,0:T(8,128)(2,1)}, s16[2080,128]{1,0:T(8,128)(2,1)}, u32[]{:S(2)}, u32[]{:S(2)}) collective-permute-start(s16[2080,128]{1,0:T(8,128)(2,1)} %get-tuple-element.112), channel_id=1, source_target_pairs={{0,4},{2,6},{4,0},{6,2},{8,12},{10,14},{12,8},{14,10},{16,20},{18,... | collective-permute-start | bytes 1597448 | tf_op jit(solution)/shard_map/ppermute | solution.py:220
  158.9 4.5 %copy-start.38 = (f32[512,128]{1,0:T(8,128)S(1)}, f32[512,128]{1,0:T(8,128)}, u32[]{:S(2)}) copy-start(f32[512,128]{1,0:T(8,128)} %copy-done.37) | copy-start | bytes 786436
  158.9 6.2 %copy-start = (bf16[256,1024]{1,0:T(8,128)(2,1)S(1)}, bf16[256,1024]{1,0:T(8,128)(2,1)}, u32[]{:S(2)}) copy-start(bf16[256,1024]{1,0:T(8,128)(2,1)} %get-tuple-element.113.own_g) | copy-start | bytes 1572868
  160.5 2.2 %copy-start.25 = (f32[1024,128]{1,0:T(8,128)}, f32[1024,128]{1,0:T(8,128)S(1)}, u32[]{:S(2)}) copy-start(f32[1024,128]{1,0:T(8,128)S(1)} %get-tuple-element.107._.keep) | copy-start | bytes 1572868
  160.5 2.9 %copy-start.55 = (s16[1040,128]{1,0:T(8,128)(2,1)}, s16[1040,128]{1,0:T(8,128)(2,1)S(1)}, u32[]{:S(2)}) copy-start(s16[1040,128]{1,0:T(8,128)(2,1)S(1)} %get-tuple-element.110) | copy-start | bytes 798724
  166.3 3.7 %copy-start.56 = (s16[1040,128]{1,0:T(8,128)(2,1)S(1)}, s16[1040,128]{1,0:T(8,128)(2,1)}, u32[]{:S(2)}) copy-start(s16[1040,128]{1,0:T(8,128)(2,1)} %copy-done.55) | copy-start | bytes 798724
  166.3 6.2 %copy-start.61 = (s16[528,128]{1,0:T(8,128)(2,1)S(1)}, s16[528,128]{1,0:T(8,128)(2,1)}, u32[]{:S(2)}) copy-start(s16[528,128]{1,0:T(8,128)(2,1)} %copy-done.60) | copy-start | bytes 405508
  166.3 16.3 %copy-start.19 = (f32[2048,128]{1,0:T(8,128)S(1)}, f32[2048,128]{1,0:T(8,128)}, u32[]{:S(2)}) copy-start(f32[2048,128]{1,0:T(8,128)} %copy-done.18) | copy-start | bytes 3145732
  169.3 14.9 %copy-start.26 = (f32[1024,128]{1,0:T(8,128)S(1)}, f32[1024,128]{1,0:T(8,128)}, u32[]{:S(2)}) copy-start(f32[1024,128]{1,0:T(8,128)} %copy-done.25) | copy-start | bytes 1572868
  169.3 19.1 %collective-permute-start.20 = (s16[2080,128]{1,0:T(8,128)(2,1)S(1)}, s16[2080,128]{1,0:T(8,128)(2,1)S(1)}, u32[]{:S(2)}, u32[]{:S(2)}) collective-permute-start(s16[2080,128]{1,0:T(8,128)(2,1)S(1)} %get-tuple-element.119), channel_id=1, source_target_pairs={{0,4},{2,6},{4,0},{6,2},{8,12},{10,14},{12,8},{14,10},{16,20},{18,... | collective-permute-start | bytes 1597448 | tf_op jit(solution)/shard_map/ppermute | solution.py:220
  169.9 14.3 %collective-permute-start.16 = (s16[1040,128]{1,0:T(8,128)(2,1)S(1)}, s16[1040,128]{1,0:T(8,128)(2,1)S(1)}, u32[]{:S(2)}, u32[]{:S(2)}) collective-permute-start(s16[1040,128]{1,0:T(8,128)(2,1)S(1)} %copy-done.56), channel_id=1, source_target_pairs={{0,8},{2,10},{4,12},{6,14},{8,0},{10,2},{12,4},{14,6},{16,24},{18,... | collective-permute-start | bytes 798728 | tf_op jit(solution)/shard_map/ppermute | solution.py:220
  172.5 12.1 %collective-permute-start.15 = (s16[528,128]{1,0:T(8,128)(2,1)S(1)}, s16[528,128]{1,0:T(8,128)(2,1)S(1)}, u32[]{:S(2)}, u32[]{:S(2)}) collective-permute-start(s16[528,128]{1,0:T(8,128)(2,1)S(1)} %copy-done.61), channel_id=1, source_target_pairs={{0,16},{2,18},{4,20},{6,22},{8,24},{10,26},{12,28},{14,30},{16,0},... | collective-permute-start | bytes 405512 | tf_op jit(solution)/shard_map/ppermute | solution.py:220
  182.5 2.1 copy-start.36
  182.5 2.2 copy-start.49
  184.1 7.9 %collective-permute-start.19 = (s16[1040,128]{1,0:T(8,128)(2,1)S(1)}, s16[1040,128]{1,0:T(8,128)(2,1)S(1)}, u32[]{:S(2)}, u32[]{:S(2)}) collective-permute-start(s16[1040,128]{1,0:T(8,128)(2,1)S(1)} %get-tuple-element.118), channel_id=1, source_target_pairs={{0,8},{2,10},{4,12},{6,14},{8,0},{10,2},{12,4},{14,6},{16,24},{18,... | collective-permute-start | bytes 798728 | tf_op jit(solution)/shard_map/ppermute | solution.py:220
  186.5 11.9 %collective-permute-start.23 = (s16[1040,128]{1,0:T(8,128)(2,1)S(1)}, s16[1040,128]{1,0:T(8,128)(2,1)S(1)}, u32[]{:S(2)}, u32[]{:S(2)}) collective-permute-start(s16[1040,128]{1,0:T(8,128)(2,1)S(1)} %get-tuple-element.126), channel_id=1, source_target_pairs={{0,4},{2,6},{4,0},{6,2},{8,12},{10,14},{12,8},{14,10},{16,20},{18,... | collective-permute-start | bytes 798728 | tf_op jit(solution)/shard_map/ppermute | solution.py:220
  188.0 10.3 %collective-permute-start.18 = (s16[528,128]{1,0:T(8,128)(2,1)S(1)}, s16[528,128]{1,0:T(8,128)(2,1)S(1)}, u32[]{:S(2)}, u32[]{:S(2)}) collective-permute-start(s16[528,128]{1,0:T(8,128)(2,1)S(1)} %get-tuple-element.117), channel_id=1, source_target_pairs={{0,16},{2,18},{4,20},{6,22},{8,24},{10,26},{12,28},{14,30},{16,0},... | collective-permute-start | bytes 405512 | tf_op jit(solution)/shard_map/ppermute | solution.py:220
  188.9 9.9 %collective-permute-start.22 = (s16[1040,128]{1,0:T(8,128)(2,1)S(1)}, s16[1040,128]{1,0:T(8,128)(2,1)S(1)}, u32[]{:S(2)}, u32[]{:S(2)}) collective-permute-start(s16[1040,128]{1,0:T(8,128)(2,1)S(1)} %get-tuple-element.125), channel_id=1, source_target_pairs={{0,8},{2,10},{4,12},{6,14},{8,0},{10,2},{12,4},{14,6},{16,24},{18,... | collective-permute-start | bytes 798728 | tf_op jit(solution)/shard_map/ppermute | solution.py:220
  192.4 10.4 %collective-permute-start.21 = (s16[528,128]{1,0:T(8,128)(2,1)S(1)}, s16[528,128]{1,0:T(8,128)(2,1)S(1)}, u32[]{:S(2)}, u32[]{:S(2)}) collective-permute-start(s16[528,128]{1,0:T(8,128)(2,1)S(1)} %get-tuple-element.124), channel_id=1, source_target_pairs={{0,16},{2,18},{4,20},{6,22},{8,24},{10,26},{12,28},{14,30},{16,0},... | collective-permute-start | bytes 405512 | tf_op jit(solution)/shard_map/ppermute | solution.py:220
  198.7 7.0 %collective-permute-start.25 = (s16[528,128]{1,0:T(8,128)(2,1)S(1)}, s16[528,128]{1,0:T(8,128)(2,1)S(1)}, u32[]{:S(2)}, u32[]{:S(2)}) collective-permute-start(s16[528,128]{1,0:T(8,128)(2,1)S(1)} %get-tuple-element.130), channel_id=1, source_target_pairs={{0,8},{2,10},{4,12},{6,14},{8,0},{10,2},{12,4},{14,6},{16,24},{18,... | collective-permute-start | bytes 405512 | tf_op jit(solution)/shard_map/ppermute | solution.py:220
  199.1 6.8 %collective-permute-start.24 = (s16[528,128]{1,0:T(8,128)(2,1)S(1)}, s16[528,128]{1,0:T(8,128)(2,1)S(1)}, u32[]{:S(2)}, u32[]{:S(2)}) collective-permute-start(s16[528,128]{1,0:T(8,128)(2,1)S(1)} %get-tuple-element.129), channel_id=1, source_target_pairs={{0,16},{2,18},{4,20},{6,22},{8,24},{10,26},{12,28},{14,30},{16,0},... | collective-permute-start | bytes 405512 | tf_op jit(solution)/shard_map/ppermute | solution.py:220
  205.8 5.3 %collective-permute-start.26 = (s16[272,128]{1,0:T(8,128)(2,1)S(1)}, s16[272,128]{1,0:T(8,128)(2,1)S(1)}, u32[]{:S(2)}, u32[]{:S(2)}) collective-permute-start(s16[272,128]{1,0:T(8,128)(2,1)S(1)} %get-tuple-element.132), channel_id=1, source_target_pairs={{0,16},{2,18},{4,20},{6,22},{8,24},{10,26},{12,28},{14,30},{16,0},... | collective-permute-start | bytes 208904 | tf_op jit(solution)/shard_map/ppermute | solution.py:220
  206.0 5.1 %copy-start.66 = (f32[56,64,128]{2,1,0:T(8,128)}, f32[56,64,128]{2,1,0:T(8,128)S(1)}, u32[]{:S(2)}) copy-start(f32[56,64,128]{2,1,0:T(8,128)S(1)} %constant_dynamic-update-slice_fusion.1) | copy-start | bytes 5505028
  (38 other events, 35.4 us)
Sparse Core Ops, SparseCore 0:
  14.5 27.1 all-gather.14
  43.1 23.1 all-gather.16
  67.9 21.2 all-gather.18
  90.6 21.2 all-gather.20
  113.4 21.2 all-gather.22
  136.1 21.2 all-gather.24

commit v3 on v0

v3 whole, which is shorter than its diff:
```python
import functools

import jax
import jax.numpy as jnp
from jax import lax
from jax.experimental import pallas as pl
from jax.experimental.pallas import tpu as pltpu
from jax.sharding import PartitionSpec as P

BLOCK = 128
LEVELS = 32700.0
STEPS = 128.0
SMALLEST = 2.0**-110
PAD = 16
VMEM_LIMIT = 16 * 1024 * 1024


def pad16(rows):
    return -(-rows // 16) * 16


def params():
    return pltpu.CompilerParams(vmem_limit_bytes=VMEM_LIMIT)


def encode(values):
    largest = jnp.max(jnp.abs(values), axis=0, keepdims=True)
    power = jnp.ceil(jnp.log2(jnp.maximum(largest, SMALLEST)) * STEPS)
    codes = jnp.round(values * (jnp.exp2(power * (-1.0 / STEPS)) * LEVELS))
    return codes.astype(jnp.int32).astype(jnp.int16), power


def send_powers(sent, powers, body):
    sent[pl.ds(body, powers.shape[0]), :] = powers[...].astype(jnp.int32).astype(jnp.int16)


def read_scales(got, scales, body):
    coded = got[pl.ds(body, scales.shape[0]), :].astype(jnp.int32).astype(jnp.float32)
    scales[...] = jnp.exp2(coded * (1.0 / STEPS)) * (1.0 / LEVELS)


def each(width, column):
    at_once = max(n for n in (1, 2, 3) if width % n == 0)

    def step(i, _):
        for j in range(at_once):
            column(i * at_once + j)
        return 0

    lax.fori_loop(0, width // at_once, step, 0)


def prepare_kernel(rows, me, lengths, activations, own, other):
    slots, features = activations.shape
    live = lengths[0, 0]
    for i in range(1, lengths.shape[1]):
        live = live + lengths[0, i]
    keep = lax.broadcasted_iota(jnp.int32, (BLOCK, slots), 1) < live
    for b in range(features // BLOCK):
        block = activations[:, b * BLOCK : (b + 1) * BLOCK].astype(jnp.float32).T
        block = jnp.where(keep, block, 0.0).astype(activations.dtype)
        for p in range(BLOCK // rows):
            to = pl.ds((b * (BLOCK // rows) + p) // 2 * rows, rows)
            piece = block[p * rows : (p + 1) * rows]

            @pl.when(me[0] % 2 == p % 2)
            def _():
                own[to, :] = piece

            @pl.when(me[0] % 2 != p % 2)
            def _():
                other[to, :] = piece


def multiply_kernel(width, rows, height, order, pairs, begins, me, picks, *refs):
    lefts, grads = refs[: len(pairs)], refs[len(pairs) : -4]
    keep, sent, powers = refs[-3:]
    half = len(order) // 2
    per_block = height // rows
    slots = lefts[0].shape[1]

    def column(c):
        lanes = [pl.ds(pl.multiple_of((begin + c) * BLOCK, BLOCK), BLOCK) for begin in begins]

        def product(masks):
            starts = []
            for mask in masks:
                piece = (me[0] ^ mask) // 2
                entry, part = piece // per_block, piece % per_block
                starts.append((mask & 1, pl.multiple_of(picks[c, entry] * height + part * rows, rows)))
            total = None
            for t, grad in enumerate(grads):
                left = [lefts[pairs.index((x, t))][pl.ds(s, rows), :] for x, s in starts]
                term = jnp.dot(
                    jnp.concatenate(left, axis=0), grad[:slots, lanes[t]], preferred_element_type=jnp.float32
                )
                total = term if total is None else total + term
            return total

        away = product(order[half:])
        for j in range(half):
            codes, power = encode(away[j * rows : (j + 1) * rows])
            sent[pl.ds(pl.multiple_of((c * half + j) * rows, rows), rows), :] = codes
            powers[pl.ds(c * half + j, 1), :] = power
        keep[pl.ds(pl.multiple_of(c * (half * rows), half * rows), half * rows), :] = product(order[:half])

    each(width, column)
    send_powers(sent, powers, width * half * rows)


def combine_kernel(sources, rows, pieces, coded, factor, *refs):
    count = sum(1 + has for _, has in sources)
    inputs, refs = list(refs[:count]), refs[count + 1 :]
    half = pieces // 2
    outs = 2 if coded else 1
    out, scales = refs[0], list(refs[outs:])
    if coded:
        sent, powers = refs[1], scales.pop()
    begin = 0
    for width, has in sources:
        keep = inputs.pop(0)
        got, scale = (inputs.pop(0), scales.pop(0)) if has else (None, None)
        if has:
            read_scales(got, scale, width * pieces * rows)

        def column(c, keep=keep, got=got, scale=scale, begin=begin):
            def summed(j):
                at = pl.ds(pl.multiple_of((c * pieces + j) * rows, rows), rows)
                if got is None:
                    return keep[at, :]
                return keep[at, :] + got[at, :].astype(jnp.int32).astype(jnp.float32) * scale[pl.ds(c * pieces + j, 1), :]

            if pieces == 1:
                out[begin + c] = summed(0) * factor
            elif coded:
                for j in range(half):
                    to = pl.ds(pl.multiple_of(((begin + c) * half + j) * rows, rows), rows)
                    codes, power = encode(summed(half + j))
                    sent[to, :] = codes
                    powers[pl.ds((begin + c) * half + j, 1), :] = power
                    out[to, :] = summed(j)
            else:
                for j in range(pieces):
                    out[pl.ds(pl.multiple_of(((begin + c) * pieces + j) * rows, rows), rows), :] = summed(j)

        each(width, column)
        begin += width
    if coded:
        send_powers(sent, powers, begin * half * rows)


def plan_of(columns, depth):
    if depth != 4 or columns % 56 != 0:
        return [columns], [list(range(1, depth))], [[0]], [("multiply", 0)] + [("step", 0)] * (depth - 1)
    widths = [8, 10, 12, 12, 8, 6]
    paths = [[1, 3, 2, 0], [2, 1, 3, 0], [1, 3, 2], [2, 1, 3], [1, 2, 3], [1, 2, 3]]
    messages = [[2], [3], [4], [5]]
    work = [
        ("multiply", 0),
        ("multiply", 1),
        ("multiply", 2),
        ("step", 0),
        ("step", 1),
        ("multiply", 3),
        ("step", 2),
        ("multiply", 4),
        ("step", 0),
        ("multiply", 5),
        ("step", 1),
        ("step", 3),
        ("step", 2),
        ("step", 4),
        ("step", 0),
        ("step", 3),
        ("step", 0),
        ("step", 1),
        ("step", 5),
        ("step", 4),
        ("step", 3),
        ("step", 5),
        ("step", 2),
        ("step", 1),
        ("step", 4),
        ("step", 5),
    ]
    return [w * columns // 56 for w in widths], paths, messages, work


def masks_of(bits):
    masks = [0]
    for bit in reversed(bits):
        masks = masks + [m | 1 << bit for m in masks]
    return masks


def shards(owners, groups, activations, out_grad, row_blocks, doc_lengths):
    slots, features = activations.shape
    columns, entries = row_blocks.shape
    rows = entries * BLOCK // owners
    per_block = BLOCK // rows
    height = BLOCK // 2
    factor = 1.0 / float(slots * owners) ** 0.5
    widths, paths, messages, work = plan_of(columns, owners.bit_length() - 1)
    count = len(widths)
    starts = [sum(widths[:i]) for i in range(count)]

    me = lax.axis_index("dp")
    half, place = me % 2, me.astype(jnp.int32).reshape(1)

    def swap(sent, bit):
        return lax.ppermute(sent, "dp", [(o, o ^ (1 << bit)) for o in range(owners)])

    def fetch(after):
        chunks = messages[len(near_g)]
        piece = out_grad[:, starts[chunks[0]] * BLOCK : (starts[chunks[-1]] + widths[chunks[-1]]) * BLOCK]
        piece = jnp.pad(piece, ((0, PAD), (0, 0)))
        piece, after = lax.optimization_barrier((piece, after))
        near_g.append(swap(piece, 0))
        return after

    vmem = pl.BlockSpec(memory_space=pltpu.VMEM)
    smem = pl.BlockSpec(memory_space=pltpu.SMEM)
    anywhere = pl.BlockSpec(memory_space=pl.ANY)

    own, other = pl.pallas_call(
        functools.partial(prepare_kernel, rows),
        out_shape=[jax.ShapeDtypeStruct((features // 2, slots), activations.dtype)] * 2,
        in_specs=[smem, smem, vmem],
        out_specs=[vmem, vmem],
        compiler_params=params(),
        name="prepare",
    )(place, doc_lengths, activations)
    near = swap(other, 0)
    near_g = []
    own = fetch(own)
    near, near_g[0] = lax.optimization_barrier((near, near_g[0]))
    if len(messages) > 1:
        own = fetch(own)

    def spread(part):
        parts = [part] + [
            lax.ppermute(part, "mp", [(g, (g + s) % groups) for g in range(groups)]) for s in range(1, groups)
        ]
        return jnp.concatenate(parts, axis=0)

    own_t, other_t, near_t = spread(own), spread(other), spread(near)
    blocks = features // BLOCK
    picks = (lax.axis_index("mp") - row_blocks // blocks) % groups * blocks + row_blocks % blocks

    def coded(width, n):
        return jax.ShapeDtypeStruct((width * n * rows + pad16(width * n), BLOCK), jnp.int16)

    def sums(width, n):
        return jax.ShapeDtypeStruct((width * n * rows, BLOCK), jnp.float32)

    def scale(width, n):
        return pltpu.VMEM((pad16(width * n), BLOCK), jnp.float32)

    def multiply(i, last):
        width, order = widths[i], masks_of(paths[i])
        n = len(order) // 2
        begins = [starts[i]]
        if 0 in paths[i]:
            pairs, lefts, grads = ((0, 0), (1, 0)), [own_t, other_t], [out_grad]
        else:
            pairs, lefts = ((0, 0), (0, 1)), [own_t, near_t]
            at = next(m for m, chunks in enumerate(messages) if i in chunks)
            grads = [out_grad, near_g[at]]
            begins.append(starts[i] - starts[messages[at][0]])
        return pl.pallas_call(
            functools.partial(multiply_kernel, width, rows, height, order, pairs, begins),
            out_shape=[sums(width, n), coded(width, n)],
            in_specs=[smem, smem] + [vmem] * (len(lefts) + len(grads)) + [anywhere],
            out_specs=[vmem, vmem],
            scratch_shapes=[scale(width, n)],
            compiler_params=params(),
            name="multiply",
        )(place, picks[starts[i] : starts[i] + width], *lefts, *grads, last)

    def combine(sources, n, encoded, last):
        width = sum(w for w, *_ in sources)
        arrays = [a for _, *pair in sources for a in pair]
        scratch = [scale(w, n) for w, *pair in sources if len(pair) == 2]
        if n == 1:
            outs = [jax.ShapeDtypeStruct((width, rows, BLOCK), jnp.float32)]
        elif encoded:
            outs = [sums(width, n // 2), coded(width, n // 2)]
            scratch.append(scale(width, n // 2))
        else:
            outs = [sums(width, n)]
        shapes = tuple((w, len(pair) == 2) for w, *pair in sources)
        return pl.pallas_call(
            functools.partial(combine_kernel, shapes, rows, n, encoded and n > 1, factor),
            out_shape=outs,
            in_specs=[vmem] * len(arrays) + [anywhere],
            out_specs=[vmem] * len(outs),
            scratch_shapes=scratch,
            compiler_params=params(),
            name="combine",
        )(*arrays, last)

    state, outputs, last = {}, {}, place
    for what, i, *more in work:
        if what == "multiply":
            kept, sent = multiply(i, last)
            last = kept
            if len(near_g) < len(messages) and any(i == chunks[0] for chunks in messages):
                kept = fetch(kept)
            state[i] = 1, [(widths[i], kept, swap(sent, paths[i][0]))]
            continue
        if what == "send":
            step, [(width, kept, sent)] = state[i]
            sent, last = lax.optimization_barrier((sent, last))
            state[i] = step, [(width, kept, swap(sent, paths[i][step - 1]))]
            continue
        step, sources = state.pop(i)
        for j in more:
            sources = sources + state.pop(j)[1]
        width = sum(w for w, *_ in sources)
        n = 1 << (len(paths[i]) - step)
        result = combine(sources, n, what != "add", last)
        last = result[0]
        if n == 1:
            outputs[i] = result[0]
        elif what == "add":
            state[i] = step, [(width, result[0])]
        elif what == "hold":
            state[i] = step + 1, [(width, *result)]
        else:
            state[i] = step + 1, [(width, result[0], swap(result[1], paths[i][step]))]
    return jnp.concatenate([outputs[i] for i in sorted(outputs)], axis=0)


def solution(mesh):
    in_specs = (P("dp", "mp"), P("dp", "mp"), P("mp", None), P("dp", None))
    out_specs = P("mp", "dp", None)
    body = functools.partial(shards, mesh.shape["dp"], mesh.shape["mp"])
    return jax.shard_map(body, mesh=mesh, in_specs=in_specs, out_specs=out_specs, check_vma=False)
```

time: 1070 us -> 144 us (0.13)
  blocking collectives: 641 us -> 0 us
  loops' own time: 148 us -> 0 us
  matrix products: 109 us -> 0 us
  local copies, waits for them, and re-layouts: 101 us -> 9.25 us
  waiting for transfers between devices: 6.48 us -> 68.2 us
  other arithmetic: 42.4 us -> 0.79 us
  starting transfers between devices: 0.01 us -> 41 us
  Pallas kernels: 0 us -> 23.7 us
  between operations: 13.4 us -> 0.45 us
    all_to_all x1 -> x0, blocking collectives: 641 us -> none  [shards(): lax.all_to_all(pieces, 'dp', split_axis=1, concat_axis=1, tiled=True)]
    another operation x1 -> x0, loops' own time: 148 us -> none  [block_sums(): return lax.map(one_column, jnp.arange(column_count, dtype=jnp.int32))]
    dot_general x56 -> x0, matrix products: 109 us -> none  [one_column(): lax.dot_general(chosen, piece, (((0,), (0,)), ((), ())), preferred_elemen...]
    ppermute x0 -> x28, waiting for transfers between devices: none -> 68.2 us  [the longest x25 68.2 us: swap(): return lax.ppermute(sent, 'dp', [(o, o ^ 1 << bit) for o in range(owners)])]
    gather x112 -> x0, local copies, waits for them, and re-layouts: 48.2 us -> none  [one_column(): jnp.take(blocked, row_blocks[column], axis=1).reshape(slot_count, -1)]
    ppermute x0 -> x28, starting transfers between devices: none -> 41 us  [the longest x25 40.2 us: swap(): return lax.ppermute(sent, 'dp', [(o, o ^ 1 << bit) for o in range(owners)])]
    dynamic_slice x56 -> x0, local copies, waits for them, and re-layouts: 32.6 us -> none  [block_sums(): return lax.map(one_column, jnp.arange(column_count, dtype=jnp.int32))]
    pallas_call x0 -> x27, Pallas kernels: none -> 23.7 us  [the longest x6 15.8 us: multiply(): pl.pallas_call(functools.partial(multiply_kernel, width, rows, height, or...]
  transfers between devices with their start and end apart: 1 -> 28, of which waited for: 1 -> 15; matrix products, arithmetic and copies ran while one was open for 1% -> 5% of each run, Pallas kernels for 0% -> 15%
where the time goes in v3:
time: 144 us; the launch traced here: 143 us
  waiting for transfers between devices  68.2 us (47%)
  starting transfers between devices  41 us (28%)
  Pallas kernels  23.7 us (16%)
  local copies, waits for them, and re-layouts  9.25 us (6%)
    ppermute x25, waiting for transfers between devices, swap(): return lax.ppermute(sent, 'dp', [(o, o ^ 1 << bit) for o in range(owners)])  68.2 us
    ppermute x25, starting transfers between devices, swap(): return lax.ppermute(sent, 'dp', [(o, o ^ 1 << bit) for o in range(owners)])  40.2 us
    pallas_call x6, Pallas kernels, multiply(): pl.pallas_call(functools.partial(multiply_kernel, width, rows, height, or...  15.8 us
    pallas_call x20, Pallas kernels, combine(): pl.pallas_call(functools.partial(combine_kernel, shapes, rows, n, encoded...  5.31 us
    unnamed x17, local copies, waits for them, and re-layouts  4.53 us
  transfers between devices with their start and end apart: 28, of which 15 were waited for; matrix products, arithmetic and copies ran while one was open for 5% of the time, Pallas kernels for 15%

profile of v3, /device:TPU:0, one launch (start us, length us, event | category | flops | bytes accessed | tf_op | source)
XLA Modules:
  0.0 143.4 jit_solution(16289479439758114008)
XLA Ops:
  0.0 1.2 copy-done.1
  1.2 0.7 copy-done.2
  1.9 2.7 %prepare.1 = (bf16[1024,256]{1,0:T(8,128)(2,1)S(1)}, bf16[1024,256]{1,0:T(8,128)(2,1)S(1)}) custom-call(s32[1]{0:T(128)} %bitcast.me.refs_3_, s32[1,4]{1,0:T(1,128)S(1)} %copy-done.2, bf16[256,2048]{1,0:T(8,128)(2,1)S(1)} %copy-done.1), custom_call_target="tpu_custom_call" | custom-call | tf_op jit(solution)/shard_map/prepare/pallas_call | solution.py:225
  4.6 0.5 collective-permute-start.1
  5.1 2.6 %collective-permute-start.3 = (bf16[1024,256]{1,0:T(8,128)(2,1)S(1)}, bf16[1024,256]{1,0:T(8,128)(2,1)}, u32[]{:S(2)}, u32[]{:S(2)}) collective-permute-start(bf16[1024,256]{1,0:T(8,128)(2,1)S(1)} %get-tuple-element.60), channel_id=1, source_target_pairs={{0,2},{2,0},{4,6},{6,4},{8,10},{10,8},{12,14},{14,12},{16,18},{18,... | collective-permute-start | bytes 1572872 | tf_op jit(solution)/shard_map/ppermute | solution.py:211
  7.6 1.5 %fusion.5 = (bf16[256,1536]{1,0:T(8,128)(2,1)S(1)}, bf16[256,1536]{1,0:T(8,128)(2,1)S(1)}) fusion(bf16[256,7168]{1,0:T(8,128)(2,1)} %refs_2_.11), kind=kLoop, calls=%fused_computation.26 | loop fusion | bytes 3145728 | tf_op jit(solution)/shard_map/slice | solution.py:215
  9.2 0.2 collective-permute-start
  9.5 0.3 collective-permute-start.4
  9.7 1.4 copy.5
  11.1 0.8 fusion.3
  12.0 1.2 constant_dynamic-update-slice_fusion.refs_0_
  13.3 1.1 constant_dynamic-update-slice_fusion.2.refs_1_
  14.4 2.5 %multiply.6 = (f32[4096,128]{1,0:T(8,128)S(1)}, s16[4160,128]{1,0:T(8,128)(2,1)S(1)}) custom-call(s32[1]{0:T(128)} %bitcast.me.refs_3_, s32[8,8]{1,0:T(8,128)S(1)} %get-tuple-element.114.picks, bf16[2048,256]{1,0:T(8,128)(2,1)S(1)} %constant_dynamic-update-slice_fusion.refs_0_, bf16[2048,256]{1,0:T(8,128)(2,1)S(1)} %constant_dynamic-update-slice_fusion.2.refs_1_, ...), custom_call_target="tpu_custom_call" | custom-call | tf_op jit(solution)/shard_map/multiply/pallas_call | solution.py:270
  16.9 3.1 %multiply.7 = (f32[5120,128]{1,0:T(8,128)S(1)}, s16[5200,128]{1,0:T(8,128)(2,1)S(1)}) custom-call(s32[1]{0:T(128)} %bitcast.me.refs_3_, s32[10,8]{1,0:T(8,128)S(1)} %slice.42.picks, bf16[2048,256]{1,0:T(8,128)(2,1)S(1)} %constant_dynamic-update-slice_fusion.refs_0_, bf16[2048,256]{1,0:T(8,128)(2,1)S(1)} %constant_dynamic-update-slice_fusion.2.refs_1_, ...), custom_call_target="tpu_custom_call" | custom-call | tf_op jit(solution)/shard_map/multiply/pallas_call | solution.py:270
  20.0 1.9 %collective-permute-start.10 = (s16[5200,128]{1,0:T(8,128)(2,1)S(1)}, s16[5200,128]{1,0:T(8,128)(2,1)S(1)}, u32[]{:S(2)}, u32[]{:S(2)}) collective-permute-start(s16[5200,128]{1,0:T(8,128)(2,1)S(1)} %get-tuple-element.74), channel_id=1, source_target_pairs={{0,8},{2,10},{4,12},{6,14},{8,0},{10,2},{12,4},{14,6},{16,24},{18,... | collective-permute-start | bytes 3993608 | tf_op jit(solution)/shard_map/ppermute | solution.py:211
  21.9 1.5 %collective-permute-start.2 = (s16[4160,128]{1,0:T(8,128)(2,1)S(1)}, s16[4160,128]{1,0:T(8,128)(2,1)S(1)}, u32[]{:S(2)}, u32[]{:S(2)}) collective-permute-start(s16[4160,128]{1,0:T(8,128)(2,1)S(1)} %get-tuple-element.62), channel_id=1, source_target_pairs={{0,4},{2,6},{4,0},{6,2},{8,12},{10,14},{12,8},{14,10},{16,20},{18,... | collective-permute-start | bytes 3194888 | tf_op jit(solution)/shard_map/ppermute | solution.py:211
  23.4 14.6 %collective-permute-done.4.refs_3_ = bf16[272,1536]{1,0:T(8,128)(2,1)S(1)} collective-permute-done((bf16[272,1536]{1,0:T(8,128)(2,1)S(1)}, bf16[272,1536]{1,0:T(8,128)(2,1)S(1)}, u32[]{:S(2)}, u32[]{:S(2)}) %collective-permute-start.4) | collective-permute-done | bytes 835616 | tf_op jit(solution)/shard_map/ppermute | solution.py:211
  38.1 1.8 %collective-permute-start.9 = (bf16[272,1536]{1,0:T(8,128)(2,1)S(1)}, bf16[272,1536]{1,0:T(8,128)(2,1)S(1)}, u32[]{:S(2)}, u32[]{:S(2)}) collective-permute-start(bf16[272,1536]{1,0:T(8,128)(2,1)S(1)} %pad.15), channel_id=1, source_target_pairs={{0,2},{2,0},{4,6},{6,4},{8,10},{10,8},{12,14},{14,12},{16,18},{18,... | collective-permute-start | bytes 2506760 | tf_op jit(solution)/shard_map/ppermute | solution.py:211
  39.8 1.1 constant_dynamic-update-slice_fusion.5
  41.0 3.0 %multiply.8 = (f32[3072,128]{1,0:T(8,128)S(1)}, s16[3120,128]{1,0:T(8,128)(2,1)S(1)}) custom-call(s32[1]{0:T(128)} %bitcast.me.refs_3_, s32[12,8]{1,0:T(8,128)S(1)} %get-tuple-element.112.picks, bf16[2048,256]{1,0:T(8,128)(2,1)S(1)} %constant_dynamic-update-slice_fusion.refs_0_, bf16[2048,256]{1,0:T(8,128)(2,1)S(1)} %constant_dynamic-update-slice_fusion.4.refs_1_, ...), custom_call_target="tpu_custom_call" | custom-call | tf_op jit(solution)/shard_map/multiply/pallas_call | solution.py:270
  44.0 1.6 %collective-permute-start.8 = (s16[3120,128]{1,0:T(8,128)(2,1)S(1)}, s16[3120,128]{1,0:T(8,128)(2,1)S(1)}, u32[]{:S(2)}, u32[]{:S(2)}) collective-permute-start(s16[3120,128]{1,0:T(8,128)(2,1)S(1)} %get-tuple-element.72), channel_id=1, source_target_pairs={{0,4},{2,6},{4,0},{6,2},{8,12},{10,14},{12,8},{14,10},{16,20},{18,... | collective-permute-start | bytes 2396168 | tf_op jit(solution)/shard_map/ppermute | solution.py:211
  45.6 1.1 collective-permute-start.7
  46.7 0.6 collective-permute-done.2.refs_1_
  47.3 0.6 combine.20
  47.8 2.6 %collective-permute-start.6 = (s16[2080,128]{1,0:T(8,128)(2,1)S(1)}, s16[2080,128]{1,0:T(8,128)(2,1)S(1)}, u32[]{:S(2)}, u32[]{:S(2)}) collective-permute-start(s16[2080,128]{1,0:T(8,128)(2,1)S(1)} %get-tuple-element.69), channel_id=1, source_target_pairs={{0,16},{2,18},{4,20},{6,22},{8,24},{10,26},{12,28},{14,30},{16,0},... | collective-permute-start | bytes 1597448 | tf_op jit(solution)/shard_map/ppermute | solution.py:211
  50.5 3.9 %collective-permute-done.10.refs_1_ = s16[5200,128]{1,0:T(8,128)(2,1)S(1)} collective-permute-done((s16[5200,128]{1,0:T(8,128)(2,1)S(1)}, s16[5200,128]{1,0:T(8,128)(2,1)S(1)}, u32[]{:S(2)}, u32[]{:S(2)}) %collective-permute-start.10) | collective-permute-done | bytes 1331232 | tf_op jit(solution)/shard_map/ppermute | solution.py:211
  54.4 0.7 combine.21
  55.1 4.3 %collective-permute-done.9.refs_3_ = bf16[272,1536]{1,0:T(8,128)(2,1)S(1)} collective-permute-done((bf16[272,1536]{1,0:T(8,128)(2,1)S(1)}, bf16[272,1536]{1,0:T(8,128)(2,1)S(1)}, u32[]{:S(2)}, u32[]{:S(2)}) %collective-permute-start.9) | collective-permute-done | bytes 835616 | tf_op jit(solution)/shard_map/ppermute | solution.py:211
  59.4 3.0 %multiply.9 = (f32[3072,128]{1,0:T(8,128)S(1)}, s16[3120,128]{1,0:T(8,128)(2,1)S(1)}) custom-call(s32[1]{0:T(128)} %bitcast.me.refs_3_, s32[12,8]{1,0:T(8,128)S(1)} %get-tuple-element.111.picks, bf16[2048,256]{1,0:T(8,128)(2,1)S(1)} %constant_dynamic-update-slice_fusion.refs_0_, bf16[2048,256]{1,0:T(8,128)(2,1)S(1)} %constant_dynamic-update-slice_fusion.4.refs_1_, ...), custom_call_target="tpu_custom_call" | custom-call | tf_op jit(solution)/shard_map/multiply/pallas_call | solution.py:270
  62.5 1.9 %collective-permute-start.14 = (s16[3120,128]{1,0:T(8,128)(2,1)S(1)}, s16[3120,128]{1,0:T(8,128)(2,1)S(1)}, u32[]{:S(2)}, u32[]{:S(2)}) collective-permute-start(s16[3120,128]{1,0:T(8,128)(2,1)S(1)} %get-tuple-element.84), channel_id=1, source_target_pairs={{0,8},{2,10},{4,12},{6,14},{8,0},{10,2},{12,4},{14,6},{16,24},{18,... | collective-permute-start | bytes 2396168 | tf_op jit(solution)/shard_map/ppermute | solution.py:211
  64.4 1.5 %collective-permute-start.15 = (s16[2608,128]{1,0:T(8,128)(2,1)S(1)}, s16[2608,128]{1,0:T(8,128)(2,1)S(1)}, u32[]{:S(2)}, u32[]{:S(2)}) collective-permute-start(s16[2608,128]{1,0:T(8,128)(2,1)S(1)} %get-tuple-element.85), channel_id=1, source_target_pairs={{0,4},{2,6},{4,0},{6,2},{8,12},{10,14},{12,8},{14,10},{16,20},{18,... | collective-permute-start | bytes 2002952 | tf_op jit(solution)/shard_map/ppermute | solution.py:211
  65.9 1.5 %collective-permute-start.16 = (bf16[272,768]{1,0:T(8,128)(2,1)S(1)}, bf16[272,768]{1,0:T(8,128)(2,1)S(1)}, u32[]{:S(2)}, u32[]{:S(2)}) collective-permute-start(bf16[272,768]{1,0:T(8,128)(2,1)S(1)} %pad.18), channel_id=1, source_target_pairs={{0,2},{2,0},{4,6},{6,4},{8,10},{10,8},{12,14},{14,12},{16,18},{18,... | collective-permute-start | bytes 1253384 | tf_op jit(solution)/shard_map/ppermute | solution.py:211
  67.5 0.5 combine.22
  67.9 3.4 %collective-permute-done.7.refs_3_ = bf16[272,1024]{1,0:T(8,128)(2,1)S(1)} collective-permute-done((bf16[272,1024]{1,0:T(8,128)(2,1)S(1)}, bf16[272,1024]{1,0:T(8,128)(2,1)S(1)}, u32[]{:S(2)}, u32[]{:S(2)}) %collective-permute-start.7) | collective-permute-done | bytes 557088 | tf_op jit(solution)/shard_map/ppermute | solution.py:211
  71.4 2.9 %collective-permute-start.13 = (s16[1568,128]{1,0:T(8,128)(2,1)S(1)}, s16[1568,128]{1,0:T(8,128)(2,1)S(1)}, u32[]{:S(2)}, u32[]{:S(2)}) collective-permute-start(s16[1568,128]{1,0:T(8,128)(2,1)S(1)} %get-tuple-element.82), channel_id=1, source_target_pairs={{0,16},{2,18},{4,20},{6,22},{8,24},{10,26},{12,28},{14,30},{16,0},... | collective-permute-start | bytes 1204232 | tf_op jit(solution)/shard_map/ppermute | solution.py:211
  74.2 2.4 %multiply.10 = (f32[2048,128]{1,0:T(8,128)S(1)}, s16[2080,128]{1,0:T(8,128)(2,1)S(1)}) custom-call(s32[1]{0:T(128)} %bitcast.me.refs_3_, s32[8,8]{1,0:T(8,128)S(1)} %get-tuple-element.113.picks, bf16[2048,256]{1,0:T(8,128)(2,1)S(1)} %constant_dynamic-update-slice_fusion.refs_0_, bf16[2048,256]{1,0:T(8,128)(2,1)S(1)} %constant_dynamic-update-slice_fusion.4.refs_1_, ...), custom_call_target="tpu_custom_call" | custom-call | tf_op jit(solution)/shard_map/multiply/pallas_call | solution.py:270
  76.7 1.6 %collective-permute-start.12 = (s16[2080,128]{1,0:T(8,128)(2,1)S(1)}, s16[2080,128]{1,0:T(8,128)(2,1)S(1)}, u32[]{:S(2)}, u32[]{:S(2)}) collective-permute-start(s16[2080,128]{1,0:T(8,128)(2,1)S(1)} %get-tuple-element.81), channel_id=1, source_target_pairs={{0,4},{2,6},{4,0},{6,2},{8,12},{10,14},{12,8},{14,10},{16,20},{18,... | collective-permute-start | bytes 1597448 | tf_op jit(solution)/shard_map/ppermute | solution.py:211
  78.3 0.3 combine.23
  78.6 1.4 collective-permute-done.16.refs_3_
  80.0 1.8 %multiply.11 = (f32[1536,128]{1,0:T(8,128)S(1)}, s16[1568,128]{1,0:T(8,128)(2,1)S(1)}) custom-call(s32[1]{0:T(128)} %bitcast.me.refs_3_, s32[6,8]{1,0:T(8,128)S(1)} %slice.45.picks, bf16[2048,256]{1,0:T(8,128)(2,1)S(1)} %constant_dynamic-update-slice_fusion.refs_0_, bf16[2048,256]{1,0:T(8,128)(2,1)S(1)} %constant_dynamic-update-slice_fusion.4.refs_1_, ...), custom_call_target="tpu_custom_call" | custom-call | tf_op jit(solution)/shard_map/multiply/pallas_call | solution.py:270
  81.7 0.5 collective-permute-done.15.refs_1_
  82.2 0.4 combine.24
  82.6 15.9 %collective-permute-done.14.refs_1_ = s16[3120,128]{1,0:T(8,128)(2,1)S(1)} collective-permute-done((s16[3120,128]{1,0:T(8,128)(2,1)S(1)}, s16[3120,128]{1,0:T(8,128)(2,1)S(1)}, u32[]{:S(2)}, u32[]{:S(2)}) %collective-permute-start.14) | collective-permute-done | bytes 798752 | tf_op jit(solution)/shard_map/ppermute | solution.py:211
  98.5 0.4 combine.25
  99.0 1.5 %collective-permute-start.18 = (s16[1568,128]{1,0:T(8,128)(2,1)S(1)}, s16[1568,128]{1,0:T(8,128)(2,1)S(1)}, u32[]{:S(2)}, u32[]{:S(2)}) collective-permute-start(s16[1568,128]{1,0:T(8,128)(2,1)S(1)} %get-tuple-element.94), channel_id=1, source_target_pairs={{0,4},{2,6},{4,0},{6,2},{8,12},{10,14},{12,8},{14,10},{16,20},{18,... | collective-permute-start | bytes 1204232 | tf_op jit(solution)/shard_map/ppermute | solution.py:211
  100.5 0.6 collective-permute-start.22
  101.1 4.6 %collective-permute-start.19 = (s16[1312,128]{1,0:T(8,128)(2,1)S(1)}, s16[1312,128]{1,0:T(8,128)(2,1)S(1)}, u32[]{:S(2)}, u32[]{:S(2)}) collective-permute-start(s16[1312,128]{1,0:T(8,128)(2,1)S(1)} %get-tuple-element.96), channel_id=1, source_target_pairs={{0,16},{2,18},{4,20},{6,22},{8,24},{10,26},{12,28},{14,30},{16,0},... | collective-permute-start | bytes 1007624 | tf_op jit(solution)/shard_map/ppermute | solution.py:211
  105.6 0.3 combine.26
  105.9 0.3 combine.27
  106.3 7.7 %collective-permute-done.11.refs_1_ = s16[1040,128]{1,0:T(8,128)(2,1)S(1)} collective-permute-done((s16[1040,128]{1,0:T(8,128)(2,1)S(1)}, s16[1040,128]{1,0:T(8,128)(2,1)S(1)}, u32[]{:S(2)}, u32[]{:S(2)}) %collective-permute-start.11) | collective-permute-done | bytes 266272 | tf_op jit(solution)/shard_map/ppermute | solution.py:211
  114.3 1.5 %collective-permute-start.17 = (s16[528,128]{1,0:T(8,128)(2,1)S(1)}, s16[528,128]{1,0:T(8,128)(2,1)S(1)}, u32[]{:S(2)}, u32[]{:S(2)}) collective-permute-start(s16[528,128]{1,0:T(8,128)(2,1)S(1)} %get-tuple-element.93), channel_id=1, source_target_pairs={{0,2},{2,0},{4,6},{6,4},{8,10},{10,8},{12,14},{14,12},{16,18},{18,... | collective-permute-start | bytes 405512 | tf_op jit(solution)/shard_map/ppermute | solution.py:211
  115.8 0.3 combine.29
  116.2 3.2 %collective-permute-done.17.refs_1_ = s16[528,128]{1,0:T(8,128)(2,1)S(1)} collective-permute-done((s16[528,128]{1,0:T(8,128)(2,1)S(1)}, s16[528,128]{1,0:T(8,128)(2,1)S(1)}, u32[]{:S(2)}, u32[]{:S(2)}) %collective-permute-start.17) | collective-permute-done | bytes 135200 | tf_op jit(solution)/shard_map/ppermute | solution.py:211
  119.4 2.3 %collective-permute-done.19.refs_1_ = s16[1312,128]{1,0:T(8,128)(2,1)S(1)} collective-permute-done((s16[1312,128]{1,0:T(8,128)(2,1)S(1)}, s16[1312,128]{1,0:T(8,128)(2,1)S(1)}, u32[]{:S(2)}, u32[]{:S(2)}) %collective-permute-start.19) | collective-permute-done | bytes 335904 | tf_op jit(solution)/shard_map/ppermute | solution.py:211
  121.7 0.3 combine.31
  122.0 0.2 combine.32
  122.3 3.0 %collective-permute-start.23 = (s16[784,128]{1,0:T(8,128)(2,1)S(1)}, s16[784,128]{1,0:T(8,128)(2,1)S(1)}, u32[]{:S(2)}, u32[]{:S(2)}) collective-permute-start(s16[784,128]{1,0:T(8,128)(2,1)S(1)} %get-tuple-element.102), channel_id=1, source_target_pairs={{0,8},{2,10},{4,12},{6,14},{8,0},{10,2},{12,4},{14,6},{16,24},{18,... | collective-permute-start | bytes 602120 | tf_op jit(solution)/shard_map/ppermute | solution.py:211
  125.7 4.2 %collective-permute-start.26 = (s16[528,128]{1,0:T(8,128)(2,1)S(1)}, s16[528,128]{1,0:T(8,128)(2,1)S(1)}, u32[]{:S(2)}, u32[]{:S(2)}) collective-permute-start(s16[528,128]{1,0:T(8,128)(2,1)S(1)} %get-tuple-element.107), channel_id=1, source_target_pairs={{0,16},{2,18},{4,20},{6,22},{8,24},{10,26},{12,28},{14,30},{16,0},... | collective-permute-start | bytes 405512 | tf_op jit(solution)/shard_map/ppermute | solution.py:211
  130.0 0.3 collective-permute-done.24.refs_1_
  130.4 5.3 %collective-permute-done.23.refs_1_ = s16[784,128]{1,0:T(8,128)(2,1)S(1)} collective-permute-done((s16[784,128]{1,0:T(8,128)(2,1)S(1)}, s16[784,128]{1,0:T(8,128)(2,1)S(1)}, u32[]{:S(2)}, u32[]{:S(2)}) %collective-permute-start.23) | collective-permute-done | bytes 200736 | tf_op jit(solution)/shard_map/ppermute | solution.py:211
  135.9 1.7 %collective-permute-start.27 = (s16[400,128]{1,0:T(8,128)(2,1)S(1)}, s16[400,128]{1,0:T(8,128)(2,1)S(1)}, u32[]{:S(2)}, u32[]{:S(2)}) collective-permute-start(s16[400,128]{1,0:T(8,128)(2,1)S(1)} %get-tuple-element.108), channel_id=1, source_target_pairs={{0,16},{2,18},{4,20},{6,22},{8,24},{10,26},{12,28},{14,30},{16,0},... | collective-permute-start | bytes 307208 | tf_op jit(solution)/shard_map/ppermute | solution.py:211
  137.6 0.3 collective-permute-done.21.refs_1_
  138.3 4.3 %collective-permute-done.27.refs_1_ = s16[400,128]{1,0:T(8,128)(2,1)S(1)} collective-permute-done((s16[400,128]{1,0:T(8,128)(2,1)S(1)}, s16[400,128]{1,0:T(8,128)(2,1)S(1)}, u32[]{:S(2)}, u32[]{:S(2)}) %collective-permute-start.27) | collective-permute-done | bytes 102432 | tf_op jit(solution)/shard_map/ppermute | solution.py:211
  142.7 0.7 constant_dynamic-update-slice_fusion.6
  (54 shorter events, 1.8 us)
Async XLA Ops:
  0.0 1.2 copy-start.1
  1.2 0.7 copy-start.2
  4.6 8.7 %collective-permute-start.1 = (bf16[1024,256]{1,0:T(8,128)(2,1)S(1)}, bf16[1024,256]{1,0:T(8,128)(2,1)}, u32[]{:S(2)}, u32[]{:S(2)}) collective-permute-start(bf16[1024,256]{1,0:T(8,128)(2,1)S(1)} %get-tuple-element.60), channel_id=1, source_target_pairs={{0,1},{1,0},{2,3},{3,2},{4,5},{5,4},{6,7},{7,6},{8,9},{9,8},{10,11... | collective-permute-start | bytes 1572872 | tf_op jit(solution)/shard_map/ppermute | solution.py:242
  5.1 18.3 %collective-permute-start.3 = (bf16[1024,256]{1,0:T(8,128)(2,1)S(1)}, bf16[1024,256]{1,0:T(8,128)(2,1)}, u32[]{:S(2)}, u32[]{:S(2)}) collective-permute-start(bf16[1024,256]{1,0:T(8,128)(2,1)S(1)} %get-tuple-element.60), channel_id=1, source_target_pairs={{0,2},{2,0},{4,6},{6,4},{8,10},{10,8},{12,14},{14,12},{16,18},{18,... | collective-permute-start | bytes 1572872 | tf_op jit(solution)/shard_map/ppermute | solution.py:211
  9.2 2.8 %collective-permute-start = (bf16[1024,256]{1,0:T(8,128)(2,1)S(1)}, bf16[1024,256]{1,0:T(8,128)(2,1)}, u32[]{:S(2)}, u32[]{:S(2)}) collective-permute-start(bf16[1024,256]{1,0:T(8,128)(2,1)S(1)} %get-tuple-element.59), channel_id=1, source_target_pairs={{0,1},{1,0},{2,3},{3,2},{4,5},{5,4},{6,7},{7,6},{8,9},{9,8},{10,11... | collective-permute-start | bytes 1572872 | tf_op jit(solution)/shard_map/ppermute | solution.py:242
  9.5 28.6 %collective-permute-start.4 = (bf16[272,1536]{1,0:T(8,128)(2,1)S(1)}, bf16[272,1536]{1,0:T(8,128)(2,1)S(1)}, u32[]{:S(2)}, u32[]{:S(2)}) collective-permute-start(bf16[272,1536]{1,0:T(8,128)(2,1)S(1)} %pad.16), channel_id=1, source_target_pairs={{0,2},{2,0},{4,6},{6,4},{8,10},{10,8},{12,14},{14,12},{16,18},{18,... | collective-permute-start | bytes 2506760 | tf_op jit(solution)/shard_map/ppermute | solution.py:211
  11.9 2.5 %copy-start = (bf16[256,7168]{1,0:T(8,128)(2,1)S(1)}, bf16[256,7168]{1,0:T(8,128)(2,1)}, u32[]{:S(2)}) copy-start(bf16[256,7168]{1,0:T(8,128)(2,1)} %refs_2_.11) | copy-start | bytes 11010052
  20.0 34.4 %collective-permute-start.10 = (s16[5200,128]{1,0:T(8,128)(2,1)S(1)}, s16[5200,128]{1,0:T(8,128)(2,1)S(1)}, u32[]{:S(2)}, u32[]{:S(2)}) collective-permute-start(s16[5200,128]{1,0:T(8,128)(2,1)S(1)} %get-tuple-element.74), channel_id=1, source_target_pairs={{0,8},{2,10},{4,12},{6,14},{8,0},{10,2},{12,4},{14,6},{16,24},{18,... | collective-permute-start | bytes 3993608 | tf_op jit(solution)/shard_map/ppermute | solution.py:211
  21.9 25.4 %collective-permute-start.2 = (s16[4160,128]{1,0:T(8,128)(2,1)S(1)}, s16[4160,128]{1,0:T(8,128)(2,1)S(1)}, u32[]{:S(2)}, u32[]{:S(2)}) collective-permute-start(s16[4160,128]{1,0:T(8,128)(2,1)S(1)} %get-tuple-element.62), channel_id=1, source_target_pairs={{0,4},{2,6},{4,0},{6,2},{8,12},{10,14},{12,8},{14,10},{16,20},{18,... | collective-permute-start | bytes 3194888 | tf_op jit(solution)/shard_map/ppermute | solution.py:211
  38.0 2.8 %collective-permute-start.5 = (bf16[1024,256]{1,0:T(8,128)(2,1)}, bf16[1024,256]{1,0:T(8,128)(2,1)S(1)}, u32[]{:S(2)}, u32[]{:S(2)}) collective-permute-start(bf16[1024,256]{1,0:T(8,128)(2,1)} %collective-permute-done.3), channel_id=1, source_target_pairs={{0,1},{1,0},{2,3},{3,2},{4,5},{5,4},{6,7},{7,6},{8,9},{9,8},{10,11... | collective-permute-start | bytes 1572872 | tf_op jit(solution)/shard_map/ppermute | solution.py:242
  38.1 21.4 %collective-permute-start.9 = (bf16[272,1536]{1,0:T(8,128)(2,1)S(1)}, bf16[272,1536]{1,0:T(8,128)(2,1)S(1)}, u32[]{:S(2)}, u32[]{:S(2)}) collective-permute-start(bf16[272,1536]{1,0:T(8,128)(2,1)S(1)} %pad.15), channel_id=1, source_target_pairs={{0,2},{2,0},{4,6},{6,4},{8,10},{10,8},{12,14},{14,12},{16,18},{18,... | collective-permute-start | bytes 2506760 | tf_op jit(solution)/shard_map/ppermute | solution.py:211
  40.9 4.6 %slice-start = ((bf16[256,7168]{1,0:T(8,128)(2,1)}), bf16[256,1024]{1,0:T(8,128)(2,1)S(1)}, s32[]{:S(2)}) async-start(bf16[256,7168]{1,0:T(8,128)(2,1)} %refs_2_.11), calls=%async_computation | async-start | bytes 1048576 | tf_op jit(solution)/shard_map/slice | solution.py:215
  44.0 22.0 %collective-permute-start.8 = (s16[3120,128]{1,0:T(8,128)(2,1)S(1)}, s16[3120,128]{1,0:T(8,128)(2,1)S(1)}, u32[]{:S(2)}, u32[]{:S(2)}) collective-permute-start(s16[3120,128]{1,0:T(8,128)(2,1)S(1)} %get-tuple-element.72), channel_id=1, source_target_pairs={{0,4},{2,6},{4,0},{6,2},{8,12},{10,14},{12,8},{14,10},{16,20},{18,... | collective-permute-start | bytes 2396168 | tf_op jit(solution)/shard_map/ppermute | solution.py:211
  45.6 25.8 %collective-permute-start.7 = (bf16[272,1024]{1,0:T(8,128)(2,1)S(1)}, bf16[272,1024]{1,0:T(8,128)(2,1)S(1)}, u32[]{:S(2)}, u32[]{:S(2)}) collective-permute-start(bf16[272,1024]{1,0:T(8,128)(2,1)S(1)} %pad.17), channel_id=1, source_target_pairs={{0,2},{2,0},{4,6},{6,4},{8,10},{10,8},{12,14},{14,12},{16,18},{18,... | collective-permute-start | bytes 1671176 | tf_op jit(solution)/shard_map/ppermute | solution.py:211
  47.8 28.8 %collective-permute-start.6 = (s16[2080,128]{1,0:T(8,128)(2,1)S(1)}, s16[2080,128]{1,0:T(8,128)(2,1)S(1)}, u32[]{:S(2)}, u32[]{:S(2)}) collective-permute-start(s16[2080,128]{1,0:T(8,128)(2,1)S(1)} %get-tuple-element.69), channel_id=1, source_target_pairs={{0,16},{2,18},{4,20},{6,22},{8,24},{10,26},{12,28},{14,30},{16,0},... | collective-permute-start | bytes 1597448 | tf_op jit(solution)/shard_map/ppermute | solution.py:211
  59.4 6.4 %slice-start.1 = ((bf16[256,7168]{1,0:T(8,128)(2,1)}), bf16[256,768]{1,0:T(8,128)(2,1)S(1)}, s32[]{:S(2)}) async-start(bf16[256,7168]{1,0:T(8,128)(2,1)} %refs_2_.11), calls=%async_computation.1 | async-start | bytes 786432 | tf_op jit(solution)/shard_map/slice | solution.py:215
  62.5 36.1 %collective-permute-start.14 = (s16[3120,128]{1,0:T(8,128)(2,1)S(1)}, s16[3120,128]{1,0:T(8,128)(2,1)S(1)}, u32[]{:S(2)}, u32[]{:S(2)}) collective-permute-start(s16[3120,128]{1,0:T(8,128)(2,1)S(1)} %get-tuple-element.84), channel_id=1, source_target_pairs={{0,8},{2,10},{4,12},{6,14},{8,0},{10,2},{12,4},{14,6},{16,24},{18,... | collective-permute-start | bytes 2396168 | tf_op jit(solution)/shard_map/ppermute | solution.py:211
  64.4 17.8 %collective-permute-start.15 = (s16[2608,128]{1,0:T(8,128)(2,1)S(1)}, s16[2608,128]{1,0:T(8,128)(2,1)S(1)}, u32[]{:S(2)}, u32[]{:S(2)}) collective-permute-start(s16[2608,128]{1,0:T(8,128)(2,1)S(1)} %get-tuple-element.85), channel_id=1, source_target_pairs={{0,4},{2,6},{4,0},{6,2},{8,12},{10,14},{12,8},{14,10},{16,20},{18,... | collective-permute-start | bytes 2002952 | tf_op jit(solution)/shard_map/ppermute | solution.py:211
  65.9 14.0 %collective-permute-start.16 = (bf16[272,768]{1,0:T(8,128)(2,1)S(1)}, bf16[272,768]{1,0:T(8,128)(2,1)S(1)}, u32[]{:S(2)}, u32[]{:S(2)}) collective-permute-start(bf16[272,768]{1,0:T(8,128)(2,1)S(1)} %pad.18), channel_id=1, source_target_pairs={{0,2},{2,0},{4,6},{6,4},{8,10},{10,8},{12,14},{14,12},{16,18},{18,... | collective-permute-start | bytes 1253384 | tf_op jit(solution)/shard_map/ppermute | solution.py:211
  71.4 29.7 %collective-permute-start.13 = (s16[1568,128]{1,0:T(8,128)(2,1)S(1)}, s16[1568,128]{1,0:T(8,128)(2,1)S(1)}, u32[]{:S(2)}, u32[]{:S(2)}) collective-permute-start(s16[1568,128]{1,0:T(8,128)(2,1)S(1)} %get-tuple-element.82), channel_id=1, source_target_pairs={{0,16},{2,18},{4,20},{6,22},{8,24},{10,26},{12,28},{14,30},{16,0},... | collective-permute-start | bytes 1204232 | tf_op jit(solution)/shard_map/ppermute | solution.py:211
  76.7 29.2 %collective-permute-start.12 = (s16[2080,128]{1,0:T(8,128)(2,1)S(1)}, s16[2080,128]{1,0:T(8,128)(2,1)S(1)}, u32[]{:S(2)}, u32[]{:S(2)}) collective-permute-start(s16[2080,128]{1,0:T(8,128)(2,1)S(1)} %get-tuple-element.81), channel_id=1, source_target_pairs={{0,4},{2,6},{4,0},{6,2},{8,12},{10,14},{12,8},{14,10},{16,20},{18,... | collective-permute-start | bytes 1597448 | tf_op jit(solution)/shard_map/ppermute | solution.py:211
  99.0 16.9 %collective-permute-start.18 = (s16[1568,128]{1,0:T(8,128)(2,1)S(1)}, s16[1568,128]{1,0:T(8,128)(2,1)S(1)}, u32[]{:S(2)}, u32[]{:S(2)}) collective-permute-start(s16[1568,128]{1,0:T(8,128)(2,1)S(1)} %get-tuple-element.94), channel_id=1, source_target_pairs={{0,4},{2,6},{4,0},{6,2},{8,12},{10,14},{12,8},{14,10},{16,20},{18,... | collective-permute-start | bytes 1204232 | tf_op jit(solution)/shard_map/ppermute | solution.py:211
  100.5 13.6 %collective-permute-start.11 = (s16[1040,128]{1,0:T(8,128)(2,1)S(1)}, s16[1040,128]{1,0:T(8,128)(2,1)S(1)}, u32[]{:S(2)}, u32[]{:S(2)}) collective-permute-start(s16[1040,128]{1,0:T(8,128)(2,1)S(1)} %get-tuple-element.80), channel_id=1, source_target_pairs={{0,8},{2,10},{4,12},{6,14},{8,0},{10,2},{12,4},{14,6},{16,24},{18,... | collective-permute-start | bytes 798728 | tf_op jit(solution)/shard_map/ppermute | solution.py:211
  100.5 21.6 %collective-permute-start.22 = (s16[1568,128]{1,0:T(8,128)(2,1)S(1)}, s16[1568,128]{1,0:T(8,128)(2,1)S(1)}, u32[]{:S(2)}, u32[]{:S(2)}) collective-permute-start(s16[1568,128]{1,0:T(8,128)(2,1)S(1)} %get-tuple-element.100), channel_id=1, source_target_pairs={{0,4},{2,6},{4,0},{6,2},{8,12},{10,14},{12,8},{14,10},{16,20},{18,... | collective-permute-start | bytes 1204232 | tf_op jit(solution)/shard_map/ppermute | solution.py:211
  101.1 20.7 %collective-permute-start.19 = (s16[1312,128]{1,0:T(8,128)(2,1)S(1)}, s16[1312,128]{1,0:T(8,128)(2,1)S(1)}, u32[]{:S(2)}, u32[]{:S(2)}) collective-permute-start(s16[1312,128]{1,0:T(8,128)(2,1)S(1)} %get-tuple-element.96), channel_id=1, source_target_pairs={{0,16},{2,18},{4,20},{6,22},{8,24},{10,26},{12,28},{14,30},{16,0},... | collective-permute-start | bytes 1007624 | tf_op jit(solution)/shard_map/ppermute | solution.py:211
  106.3 19.2 %collective-permute-start.25 = (s16[1040,128]{1,0:T(8,128)(2,1)S(1)}, s16[1040,128]{1,0:T(8,128)(2,1)S(1)}, u32[]{:S(2)}, u32[]{:S(2)}) collective-permute-start(s16[1040,128]{1,0:T(8,128)(2,1)S(1)} %get-tuple-element.104), channel_id=1, source_target_pairs={{0,8},{2,10},{4,12},{6,14},{8,0},{10,2},{12,4},{14,6},{16,24},{18,... | collective-permute-start | bytes 798728 | tf_op jit(solution)/shard_map/ppermute | solution.py:211
  114.3 5.1 %collective-permute-start.17 = (s16[528,128]{1,0:T(8,128)(2,1)S(1)}, s16[528,128]{1,0:T(8,128)(2,1)S(1)}, u32[]{:S(2)}, u32[]{:S(2)}) collective-permute-start(s16[528,128]{1,0:T(8,128)(2,1)S(1)} %get-tuple-element.93), channel_id=1, source_target_pairs={{0,2},{2,0},{4,6},{6,4},{8,10},{10,8},{12,14},{14,12},{16,18},{18,... | collective-permute-start | bytes 405512 | tf_op jit(solution)/shard_map/ppermute | solution.py:211
  116.1 14.2 %collective-permute-start.24 = (s16[784,128]{1,0:T(8,128)(2,1)S(1)}, s16[784,128]{1,0:T(8,128)(2,1)S(1)}, u32[]{:S(2)}, u32[]{:S(2)}) collective-permute-start(s16[784,128]{1,0:T(8,128)(2,1)S(1)} %get-tuple-element.103), channel_id=1, source_target_pairs={{0,16},{2,18},{4,20},{6,22},{8,24},{10,26},{12,28},{14,30},{16,0},... | collective-permute-start | bytes 602120 | tf_op jit(solution)/shard_map/ppermute | solution.py:211
  122.3 13.5 %collective-permute-start.23 = (s16[784,128]{1,0:T(8,128)(2,1)S(1)}, s16[784,128]{1,0:T(8,128)(2,1)S(1)}, u32[]{:S(2)}, u32[]{:S(2)}) collective-permute-start(s16[784,128]{1,0:T(8,128)(2,1)S(1)} %get-tuple-element.102), channel_id=1, source_target_pairs={{0,8},{2,10},{4,12},{6,14},{8,0},{10,2},{12,4},{14,6},{16,24},{18,... | collective-permute-start | bytes 602120 | tf_op jit(solution)/shard_map/ppermute | solution.py:211
  125.3 12.6 %collective-permute-start.21 = (s16[784,128]{1,0:T(8,128)(2,1)S(1)}, s16[784,128]{1,0:T(8,128)(2,1)S(1)}, u32[]{:S(2)}, u32[]{:S(2)}) collective-permute-start(s16[784,128]{1,0:T(8,128)(2,1)S(1)} %get-tuple-element.99), channel_id=1, source_target_pairs={{0,8},{2,10},{4,12},{6,14},{8,0},{10,2},{12,4},{14,6},{16,24},{18,... | collective-permute-start | bytes 602120 | tf_op jit(solution)/shard_map/ppermute | solution.py:211
  125.4 12.6 %collective-permute-start.20 = (s16[656,128]{1,0:T(8,128)(2,1)S(1)}, s16[656,128]{1,0:T(8,128)(2,1)S(1)}, u32[]{:S(2)}, u32[]{:S(2)}) collective-permute-start(s16[656,128]{1,0:T(8,128)(2,1)S(1)} %get-tuple-element.98), channel_id=1, source_target_pairs={{0,2},{2,0},{4,6},{6,4},{8,10},{10,8},{12,14},{14,12},{16,18},{18,... | collective-permute-start | bytes 503816 | tf_op jit(solution)/shard_map/ppermute | solution.py:211
  125.7 12.5 %collective-permute-start.26 = (s16[528,128]{1,0:T(8,128)(2,1)S(1)}, s16[528,128]{1,0:T(8,128)(2,1)S(1)}, u32[]{:S(2)}, u32[]{:S(2)}) collective-permute-start(s16[528,128]{1,0:T(8,128)(2,1)S(1)} %get-tuple-element.107), channel_id=1, source_target_pairs={{0,16},{2,18},{4,20},{6,22},{8,24},{10,26},{12,28},{14,30},{16,0},... | collective-permute-start | bytes 405512 | tf_op jit(solution)/shard_map/ppermute | solution.py:211
  135.9 6.7 %collective-permute-start.27 = (s16[400,128]{1,0:T(8,128)(2,1)S(1)}, s16[400,128]{1,0:T(8,128)(2,1)S(1)}, u32[]{:S(2)}, u32[]{:S(2)}) collective-permute-start(s16[400,128]{1,0:T(8,128)(2,1)S(1)} %get-tuple-element.108), channel_id=1, source_target_pairs={{0,16},{2,18},{4,20},{6,22},{8,24},{10,26},{12,28},{14,30},{16,0},... | collective-permute-start | bytes 307208 | tf_op jit(solution)/shard_map/ppermute | solution.py:211
  138.3 4.4 %copy-start.3 = (f32[56,64,128]{2,1,0:T(8,128)}, f32[56,64,128]{2,1,0:T(8,128)S(1)}, u32[]{:S(2)}) copy-start(f32[56,64,128]{2,1,0:T(8,128)S(1)} %constant_dynamic-update-slice_fusion.7) | copy-start | bytes 5505028

commit v4 on v3

--- a/solution.py
+++ b/solution.py
@@ -11,7 +11,7 @@
 LEVELS = 32700.0
 STEPS = 128.0
 SMALLEST = 2.0**-110
-PAD = 16
+PAD = 8
 VMEM_LIMIT = 16 * 1024 * 1024
 
 
@@ -152,33 +152,33 @@
 def plan_of(columns, depth):
     if depth != 4 or columns % 56 != 0:
         return [columns], [list(range(1, depth))], [[0]], [("multiply", 0)] + [("step", 0)] * (depth - 1)
-    widths = [8, 10, 12, 12, 8, 6]
-    paths = [[1, 3, 2, 0], [2, 1, 3, 0], [1, 3, 2], [2, 1, 3], [1, 2, 3], [1, 2, 3]]
+    widths = [8, 10, 8, 10, 10, 10]
+    paths = [[1, 2, 3, 0], [2, 1, 3, 0], [1, 2, 3], [1, 2, 3], [2, 1, 3], [1, 2, 3]]
     messages = [[2], [3], [4], [5]]
     work = [
         ("multiply", 0),
         ("multiply", 1),
         ("multiply", 2),
         ("step", 0),
+        ("multiply", 3),
         ("step", 1),
-        ("multiply", 3),
         ("step", 2),
+        ("step", 0),
         ("multiply", 4),
+        ("step", 2),
+        ("step", 3),
         ("step", 0),
         ("multiply", 5),
+        ("step", 4),
         ("step", 1),
+        ("step", 2),
+        ("step", 5),
         ("step", 3),
-        ("step", 2),
+        ("step", 1),
         ("step", 4),
+        ("step", 5),
         ("step", 0),
         ("step", 3),
-        ("step", 0),
-        ("step", 1),
-        ("step", 5),
-        ("step", 4),
-        ("step", 3),
-        ("step", 5),
-        ("step", 2),
         ("step", 1),
         ("step", 4),
         ("step", 5),

time: 144 us -> 134 us (0.931)
  waiting for transfers between devices: 68.2 us -> 59.2 us
    ppermute x25, waiting for transfers between devices: 68.2 us -> 57.8 us  [swap(): return lax.ppermute(sent, 'dp', [(o, o ^ 1 << bit) for o in range(owners)])]
    unnamed x17 -> x21, local copies, waits for them, and re-layouts: 4.53 us -> 3.24 us
  transfers between devices with their start and end apart: 28 -> 28, of which waited for: 15 -> 15; matrix products, arithmetic and copies ran while one was open for 5% -> 5% of each run, Pallas kernels for 15% -> 16%
where the time goes in v4:
time: 134 us
  waiting for transfers between devices  59.2 us (44%)
  starting transfers between devices  40.7 us (30%)
  Pallas kernels  24.7 us (18%)
  local copies, waits for them, and re-layouts  8.89 us (7%)
    ppermute x25, waiting for transfers between devices, swap(): return lax.ppermute(sent, 'dp', [(o, o ^ 1 << bit) for o in range(owners)])  57.8 us
    ppermute x25, starting transfers between devices, swap(): return lax.ppermute(sent, 'dp', [(o, o ^ 1 << bit) for o in range(owners)])  40 us
    pallas_call x6, Pallas kernels, multiply(): pl.pallas_call(functools.partial(multiply_kernel, width, rows, height, or...  16.5 us
    pallas_call x20, Pallas kernels, combine(): pl.pallas_call(functools.partial(combine_kernel, shapes, rows, n, encoded...  5.55 us
    unnamed x21, local copies, waits for them, and re-layouts  3.24 us
  transfers between devices with their start and end apart: 28, of which 15 were waited for; matrix products, arithmetic and copies ran while one was open for 5% of the time, Pallas kernels for 16%

profile of v4, /device:TPU:0, one launch (start us, length us, event | category | flops | bytes accessed | tf_op | source)
XLA Modules:
  0.0 134.0 jit_solution(9349892546362401065)
XLA Ops:
  0.0 1.2 copy-done.1
  1.2 0.7 copy-done.2
  1.9 2.7 %prepare.1 = (bf16[1024,256]{1,0:T(8,128)(2,1)S(1)}, bf16[1024,256]{1,0:T(8,128)(2,1)S(1)}) custom-call(s32[1]{0:T(128)} %bitcast.me.refs_3_, s32[1,4]{1,0:T(1,128)S(1)} %copy-done.2, bf16[256,2048]{1,0:T(8,128)(2,1)S(1)} %copy-done.1), custom_call_target="tpu_custom_call" | custom-call | tf_op jit(solution)/shard_map/prepare/pallas_call | solution.py:225
  4.6 0.5 collective-permute-start.1
  5.1 2.6 %collective-permute-start.3 = (bf16[1024,256]{1,0:T(8,128)(2,1)S(1)}, bf16[1024,256]{1,0:T(8,128)(2,1)}, u32[]{:S(2)}, u32[]{:S(2)}) collective-permute-start(bf16[1024,256]{1,0:T(8,128)(2,1)S(1)} %get-tuple-element.60), channel_id=1, source_target_pairs={{0,2},{2,0},{4,6},{6,4},{8,10},{10,8},{12,14},{14,12},{16,18},{18,... | collective-permute-start | bytes 1572872 | tf_op jit(solution)/shard_map/ppermute | solution.py:211
  7.6 1.7 %fusion.5 = (bf16[256,1280]{1,0:T(8,128)(2,1)S(1)}, bf16[256,1280]{1,0:T(8,128)(2,1)S(1)}, bf16[256,1280]{1,0:T(8,128)(2,1)S(1)}) fusion(bf16[256,7168]{1,0:T(8,128)(2,1)} %refs_2_.11), kind=kLoop, calls=%fused_computation.26 | loop fusion | bytes 3932160 | tf_op jit(solution)/shard_map/slice | solution.py:215
  9.4 0.9 pad.14
  11.0 1.3 %collective-permute-done = bf16[1024,256]{1,0:T(8,128)(2,1)} collective-permute-done((bf16[1024,256]{1,0:T(8,128)(2,1)S(1)}, bf16[1024,256]{1,0:T(8,128)(2,1)}, u32[]{:S(2)}, u32[]{:S(2)}) %collective-permute-start) | collective-permute-done | bytes 524320 | tf_op jit(solution)/shard_map/ppermute | solution.py:242
  12.3 1.1 constant_dynamic-update-slice_fusion.refs_0_
  13.4 1.1 constant_dynamic-update-slice_fusion.2.refs_1_
  14.5 2.5 %multiply.6 = (f32[4096,128]{1,0:T(8,128)S(1)}, s16[4160,128]{1,0:T(8,128)(2,1)S(1)}) custom-call(s32[1]{0:T(128)} %bitcast.me.refs_3_, s32[8,8]{1,0:T(8,128)S(1)} %get-tuple-element.117.picks, bf16[2048,256]{1,0:T(8,128)(2,1)S(1)} %constant_dynamic-update-slice_fusion.refs_0_, bf16[2048,256]{1,0:T(8,128)(2,1)S(1)} %constant_dynamic-update-slice_fusion.2.refs_1_, ...), custom_call_target="tpu_custom_call" | custom-call | tf_op jit(solution)/shard_map/multiply/pallas_call | solution.py:270
  17.0 3.1 %multiply.7 = (f32[5120,128]{1,0:T(8,128)S(1)}, s16[5200,128]{1,0:T(8,128)(2,1)S(1)}) custom-call(s32[1]{0:T(128)} %bitcast.me.refs_3_, s32[10,8]{1,0:T(8,128)S(1)} %get-tuple-element.115.picks, bf16[2048,256]{1,0:T(8,128)(2,1)S(1)} %constant_dynamic-update-slice_fusion.refs_0_, bf16[2048,256]{1,0:T(8,128)(2,1)S(1)} %constant_dynamic-update-slice_fusion.2.refs_1_, ...), custom_call_target="tpu_custom_call" | custom-call | tf_op jit(solution)/shard_map/multiply/pallas_call | solution.py:270
  20.1 1.6 %collective-permute-start.8 = (s16[5200,128]{1,0:T(8,128)(2,1)S(1)}, s16[5200,128]{1,0:T(8,128)(2,1)S(1)}, u32[]{:S(2)}, u32[]{:S(2)}) collective-permute-start(s16[5200,128]{1,0:T(8,128)(2,1)S(1)} %get-tuple-element.72), channel_id=1, source_target_pairs={{0,8},{2,10},{4,12},{6,14},{8,0},{10,2},{12,4},{14,6},{16,24},{18,... | collective-permute-start | bytes 3993608 | tf_op jit(solution)/shard_map/ppermute | solution.py:211
  21.8 1.5 %collective-permute-start.2 = (s16[4160,128]{1,0:T(8,128)(2,1)S(1)}, s16[4160,128]{1,0:T(8,128)(2,1)S(1)}, u32[]{:S(2)}, u32[]{:S(2)}) collective-permute-start(s16[4160,128]{1,0:T(8,128)(2,1)S(1)} %get-tuple-element.62), channel_id=1, source_target_pairs={{0,4},{2,6},{4,0},{6,2},{8,12},{10,14},{12,8},{14,10},{16,20},{18,... | collective-permute-start | bytes 3194888 | tf_op jit(solution)/shard_map/ppermute | solution.py:211
  23.3 8.5 %collective-permute-done.4.refs_3_ = bf16[264,1024]{1,0:T(8,128)(2,1)S(1)} collective-permute-done((bf16[264,1024]{1,0:T(8,128)(2,1)S(1)}, bf16[264,1024]{1,0:T(8,128)(2,1)S(1)}, u32[]{:S(2)}, u32[]{:S(2)}) %collective-permute-start.4) | collective-permute-done | bytes 540704 | tf_op jit(solution)/shard_map/ppermute | solution.py:211
  31.7 1.8 %collective-permute-start.9 = (bf16[264,1280]{1,0:T(8,128)(2,1)S(1)}, bf16[264,1280]{1,0:T(8,128)(2,1)S(1)}, u32[]{:S(2)}, u32[]{:S(2)}) collective-permute-start(bf16[264,1280]{1,0:T(8,128)(2,1)S(1)} %copy-done.3), channel_id=1, source_target_pairs={{0,2},{2,0},{4,6},{6,4},{8,10},{10,8},{12,14},{14,12},{16,18},{18,... | collective-permute-start | bytes 2027528 | tf_op jit(solution)/shard_map/ppermute | solution.py:211
  33.5 1.1 constant_dynamic-update-slice_fusion.5
  34.6 2.4 %multiply.8 = (f32[2048,128]{1,0:T(8,128)S(1)}, s16[2080,128]{1,0:T(8,128)(2,1)S(1)}) custom-call(s32[1]{0:T(128)} %bitcast.me.refs_3_, s32[8,8]{1,0:T(8,128)S(1)} %get-tuple-element.116.picks, bf16[2048,256]{1,0:T(8,128)(2,1)S(1)} %constant_dynamic-update-slice_fusion.refs_0_, bf16[2048,256]{1,0:T(8,128)(2,1)S(1)} %constant_dynamic-update-slice_fusion.4.refs_1_, ...), custom_call_target="tpu_custom_call" | custom-call | tf_op jit(solution)/shard_map/multiply/pallas_call | solution.py:270
  37.0 1.6 %collective-permute-start.7 = (s16[2080,128]{1,0:T(8,128)(2,1)S(1)}, s16[2080,128]{1,0:T(8,128)(2,1)S(1)}, u32[]{:S(2)}, u32[]{:S(2)}) collective-permute-start(s16[2080,128]{1,0:T(8,128)(2,1)S(1)} %get-tuple-element.71), channel_id=1, source_target_pairs={{0,4},{2,6},{4,0},{6,2},{8,12},{10,14},{12,8},{14,10},{16,20},{18,... | collective-permute-start | bytes 1597448 | tf_op jit(solution)/shard_map/ppermute | solution.py:211
  38.6 9.5 %collective-permute-done.2.refs_1_ = s16[4160,128]{1,0:T(8,128)(2,1)S(1)} collective-permute-done((s16[4160,128]{1,0:T(8,128)(2,1)S(1)}, s16[4160,128]{1,0:T(8,128)(2,1)S(1)}, u32[]{:S(2)}, u32[]{:S(2)}) %collective-permute-start.2) | collective-permute-done | bytes 1064992 | tf_op jit(solution)/shard_map/ppermute | solution.py:211
  48.1 0.6 combine.20
  48.7 0.5 collective-permute-start.6
  49.3 0.6 collective-permute-start.13
  50.0 2.8 %multiply.9 = (f32[2560,128]{1,0:T(8,128)S(1)}, s16[2608,128]{1,0:T(8,128)(2,1)S(1)}) custom-call(s32[1]{0:T(128)} %bitcast.me.refs_3_, s32[10,8]{1,0:T(8,128)S(1)} %get-tuple-element.114.picks, bf16[2048,256]{1,0:T(8,128)(2,1)S(1)} %constant_dynamic-update-slice_fusion.refs_0_, bf16[2048,256]{1,0:T(8,128)(2,1)S(1)} %constant_dynamic-update-slice_fusion.4.refs_1_, ...), custom_call_target="tpu_custom_call" | custom-call | tf_op jit(solution)/shard_map/multiply/pallas_call | solution.py:270
  52.8 1.5 %collective-permute-start.15 = (bf16[264,1280]{1,0:T(8,128)(2,1)S(1)}, bf16[264,1280]{1,0:T(8,128)(2,1)S(1)}, u32[]{:S(2)}, u32[]{:S(2)}) collective-permute-start(bf16[264,1280]{1,0:T(8,128)(2,1)S(1)} %pad.17), channel_id=1, source_target_pairs={{0,2},{2,0},{4,6},{6,4},{8,10},{10,8},{12,14},{14,12},{16,18},{18,... | collective-permute-start | bytes 2027528 | tf_op jit(solution)/shard_map/ppermute | solution.py:211
  54.4 1.5 %collective-permute-start.11 = (s16[2608,128]{1,0:T(8,128)(2,1)S(1)}, s16[2608,128]{1,0:T(8,128)(2,1)S(1)}, u32[]{:S(2)}, u32[]{:S(2)}) collective-permute-start(s16[2608,128]{1,0:T(8,128)(2,1)S(1)} %get-tuple-element.80), channel_id=1, source_target_pairs={{0,4},{2,6},{4,0},{6,2},{8,12},{10,14},{12,8},{14,10},{16,20},{18,... | collective-permute-start | bytes 2002952 | tf_op jit(solution)/shard_map/ppermute | solution.py:211
  55.9 0.7 combine.21
  56.6 3.0 %collective-permute-done.7.refs_1_ = s16[2080,128]{1,0:T(8,128)(2,1)S(1)} collective-permute-done((s16[2080,128]{1,0:T(8,128)(2,1)S(1)}, s16[2080,128]{1,0:T(8,128)(2,1)S(1)}, u32[]{:S(2)}, u32[]{:S(2)}) %collective-permute-start.7) | collective-permute-done | bytes 532512 | tf_op jit(solution)/shard_map/ppermute | solution.py:211
  59.6 0.3 combine.22
  59.9 0.5 collective-permute-start.12
  60.4 3.4 %collective-permute-done.6.refs_1_ = s16[2080,128]{1,0:T(8,128)(2,1)S(1)} collective-permute-done((s16[2080,128]{1,0:T(8,128)(2,1)S(1)}, s16[2080,128]{1,0:T(8,128)(2,1)S(1)}, u32[]{:S(2)}, u32[]{:S(2)}) %collective-permute-start.6) | collective-permute-done | bytes 532512 | tf_op jit(solution)/shard_map/ppermute | solution.py:211
  63.8 0.3 combine.23
  64.2 2.7 %collective-permute-start.10 = (s16[1040,128]{1,0:T(8,128)(2,1)S(1)}, s16[1040,128]{1,0:T(8,128)(2,1)S(1)}, u32[]{:S(2)}, u32[]{:S(2)}) collective-permute-start(s16[1040,128]{1,0:T(8,128)(2,1)S(1)} %get-tuple-element.78), channel_id=1, source_target_pairs={{0,16},{2,18},{4,20},{6,22},{8,24},{10,26},{12,28},{14,30},{16,0},... | collective-permute-start | bytes 798728 | tf_op jit(solution)/shard_map/ppermute | solution.py:211
  66.8 0.6 collective-permute-done.13.refs_3_
  67.5 2.8 %multiply.10 = (f32[2560,128]{1,0:T(8,128)S(1)}, s16[2608,128]{1,0:T(8,128)(2,1)S(1)}) custom-call(s32[1]{0:T(128)} %bitcast.me.refs_3_, s32[10,8]{1,0:T(8,128)S(1)} %get-tuple-element.113.picks, bf16[2048,256]{1,0:T(8,128)(2,1)S(1)} %constant_dynamic-update-slice_fusion.refs_0_, bf16[2048,256]{1,0:T(8,128)(2,1)S(1)} %constant_dynamic-update-slice_fusion.4.refs_1_, ...), custom_call_target="tpu_custom_call" | custom-call | tf_op jit(solution)/shard_map/multiply/pallas_call | solution.py:270
  70.3 1.6 %collective-permute-start.19 = (s16[2608,128]{1,0:T(8,128)(2,1)S(1)}, s16[2608,128]{1,0:T(8,128)(2,1)S(1)}, u32[]{:S(2)}, u32[]{:S(2)}) collective-permute-start(s16[2608,128]{1,0:T(8,128)(2,1)S(1)} %get-tuple-element.93), channel_id=1, source_target_pairs={{0,8},{2,10},{4,12},{6,14},{8,0},{10,2},{12,4},{14,6},{16,24},{18,... | collective-permute-start | bytes 2002952 | tf_op jit(solution)/shard_map/ppermute | solution.py:211
  71.9 2.3 %collective-permute-done.12.refs_1_ = s16[1040,128]{1,0:T(8,128)(2,1)S(1)} collective-permute-done((s16[1040,128]{1,0:T(8,128)(2,1)S(1)}, s16[1040,128]{1,0:T(8,128)(2,1)S(1)}, u32[]{:S(2)}, u32[]{:S(2)}) %collective-permute-start.12) | collective-permute-done | bytes 266272 | tf_op jit(solution)/shard_map/ppermute | solution.py:211
  74.3 1.5 %collective-permute-start.18 = (s16[2608,128]{1,0:T(8,128)(2,1)S(1)}, s16[2608,128]{1,0:T(8,128)(2,1)S(1)}, u32[]{:S(2)}, u32[]{:S(2)}) collective-permute-start(s16[2608,128]{1,0:T(8,128)(2,1)S(1)} %get-tuple-element.92), channel_id=1, source_target_pairs={{0,4},{2,6},{4,0},{6,2},{8,12},{10,14},{12,8},{14,10},{16,20},{18,... | collective-permute-start | bytes 2002952 | tf_op jit(solution)/shard_map/ppermute | solution.py:211
  76.0 0.4 combine.25
  76.5 1.0 collective-permute-done.10.refs_1_
  77.7 0.8 collective-permute-done.15.refs_3_
  78.6 2.9 %multiply.11 = (f32[2560,128]{1,0:T(8,128)S(1)}, s16[2608,128]{1,0:T(8,128)(2,1)S(1)}) custom-call(s32[1]{0:T(128)} %bitcast.me.refs_3_, s32[10,8]{1,0:T(8,128)S(1)} %get-tuple-element.112.picks, bf16[2048,256]{1,0:T(8,128)(2,1)S(1)} %constant_dynamic-update-slice_fusion.refs_0_, bf16[2048,256]{1,0:T(8,128)(2,1)S(1)} %constant_dynamic-update-slice_fusion.4.refs_1_, ...), custom_call_target="tpu_custom_call" | custom-call | tf_op jit(solution)/shard_map/multiply/pallas_call | solution.py:270
  81.4 1.6 %collective-permute-start.16 = (s16[2608,128]{1,0:T(8,128)(2,1)S(1)}, s16[2608,128]{1,0:T(8,128)(2,1)S(1)}, u32[]{:S(2)}, u32[]{:S(2)}) collective-permute-start(s16[2608,128]{1,0:T(8,128)(2,1)S(1)} %get-tuple-element.90), channel_id=1, source_target_pairs={{0,4},{2,6},{4,0},{6,2},{8,12},{10,14},{12,8},{14,10},{16,20},{18,... | collective-permute-start | bytes 2002952 | tf_op jit(solution)/shard_map/ppermute | solution.py:211
  83.0 1.6 %collective-permute-start.23 = (s16[1312,128]{1,0:T(8,128)(2,1)S(1)}, s16[1312,128]{1,0:T(8,128)(2,1)S(1)}, u32[]{:S(2)}, u32[]{:S(2)}) collective-permute-start(s16[1312,128]{1,0:T(8,128)(2,1)S(1)} %get-tuple-element.100), channel_id=1, source_target_pairs={{0,8},{2,10},{4,12},{6,14},{8,0},{10,2},{12,4},{14,6},{16,24},{18,... | collective-permute-start | bytes 1007624 | tf_op jit(solution)/shard_map/ppermute | solution.py:211
  84.6 2.6 %collective-permute-start.17 = (s16[528,128]{1,0:T(8,128)(2,1)S(1)}, s16[528,128]{1,0:T(8,128)(2,1)S(1)}, u32[]{:S(2)}, u32[]{:S(2)}) collective-permute-start(s16[528,128]{1,0:T(8,128)(2,1)S(1)} %get-tuple-element.91), channel_id=1, source_target_pairs={{0,16},{2,18},{4,20},{6,22},{8,24},{10,26},{12,28},{14,30},{16,0},... | collective-permute-start | bytes 405512 | tf_op jit(solution)/shard_map/ppermute | solution.py:211
  87.2 5.3 %collective-permute-done.19.refs_1_ = s16[2608,128]{1,0:T(8,128)(2,1)S(1)} collective-permute-done((s16[2608,128]{1,0:T(8,128)(2,1)S(1)}, s16[2608,128]{1,0:T(8,128)(2,1)S(1)}, u32[]{:S(2)}, u32[]{:S(2)}) %collective-permute-start.19) | collective-permute-done | bytes 667680 | tf_op jit(solution)/shard_map/ppermute | solution.py:211
  92.4 0.4 combine.27
  92.9 0.4 combine.28
  93.3 7.2 %collective-permute-start.22 = (s16[1312,128]{1,0:T(8,128)(2,1)S(1)}, s16[1312,128]{1,0:T(8,128)(2,1)S(1)}, u32[]{:S(2)}, u32[]{:S(2)}) collective-permute-start(s16[1312,128]{1,0:T(8,128)(2,1)S(1)} %get-tuple-element.99), channel_id=1, source_target_pairs={{0,16},{2,18},{4,20},{6,22},{8,24},{10,26},{12,28},{14,30},{16,0},... | collective-permute-start | bytes 1007624 | tf_op jit(solution)/shard_map/ppermute | solution.py:211
  100.5 0.3 collective-permute-start.21
  100.9 5.6 %collective-permute-done.16.refs_1_ = s16[2608,128]{1,0:T(8,128)(2,1)S(1)} collective-permute-done((s16[2608,128]{1,0:T(8,128)(2,1)S(1)}, s16[2608,128]{1,0:T(8,128)(2,1)S(1)}, u32[]{:S(2)}, u32[]{:S(2)}) %collective-permute-start.16) | collective-permute-done | bytes 667680 | tf_op jit(solution)/shard_map/ppermute | solution.py:211
  106.5 0.4 combine.30
  107.0 0.3 combine.31
  107.3 1.6 %collective-permute-start.25 = (s16[656,128]{1,0:T(8,128)(2,1)S(1)}, s16[656,128]{1,0:T(8,128)(2,1)S(1)}, u32[]{:S(2)}, u32[]{:S(2)}) collective-permute-start(s16[656,128]{1,0:T(8,128)(2,1)S(1)} %get-tuple-element.106), channel_id=1, source_target_pairs={{0,16},{2,18},{4,20},{6,22},{8,24},{10,26},{12,28},{14,30},{16,0},... | collective-permute-start | bytes 503816 | tf_op jit(solution)/shard_map/ppermute | solution.py:211
  108.9 0.7 collective-permute-start.14
  109.5 7.8 %collective-permute-done.22.refs_1_ = s16[1312,128]{1,0:T(8,128)(2,1)S(1)} collective-permute-done((s16[1312,128]{1,0:T(8,128)(2,1)S(1)}, s16[1312,128]{1,0:T(8,128)(2,1)S(1)}, u32[]{:S(2)}, u32[]{:S(2)}) %collective-permute-start.22) | collective-permute-done | bytes 335904 | tf_op jit(solution)/shard_map/ppermute | solution.py:211
  117.6 1.5 %collective-permute-start.24 = (s16[656,128]{1,0:T(8,128)(2,1)S(1)}, s16[656,128]{1,0:T(8,128)(2,1)S(1)}, u32[]{:S(2)}, u32[]{:S(2)}) collective-permute-start(s16[656,128]{1,0:T(8,128)(2,1)S(1)} %get-tuple-element.105), channel_id=1, source_target_pairs={{0,2},{2,0},{4,6},{6,4},{8,10},{10,8},{12,14},{14,12},{16,18},{18,... | collective-permute-start | bytes 503816 | tf_op jit(solution)/shard_map/ppermute | solution.py:211
  119.1 0.3 combine.33
  119.5 0.3 combine.34
  119.8 3.0 %collective-permute-start.27 = (s16[656,128]{1,0:T(8,128)(2,1)S(1)}, s16[656,128]{1,0:T(8,128)(2,1)S(1)}, u32[]{:S(2)}, u32[]{:S(2)}) collective-permute-start(s16[656,128]{1,0:T(8,128)(2,1)S(1)} %get-tuple-element.108), channel_id=1, source_target_pairs={{0,16},{2,18},{4,20},{6,22},{8,24},{10,26},{12,28},{14,30},{16,0},... | collective-permute-start | bytes 503816 | tf_op jit(solution)/shard_map/ppermute | solution.py:211
  122.8 2.6 %collective-permute-done.25.refs_1_ = s16[656,128]{1,0:T(8,128)(2,1)S(1)} collective-permute-done((s16[656,128]{1,0:T(8,128)(2,1)S(1)}, s16[656,128]{1,0:T(8,128)(2,1)S(1)}, u32[]{:S(2)}, u32[]{:S(2)}) %collective-permute-start.25) | collective-permute-done | bytes 167968 | tf_op jit(solution)/shard_map/ppermute | solution.py:211
  125.8 3.8 %collective-permute-done.26.refs_1_ = s16[656,128]{1,0:T(8,128)(2,1)S(1)} collective-permute-done((s16[656,128]{1,0:T(8,128)(2,1)S(1)}, s16[656,128]{1,0:T(8,128)(2,1)S(1)}, u32[]{:S(2)}, u32[]{:S(2)}) %collective-permute-start.26) | collective-permute-done | bytes 167968 | tf_op jit(solution)/shard_map/ppermute | solution.py:211
  129.7 3.5 %collective-permute-done.27.refs_1_ = s16[656,128]{1,0:T(8,128)(2,1)S(1)} collective-permute-done((s16[656,128]{1,0:T(8,128)(2,1)S(1)}, s16[656,128]{1,0:T(8,128)(2,1)S(1)}, u32[]{:S(2)}, u32[]{:S(2)}) %collective-permute-start.27) | collective-permute-done | bytes 167968 | tf_op jit(solution)/shard_map/ppermute | solution.py:211
  133.2 0.8 constant_dynamic-update-slice_fusion.6
  (54 shorter events, 2.3 us)
Async XLA Ops:
  0.0 1.2 copy-start.1
  1.2 0.7 copy-start.2
  4.6 8.8 %collective-permute-start.1 = (bf16[1024,256]{1,0:T(8,128)(2,1)S(1)}, bf16[1024,256]{1,0:T(8,128)(2,1)}, u32[]{:S(2)}, u32[]{:S(2)}) collective-permute-start(bf16[1024,256]{1,0:T(8,128)(2,1)S(1)} %get-tuple-element.60), channel_id=1, source_target_pairs={{0,1},{1,0},{2,3},{3,2},{4,5},{5,4},{6,7},{7,6},{8,9},{9,8},{10,11... | collective-permute-start | bytes 1572872 | tf_op jit(solution)/shard_map/ppermute | solution.py:242
  5.1 18.2 %collective-permute-start.3 = (bf16[1024,256]{1,0:T(8,128)(2,1)S(1)}, bf16[1024,256]{1,0:T(8,128)(2,1)}, u32[]{:S(2)}, u32[]{:S(2)}) collective-permute-start(bf16[1024,256]{1,0:T(8,128)(2,1)S(1)} %get-tuple-element.60), channel_id=1, source_target_pairs={{0,2},{2,0},{4,6},{6,4},{8,10},{10,8},{12,14},{14,12},{16,18},{18,... | collective-permute-start | bytes 1572872 | tf_op jit(solution)/shard_map/ppermute | solution.py:211
  7.6 1.7 %slice-start = ((bf16[256,7168]{1,0:T(8,128)(2,1)}), bf16[256,1024]{1,0:T(8,128)(2,1)S(1)}, s32[]{:S(2)}) async-start(bf16[256,7168]{1,0:T(8,128)(2,1)} %refs_2_.11), calls=%async_computation | async-start | bytes 1048576 | tf_op jit(solution)/shard_map/slice | solution.py:215
  9.3 1.4 %copy-start.5 = (s32[56,8]{0,1:T(8,128)S(1)}, s32[56,8]{0,1:T(8,128)}, u32[]{:S(2)}) copy-start(s32[56,8]{0,1:T(8,128)} %param.6) | copy-start | bytes 5380
  10.3 2.0 %collective-permute-start = (bf16[1024,256]{1,0:T(8,128)(2,1)S(1)}, bf16[1024,256]{1,0:T(8,128)(2,1)}, u32[]{:S(2)}, u32[]{:S(2)}) collective-permute-start(bf16[1024,256]{1,0:T(8,128)(2,1)S(1)} %get-tuple-element.59), channel_id=1, source_target_pairs={{0,1},{1,0},{2,3},{3,2},{4,5},{5,4},{6,7},{7,6},{8,9},{9,8},{10,11... | collective-permute-start | bytes 1572872 | tf_op jit(solution)/shard_map/ppermute | solution.py:242
  10.4 21.3 %collective-permute-start.4 = (bf16[264,1024]{1,0:T(8,128)(2,1)S(1)}, bf16[264,1024]{1,0:T(8,128)(2,1)S(1)}, u32[]{:S(2)}, u32[]{:S(2)}) collective-permute-start(bf16[264,1024]{1,0:T(8,128)(2,1)S(1)} %pad.15), channel_id=1, source_target_pairs={{0,2},{2,0},{4,6},{6,4},{8,10},{10,8},{12,14},{14,12},{16,18},{18,... | collective-permute-start | bytes 1622024 | tf_op jit(solution)/shard_map/ppermute | solution.py:211
  10.8 3.6 %copy-start = (bf16[256,7168]{1,0:T(8,128)(2,1)S(1)}, bf16[256,7168]{1,0:T(8,128)(2,1)}, u32[]{:S(2)}) copy-start(bf16[256,7168]{1,0:T(8,128)(2,1)} %refs_2_.11) | copy-start | bytes 11010052
  17.0 14.7 %copy-start.3 = (bf16[264,1280]{1,0:T(8,128)(2,1)S(1)}, bf16[264,1280]{1,0:T(8,128)(2,1)}, u32[]{:S(2)}) copy-start(bf16[264,1280]{1,0:T(8,128)(2,1)} %pad.14) | copy-start | bytes 2027524
  20.1 34.2 %collective-permute-start.8 = (s16[5200,128]{1,0:T(8,128)(2,1)S(1)}, s16[5200,128]{1,0:T(8,128)(2,1)S(1)}, u32[]{:S(2)}, u32[]{:S(2)}) collective-permute-start(s16[5200,128]{1,0:T(8,128)(2,1)S(1)} %get-tuple-element.72), channel_id=1, source_target_pairs={{0,8},{2,10},{4,12},{6,14},{8,0},{10,2},{12,4},{14,6},{16,24},{18,... | collective-permute-start | bytes 3993608 | tf_op jit(solution)/shard_map/ppermute | solution.py:211
  21.8 26.4 %collective-permute-start.2 = (s16[4160,128]{1,0:T(8,128)(2,1)S(1)}, s16[4160,128]{1,0:T(8,128)(2,1)S(1)}, u32[]{:S(2)}, u32[]{:S(2)}) collective-permute-start(s16[4160,128]{1,0:T(8,128)(2,1)S(1)} %get-tuple-element.62), channel_id=1, source_target_pairs={{0,4},{2,6},{4,0},{6,2},{8,12},{10,14},{12,8},{14,10},{16,20},{18,... | collective-permute-start | bytes 3194888 | tf_op jit(solution)/shard_map/ppermute | solution.py:211
  31.7 2.8 %collective-permute-start.5 = (bf16[1024,256]{1,0:T(8,128)(2,1)}, bf16[1024,256]{1,0:T(8,128)(2,1)S(1)}, u32[]{:S(2)}, u32[]{:S(2)}) collective-permute-start(bf16[1024,256]{1,0:T(8,128)(2,1)} %collective-permute-done.3), channel_id=1, source_target_pairs={{0,1},{1,0},{2,3},{3,2},{4,5},{5,4},{6,7},{7,6},{8,9},{9,8},{10,11... | collective-permute-start | bytes 1572872 | tf_op jit(solution)/shard_map/ppermute | solution.py:242
  31.7 18.2 %collective-permute-start.9 = (bf16[264,1280]{1,0:T(8,128)(2,1)S(1)}, bf16[264,1280]{1,0:T(8,128)(2,1)S(1)}, u32[]{:S(2)}, u32[]{:S(2)}) collective-permute-start(bf16[264,1280]{1,0:T(8,128)(2,1)S(1)} %copy-done.3), channel_id=1, source_target_pairs={{0,2},{2,0},{4,6},{6,4},{8,10},{10,8},{12,14},{14,12},{16,18},{18,... | collective-permute-start | bytes 2027528 | tf_op jit(solution)/shard_map/ppermute | solution.py:211
  37.0 22.5 %collective-permute-start.7 = (s16[2080,128]{1,0:T(8,128)(2,1)S(1)}, s16[2080,128]{1,0:T(8,128)(2,1)S(1)}, u32[]{:S(2)}, u32[]{:S(2)}) collective-permute-start(s16[2080,128]{1,0:T(8,128)(2,1)S(1)} %get-tuple-element.71), channel_id=1, source_target_pairs={{0,4},{2,6},{4,0},{6,2},{8,12},{10,14},{12,8},{14,10},{16,20},{18,... | collective-permute-start | bytes 1597448 | tf_op jit(solution)/shard_map/ppermute | solution.py:211
  48.7 15.1 %collective-permute-start.6 = (s16[2080,128]{1,0:T(8,128)(2,1)S(1)}, s16[2080,128]{1,0:T(8,128)(2,1)S(1)}, u32[]{:S(2)}, u32[]{:S(2)}) collective-permute-start(s16[2080,128]{1,0:T(8,128)(2,1)S(1)} %get-tuple-element.69), channel_id=1, source_target_pairs={{0,8},{2,10},{4,12},{6,14},{8,0},{10,2},{12,4},{14,6},{16,24},{18,... | collective-permute-start | bytes 1597448 | tf_op jit(solution)/shard_map/ppermute | solution.py:211
  49.3 18.2 %collective-permute-start.13 = (bf16[264,1280]{1,0:T(8,128)(2,1)S(1)}, bf16[264,1280]{1,0:T(8,128)(2,1)S(1)}, u32[]{:S(2)}, u32[]{:S(2)}) collective-permute-start(bf16[264,1280]{1,0:T(8,128)(2,1)S(1)} %pad.16), channel_id=1, source_target_pairs={{0,2},{2,0},{4,6},{6,4},{8,10},{10,8},{12,14},{14,12},{16,18},{18,... | collective-permute-start | bytes 2027528 | tf_op jit(solution)/shard_map/ppermute | solution.py:211
  52.8 25.7 %collective-permute-start.15 = (bf16[264,1280]{1,0:T(8,128)(2,1)S(1)}, bf16[264,1280]{1,0:T(8,128)(2,1)S(1)}, u32[]{:S(2)}, u32[]{:S(2)}) collective-permute-start(bf16[264,1280]{1,0:T(8,128)(2,1)S(1)} %pad.17), channel_id=1, source_target_pairs={{0,2},{2,0},{4,6},{6,4},{8,10},{10,8},{12,14},{14,12},{16,18},{18,... | collective-permute-start | bytes 2027528 | tf_op jit(solution)/shard_map/ppermute | solution.py:211
  54.4 21.7 %collective-permute-start.11 = (s16[2608,128]{1,0:T(8,128)(2,1)S(1)}, s16[2608,128]{1,0:T(8,128)(2,1)S(1)}, u32[]{:S(2)}, u32[]{:S(2)}) collective-permute-start(s16[2608,128]{1,0:T(8,128)(2,1)S(1)} %get-tuple-element.80), channel_id=1, source_target_pairs={{0,4},{2,6},{4,0},{6,2},{8,12},{10,14},{12,8},{14,10},{16,20},{18,... | collective-permute-start | bytes 2002952 | tf_op jit(solution)/shard_map/ppermute | solution.py:211
  59.9 14.4 %collective-permute-start.12 = (s16[1040,128]{1,0:T(8,128)(2,1)S(1)}, s16[1040,128]{1,0:T(8,128)(2,1)S(1)}, u32[]{:S(2)}, u32[]{:S(2)}) collective-permute-start(s16[1040,128]{1,0:T(8,128)(2,1)S(1)} %get-tuple-element.81), channel_id=1, source_target_pairs={{0,8},{2,10},{4,12},{6,14},{8,0},{10,2},{12,4},{14,6},{16,24},{18,... | collective-permute-start | bytes 798728 | tf_op jit(solution)/shard_map/ppermute | solution.py:211
  64.2 13.3 %collective-permute-start.10 = (s16[1040,128]{1,0:T(8,128)(2,1)S(1)}, s16[1040,128]{1,0:T(8,128)(2,1)S(1)}, u32[]{:S(2)}, u32[]{:S(2)}) collective-permute-start(s16[1040,128]{1,0:T(8,128)(2,1)S(1)} %get-tuple-element.78), channel_id=1, source_target_pairs={{0,16},{2,18},{4,20},{6,22},{8,24},{10,26},{12,28},{14,30},{16,0},... | collective-permute-start | bytes 798728 | tf_op jit(solution)/shard_map/ppermute | solution.py:211
  70.3 22.2 %collective-permute-start.19 = (s16[2608,128]{1,0:T(8,128)(2,1)S(1)}, s16[2608,128]{1,0:T(8,128)(2,1)S(1)}, u32[]{:S(2)}, u32[]{:S(2)}) collective-permute-start(s16[2608,128]{1,0:T(8,128)(2,1)S(1)} %get-tuple-element.93), channel_id=1, source_target_pairs={{0,8},{2,10},{4,12},{6,14},{8,0},{10,2},{12,4},{14,6},{16,24},{18,... | collective-permute-start | bytes 2002952 | tf_op jit(solution)/shard_map/ppermute | solution.py:211
  74.3 18.6 %collective-permute-start.18 = (s16[2608,128]{1,0:T(8,128)(2,1)S(1)}, s16[2608,128]{1,0:T(8,128)(2,1)S(1)}, u32[]{:S(2)}, u32[]{:S(2)}) collective-permute-start(s16[2608,128]{1,0:T(8,128)(2,1)S(1)} %get-tuple-element.92), channel_id=1, source_target_pairs={{0,4},{2,6},{4,0},{6,2},{8,12},{10,14},{12,8},{14,10},{16,20},{18,... | collective-permute-start | bytes 2002952 | tf_op jit(solution)/shard_map/ppermute | solution.py:211
  81.4 25.1 %collective-permute-start.16 = (s16[2608,128]{1,0:T(8,128)(2,1)S(1)}, s16[2608,128]{1,0:T(8,128)(2,1)S(1)}, u32[]{:S(2)}, u32[]{:S(2)}) collective-permute-start(s16[2608,128]{1,0:T(8,128)(2,1)S(1)} %get-tuple-element.90), channel_id=1, source_target_pairs={{0,4},{2,6},{4,0},{6,2},{8,12},{10,14},{12,8},{14,10},{16,20},{18,... | collective-permute-start | bytes 2002952 | tf_op jit(solution)/shard_map/ppermute | solution.py:211
  83.0 24.0 %collective-permute-start.23 = (s16[1312,128]{1,0:T(8,128)(2,1)S(1)}, s16[1312,128]{1,0:T(8,128)(2,1)S(1)}, u32[]{:S(2)}, u32[]{:S(2)}) collective-permute-start(s16[1312,128]{1,0:T(8,128)(2,1)S(1)} %get-tuple-element.100), channel_id=1, source_target_pairs={{0,8},{2,10},{4,12},{6,14},{8,0},{10,2},{12,4},{14,6},{16,24},{18,... | collective-permute-start | bytes 1007624 | tf_op jit(solution)/shard_map/ppermute | solution.py:211
  84.6 16.2 %collective-permute-start.17 = (s16[528,128]{1,0:T(8,128)(2,1)S(1)}, s16[528,128]{1,0:T(8,128)(2,1)S(1)}, u32[]{:S(2)}, u32[]{:S(2)}) collective-permute-start(s16[528,128]{1,0:T(8,128)(2,1)S(1)} %get-tuple-element.91), channel_id=1, source_target_pairs={{0,16},{2,18},{4,20},{6,22},{8,24},{10,26},{12,28},{14,30},{16,0},... | collective-permute-start | bytes 405512 | tf_op jit(solution)/shard_map/ppermute | solution.py:211
  93.3 24.1 %collective-permute-start.22 = (s16[1312,128]{1,0:T(8,128)(2,1)S(1)}, s16[1312,128]{1,0:T(8,128)(2,1)S(1)}, u32[]{:S(2)}, u32[]{:S(2)}) collective-permute-start(s16[1312,128]{1,0:T(8,128)(2,1)S(1)} %get-tuple-element.99), channel_id=1, source_target_pairs={{0,16},{2,18},{4,20},{6,22},{8,24},{10,26},{12,28},{14,30},{16,0},... | collective-permute-start | bytes 1007624 | tf_op jit(solution)/shard_map/ppermute | solution.py:211
  100.5 18.6 %collective-permute-start.21 = (s16[1312,128]{1,0:T(8,128)(2,1)S(1)}, s16[1312,128]{1,0:T(8,128)(2,1)S(1)}, u32[]{:S(2)}, u32[]{:S(2)}) collective-permute-start(s16[1312,128]{1,0:T(8,128)(2,1)S(1)} %get-tuple-element.98), channel_id=1, source_target_pairs={{0,4},{2,6},{4,0},{6,2},{8,12},{10,14},{12,8},{14,10},{16,20},{18,... | collective-permute-start | bytes 1007624 | tf_op jit(solution)/shard_map/ppermute | solution.py:211
  106.9 12.6 %collective-permute-start.20 = (s16[1312,128]{1,0:T(8,128)(2,1)S(1)}, s16[1312,128]{1,0:T(8,128)(2,1)S(1)}, u32[]{:S(2)}, u32[]{:S(2)}) collective-permute-start(s16[1312,128]{1,0:T(8,128)(2,1)S(1)} %get-tuple-element.97), channel_id=1, source_target_pairs={{0,8},{2,10},{4,12},{6,14},{8,0},{10,2},{12,4},{14,6},{16,24},{18,... | collective-permute-start | bytes 1007624 | tf_op jit(solution)/shard_map/ppermute | solution.py:211
  107.3 18.2 %collective-permute-start.25 = (s16[656,128]{1,0:T(8,128)(2,1)S(1)}, s16[656,128]{1,0:T(8,128)(2,1)S(1)}, u32[]{:S(2)}, u32[]{:S(2)}) collective-permute-start(s16[656,128]{1,0:T(8,128)(2,1)S(1)} %get-tuple-element.106), channel_id=1, source_target_pairs={{0,16},{2,18},{4,20},{6,22},{8,24},{10,26},{12,28},{14,30},{16,0},... | collective-permute-start | bytes 503816 | tf_op jit(solution)/shard_map/ppermute | solution.py:211
  108.9 13.9 %collective-permute-start.14 = (s16[528,128]{1,0:T(8,128)(2,1)S(1)}, s16[528,128]{1,0:T(8,128)(2,1)S(1)}, u32[]{:S(2)}, u32[]{:S(2)}) collective-permute-start(s16[528,128]{1,0:T(8,128)(2,1)S(1)} %get-tuple-element.87), channel_id=1, source_target_pairs={{0,2},{2,0},{4,6},{6,4},{8,10},{10,8},{12,14},{14,12},{16,18},{18,... | collective-permute-start | bytes 405512 | tf_op jit(solution)/shard_map/ppermute | solution.py:211
  117.6 7.9 %collective-permute-start.24 = (s16[656,128]{1,0:T(8,128)(2,1)S(1)}, s16[656,128]{1,0:T(8,128)(2,1)S(1)}, u32[]{:S(2)}, u32[]{:S(2)}) collective-permute-start(s16[656,128]{1,0:T(8,128)(2,1)S(1)} %get-tuple-element.105), channel_id=1, source_target_pairs={{0,2},{2,0},{4,6},{6,4},{8,10},{10,8},{12,14},{14,12},{16,18},{18,... | collective-permute-start | bytes 503816 | tf_op jit(solution)/shard_map/ppermute | solution.py:211
  119.4 10.2 %collective-permute-start.26 = (s16[656,128]{1,0:T(8,128)(2,1)S(1)}, s16[656,128]{1,0:T(8,128)(2,1)S(1)}, u32[]{:S(2)}, u32[]{:S(2)}) collective-permute-start(s16[656,128]{1,0:T(8,128)(2,1)S(1)} %get-tuple-element.107), channel_id=1, source_target_pairs={{0,16},{2,18},{4,20},{6,22},{8,24},{10,26},{12,28},{14,30},{16,0},... | collective-permute-start | bytes 503816 | tf_op jit(solution)/shard_map/ppermute | solution.py:211
  119.8 13.4 %collective-permute-start.27 = (s16[656,128]{1,0:T(8,128)(2,1)S(1)}, s16[656,128]{1,0:T(8,128)(2,1)S(1)}, u32[]{:S(2)}, u32[]{:S(2)}) collective-permute-start(s16[656,128]{1,0:T(8,128)(2,1)S(1)} %get-tuple-element.108), channel_id=1, source_target_pairs={{0,16},{2,18},{4,20},{6,22},{8,24},{10,26},{12,28},{14,30},{16,0},... | collective-permute-start | bytes 503816 | tf_op jit(solution)/shard_map/ppermute | solution.py:211
  129.7 3.6 %copy-start.4 = (f32[56,64,128]{2,1,0:T(8,128)}, f32[56,64,128]{2,1,0:T(8,128)S(1)}, u32[]{:S(2)}) copy-start(f32[56,64,128]{2,1,0:T(8,128)S(1)} %constant_dynamic-update-slice_fusion.7) | copy-start | bytes 5505028

commit v5 on v3

--- a/solution.py
+++ b/solution.py
@@ -11,7 +11,7 @@
 LEVELS = 32700.0
 STEPS = 128.0
 SMALLEST = 2.0**-110
-PAD = 16
+PAD = 8
 VMEM_LIMIT = 16 * 1024 * 1024
 
 
@@ -56,9 +56,9 @@
     for i in range(1, lengths.shape[1]):
         live = live + lengths[0, i]
     keep = lax.broadcasted_iota(jnp.int32, (BLOCK, slots), 1) < live
+    keep = jnp.where(keep, 1.0, 0.0).astype(activations.dtype)
     for b in range(features // BLOCK):
-        block = activations[:, b * BLOCK : (b + 1) * BLOCK].astype(jnp.float32).T
-        block = jnp.where(keep, block, 0.0).astype(activations.dtype)
+        block = activations[:, b * BLOCK : (b + 1) * BLOCK].T * keep
         for p in range(BLOCK // rows):
             to = pl.ds((b * (BLOCK // rows) + p) // 2 * rows, rows)
             piece = block[p * rows : (p + 1) * rows]
@@ -152,8 +152,8 @@
 def plan_of(columns, depth):
     if depth != 4 or columns % 56 != 0:
         return [columns], [list(range(1, depth))], [[0]], [("multiply", 0)] + [("step", 0)] * (depth - 1)
-    widths = [8, 10, 12, 12, 8, 6]
-    paths = [[1, 3, 2, 0], [2, 1, 3, 0], [1, 3, 2], [2, 1, 3], [1, 2, 3], [1, 2, 3]]
+    widths = [8, 10, 12, 10, 10, 6]
+    paths = [[2, 1, 3, 0], [1, 2, 3, 0], [2, 1, 3], [1, 2, 3], [1, 2, 3], [1, 2, 3]]
     messages = [[2], [3], [4], [5]]
     work = [
         ("multiply", 0),
@@ -163,23 +163,23 @@
         ("step", 1),
         ("multiply", 3),
         ("step", 2),
+        ("step", 0),
         ("multiply", 4),
-        ("step", 0),
+        ("step", 3),
         ("multiply", 5),
         ("step", 1),
+        ("step", 0),
+        ("step", 4),
         ("step", 3),
+        ("step", 1),
         ("step", 2),
-        ("step", 4),
-        ("step", 0),
         ("step", 3),
-        ("step", 0),
         ("step", 1),
         ("step", 5),
         ("step", 4),
-        ("step", 3),
+        ("step", 2),
+        ("step", 0),
         ("step", 5),
-        ("step", 2),
-        ("step", 1),
         ("step", 4),
         ("step", 5),
     ]

time: 144 us -> 134 us (0.931)
  starting transfers between devices: 41 us -> 35.1 us
  waiting for transfers between devices: 68.2 us -> 65.6 us
    ppermute x25, starting transfers between devices: 40.2 us -> 34.4 us  [swap(): return lax.ppermute(sent, 'dp', [(o, o ^ 1 << bit) for o in range(owners)])]
    ppermute x25, waiting for transfers between devices: 68.2 us -> 64.2 us  [swap(): return lax.ppermute(sent, 'dp', [(o, o ^ 1 << bit) for o in range(owners)])]
    unnamed x17 -> x21, local copies, waits for them, and re-layouts: 4.53 us -> 3.25 us
  transfers between devices with their start and end apart: 28 -> 28, of which waited for: 15 -> 15; matrix products, arithmetic and copies ran while one was open for 5% -> 4% of each run, Pallas kernels for 15% -> 16%
where the time goes in v5:
time: 134 us; the launch traced here: 133 us
  waiting for transfers between devices  65.6 us (49%)
  starting transfers between devices  35.1 us (26%)
  Pallas kernels  23.6 us (18%)
  local copies, waits for them, and re-layouts  8.55 us (6%)
    ppermute x25, waiting for transfers between devices, swap(): return lax.ppermute(sent, 'dp', [(o, o ^ 1 << bit) for o in range(owners)])  64.2 us
    ppermute x25, starting transfers between devices, swap(): return lax.ppermute(sent, 'dp', [(o, o ^ 1 << bit) for o in range(owners)])  34.4 us
    pallas_call x6, Pallas kernels, multiply(): pl.pallas_call(functools.partial(multiply_kernel, width, rows, height, or...  16 us
    pallas_call x20, Pallas kernels, combine(): pl.pallas_call(functools.partial(combine_kernel, shapes, rows, n, encoded...  5.41 us
    unnamed x21, local copies, waits for them, and re-layouts  3.25 us
  transfers between devices with their start and end apart: 28, of which 15 were waited for; matrix products, arithmetic and copies ran while one was open for 4% of the time, Pallas kernels for 16%

profile of v5, /device:TPU:0, one launch (start us, length us, event | category | flops | bytes accessed | tf_op | source)
XLA Modules:
  0.0 133.3 jit_solution(5872377094400465787)
XLA Ops:
  0.0 1.2 copy-done.1
  1.2 0.7 copy-done.2
  1.9 2.2 %prepare.1 = (bf16[1024,256]{1,0:T(8,128)(2,1)S(1)}, bf16[1024,256]{1,0:T(8,128)(2,1)S(1)}) custom-call(s32[1]{0:T(128)} %bitcast.me.refs_3_, s32[1,4]{1,0:T(1,128)S(1)} %copy-done.2, bf16[256,2048]{1,0:T(8,128)(2,1)S(1)} %copy-done.1), custom_call_target="tpu_custom_call" | custom-call | tf_op jit(solution)/shard_map/prepare/pallas_call | solution.py:225
  4.1 0.5 collective-permute-start.1
  4.6 2.6 %collective-permute-start.3 = (bf16[1024,256]{1,0:T(8,128)(2,1)S(1)}, bf16[1024,256]{1,0:T(8,128)(2,1)}, u32[]{:S(2)}, u32[]{:S(2)}) collective-permute-start(bf16[1024,256]{1,0:T(8,128)(2,1)S(1)} %get-tuple-element.60), channel_id=1, source_target_pairs={{0,2},{2,0},{4,6},{6,4},{8,10},{10,8},{12,14},{14,12},{16,18},{18,... | collective-permute-start | bytes 1572872 | tf_op jit(solution)/shard_map/ppermute | solution.py:211
  7.2 1.4 %fusion.5 = (bf16[256,1280]{1,0:T(8,128)(2,1)S(1)}, bf16[256,1280]{1,0:T(8,128)(2,1)S(1)}) fusion(bf16[256,7168]{1,0:T(8,128)(2,1)} %refs_2_.11), kind=kLoop, calls=%fused_computation.26 | loop fusion | bytes 2621440 | tf_op jit(solution)/shard_map/slice | solution.py:215
  8.6 0.9 pad.15
  9.7 0.3 collective-permute-start.4
  10.2 1.4 %collective-permute-done = bf16[1024,256]{1,0:T(8,128)(2,1)} collective-permute-done((bf16[1024,256]{1,0:T(8,128)(2,1)S(1)}, bf16[1024,256]{1,0:T(8,128)(2,1)}, u32[]{:S(2)}, u32[]{:S(2)}) %collective-permute-start) | collective-permute-done | bytes 524320 | tf_op jit(solution)/shard_map/ppermute | solution.py:242
  11.6 1.1 constant_dynamic-update-slice_fusion.refs_0_
  12.7 1.1 constant_dynamic-update-slice_fusion.2.refs_1_
  13.7 2.5 %multiply.6 = (f32[4096,128]{1,0:T(8,128)S(1)}, s16[4160,128]{1,0:T(8,128)(2,1)S(1)}) custom-call(s32[1]{0:T(128)} %bitcast.me.refs_3_, s32[8,8]{1,0:T(8,128)S(1)} %slice.40.picks, bf16[2048,256]{1,0:T(8,128)(2,1)S(1)} %constant_dynamic-update-slice_fusion.refs_0_, bf16[2048,256]{1,0:T(8,128)(2,1)S(1)} %constant_dynamic-update-slice_fusion.2.refs_1_, ...), custom_call_target="tpu_custom_call" | custom-call | tf_op jit(solution)/shard_map/multiply/pallas_call | solution.py:270
  16.3 3.1 %multiply.7 = (f32[5120,128]{1,0:T(8,128)S(1)}, s16[5200,128]{1,0:T(8,128)(2,1)S(1)}) custom-call(s32[1]{0:T(128)} %bitcast.me.refs_3_, s32[10,8]{1,0:T(8,128)S(1)} %get-tuple-element.113.picks, bf16[2048,256]{1,0:T(8,128)(2,1)S(1)} %constant_dynamic-update-slice_fusion.refs_0_, bf16[2048,256]{1,0:T(8,128)(2,1)S(1)} %constant_dynamic-update-slice_fusion.2.refs_1_, ...), custom_call_target="tpu_custom_call" | custom-call | tf_op jit(solution)/shard_map/multiply/pallas_call | solution.py:270
  19.4 1.6 %collective-permute-start.9 = (s16[5200,128]{1,0:T(8,128)(2,1)S(1)}, s16[5200,128]{1,0:T(8,128)(2,1)S(1)}, u32[]{:S(2)}, u32[]{:S(2)}) collective-permute-start(s16[5200,128]{1,0:T(8,128)(2,1)S(1)} %get-tuple-element.73), channel_id=1, source_target_pairs={{0,4},{2,6},{4,0},{6,2},{8,12},{10,14},{12,8},{14,10},{16,20},{18,... | collective-permute-start | bytes 3993608 | tf_op jit(solution)/shard_map/ppermute | solution.py:211
  21.0 1.6 %collective-permute-start.2 = (s16[4160,128]{1,0:T(8,128)(2,1)S(1)}, s16[4160,128]{1,0:T(8,128)(2,1)S(1)}, u32[]{:S(2)}, u32[]{:S(2)}) collective-permute-start(s16[4160,128]{1,0:T(8,128)(2,1)S(1)} %get-tuple-element.62), channel_id=1, source_target_pairs={{0,8},{2,10},{4,12},{6,14},{8,0},{10,2},{12,4},{14,6},{16,24},{18,... | collective-permute-start | bytes 3194888 | tf_op jit(solution)/shard_map/ppermute | solution.py:211
  22.5 14.5 %collective-permute-done.4.refs_3_ = bf16[264,1536]{1,0:T(8,128)(2,1)S(1)} collective-permute-done((bf16[264,1536]{1,0:T(8,128)(2,1)S(1)}, bf16[264,1536]{1,0:T(8,128)(2,1)S(1)}, u32[]{:S(2)}, u32[]{:S(2)}) %collective-permute-start.4) | collective-permute-done | bytes 811040 | tf_op jit(solution)/shard_map/ppermute | solution.py:211
  37.1 1.8 %collective-permute-start.8 = (bf16[264,1280]{1,0:T(8,128)(2,1)S(1)}, bf16[264,1280]{1,0:T(8,128)(2,1)S(1)}, u32[]{:S(2)}, u32[]{:S(2)}) collective-permute-start(bf16[264,1280]{1,0:T(8,128)(2,1)S(1)} %copy-done.3), channel_id=1, source_target_pairs={{0,2},{2,0},{4,6},{6,4},{8,10},{10,8},{12,14},{14,12},{16,18},{18,... | collective-permute-start | bytes 2027528 | tf_op jit(solution)/shard_map/ppermute | solution.py:211
  38.8 1.1 constant_dynamic-update-slice_fusion.5
  40.0 3.0 %multiply.8 = (f32[3072,128]{1,0:T(8,128)S(1)}, s16[3120,128]{1,0:T(8,128)(2,1)S(1)}) custom-call(s32[1]{0:T(128)} %bitcast.me.refs_3_, s32[12,8]{1,0:T(8,128)S(1)} %slice.41.picks, bf16[2048,256]{1,0:T(8,128)(2,1)S(1)} %constant_dynamic-update-slice_fusion.refs_0_, bf16[2048,256]{1,0:T(8,128)(2,1)S(1)} %constant_dynamic-update-slice_fusion.4.refs_1_, ...), custom_call_target="tpu_custom_call" | custom-call | tf_op jit(solution)/shard_map/multiply/pallas_call | solution.py:270
  43.0 1.6 %collective-permute-start.7 = (s16[3120,128]{1,0:T(8,128)(2,1)S(1)}, s16[3120,128]{1,0:T(8,128)(2,1)S(1)}, u32[]{:S(2)}, u32[]{:S(2)}) collective-permute-start(s16[3120,128]{1,0:T(8,128)(2,1)S(1)} %get-tuple-element.71), channel_id=1, source_target_pairs={{0,8},{2,10},{4,12},{6,14},{8,0},{10,2},{12,4},{14,6},{16,24},{18,... | collective-permute-start | bytes 2396168 | tf_op jit(solution)/shard_map/ppermute | solution.py:211
  44.7 1.1 collective-permute-start.14
  45.8 0.8 collective-permute-done.2.refs_1_
  46.6 0.6 combine.20
  47.2 0.8 collective-permute-start.6
  47.9 3.6 %collective-permute-done.9.refs_1_ = s16[5200,128]{1,0:T(8,128)(2,1)S(1)} collective-permute-done((s16[5200,128]{1,0:T(8,128)(2,1)S(1)}, s16[5200,128]{1,0:T(8,128)(2,1)S(1)}, u32[]{:S(2)}, u32[]{:S(2)}) %collective-permute-start.9) | collective-permute-done | bytes 1331232 | tf_op jit(solution)/shard_map/ppermute | solution.py:211
  51.5 0.7 combine.21
  52.2 2.8 %collective-permute-done.8.refs_3_ = bf16[264,1280]{1,0:T(8,128)(2,1)S(1)} collective-permute-done((bf16[264,1280]{1,0:T(8,128)(2,1)S(1)}, bf16[264,1280]{1,0:T(8,128)(2,1)S(1)}, u32[]{:S(2)}, u32[]{:S(2)}) %collective-permute-start.8) | collective-permute-done | bytes 675872 | tf_op jit(solution)/shard_map/ppermute | solution.py:211
  55.0 2.8 %multiply.9 = (f32[2560,128]{1,0:T(8,128)S(1)}, s16[2608,128]{1,0:T(8,128)(2,1)S(1)}) custom-call(s32[1]{0:T(128)} %bitcast.me.refs_3_, s32[10,8]{1,0:T(8,128)S(1)} %get-tuple-element.112.picks, bf16[2048,256]{1,0:T(8,128)(2,1)S(1)} %constant_dynamic-update-slice_fusion.refs_0_, bf16[2048,256]{1,0:T(8,128)(2,1)S(1)} %constant_dynamic-update-slice_fusion.4.refs_1_, ...), custom_call_target="tpu_custom_call" | custom-call | tf_op jit(solution)/shard_map/multiply/pallas_call | solution.py:270
  57.9 1.9 %collective-permute-start.13 = (s16[2608,128]{1,0:T(8,128)(2,1)S(1)}, s16[2608,128]{1,0:T(8,128)(2,1)S(1)}, u32[]{:S(2)}, u32[]{:S(2)}) collective-permute-start(s16[2608,128]{1,0:T(8,128)(2,1)S(1)} %get-tuple-element.82), channel_id=1, source_target_pairs={{0,4},{2,6},{4,0},{6,2},{8,12},{10,14},{12,8},{14,10},{16,20},{18,... | collective-permute-start | bytes 2002952 | tf_op jit(solution)/shard_map/ppermute | solution.py:211
  59.7 1.6 %collective-permute-start.11 = (s16[2608,128]{1,0:T(8,128)(2,1)S(1)}, s16[2608,128]{1,0:T(8,128)(2,1)S(1)}, u32[]{:S(2)}, u32[]{:S(2)}) collective-permute-start(s16[2608,128]{1,0:T(8,128)(2,1)S(1)} %get-tuple-element.79), channel_id=1, source_target_pairs={{0,8},{2,10},{4,12},{6,14},{8,0},{10,2},{12,4},{14,6},{16,24},{18,... | collective-permute-start | bytes 2002952 | tf_op jit(solution)/shard_map/ppermute | solution.py:211
  61.3 2.3 %collective-permute-done.7.refs_1_ = s16[3120,128]{1,0:T(8,128)(2,1)S(1)} collective-permute-done((s16[3120,128]{1,0:T(8,128)(2,1)S(1)}, s16[3120,128]{1,0:T(8,128)(2,1)S(1)}, u32[]{:S(2)}, u32[]{:S(2)}) %collective-permute-start.7) | collective-permute-done | bytes 798752 | tf_op jit(solution)/shard_map/ppermute | solution.py:211
  63.7 1.0 collective-permute-start.12
  64.7 0.4 combine.22
  65.2 0.3 combine.23
  65.5 4.0 %collective-permute-done.14.refs_3_ = bf16[264,1280]{1,0:T(8,128)(2,1)S(1)} collective-permute-done((bf16[264,1280]{1,0:T(8,128)(2,1)S(1)}, bf16[264,1280]{1,0:T(8,128)(2,1)S(1)}, u32[]{:S(2)}, u32[]{:S(2)}) %collective-permute-start.14) | collective-permute-done | bytes 675872 | tf_op jit(solution)/shard_map/ppermute | solution.py:211
  69.5 2.9 %multiply.10 = (f32[2560,128]{1,0:T(8,128)S(1)}, s16[2608,128]{1,0:T(8,128)(2,1)S(1)}) custom-call(s32[1]{0:T(128)} %bitcast.me.refs_3_, s32[10,8]{1,0:T(8,128)S(1)} %get-tuple-element.111.picks, bf16[2048,256]{1,0:T(8,128)(2,1)S(1)} %constant_dynamic-update-slice_fusion.refs_0_, bf16[2048,256]{1,0:T(8,128)(2,1)S(1)} %constant_dynamic-update-slice_fusion.4.refs_1_, ...), custom_call_target="tpu_custom_call" | custom-call | tf_op jit(solution)/shard_map/multiply/pallas_call | solution.py:270
  72.4 1.9 %collective-permute-start.19 = (s16[2608,128]{1,0:T(8,128)(2,1)S(1)}, s16[2608,128]{1,0:T(8,128)(2,1)S(1)}, u32[]{:S(2)}, u32[]{:S(2)}) collective-permute-start(s16[2608,128]{1,0:T(8,128)(2,1)S(1)} %get-tuple-element.93), channel_id=1, source_target_pairs={{0,4},{2,6},{4,0},{6,2},{8,12},{10,14},{12,8},{14,10},{16,20},{18,... | collective-permute-start | bytes 2002952 | tf_op jit(solution)/shard_map/ppermute | solution.py:211
  74.3 2.6 %collective-permute-start.10 = (s16[1040,128]{1,0:T(8,128)(2,1)S(1)}, s16[1040,128]{1,0:T(8,128)(2,1)S(1)}, u32[]{:S(2)}, u32[]{:S(2)}) collective-permute-start(s16[1040,128]{1,0:T(8,128)(2,1)S(1)} %get-tuple-element.78), channel_id=1, source_target_pairs={{0,16},{2,18},{4,20},{6,22},{8,24},{10,26},{12,28},{14,30},{16,0},... | collective-permute-start | bytes 798728 | tf_op jit(solution)/shard_map/ppermute | solution.py:211
  76.8 0.4 collective-permute-done.13.refs_1_
  77.2 0.4 combine.24
  77.6 1.6 %collective-permute-start.18 = (s16[1312,128]{1,0:T(8,128)(2,1)S(1)}, s16[1312,128]{1,0:T(8,128)(2,1)S(1)}, u32[]{:S(2)}, u32[]{:S(2)}) collective-permute-start(s16[1312,128]{1,0:T(8,128)(2,1)S(1)} %get-tuple-element.92), channel_id=1, source_target_pairs={{0,8},{2,10},{4,12},{6,14},{8,0},{10,2},{12,4},{14,6},{16,24},{18,... | collective-permute-start | bytes 1007624 | tf_op jit(solution)/shard_map/ppermute | solution.py:211
  79.3 1.5 %collective-permute-start.16 = (s16[1568,128]{1,0:T(8,128)(2,1)S(1)}, s16[1568,128]{1,0:T(8,128)(2,1)S(1)}, u32[]{:S(2)}, u32[]{:S(2)}) collective-permute-start(s16[1568,128]{1,0:T(8,128)(2,1)S(1)} %get-tuple-element.90), channel_id=1, source_target_pairs={{0,4},{2,6},{4,0},{6,2},{8,12},{10,14},{12,8},{14,10},{16,20},{18,... | collective-permute-start | bytes 1204232 | tf_op jit(solution)/shard_map/ppermute | solution.py:211
  80.8 1.7 %multiply.11 = (f32[1536,128]{1,0:T(8,128)S(1)}, s16[1568,128]{1,0:T(8,128)(2,1)S(1)}) custom-call(s32[1]{0:T(128)} %bitcast.me.refs_3_, s32[6,8]{1,0:T(8,128)S(1)} %slice.44.picks, bf16[2048,256]{1,0:T(8,128)(2,1)S(1)} %constant_dynamic-update-slice_fusion.refs_0_, bf16[2048,256]{1,0:T(8,128)(2,1)S(1)} %constant_dynamic-update-slice_fusion.4.refs_1_, ...), custom_call_target="tpu_custom_call" | custom-call | tf_op jit(solution)/shard_map/multiply/pallas_call | solution.py:270
  82.5 0.4 combine.25
  83.0 2.6 %collective-permute-start.17 = (s16[1312,128]{1,0:T(8,128)(2,1)S(1)}, s16[1312,128]{1,0:T(8,128)(2,1)S(1)}, u32[]{:S(2)}, u32[]{:S(2)}) collective-permute-start(s16[1312,128]{1,0:T(8,128)(2,1)S(1)} %get-tuple-element.91), channel_id=1, source_target_pairs={{0,16},{2,18},{4,20},{6,22},{8,24},{10,26},{12,28},{14,30},{16,0},... | collective-permute-start | bytes 1007624 | tf_op jit(solution)/shard_map/ppermute | solution.py:211
  85.6 4.7 %collective-permute-done.10.refs_1_ = s16[1040,128]{1,0:T(8,128)(2,1)S(1)} collective-permute-done((s16[1040,128]{1,0:T(8,128)(2,1)S(1)}, s16[1040,128]{1,0:T(8,128)(2,1)S(1)}, u32[]{:S(2)}, u32[]{:S(2)}) %collective-permute-start.10) | collective-permute-done | bytes 266272 | tf_op jit(solution)/shard_map/ppermute | solution.py:211
  90.8 0.8 collective-permute-done.19.refs_1_
  91.5 0.4 combine.27
  91.9 1.6 %collective-permute-start.21 = (s16[1312,128]{1,0:T(8,128)(2,1)S(1)}, s16[1312,128]{1,0:T(8,128)(2,1)S(1)}, u32[]{:S(2)}, u32[]{:S(2)}) collective-permute-start(s16[1312,128]{1,0:T(8,128)(2,1)S(1)} %get-tuple-element.99), channel_id=1, source_target_pairs={{0,8},{2,10},{4,12},{6,14},{8,0},{10,2},{12,4},{14,6},{16,24},{18,... | collective-permute-start | bytes 1007624 | tf_op jit(solution)/shard_map/ppermute | solution.py:211
  93.6 2.1 %collective-permute-done.18.refs_1_ = s16[1312,128]{1,0:T(8,128)(2,1)S(1)} collective-permute-done((s16[1312,128]{1,0:T(8,128)(2,1)S(1)}, s16[1312,128]{1,0:T(8,128)(2,1)S(1)}, u32[]{:S(2)}, u32[]{:S(2)}) %collective-permute-start.18) | collective-permute-done | bytes 335904 | tf_op jit(solution)/shard_map/ppermute | solution.py:211
  95.7 0.3 combine.28
  96.0 0.5 collective-permute-start.24
  96.5 8.1 %collective-permute-done.17.refs_1_ = s16[1312,128]{1,0:T(8,128)(2,1)S(1)} collective-permute-done((s16[1312,128]{1,0:T(8,128)(2,1)S(1)}, s16[1312,128]{1,0:T(8,128)(2,1)S(1)}, u32[]{:S(2)}, u32[]{:S(2)}) %collective-permute-start.17) | collective-permute-done | bytes 335904 | tf_op jit(solution)/shard_map/ppermute | solution.py:211
  104.6 0.3 combine.29
  104.9 0.3 combine.30
  105.3 1.4 %collective-permute-start.23 = (s16[656,128]{1,0:T(8,128)(2,1)S(1)}, s16[656,128]{1,0:T(8,128)(2,1)S(1)}, u32[]{:S(2)}, u32[]{:S(2)}) collective-permute-start(s16[656,128]{1,0:T(8,128)(2,1)S(1)} %get-tuple-element.101), channel_id=1, source_target_pairs={{0,2},{2,0},{4,6},{6,4},{8,10},{10,8},{12,14},{14,12},{16,18},{18,... | collective-permute-start | bytes 503816 | tf_op jit(solution)/shard_map/ppermute | solution.py:211
  106.7 8.9 %collective-permute-done.24.refs_1_ = s16[656,128]{1,0:T(8,128)(2,1)S(1)} collective-permute-done((s16[656,128]{1,0:T(8,128)(2,1)S(1)}, s16[656,128]{1,0:T(8,128)(2,1)S(1)}, u32[]{:S(2)}, u32[]{:S(2)}) %collective-permute-start.24) | collective-permute-done | bytes 167968 | tf_op jit(solution)/shard_map/ppermute | solution.py:211
  115.5 1.2 collective-permute-start.15
  116.9 0.2 combine.33
  117.2 0.3 combine.34
  117.5 3.2 %collective-permute-start.25 = (s16[656,128]{1,0:T(8,128)(2,1)S(1)}, s16[656,128]{1,0:T(8,128)(2,1)S(1)}, u32[]{:S(2)}, u32[]{:S(2)}) collective-permute-start(s16[656,128]{1,0:T(8,128)(2,1)S(1)} %get-tuple-element.105), channel_id=1, source_target_pairs={{0,16},{2,18},{4,20},{6,22},{8,24},{10,26},{12,28},{14,30},{16,0},... | collective-permute-start | bytes 503816 | tf_op jit(solution)/shard_map/ppermute | solution.py:211
  121.0 5.5 %collective-permute-done.26.refs_1_ = s16[784,128]{1,0:T(8,128)(2,1)S(1)} collective-permute-done((s16[784,128]{1,0:T(8,128)(2,1)S(1)}, s16[784,128]{1,0:T(8,128)(2,1)S(1)}, u32[]{:S(2)}, u32[]{:S(2)}) %collective-permute-start.26) | collective-permute-done | bytes 200736 | tf_op jit(solution)/shard_map/ppermute | solution.py:211
  126.9 5.6 %collective-permute-done.27.refs_1_ = s16[400,128]{1,0:T(8,128)(2,1)S(1)} collective-permute-done((s16[400,128]{1,0:T(8,128)(2,1)S(1)}, s16[400,128]{1,0:T(8,128)(2,1)S(1)}, u32[]{:S(2)}, u32[]{:S(2)}) %collective-permute-start.27) | collective-permute-done | bytes 102432 | tf_op jit(solution)/shard_map/ppermute | solution.py:211
  132.6 0.7 constant_dynamic-update-slice_fusion.6
  (58 shorter events, 2.1 us)
Async XLA Ops:
  0.0 1.2 copy-start.1
  1.2 0.7 copy-start.2
  4.1 4.5 %slice-start = ((bf16[256,7168]{1,0:T(8,128)(2,1)}), bf16[256,1536]{1,0:T(8,128)(2,1)S(1)}, s32[]{:S(2)}) async-start(bf16[256,7168]{1,0:T(8,128)(2,1)} %refs_2_.11), calls=%async_computation | async-start | bytes 1572864 | tf_op jit(solution)/shard_map/slice | solution.py:215
  4.1 8.5 %collective-permute-start.1 = (bf16[1024,256]{1,0:T(8,128)(2,1)S(1)}, bf16[1024,256]{1,0:T(8,128)(2,1)}, u32[]{:S(2)}, u32[]{:S(2)}) collective-permute-start(bf16[1024,256]{1,0:T(8,128)(2,1)S(1)} %get-tuple-element.60), channel_id=1, source_target_pairs={{0,1},{1,0},{2,3},{3,2},{4,5},{5,4},{6,7},{7,6},{8,9},{9,8},{10,11... | collective-permute-start | bytes 1572872 | tf_op jit(solution)/shard_map/ppermute | solution.py:242
  4.6 17.9 %collective-permute-start.3 = (bf16[1024,256]{1,0:T(8,128)(2,1)S(1)}, bf16[1024,256]{1,0:T(8,128)(2,1)}, u32[]{:S(2)}, u32[]{:S(2)}) collective-permute-start(bf16[1024,256]{1,0:T(8,128)(2,1)S(1)} %get-tuple-element.60), channel_id=1, source_target_pairs={{0,2},{2,0},{4,6},{6,4},{8,10},{10,8},{12,14},{14,12},{16,18},{18,... | collective-permute-start | bytes 1572872 | tf_op jit(solution)/shard_map/ppermute | solution.py:211
  8.6 1.4 %copy-start.5 = (s32[56,8]{0,1:T(8,128)S(1)}, s32[56,8]{0,1:T(8,128)}, u32[]{:S(2)}) copy-start(s32[56,8]{0,1:T(8,128)} %param.6) | copy-start | bytes 5380
  9.5 2.0 %collective-permute-start = (bf16[1024,256]{1,0:T(8,128)(2,1)S(1)}, bf16[1024,256]{1,0:T(8,128)(2,1)}, u32[]{:S(2)}, u32[]{:S(2)}) collective-permute-start(bf16[1024,256]{1,0:T(8,128)(2,1)S(1)} %get-tuple-element.59), channel_id=1, source_target_pairs={{0,1},{1,0},{2,3},{3,2},{4,5},{5,4},{6,7},{7,6},{8,9},{9,8},{10,11... | collective-permute-start | bytes 1572872 | tf_op jit(solution)/shard_map/ppermute | solution.py:242
  9.7 27.4 %collective-permute-start.4 = (bf16[264,1536]{1,0:T(8,128)(2,1)S(1)}, bf16[264,1536]{1,0:T(8,128)(2,1)S(1)}, u32[]{:S(2)}, u32[]{:S(2)}) collective-permute-start(bf16[264,1536]{1,0:T(8,128)(2,1)S(1)} %pad.16), channel_id=1, source_target_pairs={{0,2},{2,0},{4,6},{6,4},{8,10},{10,8},{12,14},{14,12},{16,18},{18,... | collective-permute-start | bytes 2433032 | tf_op jit(solution)/shard_map/ppermute | solution.py:211
  10.1 3.6 %copy-start = (bf16[256,7168]{1,0:T(8,128)(2,1)S(1)}, bf16[256,7168]{1,0:T(8,128)(2,1)}, u32[]{:S(2)}) copy-start(bf16[256,7168]{1,0:T(8,128)(2,1)} %refs_2_.11) | copy-start | bytes 11010052
  16.3 20.8 %copy-start.3 = (bf16[264,1280]{1,0:T(8,128)(2,1)S(1)}, bf16[264,1280]{1,0:T(8,128)(2,1)}, u32[]{:S(2)}) copy-start(bf16[264,1280]{1,0:T(8,128)(2,1)} %pad.15) | copy-start | bytes 2027524
  19.4 32.1 %collective-permute-start.9 = (s16[5200,128]{1,0:T(8,128)(2,1)S(1)}, s16[5200,128]{1,0:T(8,128)(2,1)S(1)}, u32[]{:S(2)}, u32[]{:S(2)}) collective-permute-start(s16[5200,128]{1,0:T(8,128)(2,1)S(1)} %get-tuple-element.73), channel_id=1, source_target_pairs={{0,4},{2,6},{4,0},{6,2},{8,12},{10,14},{12,8},{14,10},{16,20},{18,... | collective-permute-start | bytes 3993608 | tf_op jit(solution)/shard_map/ppermute | solution.py:211
  21.0 25.6 %collective-permute-start.2 = (s16[4160,128]{1,0:T(8,128)(2,1)S(1)}, s16[4160,128]{1,0:T(8,128)(2,1)S(1)}, u32[]{:S(2)}, u32[]{:S(2)}) collective-permute-start(s16[4160,128]{1,0:T(8,128)(2,1)S(1)} %get-tuple-element.62), channel_id=1, source_target_pairs={{0,8},{2,10},{4,12},{6,14},{8,0},{10,2},{12,4},{14,6},{16,24},{18,... | collective-permute-start | bytes 3194888 | tf_op jit(solution)/shard_map/ppermute | solution.py:211
  37.1 2.9 %collective-permute-start.5 = (bf16[1024,256]{1,0:T(8,128)(2,1)}, bf16[1024,256]{1,0:T(8,128)(2,1)S(1)}, u32[]{:S(2)}, u32[]{:S(2)}) collective-permute-start(bf16[1024,256]{1,0:T(8,128)(2,1)} %collective-permute-done.3), channel_id=1, source_target_pairs={{0,1},{1,0},{2,3},{3,2},{4,5},{5,4},{6,7},{7,6},{8,9},{9,8},{10,11... | collective-permute-start | bytes 1572872 | tf_op jit(solution)/shard_map/ppermute | solution.py:242
  37.1 18.0 %collective-permute-start.8 = (bf16[264,1280]{1,0:T(8,128)(2,1)S(1)}, bf16[264,1280]{1,0:T(8,128)(2,1)S(1)}, u32[]{:S(2)}, u32[]{:S(2)}) collective-permute-start(bf16[264,1280]{1,0:T(8,128)(2,1)S(1)} %copy-done.3), channel_id=1, source_target_pairs={{0,2},{2,0},{4,6},{6,4},{8,10},{10,8},{12,14},{14,12},{16,18},{18,... | collective-permute-start | bytes 2027528 | tf_op jit(solution)/shard_map/ppermute | solution.py:211
  43.0 20.7 %collective-permute-start.7 = (s16[3120,128]{1,0:T(8,128)(2,1)S(1)}, s16[3120,128]{1,0:T(8,128)(2,1)S(1)}, u32[]{:S(2)}, u32[]{:S(2)}) collective-permute-start(s16[3120,128]{1,0:T(8,128)(2,1)S(1)} %get-tuple-element.71), channel_id=1, source_target_pairs={{0,8},{2,10},{4,12},{6,14},{8,0},{10,2},{12,4},{14,6},{16,24},{18,... | collective-permute-start | bytes 2396168 | tf_op jit(solution)/shard_map/ppermute | solution.py:211
  44.7 24.9 %collective-permute-start.14 = (bf16[264,1280]{1,0:T(8,128)(2,1)S(1)}, bf16[264,1280]{1,0:T(8,128)(2,1)S(1)}, u32[]{:S(2)}, u32[]{:S(2)}) collective-permute-start(bf16[264,1280]{1,0:T(8,128)(2,1)S(1)} %pad.17), channel_id=1, source_target_pairs={{0,2},{2,0},{4,6},{6,4},{8,10},{10,8},{12,14},{14,12},{16,18},{18,... | collective-permute-start | bytes 2027528 | tf_op jit(solution)/shard_map/ppermute | solution.py:211
  47.2 18.0 %collective-permute-start.6 = (s16[2080,128]{1,0:T(8,128)(2,1)S(1)}, s16[2080,128]{1,0:T(8,128)(2,1)S(1)}, u32[]{:S(2)}, u32[]{:S(2)}) collective-permute-start(s16[2080,128]{1,0:T(8,128)(2,1)S(1)} %get-tuple-element.69), channel_id=1, source_target_pairs={{0,4},{2,6},{4,0},{6,2},{8,12},{10,14},{12,8},{14,10},{16,20},{18,... | collective-permute-start | bytes 1597448 | tf_op jit(solution)/shard_map/ppermute | solution.py:211
  55.0 6.3 %slice-start.1 = ((bf16[256,7168]{1,0:T(8,128)(2,1)}), bf16[256,768]{1,0:T(8,128)(2,1)S(1)}, s32[]{:S(2)}) async-start(bf16[256,7168]{1,0:T(8,128)(2,1)} %refs_2_.11), calls=%async_computation.1 | async-start | bytes 786432 | tf_op jit(solution)/shard_map/slice | solution.py:215
  57.9 19.3 %collective-permute-start.13 = (s16[2608,128]{1,0:T(8,128)(2,1)S(1)}, s16[2608,128]{1,0:T(8,128)(2,1)S(1)}, u32[]{:S(2)}, u32[]{:S(2)}) collective-permute-start(s16[2608,128]{1,0:T(8,128)(2,1)S(1)} %get-tuple-element.82), channel_id=1, source_target_pairs={{0,4},{2,6},{4,0},{6,2},{8,12},{10,14},{12,8},{14,10},{16,20},{18,... | collective-permute-start | bytes 2002952 | tf_op jit(solution)/shard_map/ppermute | solution.py:211
  59.7 22.8 %collective-permute-start.11 = (s16[2608,128]{1,0:T(8,128)(2,1)S(1)}, s16[2608,128]{1,0:T(8,128)(2,1)S(1)}, u32[]{:S(2)}, u32[]{:S(2)}) collective-permute-start(s16[2608,128]{1,0:T(8,128)(2,1)S(1)} %get-tuple-element.79), channel_id=1, source_target_pairs={{0,8},{2,10},{4,12},{6,14},{8,0},{10,2},{12,4},{14,6},{16,24},{18,... | collective-permute-start | bytes 2002952 | tf_op jit(solution)/shard_map/ppermute | solution.py:211
  63.7 15.6 %collective-permute-start.12 = (bf16[264,768]{1,0:T(8,128)(2,1)S(1)}, bf16[264,768]{1,0:T(8,128)(2,1)S(1)}, u32[]{:S(2)}, u32[]{:S(2)}) collective-permute-start(bf16[264,768]{1,0:T(8,128)(2,1)S(1)} %pad.18), channel_id=1, source_target_pairs={{0,2},{2,0},{4,6},{6,4},{8,10},{10,8},{12,14},{14,12},{16,18},{18,... | collective-permute-start | bytes 1216520 | tf_op jit(solution)/shard_map/ppermute | solution.py:211
  72.4 19.1 %collective-permute-start.19 = (s16[2608,128]{1,0:T(8,128)(2,1)S(1)}, s16[2608,128]{1,0:T(8,128)(2,1)S(1)}, u32[]{:S(2)}, u32[]{:S(2)}) collective-permute-start(s16[2608,128]{1,0:T(8,128)(2,1)S(1)} %get-tuple-element.93), channel_id=1, source_target_pairs={{0,4},{2,6},{4,0},{6,2},{8,12},{10,14},{12,8},{14,10},{16,20},{18,... | collective-permute-start | bytes 2002952 | tf_op jit(solution)/shard_map/ppermute | solution.py:211
  74.3 16.0 %collective-permute-start.10 = (s16[1040,128]{1,0:T(8,128)(2,1)S(1)}, s16[1040,128]{1,0:T(8,128)(2,1)S(1)}, u32[]{:S(2)}, u32[]{:S(2)}) collective-permute-start(s16[1040,128]{1,0:T(8,128)(2,1)S(1)} %get-tuple-element.78), channel_id=1, source_target_pairs={{0,16},{2,18},{4,20},{6,22},{8,24},{10,26},{12,28},{14,30},{16,0},... | collective-permute-start | bytes 798728 | tf_op jit(solution)/shard_map/ppermute | solution.py:211
  77.6 18.1 %collective-permute-start.18 = (s16[1312,128]{1,0:T(8,128)(2,1)S(1)}, s16[1312,128]{1,0:T(8,128)(2,1)S(1)}, u32[]{:S(2)}, u32[]{:S(2)}) collective-permute-start(s16[1312,128]{1,0:T(8,128)(2,1)S(1)} %get-tuple-element.92), channel_id=1, source_target_pairs={{0,8},{2,10},{4,12},{6,14},{8,0},{10,2},{12,4},{14,6},{16,24},{18,... | collective-permute-start | bytes 1007624 | tf_op jit(solution)/shard_map/ppermute | solution.py:211
  79.3 25.6 %collective-permute-start.16 = (s16[1568,128]{1,0:T(8,128)(2,1)S(1)}, s16[1568,128]{1,0:T(8,128)(2,1)S(1)}, u32[]{:S(2)}, u32[]{:S(2)}) collective-permute-start(s16[1568,128]{1,0:T(8,128)(2,1)S(1)} %get-tuple-element.90), channel_id=1, source_target_pairs={{0,4},{2,6},{4,0},{6,2},{8,12},{10,14},{12,8},{14,10},{16,20},{18,... | collective-permute-start | bytes 1204232 | tf_op jit(solution)/shard_map/ppermute | solution.py:211
  83.0 21.7 %collective-permute-start.17 = (s16[1312,128]{1,0:T(8,128)(2,1)S(1)}, s16[1312,128]{1,0:T(8,128)(2,1)S(1)}, u32[]{:S(2)}, u32[]{:S(2)}) collective-permute-start(s16[1312,128]{1,0:T(8,128)(2,1)S(1)} %get-tuple-element.91), channel_id=1, source_target_pairs={{0,16},{2,18},{4,20},{6,22},{8,24},{10,26},{12,28},{14,30},{16,0},... | collective-permute-start | bytes 1007624 | tf_op jit(solution)/shard_map/ppermute | solution.py:211
  90.3 26.6 %collective-permute-start.22 = (s16[1568,128]{1,0:T(8,128)(2,1)S(1)}, s16[1568,128]{1,0:T(8,128)(2,1)S(1)}, u32[]{:S(2)}, u32[]{:S(2)}) collective-permute-start(s16[1568,128]{1,0:T(8,128)(2,1)S(1)} %get-tuple-element.100), channel_id=1, source_target_pairs={{0,4},{2,6},{4,0},{6,2},{8,12},{10,14},{12,8},{14,10},{16,20},{18,... | collective-permute-start | bytes 1204232 | tf_op jit(solution)/shard_map/ppermute | solution.py:211
  91.9 25.3 %collective-permute-start.21 = (s16[1312,128]{1,0:T(8,128)(2,1)S(1)}, s16[1312,128]{1,0:T(8,128)(2,1)S(1)}, u32[]{:S(2)}, u32[]{:S(2)}) collective-permute-start(s16[1312,128]{1,0:T(8,128)(2,1)S(1)} %get-tuple-element.99), channel_id=1, source_target_pairs={{0,8},{2,10},{4,12},{6,14},{8,0},{10,2},{12,4},{14,6},{16,24},{18,... | collective-permute-start | bytes 1007624 | tf_op jit(solution)/shard_map/ppermute | solution.py:211
  96.0 19.5 %collective-permute-start.24 = (s16[656,128]{1,0:T(8,128)(2,1)S(1)}, s16[656,128]{1,0:T(8,128)(2,1)S(1)}, u32[]{:S(2)}, u32[]{:S(2)}) collective-permute-start(s16[656,128]{1,0:T(8,128)(2,1)S(1)} %get-tuple-element.102), channel_id=1, source_target_pairs={{0,16},{2,18},{4,20},{6,22},{8,24},{10,26},{12,28},{14,30},{16,0},... | collective-permute-start | bytes 503816 | tf_op jit(solution)/shard_map/ppermute | solution.py:211
  105.2 15.5 %collective-permute-start.20 = (s16[784,128]{1,0:T(8,128)(2,1)S(1)}, s16[784,128]{1,0:T(8,128)(2,1)S(1)}, u32[]{:S(2)}, u32[]{:S(2)}) collective-permute-start(s16[784,128]{1,0:T(8,128)(2,1)S(1)} %get-tuple-element.98), channel_id=1, source_target_pairs={{0,16},{2,18},{4,20},{6,22},{8,24},{10,26},{12,28},{14,30},{16,0},... | collective-permute-start | bytes 602120 | tf_op jit(solution)/shard_map/ppermute | solution.py:211
  105.3 11.5 %collective-permute-start.23 = (s16[656,128]{1,0:T(8,128)(2,1)S(1)}, s16[656,128]{1,0:T(8,128)(2,1)S(1)}, u32[]{:S(2)}, u32[]{:S(2)}) collective-permute-start(s16[656,128]{1,0:T(8,128)(2,1)S(1)} %get-tuple-element.101), channel_id=1, source_target_pairs={{0,2},{2,0},{4,6},{6,4},{8,10},{10,8},{12,14},{14,12},{16,18},{18,... | collective-permute-start | bytes 503816 | tf_op jit(solution)/shard_map/ppermute | solution.py:211
  115.5 5.3 %collective-permute-start.15 = (s16[528,128]{1,0:T(8,128)(2,1)S(1)}, s16[528,128]{1,0:T(8,128)(2,1)S(1)}, u32[]{:S(2)}, u32[]{:S(2)}) collective-permute-start(s16[528,128]{1,0:T(8,128)(2,1)S(1)} %get-tuple-element.89), channel_id=1, source_target_pairs={{0,2},{2,0},{4,6},{6,4},{8,10},{10,8},{12,14},{14,12},{16,18},{18,... | collective-permute-start | bytes 405512 | tf_op jit(solution)/shard_map/ppermute | solution.py:211
  117.1 9.4 %collective-permute-start.26 = (s16[784,128]{1,0:T(8,128)(2,1)S(1)}, s16[784,128]{1,0:T(8,128)(2,1)S(1)}, u32[]{:S(2)}, u32[]{:S(2)}) collective-permute-start(s16[784,128]{1,0:T(8,128)(2,1)S(1)} %get-tuple-element.106), channel_id=1, source_target_pairs={{0,8},{2,10},{4,12},{6,14},{8,0},{10,2},{12,4},{14,6},{16,24},{18,... | collective-permute-start | bytes 602120 | tf_op jit(solution)/shard_map/ppermute | solution.py:211
  117.5 9.3 %collective-permute-start.25 = (s16[656,128]{1,0:T(8,128)(2,1)S(1)}, s16[656,128]{1,0:T(8,128)(2,1)S(1)}, u32[]{:S(2)}, u32[]{:S(2)}) collective-permute-start(s16[656,128]{1,0:T(8,128)(2,1)S(1)} %get-tuple-element.105), channel_id=1, source_target_pairs={{0,16},{2,18},{4,20},{6,22},{8,24},{10,26},{12,28},{14,30},{16,0},... | collective-permute-start | bytes 503816 | tf_op jit(solution)/shard_map/ppermute | solution.py:211
  126.7 5.9 %collective-permute-start.27 = (s16[400,128]{1,0:T(8,128)(2,1)S(1)}, s16[400,128]{1,0:T(8,128)(2,1)S(1)}, u32[]{:S(2)}, u32[]{:S(2)}) collective-permute-start(s16[400,128]{1,0:T(8,128)(2,1)S(1)} %get-tuple-element.108), channel_id=1, source_target_pairs={{0,16},{2,18},{4,20},{6,22},{8,24},{10,26},{12,28},{14,30},{16,0},... | collective-permute-start | bytes 307208 | tf_op jit(solution)/shard_map/ppermute | solution.py:211
  126.9 5.7 %copy-start.4 = (f32[56,64,128]{2,1,0:T(8,128)}, f32[56,64,128]{2,1,0:T(8,128)S(1)}, u32[]{:S(2)}) copy-start(f32[56,64,128]{2,1,0:T(8,128)S(1)} %constant_dynamic-update-slice_fusion.7) | copy-start | bytes 5505028

commit v6 on v5

--- a/solution.py
+++ b/solution.py
@@ -87,7 +87,8 @@
             for mask in masks:
                 piece = (me[0] ^ mask) // 2
                 entry, part = piece // per_block, piece % per_block
-                starts.append((mask & 1, pl.multiple_of(picks[c, entry] * height + part * rows, rows)))
+                block = picks[begins[0] + c, entry] ^ me[1]
+                starts.append((mask & 1, pl.multiple_of(block * height + part * rows, rows)))
             total = None
             for t, grad in enumerate(grads):
                 left = [lefts[pairs.index((x, t))][pl.ds(s, rows), :] for x, s in starts]
@@ -152,7 +153,7 @@
 def plan_of(columns, depth):
     if depth != 4 or columns % 56 != 0:
         return [columns], [list(range(1, depth))], [[0]], [("multiply", 0)] + [("step", 0)] * (depth - 1)
-    widths = [8, 10, 12, 10, 10, 6]
+    widths = [8, 8, 14, 10, 10, 6]
     paths = [[2, 1, 3, 0], [1, 2, 3, 0], [2, 1, 3], [1, 2, 3], [1, 2, 3], [1, 2, 3]]
     messages = [[2], [3], [4], [5]]
     work = [
@@ -160,11 +161,11 @@
         ("multiply", 1),
         ("multiply", 2),
         ("step", 0),
+        ("multiply", 3),
+        ("step", 0),
         ("step", 1),
-        ("multiply", 3),
+        ("multiply", 4),
         ("step", 2),
-        ("step", 0),
-        ("multiply", 4),
         ("step", 3),
         ("multiply", 5),
         ("step", 1),
@@ -174,12 +175,12 @@
         ("step", 1),
         ("step", 2),
         ("step", 3),
-        ("step", 1),
+        ("step", 0),
         ("step", 5),
         ("step", 4),
         ("step", 2),
-        ("step", 0),
         ("step", 5),
+        ("step", 1),
         ("step", 4),
         ("step", 5),
     ]
@@ -205,7 +206,8 @@
     starts = [sum(widths[:i]) for i in range(count)]
 
     me = lax.axis_index("dp")
-    half, place = me % 2, me.astype(jnp.int32).reshape(1)
+    blocks = features // BLOCK
+    place = jnp.stack([me, lax.axis_index("mp") * blocks]).astype(jnp.int32)
 
     def swap(sent, bit):
         return lax.ppermute(sent, "dp", [(o, o ^ (1 << bit)) for o in range(owners)])
@@ -233,19 +235,16 @@
     near = swap(other, 0)
     near_g = []
     own = fetch(own)
-    near, near_g[0] = lax.optimization_barrier((near, near_g[0]))
     if len(messages) > 1:
         own = fetch(own)
 
     def spread(part):
         parts = [part] + [
-            lax.ppermute(part, "mp", [(g, (g + s) % groups) for g in range(groups)]) for s in range(1, groups)
+            lax.ppermute(part, "mp", [(g, g ^ s) for g in range(groups)]) for s in range(1, groups)
         ]
         return jnp.concatenate(parts, axis=0)
 
     own_t, other_t, near_t = spread(own), spread(other), spread(near)
-    blocks = features // BLOCK
-    picks = (lax.axis_index("mp") - row_blocks // blocks) % groups * blocks + row_blocks % blocks
 
     def coded(width, n):
         return jax.ShapeDtypeStruct((width * n * rows + pad16(width * n), BLOCK), jnp.int16)
@@ -275,7 +274,7 @@
             scratch_shapes=[scale(width, n)],
             compiler_params=params(),
             name="multiply",
-        )(place, picks[starts[i] : starts[i] + width], *lefts, *grads, last)
+        )(place, row_blocks, *lefts, *grads, last)
 
     def combine(sources, n, encoded, last):
         width = sum(w for w, *_ in sources)

time: 134 us -> 130 us (0.970)
  waiting for transfers between devices: 65.6 us -> 54.7 us
  starting transfers between devices: 35.1 us -> 41.4 us
  Pallas kernels: 23.6 us -> 26.1 us
    ppermute x25, waiting for transfers between devices: 64.2 us -> 54.7 us  [swap(): return lax.ppermute(sent, 'dp', [(o, o ^ 1 << bit) for o in range(owners)])]
    ppermute x25, starting transfers between devices: 34.4 us -> 40.8 us  [swap(): return lax.ppermute(sent, 'dp', [(o, o ^ 1 << bit) for o in range(owners)])]
    unnamed x21 -> x23, local copies, waits for them, and re-layouts: 3.25 us -> 0.53 us
    pallas_call x6, Pallas kernels: 16 us -> 18.5 us  [multiply(): pl.pallas_call(functools.partial(multiply_kernel, width, rows, height, or...]
    ppermute x3, waiting for transfers between devices: 1.36 us -> 0.01 us  [spread(): lax.ppermute(part, 'mp', [(g, g ^ s) for g in range(groups)])]
  transfers between devices with their start and end apart: 28 -> 28, of which waited for: 15 -> 14; matrix products, arithmetic and copies ran while one was open for 4% -> 2% of each run, Pallas kernels for 16% -> 18%
where the time goes in v6:
time: 130 us
  waiting for transfers between devices  54.7 us (42%)
  starting transfers between devices  41.4 us (32%)
  Pallas kernels  26.1 us (20%)
  local copies, waits for them, and re-layouts  7.29 us (6%)
    ppermute x25, waiting for transfers between devices, swap(): return lax.ppermute(sent, 'dp', [(o, o ^ 1 << bit) for o in range(owners)])  54.7 us
    ppermute x25, starting transfers between devices, swap(): return lax.ppermute(sent, 'dp', [(o, o ^ 1 << bit) for o in range(owners)])  40.8 us
    pallas_call x6, Pallas kernels, multiply(): pl.pallas_call(functools.partial(multiply_kernel, width, rows, height, or...  18.5 us
    pallas_call x20, Pallas kernels, combine(): pl.pallas_call(functools.partial(combine_kernel, shapes, rows, n, encoded...  5.41 us
    slice x5, local copies, waits for them, and re-layouts, fetch(): out_grad[:, starts[chunks[0]] * BLOCK:(starts[chunks[-1]] + widths[chunks...  2.62 us
  transfers between devices with their start and end apart: 28, of which 14 were waited for; matrix products, arithmetic and copies ran while one was open for 2% of the time, Pallas kernels for 18%

profile of v6, /device:TPU:0, one launch (start us, length us, event | category | flops | bytes accessed | tf_op | source)
XLA Modules:
  0.0 130.1 jit_solution(741232583718975290)
XLA Ops:
  0.0 2.6 %fusion = (bf16[256,1280]{1,0:T(8,128)(2,1)}, bf16[256,1280]{1,0:T(8,128)(2,1)}) fusion(bf16[256,7168]{1,0:T(8,128)(2,1)} %refs_2_.11), kind=kLoop, calls=%fused_computation.13 | loop fusion | bytes 2621440 | tf_op jit(solution)/shard_map/slice | solution.py:217
  2.7 1.0 pad.16
  3.7 2.2 %prepare.1 = (bf16[1024,256]{1,0:T(8,128)(2,1)S(1)}, bf16[1024,256]{1,0:T(8,128)(2,1)S(1)}) custom-call(s32[2]{0:T(128)S(1)} %pad_add_fusion.me.refs_3_, s32[1,4]{1,0:T(1,128)S(1)} %copy-done.2, bf16[256,2048]{1,0:T(8,128)(2,1)S(1)} %copy-done.1), custom_call_target="tpu_custom_call" | custom-call | tf_op jit(solution)/shard_map/prepare/pallas_call | solution.py:227
  6.0 0.5 collective-permute-start
  6.6 2.9 %collective-permute-start.3 = (bf16[1024,256]{1,0:T(8,128)(2,1)S(1)}, bf16[1024,256]{1,0:T(8,128)(2,1)S(1)}, u32[]{:S(2)}, u32[]{:S(2)}) collective-permute-start(bf16[1024,256]{1,0:T(8,128)(2,1)S(1)} %get-tuple-element.58), channel_id=1, source_target_pairs={{0,2},{2,0},{4,6},{6,4},{8,10},{10,8},{12,14},{14,12},{16,18},{18,... | collective-permute-start | bytes 1572872 | tf_op jit(solution)/shard_map/ppermute | solution.py:213
  9.7 1.2 constant_dynamic-update-slice_fusion.refs_0_
  10.9 1.1 constant_dynamic-update-slice_fusion.2.refs_1_
  12.0 2.9 %multiply.6 = (f32[4096,128]{1,0:T(8,128)S(1)}, s16[4160,128]{1,0:T(8,128)(2,1)S(1)}) custom-call(s32[2]{0:T(128)S(1)} %pad_add_fusion.me.refs_3_, s32[56,8]{1,0:T(8,128)S(1)} %copy.5.picks, bf16[2048,256]{1,0:T(8,128)(2,1)S(1)} %constant_dynamic-update-slice_fusion.refs_0_, bf16[2048,256]{1,0:T(8,128)(2,1)S(1)} %constant_dynamic-update-slice_fusion.2.refs_1_, ...), custom_call_target="tpu_custom_call" | custom-call | tf_op jit(solution)/shard_map/multiply/pallas_call | solution.py:269
  15.0 2.2 %collective-permute-start.2 = (s16[4160,128]{1,0:T(8,128)(2,1)S(1)}, s16[4160,128]{1,0:T(8,128)(2,1)S(1)}, u32[]{:S(2)}, u32[]{:S(2)}) collective-permute-start(s16[4160,128]{1,0:T(8,128)(2,1)S(1)} %get-tuple-element.60), channel_id=1, source_target_pairs={{0,8},{2,10},{4,12},{6,14},{8,0},{10,2},{12,4},{14,6},{16,24},{18,... | collective-permute-start | bytes 3194888 | tf_op jit(solution)/shard_map/ppermute | solution.py:213
  17.1 5.1 %collective-permute-done.3 = bf16[1024,256]{1,0:T(8,128)(2,1)S(1)} collective-permute-done((bf16[1024,256]{1,0:T(8,128)(2,1)S(1)}, bf16[1024,256]{1,0:T(8,128)(2,1)S(1)}, u32[]{:S(2)}, u32[]{:S(2)}) %collective-permute-start.3) | collective-permute-done | bytes 524320 | tf_op jit(solution)/shard_map/ppermute | solution.py:213
  22.2 2.9 %multiply.7 = (f32[4096,128]{1,0:T(8,128)S(1)}, s16[4160,128]{1,0:T(8,128)(2,1)S(1)}) custom-call(s32[2]{0:T(128)S(1)} %pad_add_fusion.me.refs_3_, s32[56,8]{1,0:T(8,128)S(1)} %copy.5.picks, bf16[2048,256]{1,0:T(8,128)(2,1)S(1)} %constant_dynamic-update-slice_fusion.refs_0_, bf16[2048,256]{1,0:T(8,128)(2,1)S(1)} %constant_dynamic-update-slice_fusion.2.refs_1_, ...), custom_call_target="tpu_custom_call" | custom-call | tf_op jit(solution)/shard_map/multiply/pallas_call | solution.py:269
  25.1 2.2 %collective-permute-start.9 = (s16[4160,128]{1,0:T(8,128)(2,1)S(1)}, s16[4160,128]{1,0:T(8,128)(2,1)S(1)}, u32[]{:S(2)}, u32[]{:S(2)}) collective-permute-start(s16[4160,128]{1,0:T(8,128)(2,1)S(1)} %get-tuple-element.70), channel_id=1, source_target_pairs={{0,4},{2,6},{4,0},{6,2},{8,12},{10,14},{12,8},{14,10},{16,20},{18,... | collective-permute-start | bytes 3194888 | tf_op jit(solution)/shard_map/ppermute | solution.py:213
  27.3 1.5 %collective-permute-start.7 = (bf16[264,1280]{1,0:T(8,128)(2,1)S(1)}, bf16[264,1280]{1,0:T(8,128)(2,1)S(1)}, u32[]{:S(2)}, u32[]{:S(2)}) collective-permute-start(bf16[264,1280]{1,0:T(8,128)(2,1)S(1)} %pad.15), channel_id=1, source_target_pairs={{0,2},{2,0},{4,6},{6,4},{8,10},{10,8},{12,14},{14,12},{16,18},{18,... | collective-permute-start | bytes 2027528 | tf_op jit(solution)/shard_map/ppermute | solution.py:213
  28.9 13.6 %collective-permute-done.5.refs_3_ = bf16[264,1792]{1,0:T(8,128)(2,1)S(1)} collective-permute-done((bf16[264,1792]{1,0:T(8,128)(2,1)}, bf16[264,1792]{1,0:T(8,128)(2,1)S(1)}, u32[]{:S(2)}, u32[]{:S(2)}) %collective-permute-start.5) | collective-permute-done | bytes 946208 | tf_op jit(solution)/shard_map/ppermute | solution.py:213
  42.5 4.1 %multiply.8 = (f32[3584,128]{1,0:T(8,128)S(1)}, s16[3648,128]{1,0:T(8,128)(2,1)S(1)}) custom-call(s32[2]{0:T(128)S(1)} %pad_add_fusion.me.refs_3_, s32[56,8]{1,0:T(8,128)S(1)} %copy.5.picks, bf16[2048,256]{1,0:T(8,128)(2,1)S(1)} %constant_dynamic-update-slice_fusion.refs_0_, bf16[2048,256]{1,0:T(8,128)(2,1)S(1)} %constant_dynamic-update-slice_fusion.4.refs_1_, ...), custom_call_target="tpu_custom_call" | custom-call | tf_op jit(solution)/shard_map/multiply/pallas_call | solution.py:269
  46.5 2.2 %collective-permute-start.13 = (s16[3648,128]{1,0:T(8,128)(2,1)S(1)}, s16[3648,128]{1,0:T(8,128)(2,1)S(1)}, u32[]{:S(2)}, u32[]{:S(2)}) collective-permute-start(s16[3648,128]{1,0:T(8,128)(2,1)S(1)} %get-tuple-element.77), channel_id=1, source_target_pairs={{0,8},{2,10},{4,12},{6,14},{8,0},{10,2},{12,4},{14,6},{16,24},{18,... | collective-permute-start | bytes 2801672 | tf_op jit(solution)/shard_map/ppermute | solution.py:213
  48.8 1.5 %collective-permute-start.14 = (bf16[264,1280]{1,0:T(8,128)(2,1)S(1)}, bf16[264,1280]{1,0:T(8,128)(2,1)S(1)}, u32[]{:S(2)}, u32[]{:S(2)}) collective-permute-start(bf16[264,1280]{1,0:T(8,128)(2,1)S(1)} %pad.18), channel_id=1, source_target_pairs={{0,2},{2,0},{4,6},{6,4},{8,10},{10,8},{12,14},{14,12},{16,18},{18,... | collective-permute-start | bytes 2027528 | tf_op jit(solution)/shard_map/ppermute | solution.py:213
  50.4 0.6 combine.20
  50.9 1.6 %collective-permute-start.6 = (s16[2080,128]{1,0:T(8,128)(2,1)S(1)}, s16[2080,128]{1,0:T(8,128)(2,1)S(1)}, u32[]{:S(2)}, u32[]{:S(2)}) collective-permute-start(s16[2080,128]{1,0:T(8,128)(2,1)S(1)} %get-tuple-element.65), channel_id=1, source_target_pairs={{0,4},{2,6},{4,0},{6,2},{8,12},{10,14},{12,8},{14,10},{16,20},{18,... | collective-permute-start | bytes 1597448 | tf_op jit(solution)/shard_map/ppermute | solution.py:213
  52.5 4.4 %collective-permute-done.7.refs_3_ = bf16[264,1280]{1,0:T(8,128)(2,1)S(1)} collective-permute-done((bf16[264,1280]{1,0:T(8,128)(2,1)S(1)}, bf16[264,1280]{1,0:T(8,128)(2,1)S(1)}, u32[]{:S(2)}, u32[]{:S(2)}) %collective-permute-start.7) | collective-permute-done | bytes 675872 | tf_op jit(solution)/shard_map/ppermute | solution.py:213
  57.0 3.2 %multiply.9 = (f32[2560,128]{1,0:T(8,128)S(1)}, s16[2608,128]{1,0:T(8,128)(2,1)S(1)}) custom-call(s32[2]{0:T(128)S(1)} %pad_add_fusion.me.refs_3_, s32[56,8]{1,0:T(8,128)S(1)} %copy.5.picks, bf16[2048,256]{1,0:T(8,128)(2,1)S(1)} %constant_dynamic-update-slice_fusion.refs_0_, bf16[2048,256]{1,0:T(8,128)(2,1)S(1)} %constant_dynamic-update-slice_fusion.4.refs_1_, ...), custom_call_target="tpu_custom_call" | custom-call | tf_op jit(solution)/shard_map/multiply/pallas_call | solution.py:269
  60.2 2.2 %collective-permute-start.12 = (s16[2608,128]{1,0:T(8,128)(2,1)S(1)}, s16[2608,128]{1,0:T(8,128)(2,1)S(1)}, u32[]{:S(2)}, u32[]{:S(2)}) collective-permute-start(s16[2608,128]{1,0:T(8,128)(2,1)S(1)} %get-tuple-element.75), channel_id=1, source_target_pairs={{0,4},{2,6},{4,0},{6,2},{8,12},{10,14},{12,8},{14,10},{16,20},{18,... | collective-permute-start | bytes 2002952 | tf_op jit(solution)/shard_map/ppermute | solution.py:213
  62.3 1.5 %collective-permute-done.6.refs_1_ = s16[2080,128]{1,0:T(8,128)(2,1)S(1)} collective-permute-done((s16[2080,128]{1,0:T(8,128)(2,1)S(1)}, s16[2080,128]{1,0:T(8,128)(2,1)S(1)}, u32[]{:S(2)}, u32[]{:S(2)}) %collective-permute-start.6) | collective-permute-done | bytes 532512 | tf_op jit(solution)/shard_map/ppermute | solution.py:213
  63.9 0.3 combine.21
  64.2 0.6 combine.22
  64.8 2.1 %collective-permute-start.10 = (s16[2080,128]{1,0:T(8,128)(2,1)S(1)}, s16[2080,128]{1,0:T(8,128)(2,1)S(1)}, u32[]{:S(2)}, u32[]{:S(2)}) collective-permute-start(s16[2080,128]{1,0:T(8,128)(2,1)S(1)} %get-tuple-element.72), channel_id=1, source_target_pairs={{0,8},{2,10},{4,12},{6,14},{8,0},{10,2},{12,4},{14,6},{16,24},{18,... | collective-permute-start | bytes 1597448 | tf_op jit(solution)/shard_map/ppermute | solution.py:213
  67.0 0.8 collective-permute-start.11
  67.7 3.7 %collective-permute-done.14.refs_3_ = bf16[264,1280]{1,0:T(8,128)(2,1)S(1)} collective-permute-done((bf16[264,1280]{1,0:T(8,128)(2,1)S(1)}, bf16[264,1280]{1,0:T(8,128)(2,1)S(1)}, u32[]{:S(2)}, u32[]{:S(2)}) %collective-permute-start.14) | collective-permute-done | bytes 675872 | tf_op jit(solution)/shard_map/ppermute | solution.py:213
  71.4 3.2 %multiply.10 = (f32[2560,128]{1,0:T(8,128)S(1)}, s16[2608,128]{1,0:T(8,128)(2,1)S(1)}) custom-call(s32[2]{0:T(128)S(1)} %pad_add_fusion.me.refs_3_, s32[56,8]{1,0:T(8,128)S(1)} %copy.5.picks, bf16[2048,256]{1,0:T(8,128)(2,1)S(1)} %constant_dynamic-update-slice_fusion.refs_0_, bf16[2048,256]{1,0:T(8,128)(2,1)S(1)} %constant_dynamic-update-slice_fusion.4.refs_1_, ...), custom_call_target="tpu_custom_call" | custom-call | tf_op jit(solution)/shard_map/multiply/pallas_call | solution.py:269
  74.6 2.2 %collective-permute-start.17 = (s16[2608,128]{1,0:T(8,128)(2,1)S(1)}, s16[2608,128]{1,0:T(8,128)(2,1)S(1)}, u32[]{:S(2)}, u32[]{:S(2)}) collective-permute-start(s16[2608,128]{1,0:T(8,128)(2,1)S(1)} %get-tuple-element.87), channel_id=1, source_target_pairs={{0,4},{2,6},{4,0},{6,2},{8,12},{10,14},{12,8},{14,10},{16,20},{18,... | collective-permute-start | bytes 2002952 | tf_op jit(solution)/shard_map/ppermute | solution.py:213
  76.8 2.6 %collective-permute-start.8 = (s16[1040,128]{1,0:T(8,128)(2,1)S(1)}, s16[1040,128]{1,0:T(8,128)(2,1)S(1)}, u32[]{:S(2)}, u32[]{:S(2)}) collective-permute-start(s16[1040,128]{1,0:T(8,128)(2,1)S(1)} %get-tuple-element.69), channel_id=1, source_target_pairs={{0,16},{2,18},{4,20},{6,22},{8,24},{10,26},{12,28},{14,30},{16,0},... | collective-permute-start | bytes 798728 | tf_op jit(solution)/shard_map/ppermute | solution.py:213
  79.4 0.6 combine.23
  80.0 0.4 combine.24
  80.4 1.7 %collective-permute-start.16 = (s16[1312,128]{1,0:T(8,128)(2,1)S(1)}, s16[1312,128]{1,0:T(8,128)(2,1)S(1)}, u32[]{:S(2)}, u32[]{:S(2)}) collective-permute-start(s16[1312,128]{1,0:T(8,128)(2,1)S(1)} %get-tuple-element.86), channel_id=1, source_target_pairs={{0,8},{2,10},{4,12},{6,14},{8,0},{10,2},{12,4},{14,6},{16,24},{18,... | collective-permute-start | bytes 1007624 | tf_op jit(solution)/shard_map/ppermute | solution.py:213
  82.0 0.5 collective-permute-start.19
  82.6 2.2 %multiply.11 = (f32[1536,128]{1,0:T(8,128)S(1)}, s16[1568,128]{1,0:T(8,128)(2,1)S(1)}) custom-call(s32[2]{0:T(128)S(1)} %pad_add_fusion.me.refs_3_, s32[56,8]{1,0:T(8,128)S(1)} %copy.5.picks, bf16[2048,256]{1,0:T(8,128)(2,1)S(1)} %constant_dynamic-update-slice_fusion.refs_0_, bf16[2048,256]{1,0:T(8,128)(2,1)S(1)} %constant_dynamic-update-slice_fusion.4.refs_1_, ...), custom_call_target="tpu_custom_call" | custom-call | tf_op jit(solution)/shard_map/multiply/pallas_call | solution.py:269
  84.7 0.3 combine.25
  85.1 2.2 %collective-permute-start.20 = (s16[1040,128]{1,0:T(8,128)(2,1)S(1)}, s16[1040,128]{1,0:T(8,128)(2,1)S(1)}, u32[]{:S(2)}, u32[]{:S(2)}) collective-permute-start(s16[1040,128]{1,0:T(8,128)(2,1)S(1)} %get-tuple-element.92), channel_id=1, source_target_pairs={{0,16},{2,18},{4,20},{6,22},{8,24},{10,26},{12,28},{14,30},{16,0},... | collective-permute-start | bytes 798728 | tf_op jit(solution)/shard_map/ppermute | solution.py:213
  87.3 4.5 %collective-permute-done.8.refs_1_ = s16[1040,128]{1,0:T(8,128)(2,1)S(1)} collective-permute-done((s16[1040,128]{1,0:T(8,128)(2,1)S(1)}, s16[1040,128]{1,0:T(8,128)(2,1)S(1)}, u32[]{:S(2)}, u32[]{:S(2)}) %collective-permute-start.8) | collective-permute-done | bytes 266272 | tf_op jit(solution)/shard_map/ppermute | solution.py:213
  91.8 0.2 combine.26
  92.0 0.7 collective-permute-done.17.refs_1_
  92.7 0.4 combine.27
  93.1 4.2 %collective-permute-done.16.refs_1_ = s16[1312,128]{1,0:T(8,128)(2,1)S(1)} collective-permute-done((s16[1312,128]{1,0:T(8,128)(2,1)S(1)}, s16[1312,128]{1,0:T(8,128)(2,1)S(1)}, u32[]{:S(2)}, u32[]{:S(2)}) %collective-permute-start.16) | collective-permute-done | bytes 335904 | tf_op jit(solution)/shard_map/ppermute | solution.py:213
  97.3 0.3 combine.28
  97.7 1.9 %collective-permute-start.25 = (s16[1312,128]{1,0:T(8,128)(2,1)S(1)}, s16[1312,128]{1,0:T(8,128)(2,1)S(1)}, u32[]{:S(2)}, u32[]{:S(2)}) collective-permute-start(s16[1312,128]{1,0:T(8,128)(2,1)S(1)} %get-tuple-element.100), channel_id=1, source_target_pairs={{0,8},{2,10},{4,12},{6,14},{8,0},{10,2},{12,4},{14,6},{16,24},{18,... | collective-permute-start | bytes 1007624 | tf_op jit(solution)/shard_map/ppermute | solution.py:213
  99.6 5.9 %collective-permute-done.20.refs_1_ = s16[1040,128]{1,0:T(8,128)(2,1)S(1)} collective-permute-done((s16[1040,128]{1,0:T(8,128)(2,1)S(1)}, s16[1040,128]{1,0:T(8,128)(2,1)S(1)}, u32[]{:S(2)}, u32[]{:S(2)}) %collective-permute-start.20) | collective-permute-done | bytes 266272 | tf_op jit(solution)/shard_map/ppermute | solution.py:213
  105.4 1.5 %collective-permute-start.15 = (s16[528,128]{1,0:T(8,128)(2,1)S(1)}, s16[528,128]{1,0:T(8,128)(2,1)S(1)}, u32[]{:S(2)}, u32[]{:S(2)}) collective-permute-start(s16[528,128]{1,0:T(8,128)(2,1)S(1)} %get-tuple-element.85), channel_id=1, source_target_pairs={{0,2},{2,0},{4,6},{6,4},{8,10},{10,8},{12,14},{14,12},{16,18},{18,... | collective-permute-start | bytes 405512 | tf_op jit(solution)/shard_map/ppermute | solution.py:213
  107.0 0.2 combine.29
  107.2 0.4 combine.30
  107.7 1.8 %collective-permute-done.18.refs_1_ = s16[656,128]{1,0:T(8,128)(2,1)S(1)} collective-permute-done((s16[656,128]{1,0:T(8,128)(2,1)S(1)}, s16[656,128]{1,0:T(8,128)(2,1)S(1)}, u32[]{:S(2)}, u32[]{:S(2)}) %collective-permute-start.18) | collective-permute-done | bytes 167968 | tf_op jit(solution)/shard_map/ppermute | solution.py:213
  109.6 0.9 collective-permute-done.15.refs_1_
  110.5 0.2 combine.33
  110.8 2.1 %collective-permute-start.23 = (s16[784,128]{1,0:T(8,128)(2,1)S(1)}, s16[784,128]{1,0:T(8,128)(2,1)S(1)}, u32[]{:S(2)}, u32[]{:S(2)}) collective-permute-start(s16[784,128]{1,0:T(8,128)(2,1)S(1)} %get-tuple-element.98), channel_id=1, source_target_pairs={{0,8},{2,10},{4,12},{6,14},{8,0},{10,2},{12,4},{14,6},{16,24},{18,... | collective-permute-start | bytes 602120 | tf_op jit(solution)/shard_map/ppermute | solution.py:213
  112.9 0.8 collective-permute-start.21
  113.7 0.3 combine.34
  114.0 5.3 %collective-permute-start.26 = (s16[656,128]{1,0:T(8,128)(2,1)S(1)}, s16[656,128]{1,0:T(8,128)(2,1)S(1)}, u32[]{:S(2)}, u32[]{:S(2)}) collective-permute-start(s16[656,128]{1,0:T(8,128)(2,1)S(1)} %get-tuple-element.103), channel_id=1, source_target_pairs={{0,16},{2,18},{4,20},{6,22},{8,24},{10,26},{12,28},{14,30},{16,0},... | collective-permute-start | bytes 503816 | tf_op jit(solution)/shard_map/ppermute | solution.py:213
  119.3 2.6 %collective-permute-done.24.refs_1_ = s16[912,128]{1,0:T(8,128)(2,1)S(1)} collective-permute-done((s16[912,128]{1,0:T(8,128)(2,1)S(1)}, s16[912,128]{1,0:T(8,128)(2,1)S(1)}, u32[]{:S(2)}, u32[]{:S(2)}) %collective-permute-start.24) | collective-permute-done | bytes 233504 | tf_op jit(solution)/shard_map/ppermute | solution.py:213
  121.9 0.1 combine.35.refs_2_
  122.1 0.1 combine.36
  122.2 0.8 collective-permute-start.27
  123.2 4.8 %collective-permute-done.26.refs_1_ = s16[656,128]{1,0:T(8,128)(2,1)S(1)} collective-permute-done((s16[656,128]{1,0:T(8,128)(2,1)S(1)}, s16[656,128]{1,0:T(8,128)(2,1)S(1)}, u32[]{:S(2)}, u32[]{:S(2)}) %collective-permute-start.26) | collective-permute-done | bytes 167968 | tf_op jit(solution)/shard_map/ppermute | solution.py:213
  128.1 1.0 collective-permute-done.27.refs_1_
  129.2 0.2 copy-done.5
  129.4 0.7 constant_dynamic-update-slice_fusion.6
  (56 shorter events, 1.2 us)
Async XLA Ops:
  0.0 2.7 %slice-start = ((bf16[256,7168]{1,0:T(8,128)(2,1)}), bf16[256,1792]{1,0:T(8,128)(2,1)S(1)}, s32[]{:S(2)}) async-start(bf16[256,7168]{1,0:T(8,128)(2,1)} %refs_2_.11), calls=%async_computation | async-start | bytes 1835008 | tf_op jit(solution)/shard_map/slice | solution.py:217
  0.0 3.7 %copy-start.1 = (bf16[256,2048]{1,0:T(8,128)(2,1)S(1)}, bf16[256,2048]{1,0:T(8,128)(2,1)}, u32[]{:S(2)}) copy-start(bf16[256,2048]{1,0:T(8,128)(2,1)} %activations.1) | copy-start | bytes 3145732
  0.0 3.7 %copy-start.2 = (s32[1,4]{1,0:T(1,128)S(1)}, s32[1,4]{1,0:T(1,128)}, u32[]{:S(2)}) copy-start(s32[1,4]{1,0:T(1,128)} %lengths.1) | copy-start | bytes 52
  2.6 3.3 %copy-start.4 = (bf16[256,1280]{1,0:T(8,128)(2,1)S(1)}, bf16[256,1280]{1,0:T(8,128)(2,1)}, u32[]{:S(2)}) copy-start(bf16[256,1280]{1,0:T(8,128)(2,1)} %get-tuple-element.106) | copy-start | bytes 1966084
  2.7 6.8 %copy-start.6 = (s32[56,8]{0,1:T(8,128)S(1)}, s32[56,8]{0,1:T(8,128)}, u32[]{:S(2)}) copy-start(s32[56,8]{0,1:T(8,128)} %param.6) | copy-start | bytes 5380
  6.0 3.7 %collective-permute-start = (bf16[1024,256]{1,0:T(8,128)(2,1)S(1)}, bf16[1024,256]{1,0:T(8,128)(2,1)}, u32[]{:S(2)}, u32[]{:S(2)}) collective-permute-start(bf16[1024,256]{1,0:T(8,128)(2,1)S(1)} %get-tuple-element.57), channel_id=1, source_target_pairs={{0,1},{1,0},{2,3},{3,2},{4,5},{5,4},{6,7},{7,6},{8,9},{9,8},{10,11... | collective-permute-start | bytes 1572872 | tf_op jit(solution)/shard_map/ppermute | solution.py:243
  6.5 4.4 %collective-permute-start.1 = (bf16[1024,256]{1,0:T(8,128)(2,1)S(1)}, bf16[1024,256]{1,0:T(8,128)(2,1)}, u32[]{:S(2)}, u32[]{:S(2)}) collective-permute-start(bf16[1024,256]{1,0:T(8,128)(2,1)S(1)} %get-tuple-element.58), channel_id=1, source_target_pairs={{0,1},{1,0},{2,3},{3,2},{4,5},{5,4},{6,7},{7,6},{8,9},{9,8},{10,11... | collective-permute-start | bytes 1572872 | tf_op jit(solution)/shard_map/ppermute | solution.py:243
  6.6 15.6 %collective-permute-start.3 = (bf16[1024,256]{1,0:T(8,128)(2,1)S(1)}, bf16[1024,256]{1,0:T(8,128)(2,1)S(1)}, u32[]{:S(2)}, u32[]{:S(2)}) collective-permute-start(bf16[1024,256]{1,0:T(8,128)(2,1)S(1)} %get-tuple-element.58), channel_id=1, source_target_pairs={{0,2},{2,0},{4,6},{6,4},{8,10},{10,8},{12,14},{14,12},{16,18},{18,... | collective-permute-start | bytes 1572872 | tf_op jit(solution)/shard_map/ppermute | solution.py:213
  9.5 33.0 %collective-permute-start.5 = (bf16[264,1792]{1,0:T(8,128)(2,1)}, bf16[264,1792]{1,0:T(8,128)(2,1)S(1)}, u32[]{:S(2)}, u32[]{:S(2)}) collective-permute-start(bf16[264,1792]{1,0:T(8,128)(2,1)} %pad.16), channel_id=1, source_target_pairs={{0,2},{2,0},{4,6},{6,4},{8,10},{10,8},{12,14},{14,12},{16,18},{18,... | collective-permute-start | bytes 2838536 | tf_op jit(solution)/shard_map/ppermute | solution.py:213
  9.6 2.4 %copy-start = (bf16[256,7168]{1,0:T(8,128)(2,1)S(1)}, bf16[256,7168]{1,0:T(8,128)(2,1)}, u32[]{:S(2)}) copy-start(bf16[256,7168]{1,0:T(8,128)(2,1)} %refs_2_.11) | copy-start | bytes 11010052
  15.0 35.4 %collective-permute-start.2 = (s16[4160,128]{1,0:T(8,128)(2,1)S(1)}, s16[4160,128]{1,0:T(8,128)(2,1)S(1)}, u32[]{:S(2)}, u32[]{:S(2)}) collective-permute-start(s16[4160,128]{1,0:T(8,128)(2,1)S(1)} %get-tuple-element.60), channel_id=1, source_target_pairs={{0,8},{2,10},{4,12},{6,14},{8,0},{10,2},{12,4},{14,6},{16,24},{18,... | collective-permute-start | bytes 3194888 | tf_op jit(solution)/shard_map/ppermute | solution.py:213
  22.2 6.6 %collective-permute-start.4 = (bf16[1024,256]{1,0:T(8,128)(2,1)S(1)}, bf16[1024,256]{1,0:T(8,128)(2,1)S(1)}, u32[]{:S(2)}, u32[]{:S(2)}) collective-permute-start(bf16[1024,256]{1,0:T(8,128)(2,1)S(1)} %collective-permute-done.3), channel_id=1, source_target_pairs={{0,1},{1,0},{2,3},{3,2},{4,5},{5,4},{6,7},{7,6},{8,9},{9,8},{10,11... | collective-permute-start | bytes 1572872 | tf_op jit(solution)/shard_map/ppermute | solution.py:243
  25.1 39.1 %collective-permute-start.9 = (s16[4160,128]{1,0:T(8,128)(2,1)S(1)}, s16[4160,128]{1,0:T(8,128)(2,1)S(1)}, u32[]{:S(2)}, u32[]{:S(2)}) collective-permute-start(s16[4160,128]{1,0:T(8,128)(2,1)S(1)} %get-tuple-element.70), channel_id=1, source_target_pairs={{0,4},{2,6},{4,0},{6,2},{8,12},{10,14},{12,8},{14,10},{16,20},{18,... | collective-permute-start | bytes 3194888 | tf_op jit(solution)/shard_map/ppermute | solution.py:213
  27.3 29.7 %collective-permute-start.7 = (bf16[264,1280]{1,0:T(8,128)(2,1)S(1)}, bf16[264,1280]{1,0:T(8,128)(2,1)S(1)}, u32[]{:S(2)}, u32[]{:S(2)}) collective-permute-start(bf16[264,1280]{1,0:T(8,128)(2,1)S(1)} %pad.15), channel_id=1, source_target_pairs={{0,2},{2,0},{4,6},{6,4},{8,10},{10,8},{12,14},{14,12},{16,18},{18,... | collective-permute-start | bytes 2027528 | tf_op jit(solution)/shard_map/ppermute | solution.py:213
  42.5 6.3 %copy-start.3 = (bf16[256,1280]{1,0:T(8,128)(2,1)S(1)}, bf16[256,1280]{1,0:T(8,128)(2,1)}, u32[]{:S(2)}) copy-start(bf16[256,1280]{1,0:T(8,128)(2,1)} %get-tuple-element.105) | copy-start | bytes 1966084
  46.5 30.3 %collective-permute-start.13 = (s16[3648,128]{1,0:T(8,128)(2,1)S(1)}, s16[3648,128]{1,0:T(8,128)(2,1)S(1)}, u32[]{:S(2)}, u32[]{:S(2)}) collective-permute-start(s16[3648,128]{1,0:T(8,128)(2,1)S(1)} %get-tuple-element.77), channel_id=1, source_target_pairs={{0,8},{2,10},{4,12},{6,14},{8,0},{10,2},{12,4},{14,6},{16,24},{18,... | collective-permute-start | bytes 2801672 | tf_op jit(solution)/shard_map/ppermute | solution.py:213
  48.8 22.6 %collective-permute-start.14 = (bf16[264,1280]{1,0:T(8,128)(2,1)S(1)}, bf16[264,1280]{1,0:T(8,128)(2,1)S(1)}, u32[]{:S(2)}, u32[]{:S(2)}) collective-permute-start(bf16[264,1280]{1,0:T(8,128)(2,1)S(1)} %pad.18), channel_id=1, source_target_pairs={{0,2},{2,0},{4,6},{6,4},{8,10},{10,8},{12,14},{14,12},{16,18},{18,... | collective-permute-start | bytes 2027528 | tf_op jit(solution)/shard_map/ppermute | solution.py:213
  50.9 12.9 %collective-permute-start.6 = (s16[2080,128]{1,0:T(8,128)(2,1)S(1)}, s16[2080,128]{1,0:T(8,128)(2,1)S(1)}, u32[]{:S(2)}, u32[]{:S(2)}) collective-permute-start(s16[2080,128]{1,0:T(8,128)(2,1)S(1)} %get-tuple-element.65), channel_id=1, source_target_pairs={{0,4},{2,6},{4,0},{6,2},{8,12},{10,14},{12,8},{14,10},{16,20},{18,... | collective-permute-start | bytes 1597448 | tf_op jit(solution)/shard_map/ppermute | solution.py:213
  60.2 19.8 %collective-permute-start.12 = (s16[2608,128]{1,0:T(8,128)(2,1)S(1)}, s16[2608,128]{1,0:T(8,128)(2,1)S(1)}, u32[]{:S(2)}, u32[]{:S(2)}) collective-permute-start(s16[2608,128]{1,0:T(8,128)(2,1)S(1)} %get-tuple-element.75), channel_id=1, source_target_pairs={{0,4},{2,6},{4,0},{6,2},{8,12},{10,14},{12,8},{14,10},{16,20},{18,... | collective-permute-start | bytes 2002952 | tf_op jit(solution)/shard_map/ppermute | solution.py:213
  64.2 2.8 %slice-start.1 = ((bf16[256,7168]{1,0:T(8,128)(2,1)}), bf16[256,768]{1,0:T(8,128)(2,1)S(1)}, s32[]{:S(2)}) async-start(bf16[256,7168]{1,0:T(8,128)(2,1)} %refs_2_.11), calls=%async_computation.1 | async-start | bytes 786432 | tf_op jit(solution)/shard_map/slice | solution.py:217
  64.8 19.9 %collective-permute-start.10 = (s16[2080,128]{1,0:T(8,128)(2,1)S(1)}, s16[2080,128]{1,0:T(8,128)(2,1)S(1)}, u32[]{:S(2)}, u32[]{:S(2)}) collective-permute-start(s16[2080,128]{1,0:T(8,128)(2,1)S(1)} %get-tuple-element.72), channel_id=1, source_target_pairs={{0,8},{2,10},{4,12},{6,14},{8,0},{10,2},{12,4},{14,6},{16,24},{18,... | collective-permute-start | bytes 1597448 | tf_op jit(solution)/shard_map/ppermute | solution.py:213
  67.0 15.1 %collective-permute-start.11 = (bf16[264,768]{1,0:T(8,128)(2,1)S(1)}, bf16[264,768]{1,0:T(8,128)(2,1)S(1)}, u32[]{:S(2)}, u32[]{:S(2)}) collective-permute-start(bf16[264,768]{1,0:T(8,128)(2,1)S(1)} %pad.17), channel_id=1, source_target_pairs={{0,2},{2,0},{4,6},{6,4},{8,10},{10,8},{12,14},{14,12},{16,18},{18,... | collective-permute-start | bytes 1216520 | tf_op jit(solution)/shard_map/ppermute | solution.py:213
  74.6 18.1 %collective-permute-start.17 = (s16[2608,128]{1,0:T(8,128)(2,1)S(1)}, s16[2608,128]{1,0:T(8,128)(2,1)S(1)}, u32[]{:S(2)}, u32[]{:S(2)}) collective-permute-start(s16[2608,128]{1,0:T(8,128)(2,1)S(1)} %get-tuple-element.87), channel_id=1, source_target_pairs={{0,4},{2,6},{4,0},{6,2},{8,12},{10,14},{12,8},{14,10},{16,20},{18,... | collective-permute-start | bytes 2002952 | tf_op jit(solution)/shard_map/ppermute | solution.py:213
  76.8 14.9 %collective-permute-start.8 = (s16[1040,128]{1,0:T(8,128)(2,1)S(1)}, s16[1040,128]{1,0:T(8,128)(2,1)S(1)}, u32[]{:S(2)}, u32[]{:S(2)}) collective-permute-start(s16[1040,128]{1,0:T(8,128)(2,1)S(1)} %get-tuple-element.69), channel_id=1, source_target_pairs={{0,16},{2,18},{4,20},{6,22},{8,24},{10,26},{12,28},{14,30},{16,0},... | collective-permute-start | bytes 798728 | tf_op jit(solution)/shard_map/ppermute | solution.py:213
  80.4 16.9 %collective-permute-start.16 = (s16[1312,128]{1,0:T(8,128)(2,1)S(1)}, s16[1312,128]{1,0:T(8,128)(2,1)S(1)}, u32[]{:S(2)}, u32[]{:S(2)}) collective-permute-start(s16[1312,128]{1,0:T(8,128)(2,1)S(1)} %get-tuple-element.86), channel_id=1, source_target_pairs={{0,8},{2,10},{4,12},{6,14},{8,0},{10,2},{12,4},{14,6},{16,24},{18,... | collective-permute-start | bytes 1007624 | tf_op jit(solution)/shard_map/ppermute | solution.py:213
  82.0 25.2 %collective-permute-start.19 = (s16[1824,128]{1,0:T(8,128)(2,1)S(1)}, s16[1824,128]{1,0:T(8,128)(2,1)S(1)}, u32[]{:S(2)}, u32[]{:S(2)}) collective-permute-start(s16[1824,128]{1,0:T(8,128)(2,1)S(1)} %get-tuple-element.91), channel_id=1, source_target_pairs={{0,4},{2,6},{4,0},{6,2},{8,12},{10,14},{12,8},{14,10},{16,20},{18,... | collective-permute-start | bytes 1400840 | tf_op jit(solution)/shard_map/ppermute | solution.py:213
  85.1 20.4 %collective-permute-start.20 = (s16[1040,128]{1,0:T(8,128)(2,1)S(1)}, s16[1040,128]{1,0:T(8,128)(2,1)S(1)}, u32[]{:S(2)}, u32[]{:S(2)}) collective-permute-start(s16[1040,128]{1,0:T(8,128)(2,1)S(1)} %get-tuple-element.92), channel_id=1, source_target_pairs={{0,16},{2,18},{4,20},{6,22},{8,24},{10,26},{12,28},{14,30},{16,0},... | collective-permute-start | bytes 798728 | tf_op jit(solution)/shard_map/ppermute | solution.py:213
  91.8 18.8 %collective-permute-start.22 = (s16[1568,128]{1,0:T(8,128)(2,1)S(1)}, s16[1568,128]{1,0:T(8,128)(2,1)S(1)}, u32[]{:S(2)}, u32[]{:S(2)}) collective-permute-start(s16[1568,128]{1,0:T(8,128)(2,1)S(1)} %get-tuple-element.96), channel_id=1, source_target_pairs={{0,4},{2,6},{4,0},{6,2},{8,12},{10,14},{12,8},{14,10},{16,20},{18,... | collective-permute-start | bytes 1204232 | tf_op jit(solution)/shard_map/ppermute | solution.py:213
  97.6 11.9 %collective-permute-start.18 = (s16[656,128]{1,0:T(8,128)(2,1)S(1)}, s16[656,128]{1,0:T(8,128)(2,1)S(1)}, u32[]{:S(2)}, u32[]{:S(2)}) collective-permute-start(s16[656,128]{1,0:T(8,128)(2,1)S(1)} %get-tuple-element.90), channel_id=1, source_target_pairs={{0,16},{2,18},{4,20},{6,22},{8,24},{10,26},{12,28},{14,30},{16,0},... | collective-permute-start | bytes 503816 | tf_op jit(solution)/shard_map/ppermute | solution.py:213
  97.7 16.0 %collective-permute-start.25 = (s16[1312,128]{1,0:T(8,128)(2,1)S(1)}, s16[1312,128]{1,0:T(8,128)(2,1)S(1)}, u32[]{:S(2)}, u32[]{:S(2)}) collective-permute-start(s16[1312,128]{1,0:T(8,128)(2,1)S(1)} %get-tuple-element.100), channel_id=1, source_target_pairs={{0,8},{2,10},{4,12},{6,14},{8,0},{10,2},{12,4},{14,6},{16,24},{18,... | collective-permute-start | bytes 1007624 | tf_op jit(solution)/shard_map/ppermute | solution.py:213
  105.4 5.0 %collective-permute-start.15 = (s16[528,128]{1,0:T(8,128)(2,1)S(1)}, s16[528,128]{1,0:T(8,128)(2,1)S(1)}, u32[]{:S(2)}, u32[]{:S(2)}) collective-permute-start(s16[528,128]{1,0:T(8,128)(2,1)S(1)} %get-tuple-element.85), channel_id=1, source_target_pairs={{0,2},{2,0},{4,6},{6,4},{8,10},{10,8},{12,14},{14,12},{16,18},{18,... | collective-permute-start | bytes 405512 | tf_op jit(solution)/shard_map/ppermute | solution.py:213
  107.6 14.3 %collective-permute-start.24 = (s16[912,128]{1,0:T(8,128)(2,1)S(1)}, s16[912,128]{1,0:T(8,128)(2,1)S(1)}, u32[]{:S(2)}, u32[]{:S(2)}) collective-permute-start(s16[912,128]{1,0:T(8,128)(2,1)S(1)} %get-tuple-element.99), channel_id=1, source_target_pairs={{0,16},{2,18},{4,20},{6,22},{8,24},{10,26},{12,28},{14,30},{16,0},... | collective-permute-start | bytes 700424 | tf_op jit(solution)/shard_map/ppermute | solution.py:213
  110.8 11.3 %collective-permute-start.23 = (s16[784,128]{1,0:T(8,128)(2,1)S(1)}, s16[784,128]{1,0:T(8,128)(2,1)S(1)}, u32[]{:S(2)}, u32[]{:S(2)}) collective-permute-start(s16[784,128]{1,0:T(8,128)(2,1)S(1)} %get-tuple-element.98), channel_id=1, source_target_pairs={{0,8},{2,10},{4,12},{6,14},{8,0},{10,2},{12,4},{14,6},{16,24},{18,... | collective-permute-start | bytes 602120 | tf_op jit(solution)/shard_map/ppermute | solution.py:213
  112.9 10.1 %collective-permute-start.21 = (s16[528,128]{1,0:T(8,128)(2,1)S(1)}, s16[528,128]{1,0:T(8,128)(2,1)S(1)}, u32[]{:S(2)}, u32[]{:S(2)}) collective-permute-start(s16[528,128]{1,0:T(8,128)(2,1)S(1)} %get-tuple-element.95), channel_id=1, source_target_pairs={{0,2},{2,0},{4,6},{6,4},{8,10},{10,8},{12,14},{14,12},{16,18},{18,... | collective-permute-start | bytes 405512 | tf_op jit(solution)/shard_map/ppermute | solution.py:213
  114.0 14.0 %collective-permute-start.26 = (s16[656,128]{1,0:T(8,128)(2,1)S(1)}, s16[656,128]{1,0:T(8,128)(2,1)S(1)}, u32[]{:S(2)}, u32[]{:S(2)}) collective-permute-start(s16[656,128]{1,0:T(8,128)(2,1)S(1)} %get-tuple-element.103), channel_id=1, source_target_pairs={{0,16},{2,18},{4,20},{6,22},{8,24},{10,26},{12,28},{14,30},{16,0},... | collective-permute-start | bytes 503816 | tf_op jit(solution)/shard_map/ppermute | solution.py:213
  122.2 6.9 %collective-permute-start.27 = (s16[400,128]{1,0:T(8,128)(2,1)S(1)}, s16[400,128]{1,0:T(8,128)(2,1)S(1)}, u32[]{:S(2)}, u32[]{:S(2)}) collective-permute-start(s16[400,128]{1,0:T(8,128)(2,1)S(1)} %get-tuple-element.104), channel_id=1, source_target_pairs={{0,16},{2,18},{4,20},{6,22},{8,24},{10,26},{12,28},{14,30},{16,0},... | collective-permute-start | bytes 307208 | tf_op jit(solution)/shard_map/ppermute | solution.py:213
  128.1 1.2 copy-start.5

commit v7 on v6

--- a/solution.py
+++ b/solution.py
@@ -87,7 +87,7 @@
             for mask in masks:
                 piece = (me[0] ^ mask) // 2
                 entry, part = piece // per_block, piece % per_block
-                block = picks[begins[0] + c, entry] ^ me[1]
+                block = picks[c, entry] ^ me[1]
                 starts.append((mask & 1, pl.multiple_of(block * height + part * rows, rows)))
             total = None
             for t, grad in enumerate(grads):
@@ -214,9 +214,9 @@
 
     def fetch(after):
         chunks = messages[len(near_g)]
-        piece = out_grad[:, starts[chunks[0]] * BLOCK : (starts[chunks[-1]] + widths[chunks[-1]]) * BLOCK]
+        whole, after = lax.optimization_barrier((out_grad, after))
+        piece = whole[:, starts[chunks[0]] * BLOCK : (starts[chunks[-1]] + widths[chunks[-1]]) * BLOCK]
         piece = jnp.pad(piece, ((0, PAD), (0, 0)))
-        piece, after = lax.optimization_barrier((piece, after))
         near_g.append(swap(piece, 0))
         return after
 
@@ -244,7 +244,8 @@
         ]
         return jnp.concatenate(parts, axis=0)
 
-    own_t, other_t, near_t = spread(own), spread(other), spread(near)
+    own_t, other_t = spread(own), spread(other)
+    near_t = []
 
     def coded(width, n):
         return jax.ShapeDtypeStruct((width * n * rows + pad16(width * n), BLOCK), jnp.int16)
@@ -262,7 +263,7 @@
         if 0 in paths[i]:
             pairs, lefts, grads = ((0, 0), (1, 0)), [own_t, other_t], [out_grad]
         else:
-            pairs, lefts = ((0, 0), (0, 1)), [own_t, near_t]
+            pairs, lefts = ((0, 0), (0, 1)), [own_t, near_t[0]]
             at = next(m for m, chunks in enumerate(messages) if i in chunks)
             grads = [out_grad, near_g[at]]
             begins.append(starts[i] - starts[messages[at][0]])
@@ -274,7 +275,7 @@
             scratch_shapes=[scale(width, n)],
             compiler_params=params(),
             name="multiply",
-        )(place, row_blocks, *lefts, *grads, last)
+        )(place, row_blocks[starts[i] : starts[i] + width], *lefts, *grads, last)
 
     def combine(sources, n, encoded, last):
         width = sum(w for w, *_ in sources)
@@ -301,6 +302,13 @@
     state, outputs, last = {}, {}, place
     for what, i, *more in work:
         if what == "multiply":
+            if not near_t and 0 not in paths[i]:
+                if state:
+                    j = max(state)
+                    step, [(width, kept, *rest)] = state[j]
+                    near, kept = lax.optimization_barrier((near, kept))
+                    state[j] = step, [(width, kept, *rest)]
+                near_t.append(spread(near))
             kept, sent = multiply(i, last)
             last = kept
             if len(near_g) < len(messages) and any(i == chunks[0] for chunks in messages):

time: 130 us -> 145 us (1.12)
  local copies, waits for them, and re-layouts: 7.29 us -> 31.1 us
  Pallas kernels: 26.1 us -> 44.4 us
  waiting for transfers between devices: 54.7 us -> 37.2 us
  starting transfers between devices: 41.4 us -> 31.2 us
    unnamed x23 -> x74, local copies, waits for them, and re-layouts: 0.53 us -> 23.2 us
    ppermute x25, waiting for transfers between devices: 54.7 us -> 37.2 us  [swap(): return lax.ppermute(sent, 'dp', [(o, o ^ 1 << bit) for o in range(owners)])]
    pallas_call x20, Pallas kernels: 5.41 us -> 18.8 us  [combine(): pl.pallas_call(functools.partial(combine_kernel, shapes, rows, n, encoded...]
    ppermute x25, starting transfers between devices: 40.8 us -> 30.7 us  [swap(): return lax.ppermute(sent, 'dp', [(o, o ^ 1 << bit) for o in range(owners)])]
    pallas_call x6, Pallas kernels: 18.5 us -> 22.6 us  [multiply(): pl.pallas_call(functools.partial(multiply_kernel, width, rows, height, or...]
    pad x4, local copies, waits for them, and re-layouts: 1.11 us -> 3.64 us  [fetch(): piece = jnp.pad(piece, ((0, PAD), (0, 0)))]
    slice x5 -> x12, local copies, waits for them, and re-layouts: 2.62 us -> 0.31 us  [the longest x4 0.29 us: multiply(): row_blocks[starts[i]:starts[i] + width]]
  transfers between devices with their start and end apart: 28 -> 28, of which waited for: 14 -> 8; matrix products, arithmetic and copies ran while one was open for 2% -> 7% of each run, Pallas kernels for 18% -> 29%
where the time goes in v7:
time: 145 us; the launch traced here: 144 us
  Pallas kernels  44.4 us (31%)
  waiting for transfers between devices  37.2 us (26%)
  starting transfers between devices  31.2 us (22%)
  local copies, waits for them, and re-layouts  31.1 us (21%)
    ppermute x25, waiting for transfers between devices, swap(): return lax.ppermute(sent, 'dp', [(o, o ^ 1 << bit) for o in range(owners)])  37.2 us
    ppermute x25, starting transfers between devices, swap(): return lax.ppermute(sent, 'dp', [(o, o ^ 1 << bit) for o in range(owners)])  30.7 us
    unnamed x74, local copies, waits for them, and re-layouts  23.2 us
    pallas_call x6, Pallas kernels, multiply(): pl.pallas_call(functools.partial(multiply_kernel, width, rows, height, or...  22.6 us
    pallas_call x20, Pallas kernels, combine(): pl.pallas_call(functools.partial(combine_kernel, shapes, rows, n, encoded...  18.8 us
    pad x4, local copies, waits for them, and re-layouts, fetch(): piece = jnp.pad(piece, ((0, PAD), (0, 0)))  3.64 us
    concatenate x3, local copies, waits for them, and re-layouts, spread(): return jnp.concatenate(parts, axis=0)  3.23 us
    pallas_call x1, Pallas kernels, shards(): pl.pallas_call(functools.partial(prepare_kernel, rows), out_shape=[jax.Sh...  2.99 us
  transfers between devices with their start and end apart: 28, of which 8 were waited for; matrix products, arithmetic and copies ran while one was open for 7% of the time, Pallas kernels for 29%

profile of v7, /device:TPU:0, one launch (start us, length us, event | category | flops | bytes accessed | tf_op | source)
XLA Modules:
  0.0 144.4 jit_solution(4842622445543632187)
XLA Ops:
  0.1 1.3 copy-done.26
  1.4 0.7 copy-done.27
  2.0 3.0 %prepare.1 = (bf16[1024,256]{1,0:T(8,128)(2,1)}, bf16[1024,256]{1,0:T(8,128)(2,1)S(1)}) custom-call(s32[2]{0:T(128)S(1)} %pad_add_fusion.me.refs_3_, s32[1,4]{1,0:T(1,128)S(1)} %copy-done.27, bf16[256,2048]{1,0:T(8,128)(2,1)S(1)} %copy-done.26), custom_call_target="tpu_custom_call" | custom-call | tf_op jit(solution)/shard_map/prepare/pallas_call | solution.py:227
  5.5 2.9 %collective-permute-start.3 = (bf16[1024,256]{1,0:T(8,128)(2,1)S(1)}, bf16[1024,256]{1,0:T(8,128)(2,1)}, u32[]{:S(2)}, u32[]{:S(2)}) collective-permute-start(bf16[1024,256]{1,0:T(8,128)(2,1)S(1)} %get-tuple-element.60), channel_id=1, source_target_pairs={{0,2},{2,0},{4,6},{6,4},{8,10},{10,8},{12,14},{14,12},{16,18},{18,... | collective-permute-start | bytes 1572872 | tf_op jit(solution)/shard_map/ppermute | solution.py:213
  8.5 1.0 pad.15
  9.6 1.2 constant_dynamic-update-slice_fusion.1
  10.9 1.1 constant_dynamic-update-slice_fusion.refs_0_
  12.0 1.1 constant_dynamic-update-slice_fusion.2.refs_1_
  13.1 3.6 %multiply.6 = (f32[4096,128]{1,0:T(8,128)S(1)}, s16[4160,128]{1,0:T(8,128)(2,1)}) custom-call(s32[2]{0:T(128)S(1)} %pad_add_fusion.me.refs_3_, s32[8,8]{1,0:T(8,128)S(1)} %copy.11.picks, bf16[2048,256]{1,0:T(8,128)(2,1)S(1)} %constant_dynamic-update-slice_fusion.refs_0_, bf16[2048,256]{1,0:T(8,128)(2,1)S(1)} %constant_dynamic-update-slice_fusion.2.refs_1_, ...), custom_call_target="tpu_custom_call" | custom-call | tf_op jit(solution)/shard_map/multiply/pallas_call | solution.py:270
  16.7 1.4 copy-done.6
  18.0 2.1 %collective-permute-start.2 = (s16[4160,128]{1,0:T(8,128)(2,1)}, s16[4160,128]{1,0:T(8,128)(2,1)}, u32[]{:S(2)}, u32[]{:S(2)}) collective-permute-start(s16[4160,128]{1,0:T(8,128)(2,1)} %get-tuple-element.62), channel_id=1, source_target_pairs={{0,8},{2,10},{4,12},{6,14},{8,0},{10,2},{12,4},{14,6},{16,24},{18,... | collective-permute-start | bytes 3194888 | tf_op jit(solution)/shard_map/ppermute | solution.py:213
  20.2 2.0 %copy-done.1 = bf16[256,7168]{1,0:T(8,128)(2,1)S(1)} copy-done((bf16[256,7168]{1,0:T(8,128)(2,1)S(1)}, bf16[256,7168]{1,0:T(8,128)(2,1)}, u32[]{:S(2)}) %copy-start.1) | copy-done | bytes 3670040
  22.3 1.6 %copy-done.7 = f32[4096,128]{1,0:T(8,128)S(1)} copy-done((f32[4096,128]{1,0:T(8,128)S(1)}, f32[4096,128]{1,0:T(8,128)}, u32[]{:S(2)}) %copy-start.7) | copy-done | bytes 2097176
  23.9 3.5 %multiply.7 = (f32[4096,128]{1,0:T(8,128)S(1)}, s16[4160,128]{1,0:T(8,128)(2,1)}) custom-call(s32[2]{0:T(128)S(1)} %pad_add_fusion.me.refs_3_, s32[8,8]{1,0:T(8,128)S(1)} %copy.13.picks, bf16[2048,256]{1,0:T(8,128)(2,1)S(1)} %constant_dynamic-update-slice_fusion.refs_0_, bf16[2048,256]{1,0:T(8,128)(2,1)S(1)} %constant_dynamic-update-slice_fusion.2.refs_1_, ...), custom_call_target="tpu_custom_call" | custom-call | tf_op jit(solution)/shard_map/multiply/pallas_call | solution.py:270
  27.4 1.6 %collective-permute-start.9 = (s16[4160,128]{1,0:T(8,128)(2,1)}, s16[4160,128]{1,0:T(8,128)(2,1)}, u32[]{:S(2)}, u32[]{:S(2)}) collective-permute-start(s16[4160,128]{1,0:T(8,128)(2,1)} %get-tuple-element.74), channel_id=1, source_target_pairs={{0,4},{2,6},{4,0},{6,2},{8,12},{10,14},{12,8},{14,10},{16,20},{18,... | collective-permute-start | bytes 3194888 | tf_op jit(solution)/shard_map/ppermute | solution.py:213
  29.0 1.0 pad.16
  29.9 1.5 %collective-permute-start.7 = (bf16[264,1280]{1,0:T(8,128)(2,1)}, bf16[264,1280]{1,0:T(8,128)(2,1)S(1)}, u32[]{:S(2)}, u32[]{:S(2)}) collective-permute-start(bf16[264,1280]{1,0:T(8,128)(2,1)} %pad.16), channel_id=1, source_target_pairs={{0,2},{2,0},{4,6},{6,4},{8,10},{10,8},{12,14},{14,12},{16,18},{18,... | collective-permute-start | bytes 2027528 | tf_op jit(solution)/shard_map/ppermute | solution.py:213
  31.6 1.1 constant_dynamic-update-slice_fusion.5
  32.7 1.1 constant_dynamic-update-slice_fusion.4.refs_1_
  33.7 7.8 %collective-permute-done.5.refs_3_ = bf16[264,1792]{1,0:T(8,128)(2,1)} collective-permute-done((bf16[264,1792]{1,0:T(8,128)(2,1)}, bf16[264,1792]{1,0:T(8,128)(2,1)}, u32[]{:S(2)}, u32[]{:S(2)}) %collective-permute-start.5) | collective-permute-done | bytes 946208 | tf_op jit(solution)/shard_map/ppermute | solution.py:213
  41.6 2.0 %copy-done.2 = bf16[256,7168]{1,0:T(8,128)(2,1)S(1)} copy-done((bf16[256,7168]{1,0:T(8,128)(2,1)S(1)}, bf16[256,7168]{1,0:T(8,128)(2,1)}, u32[]{:S(2)}) %copy-start.2) | copy-done | bytes 3670040
  43.6 1.6 %copy-done.10 = f32[4096,128]{1,0:T(8,128)S(1)} copy-done((f32[4096,128]{1,0:T(8,128)S(1)}, f32[4096,128]{1,0:T(8,128)}, u32[]{:S(2)}) %copy-start.10) | copy-done | bytes 2097176
  45.2 5.2 %multiply.8 = (f32[3584,128]{1,0:T(8,128)S(1)}, s16[3648,128]{1,0:T(8,128)(2,1)}) custom-call(s32[2]{0:T(128)S(1)} %pad_add_fusion.me.refs_3_, s32[14,8]{1,0:T(8,128)S(1)} %copy.12.picks, bf16[2048,256]{1,0:T(8,128)(2,1)S(1)} %constant_dynamic-update-slice_fusion.refs_0_, bf16[2048,256]{1,0:T(8,128)(2,1)S(1)} %constant_dynamic-update-slice_fusion.4.refs_1_, ...), custom_call_target="tpu_custom_call" | custom-call | tf_op jit(solution)/shard_map/multiply/pallas_call | solution.py:270
  50.4 2.2 %collective-permute-start.13 = (s16[3648,128]{1,0:T(8,128)(2,1)}, s16[3648,128]{1,0:T(8,128)(2,1)}, u32[]{:S(2)}, u32[]{:S(2)}) collective-permute-start(s16[3648,128]{1,0:T(8,128)(2,1)} %get-tuple-element.81), channel_id=1, source_target_pairs={{0,8},{2,10},{4,12},{6,14},{8,0},{10,2},{12,4},{14,6},{16,24},{18,... | collective-permute-start | bytes 2801672 | tf_op jit(solution)/shard_map/ppermute | solution.py:213
  52.6 0.9 pad.18
  53.5 1.5 %collective-permute-start.14 = (bf16[264,1280]{1,0:T(8,128)(2,1)}, bf16[264,1280]{1,0:T(8,128)(2,1)}, u32[]{:S(2)}, u32[]{:S(2)}) collective-permute-start(bf16[264,1280]{1,0:T(8,128)(2,1)} %pad.18), channel_id=1, source_target_pairs={{0,2},{2,0},{4,6},{6,4},{8,10},{10,8},{12,14},{14,12},{16,18},{18,... | collective-permute-start | bytes 2027528 | tf_op jit(solution)/shard_map/ppermute | solution.py:213
  55.0 2.6 %combine.20 = (f32[2048,128]{1,0:T(8,128)S(1)}, s16[2080,128]{1,0:T(8,128)(2,1)}) custom-call(f32[4096,128]{1,0:T(8,128)S(1)} %copy-done.8, s16[4160,128]{1,0:T(8,128)(2,1)} %collective-permute-done.2.refs_1_, f32[3584,128]{1,0:T(8,128)S(1)} %get-tuple-element.80.refs_2_.refs_0_), custom_call_target="tpu_custom_call" | custom-call | tf_op jit(solution)/shard_map/combine/pallas_call | solution.py:292
  57.6 1.1 copy-done.21
  58.7 1.5 %collective-permute-start.6 = (s16[2080,128]{1,0:T(8,128)(2,1)}, s16[2080,128]{1,0:T(8,128)(2,1)S(1)}, u32[]{:S(2)}, u32[]{:S(2)}) collective-permute-start(s16[2080,128]{1,0:T(8,128)(2,1)} %get-tuple-element.68), channel_id=1, source_target_pairs={{0,4},{2,6},{4,0},{6,2},{8,12},{10,14},{12,8},{14,10},{16,20},{18,... | collective-permute-start | bytes 1597448 | tf_op jit(solution)/shard_map/ppermute | solution.py:213
  60.4 2.0 %copy-done.3 = bf16[256,7168]{1,0:T(8,128)(2,1)S(1)} copy-done((bf16[256,7168]{1,0:T(8,128)(2,1)S(1)}, bf16[256,7168]{1,0:T(8,128)(2,1)}, u32[]{:S(2)}) %copy-start.3) | copy-done | bytes 3670040
  62.4 1.2 copy-done.22
  63.7 3.7 %multiply.9 = (f32[2560,128]{1,0:T(8,128)S(1)}, s16[2608,128]{1,0:T(8,128)(2,1)}) custom-call(s32[2]{0:T(128)S(1)} %pad_add_fusion.me.refs_3_, s32[10,8]{1,0:T(8,128)S(1)} %copy.14.picks, bf16[2048,256]{1,0:T(8,128)(2,1)S(1)} %constant_dynamic-update-slice_fusion.refs_0_, bf16[2048,256]{1,0:T(8,128)(2,1)S(1)} %constant_dynamic-update-slice_fusion.4.refs_1_, ...), custom_call_target="tpu_custom_call" | custom-call | tf_op jit(solution)/shard_map/multiply/pallas_call | solution.py:270
  67.9 5.5 %collective-permute-done.6.refs_1_ = s16[2080,128]{1,0:T(8,128)(2,1)S(1)} collective-permute-done((s16[2080,128]{1,0:T(8,128)(2,1)}, s16[2080,128]{1,0:T(8,128)(2,1)S(1)}, u32[]{:S(2)}, u32[]{:S(2)}) %collective-permute-start.6) | collective-permute-done | bytes 532512 | tf_op jit(solution)/shard_map/ppermute | solution.py:213
  73.5 1.0 combine.21
  74.5 2.7 %combine.22 = (f32[2048,128]{1,0:T(8,128)S(1)}, s16[2080,128]{1,0:T(8,128)(2,1)}) custom-call(f32[4096,128]{1,0:T(8,128)S(1)} %copy-done.11, s16[4160,128]{1,0:T(8,128)(2,1)} %collective-permute-done.9.refs_1_, f32[1024,128]{1,0:T(8,128)S(1)} %get-tuple-element.71.refs_2_.refs_0_), custom_call_target="tpu_custom_call" | custom-call | tf_op jit(solution)/shard_map/combine/pallas_call | solution.py:292
  77.2 0.7 collective-permute-start.10
  77.9 0.8 pad.17
  78.7 1.4 collective-permute-start.11
  80.1 2.0 %copy-done.4 = bf16[256,7168]{1,0:T(8,128)(2,1)S(1)} copy-done((bf16[256,7168]{1,0:T(8,128)(2,1)S(1)}, bf16[256,7168]{1,0:T(8,128)(2,1)}, u32[]{:S(2)}) %copy-start.4) | copy-done | bytes 3670040
  82.2 1.2 copy-done.19
  83.4 4.3 %multiply.10 = (f32[2560,128]{1,0:T(8,128)S(1)}, s16[2608,128]{1,0:T(8,128)(2,1)}) custom-call(s32[2]{0:T(128)S(1)} %pad_add_fusion.me.refs_3_, s32[10,8]{1,0:T(8,128)S(1)} %copy.16.picks, bf16[2048,256]{1,0:T(8,128)(2,1)S(1)} %constant_dynamic-update-slice_fusion.refs_0_, bf16[2048,256]{1,0:T(8,128)(2,1)S(1)} %constant_dynamic-update-slice_fusion.4.refs_1_, ...), custom_call_target="tpu_custom_call" | custom-call | tf_op jit(solution)/shard_map/multiply/pallas_call | solution.py:270
  87.7 1.5 %collective-permute-start.17 = (s16[2608,128]{1,0:T(8,128)(2,1)}, s16[2608,128]{1,0:T(8,128)(2,1)}, u32[]{:S(2)}, u32[]{:S(2)}) collective-permute-start(s16[2608,128]{1,0:T(8,128)(2,1)} %get-tuple-element.91), channel_id=1, source_target_pairs={{0,4},{2,6},{4,0},{6,2},{8,12},{10,14},{12,8},{14,10},{16,20},{18,... | collective-permute-start | bytes 2002952 | tf_op jit(solution)/shard_map/ppermute | solution.py:213
  89.2 2.6 %collective-permute-start.8 = (s16[1040,128]{1,0:T(8,128)(2,1)}, s16[1040,128]{1,0:T(8,128)(2,1)S(1)}, u32[]{:S(2)}, u32[]{:S(2)}) collective-permute-start(s16[1040,128]{1,0:T(8,128)(2,1)} %get-tuple-element.72), channel_id=1, source_target_pairs={{0,16},{2,18},{4,20},{6,22},{8,24},{10,26},{12,28},{14,30},{16,0},... | collective-permute-start | bytes 798728 | tf_op jit(solution)/shard_map/ppermute | solution.py:213
  91.8 2.6 %combine.23 = (f32[1792,128]{1,0:T(8,128)S(1)}, s16[1824,128]{1,0:T(8,128)(2,1)}) custom-call(f32[3584,128]{1,0:T(8,128)S(1)} %copy-done.13, s16[3648,128]{1,0:T(8,128)(2,1)} %collective-permute-done.13.refs_1_, f32[2560,128]{1,0:T(8,128)S(1)} %get-tuple-element.83.refs_2_.refs_0_), custom_call_target="tpu_custom_call" | custom-call | tf_op jit(solution)/shard_map/combine/pallas_call | solution.py:292
  94.5 2.6 %combine.24 = (f32[1280,128]{1,0:T(8,128)S(1)}, s16[1312,128]{1,0:T(8,128)(2,1)}) custom-call(f32[2560,128]{1,0:T(8,128)S(1)} %copy-done.17, s16[2608,128]{1,0:T(8,128)(2,1)} %collective-permute-done.12.refs_1_, f32[1792,128]{1,0:T(8,128)S(1)} %get-tuple-element.84.refs_2_.refs_0_), custom_call_target="tpu_custom_call" | custom-call | tf_op jit(solution)/shard_map/combine/pallas_call | solution.py:292
  97.1 1.0 collective-permute-start.16
  98.3 2.0 %copy-done.5 = bf16[256,7168]{1,0:T(8,128)(2,1)S(1)} copy-done((bf16[256,7168]{1,0:T(8,128)(2,1)S(1)}, bf16[256,7168]{1,0:T(8,128)(2,1)}, u32[]{:S(2)}) %copy-start.5) | copy-done | bytes 3670040
  100.3 2.3 %multiply.11 = (f32[1536,128]{1,0:T(8,128)S(1)}, s16[1568,128]{1,0:T(8,128)(2,1)S(1)}) custom-call(s32[2]{0:T(128)S(1)} %pad_add_fusion.me.refs_3_, s32[6,8]{1,0:T(8,128)S(1)} %copy.15.picks, bf16[2048,256]{1,0:T(8,128)(2,1)S(1)} %constant_dynamic-update-slice_fusion.refs_0_, bf16[2048,256]{1,0:T(8,128)(2,1)S(1)} %constant_dynamic-update-slice_fusion.4.refs_1_, ...), custom_call_target="tpu_custom_call" | custom-call | tf_op jit(solution)/shard_map/multiply/pallas_call | solution.py:270
  102.7 1.5 %combine.25 = (f32[1024,128]{1,0:T(8,128)S(1)}, s16[1040,128]{1,0:T(8,128)(2,1)S(1)}) custom-call(f32[2048,128]{1,0:T(8,128)S(1)} %copy-done.20, s16[2080,128]{1,0:T(8,128)(2,1)} %collective-permute-done.10.refs_1_, f32[1536,128]{1,0:T(8,128)S(1)} %get-tuple-element.86.refs_2_.refs_0_), custom_call_target="tpu_custom_call" | custom-call | tf_op jit(solution)/shard_map/combine/pallas_call | solution.py:292
  104.5 2.0 %collective-permute-start.22 = (s16[1568,128]{1,0:T(8,128)(2,1)S(1)}, s16[1568,128]{1,0:T(8,128)(2,1)S(1)}, u32[]{:S(2)}, u32[]{:S(2)}) collective-permute-start(s16[1568,128]{1,0:T(8,128)(2,1)S(1)} %get-tuple-element.100), channel_id=1, source_target_pairs={{0,4},{2,6},{4,0},{6,2},{8,12},{10,14},{12,8},{14,10},{16,20},{18,... | collective-permute-start | bytes 1204232 | tf_op jit(solution)/shard_map/ppermute | solution.py:213
  106.7 1.5 %combine.27 = (f32[1280,128]{1,0:T(8,128)S(1)}, s16[1312,128]{1,0:T(8,128)(2,1)S(1)}) custom-call(f32[2560,128]{1,0:T(8,128)S(1)} %copy-done.15, s16[2608,128]{1,0:T(8,128)(2,1)} %collective-permute-done.17.refs_1_, f32[512,128]{1,0:T(8,128)S(1)} %get-tuple-element.88.refs_2_.refs_0_), custom_call_target="tpu_custom_call" | custom-call | tf_op jit(solution)/shard_map/combine/pallas_call | solution.py:292
  108.9 1.3 combine.28
  110.2 2.1 %collective-permute-start.18 = (s16[656,128]{1,0:T(8,128)(2,1)S(1)}, s16[656,128]{1,0:T(8,128)(2,1)S(1)}, u32[]{:S(2)}, u32[]{:S(2)}) collective-permute-start(s16[656,128]{1,0:T(8,128)(2,1)S(1)} %get-tuple-element.94), channel_id=1, source_target_pairs={{0,16},{2,18},{4,20},{6,22},{8,24},{10,26},{12,28},{14,30},{16,0},... | collective-permute-start | bytes 503816 | tf_op jit(solution)/shard_map/ppermute | solution.py:213
  112.3 1.0 collective-permute-start.25
  113.3 8.6 %collective-permute-done.20.refs_1_ = s16[1040,128]{1,0:T(8,128)(2,1)S(1)} collective-permute-done((s16[1040,128]{1,0:T(8,128)(2,1)S(1)}, s16[1040,128]{1,0:T(8,128)(2,1)S(1)}, u32[]{:S(2)}, u32[]{:S(2)}) %collective-permute-start.20) | collective-permute-done | bytes 266272 | tf_op jit(solution)/shard_map/ppermute | solution.py:213
  121.9 1.0 collective-permute-start.15
  123.1 1.4 combine.30
  124.7 2.2 %collective-permute-done.15.refs_1_ = s16[528,128]{1,0:T(8,128)(2,1)S(1)} collective-permute-done((s16[528,128]{1,0:T(8,128)(2,1)S(1)}, s16[528,128]{1,0:T(8,128)(2,1)S(1)}, u32[]{:S(2)}, u32[]{:S(2)}) %collective-permute-start.15) | collective-permute-done | bytes 135200 | tf_op jit(solution)/shard_map/ppermute | solution.py:213
  127.3 1.1 collective-permute-start.21
  128.7 1.9 %collective-permute-start.26 = (s16[656,128]{1,0:T(8,128)(2,1)S(1)}, s16[656,128]{1,0:T(8,128)(2,1)S(1)}, u32[]{:S(2)}, u32[]{:S(2)}) collective-permute-start(s16[656,128]{1,0:T(8,128)(2,1)S(1)} %get-tuple-element.107), channel_id=1, source_target_pairs={{0,16},{2,18},{4,20},{6,22},{8,24},{10,26},{12,28},{14,30},{16,0},... | collective-permute-start | bytes 503816 | tf_op jit(solution)/shard_map/ppermute | solution.py:213
  130.6 6.6 %collective-permute-done.24.refs_1_ = s16[912,128]{1,0:T(8,128)(2,1)S(1)} collective-permute-done((s16[912,128]{1,0:T(8,128)(2,1)S(1)}, s16[912,128]{1,0:T(8,128)(2,1)S(1)}, u32[]{:S(2)}, u32[]{:S(2)}) %collective-permute-start.24) | collective-permute-done | bytes 233504 | tf_op jit(solution)/shard_map/ppermute | solution.py:213
  137.8 1.3 collective-permute-done.26.refs_1_
  139.1 4.5 %collective-permute-done.27.refs_1_ = s16[400,128]{1,0:T(8,128)(2,1)S(1)} collective-permute-done((s16[400,128]{1,0:T(8,128)(2,1)S(1)}, s16[400,128]{1,0:T(8,128)(2,1)S(1)}, u32[]{:S(2)}, u32[]{:S(2)}) %collective-permute-start.27) | collective-permute-done | bytes 102432 | tf_op jit(solution)/shard_map/ppermute | solution.py:213
  143.7 0.7 constant_dynamic-update-slice_fusion.6
  (114 shorter events, 5.1 us)
Async XLA Ops:
  0.0 8.5 %slice-start = ((bf16[256,7168]{1,0:T(8,128)(2,1)}), bf16[256,1792]{1,0:T(8,128)(2,1)S(1)}, s32[]{:S(2)}) async-start(bf16[256,7168]{1,0:T(8,128)(2,1)} %refs_2_.11), calls=%async_computation | async-start | bytes 1835008 | tf_op jit(solution)/shard_map/slice | solution.py:218
  0.1 1.3 copy-start.26
  1.4 0.7 copy-start.27
  5.0 5.9 %collective-permute-start = (bf16[1024,256]{1,0:T(8,128)(2,1)}, bf16[1024,256]{1,0:T(8,128)(2,1)}, u32[]{:S(2)}, u32[]{:S(2)}) collective-permute-start(bf16[1024,256]{1,0:T(8,128)(2,1)} %get-tuple-element.59), channel_id=1, source_target_pairs={{0,1},{1,0},{2,3},{3,2},{4,5},{5,4},{6,7},{7,6},{8,9},{9,8},{10,11... | collective-permute-start | bytes 1572872 | tf_op jit(solution)/shard_map/ppermute | solution.py:243
  5.5 4.0 %copy-start.28 = (s32[56,8]{0,1:T(8,128)S(1)}, s32[56,8]{0,1:T(8,128)}, u32[]{:S(2)}) copy-start(s32[56,8]{0,1:T(8,128)} %param.6) | copy-start | bytes 5380
  5.5 6.5 %collective-permute-start.1 = (bf16[1024,256]{1,0:T(8,128)(2,1)S(1)}, bf16[1024,256]{1,0:T(8,128)(2,1)}, u32[]{:S(2)}, u32[]{:S(2)}) collective-permute-start(bf16[1024,256]{1,0:T(8,128)(2,1)S(1)} %get-tuple-element.60), channel_id=1, source_target_pairs={{0,1},{1,0},{2,3},{3,2},{4,5},{5,4},{6,7},{7,6},{8,9},{9,8},{10,11... | collective-permute-start | bytes 1572872 | tf_op jit(solution)/shard_map/ppermute | solution.py:243
  5.5 21.8 %collective-permute-start.3 = (bf16[1024,256]{1,0:T(8,128)(2,1)S(1)}, bf16[1024,256]{1,0:T(8,128)(2,1)}, u32[]{:S(2)}, u32[]{:S(2)}) collective-permute-start(bf16[1024,256]{1,0:T(8,128)(2,1)S(1)} %get-tuple-element.60), channel_id=1, source_target_pairs={{0,2},{2,0},{4,6},{6,4},{8,10},{10,8},{12,14},{14,12},{16,18},{18,... | collective-permute-start | bytes 1572872 | tf_op jit(solution)/shard_map/ppermute | solution.py:213
  9.5 32.1 %collective-permute-start.5 = (bf16[264,1792]{1,0:T(8,128)(2,1)}, bf16[264,1792]{1,0:T(8,128)(2,1)}, u32[]{:S(2)}, u32[]{:S(2)}) collective-permute-start(bf16[264,1792]{1,0:T(8,128)(2,1)} %pad.15), channel_id=1, source_target_pairs={{0,2},{2,0},{4,6},{6,4},{8,10},{10,8},{12,14},{14,12},{16,18},{18,... | collective-permute-start | bytes 2838536 | tf_op jit(solution)/shard_map/ppermute | solution.py:213
  9.6 3.5 %copy-start = (bf16[256,7168]{1,0:T(8,128)(2,1)S(1)}, bf16[256,7168]{1,0:T(8,128)(2,1)}, u32[]{:S(2)}) copy-start(bf16[256,7168]{1,0:T(8,128)(2,1)} %refs_2_.11) | copy-start | bytes 11010052
  16.7 1.4 copy-start.6
  18.0 37.0 %collective-permute-start.2 = (s16[4160,128]{1,0:T(8,128)(2,1)}, s16[4160,128]{1,0:T(8,128)(2,1)}, u32[]{:S(2)}, u32[]{:S(2)}) collective-permute-start(s16[4160,128]{1,0:T(8,128)(2,1)} %get-tuple-element.62), channel_id=1, source_target_pairs={{0,8},{2,10},{4,12},{6,14},{8,0},{10,2},{12,4},{14,6},{16,24},{18,... | collective-permute-start | bytes 3194888 | tf_op jit(solution)/shard_map/ppermute | solution.py:213
  20.2 2.0 %copy-start.1 = (bf16[256,7168]{1,0:T(8,128)(2,1)S(1)}, bf16[256,7168]{1,0:T(8,128)(2,1)}, u32[]{:S(2)}) copy-start(bf16[256,7168]{1,0:T(8,128)(2,1)} %refs_2_.11) | copy-start | bytes 11010052
  22.3 1.6 %copy-start.7 = (f32[4096,128]{1,0:T(8,128)S(1)}, f32[4096,128]{1,0:T(8,128)}, u32[]{:S(2)}) copy-start(f32[4096,128]{1,0:T(8,128)} %copy-done.6) | copy-start | bytes 6291460
  23.9 5.1 %slice-start.1 = ((bf16[256,7168]{1,0:T(8,128)(2,1)}), bf16[256,1280]{1,0:T(8,128)(2,1)S(1)}, s32[]{:S(2)}) async-start(bf16[256,7168]{1,0:T(8,128)(2,1)} %refs_2_.11), calls=%async_computation.1 | async-start | bytes 1310720 | tf_op jit(solution)/shard_map/slice | solution.py:218
  27.4 2.6 %copy-start.9 = (f32[4096,128]{1,0:T(8,128)}, f32[4096,128]{1,0:T(8,128)S(1)}, u32[]{:S(2)}) copy-start(f32[4096,128]{1,0:T(8,128)S(1)} %get-tuple-element.73.refs_4_.refs_0_) | copy-start | bytes 6291460
  27.4 5.3 %collective-permute-start.4 = (bf16[1024,256]{1,0:T(8,128)(2,1)}, bf16[1024,256]{1,0:T(8,128)(2,1)}, u32[]{:S(2)}, u32[]{:S(2)}) collective-permute-start(bf16[1024,256]{1,0:T(8,128)(2,1)} %collective-permute-done.3), channel_id=1, source_target_pairs={{0,1},{1,0},{2,3},{3,2},{4,5},{5,4},{6,7},{7,6},{8,9},{9,8},{10,11... | collective-permute-start | bytes 1572872 | tf_op jit(solution)/shard_map/ppermute | solution.py:243
  27.4 47.1 %collective-permute-start.9 = (s16[4160,128]{1,0:T(8,128)(2,1)}, s16[4160,128]{1,0:T(8,128)(2,1)}, u32[]{:S(2)}, u32[]{:S(2)}) collective-permute-start(s16[4160,128]{1,0:T(8,128)(2,1)} %get-tuple-element.74), channel_id=1, source_target_pairs={{0,4},{2,6},{4,0},{6,2},{8,12},{10,14},{12,8},{14,10},{16,20},{18,... | collective-permute-start | bytes 3194888 | tf_op jit(solution)/shard_map/ppermute | solution.py:213
  29.9 30.5 %collective-permute-start.7 = (bf16[264,1280]{1,0:T(8,128)(2,1)}, bf16[264,1280]{1,0:T(8,128)(2,1)S(1)}, u32[]{:S(2)}, u32[]{:S(2)}) collective-permute-start(bf16[264,1280]{1,0:T(8,128)(2,1)} %pad.16), channel_id=1, source_target_pairs={{0,2},{2,0},{4,6},{6,4},{8,10},{10,8},{12,14},{14,12},{16,18},{18,... | collective-permute-start | bytes 2027528 | tf_op jit(solution)/shard_map/ppermute | solution.py:213
  41.6 2.0 %copy-start.2 = (bf16[256,7168]{1,0:T(8,128)(2,1)S(1)}, bf16[256,7168]{1,0:T(8,128)(2,1)}, u32[]{:S(2)}) copy-start(bf16[256,7168]{1,0:T(8,128)(2,1)} %refs_2_.11) | copy-start | bytes 11010052
  43.6 1.6 %copy-start.10 = (f32[4096,128]{1,0:T(8,128)S(1)}, f32[4096,128]{1,0:T(8,128)}, u32[]{:S(2)}) copy-start(f32[4096,128]{1,0:T(8,128)} %copy-done.9) | copy-start | bytes 6291460
  45.2 7.4 %slice-start.2 = ((bf16[256,7168]{1,0:T(8,128)(2,1)}), bf16[256,1280]{1,0:T(8,128)(2,1)S(1)}, s32[]{:S(2)}) async-start(bf16[256,7168]{1,0:T(8,128)(2,1)} %refs_2_.11), calls=%async_computation.2 | async-start | bytes 1310720 | tf_op jit(solution)/shard_map/slice | solution.py:218
  50.4 7.2 %copy-start.12 = (f32[3584,128]{1,0:T(8,128)}, f32[3584,128]{1,0:T(8,128)S(1)}, u32[]{:S(2)}) copy-start(f32[3584,128]{1,0:T(8,128)S(1)} %get-tuple-element.80.refs_2_.refs_0_) | copy-start | bytes 5505028
  50.4 4.6 %copy-start.8 = (f32[4096,128]{1,0:T(8,128)S(1)}, f32[4096,128]{1,0:T(8,128)}, u32[]{:S(2)}) copy-start(f32[4096,128]{1,0:T(8,128)} %copy-done.6) | copy-start | bytes 6291460
  50.4 38.8 %collective-permute-start.13 = (s16[3648,128]{1,0:T(8,128)(2,1)}, s16[3648,128]{1,0:T(8,128)(2,1)}, u32[]{:S(2)}, u32[]{:S(2)}) collective-permute-start(s16[3648,128]{1,0:T(8,128)(2,1)} %get-tuple-element.81), channel_id=1, source_target_pairs={{0,8},{2,10},{4,12},{6,14},{8,0},{10,2},{12,4},{14,6},{16,24},{18,... | collective-permute-start | bytes 2801672 | tf_op jit(solution)/shard_map/ppermute | solution.py:213
  53.5 26.6 %collective-permute-start.14 = (bf16[264,1280]{1,0:T(8,128)(2,1)}, bf16[264,1280]{1,0:T(8,128)(2,1)}, u32[]{:S(2)}, u32[]{:S(2)}) collective-permute-start(bf16[264,1280]{1,0:T(8,128)(2,1)} %pad.18), channel_id=1, source_target_pairs={{0,2},{2,0},{4,6},{6,4},{8,10},{10,8},{12,14},{14,12},{16,18},{18,... | collective-permute-start | bytes 2027528 | tf_op jit(solution)/shard_map/ppermute | solution.py:213
  57.6 1.1 copy-start.21
  58.7 14.7 %collective-permute-start.6 = (s16[2080,128]{1,0:T(8,128)(2,1)}, s16[2080,128]{1,0:T(8,128)(2,1)S(1)}, u32[]{:S(2)}, u32[]{:S(2)}) collective-permute-start(s16[2080,128]{1,0:T(8,128)(2,1)} %get-tuple-element.68), channel_id=1, source_target_pairs={{0,4},{2,6},{4,0},{6,2},{8,12},{10,14},{12,8},{14,10},{16,20},{18,... | collective-permute-start | bytes 1597448 | tf_op jit(solution)/shard_map/ppermute | solution.py:213
  60.4 2.0 %copy-start.3 = (bf16[256,7168]{1,0:T(8,128)(2,1)S(1)}, bf16[256,7168]{1,0:T(8,128)(2,1)}, u32[]{:S(2)}) copy-start(bf16[256,7168]{1,0:T(8,128)(2,1)} %refs_2_.11) | copy-start | bytes 11010052
  62.4 1.2 copy-start.22
  63.7 9.8 %copy-start.23 = (f32[2048,128]{1,0:T(8,128)S(1)}, f32[2048,128]{1,0:T(8,128)}, u32[]{:S(2)}) copy-start(f32[2048,128]{1,0:T(8,128)} %copy-done.21) | copy-start | bytes 3145732
  67.4 7.1 %copy-start.16 = (f32[2560,128]{1,0:T(8,128)}, f32[2560,128]{1,0:T(8,128)S(1)}, u32[]{:S(2)}) copy-start(f32[2560,128]{1,0:T(8,128)S(1)} %get-tuple-element.78.refs_2_.refs_0_) | copy-start | bytes 3932164
  67.4 7.1 %copy-start.11 = (f32[4096,128]{1,0:T(8,128)S(1)}, f32[4096,128]{1,0:T(8,128)}, u32[]{:S(2)}) copy-start(f32[4096,128]{1,0:T(8,128)} %copy-done.9) | copy-start | bytes 6291460
  67.4 27.1 %collective-permute-start.12 = (s16[2608,128]{1,0:T(8,128)(2,1)}, s16[2608,128]{1,0:T(8,128)(2,1)}, u32[]{:S(2)}, u32[]{:S(2)}) collective-permute-start(s16[2608,128]{1,0:T(8,128)(2,1)} %get-tuple-element.79), channel_id=1, source_target_pairs={{0,4},{2,6},{4,0},{6,2},{8,12},{10,14},{12,8},{14,10},{16,20},{18,... | collective-permute-start | bytes 2002952 | tf_op jit(solution)/shard_map/ppermute | solution.py:213
  74.5 3.4 %slice-start.3 = ((bf16[256,7168]{1,0:T(8,128)(2,1)}), bf16[256,768]{1,0:T(8,128)(2,1)S(1)}, s32[]{:S(2)}) async-start(bf16[256,7168]{1,0:T(8,128)(2,1)} %refs_2_.11), calls=%async_computation.3 | async-start | bytes 786432 | tf_op jit(solution)/shard_map/slice | solution.py:218
  77.2 1.5 %copy-start.18 = (f32[2048,128]{1,0:T(8,128)}, f32[2048,128]{1,0:T(8,128)S(1)}, u32[]{:S(2)}) copy-start(f32[2048,128]{1,0:T(8,128)S(1)} %get-tuple-element.75.refs_4_.refs_0_) | copy-start | bytes 3145732
  77.2 25.4 %collective-permute-start.10 = (s16[2080,128]{1,0:T(8,128)(2,1)}, s16[2080,128]{1,0:T(8,128)(2,1)}, u32[]{:S(2)}, u32[]{:S(2)}) collective-permute-start(s16[2080,128]{1,0:T(8,128)(2,1)} %get-tuple-element.76), channel_id=1, source_target_pairs={{0,8},{2,10},{4,12},{6,14},{8,0},{10,2},{12,4},{14,6},{16,24},{18,... | collective-permute-start | bytes 1597448 | tf_op jit(solution)/shard_map/ppermute | solution.py:213
  78.7 19.4 %collective-permute-start.11 = (bf16[264,768]{1,0:T(8,128)(2,1)}, bf16[264,768]{1,0:T(8,128)(2,1)}, u32[]{:S(2)}, u32[]{:S(2)}) collective-permute-start(bf16[264,768]{1,0:T(8,128)(2,1)} %pad.17), channel_id=1, source_target_pairs={{0,2},{2,0},{4,6},{6,4},{8,10},{10,8},{12,14},{14,12},{16,18},{18,... | collective-permute-start | bytes 1216520 | tf_op jit(solution)/shard_map/ppermute | solution.py:213
  80.1 2.0 %copy-start.4 = (bf16[256,7168]{1,0:T(8,128)(2,1)S(1)}, bf16[256,7168]{1,0:T(8,128)(2,1)}, u32[]{:S(2)}) copy-start(bf16[256,7168]{1,0:T(8,128)(2,1)} %refs_2_.11) | copy-start | bytes 11010052
  82.2 1.2 copy-start.19
  83.4 8.4 %copy-start.13 = (f32[3584,128]{1,0:T(8,128)S(1)}, f32[3584,128]{1,0:T(8,128)}, u32[]{:S(2)}) copy-start(f32[3584,128]{1,0:T(8,128)} %copy-done.12) | copy-start | bytes 5505028
  87.7 6.8 %copy-start.14 = (f32[2560,128]{1,0:T(8,128)}, f32[2560,128]{1,0:T(8,128)S(1)}, u32[]{:S(2)}) copy-start(f32[2560,128]{1,0:T(8,128)S(1)} %get-tuple-element.83.refs_2_.refs_0_) | copy-start | bytes 3932164
  87.7 19.0 %collective-permute-start.17 = (s16[2608,128]{1,0:T(8,128)(2,1)}, s16[2608,128]{1,0:T(8,128)(2,1)}, u32[]{:S(2)}, u32[]{:S(2)}) collective-permute-start(s16[2608,128]{1,0:T(8,128)(2,1)} %get-tuple-element.91), channel_id=1, source_target_pairs={{0,4},{2,6},{4,0},{6,2},{8,12},{10,14},{12,8},{14,10},{16,20},{18,... | collective-permute-start | bytes 2002952 | tf_op jit(solution)/shard_map/ppermute | solution.py:213
  89.2 15.3 %collective-permute-start.8 = (s16[1040,128]{1,0:T(8,128)(2,1)}, s16[1040,128]{1,0:T(8,128)(2,1)S(1)}, u32[]{:S(2)}, u32[]{:S(2)}) collective-permute-start(s16[1040,128]{1,0:T(8,128)(2,1)} %get-tuple-element.72), channel_id=1, source_target_pairs={{0,16},{2,18},{4,20},{6,22},{8,24},{10,26},{12,28},{14,30},{16,0},... | collective-permute-start | bytes 798728 | tf_op jit(solution)/shard_map/ppermute | solution.py:213
  91.8 2.7 %copy-start.17 = (f32[2560,128]{1,0:T(8,128)S(1)}, f32[2560,128]{1,0:T(8,128)}, u32[]{:S(2)}) copy-start(f32[2560,128]{1,0:T(8,128)} %copy-done.16) | copy-start | bytes 3932164
  94.5 2.6 %copy-start.24 = (f32[1792,128]{1,0:T(8,128)}, f32[1792,128]{1,0:T(8,128)S(1)}, u32[]{:S(2)}) copy-start(f32[1792,128]{1,0:T(8,128)S(1)} %get-tuple-element.84.refs_2_.refs_0_) | copy-start | bytes 2752516
  97.1 11.8 %collective-permute-start.16 = (s16[1312,128]{1,0:T(8,128)(2,1)}, s16[1312,128]{1,0:T(8,128)(2,1)}, u32[]{:S(2)}, u32[]{:S(2)}) collective-permute-start(s16[1312,128]{1,0:T(8,128)(2,1)} %get-tuple-element.90), channel_id=1, source_target_pairs={{0,8},{2,10},{4,12},{6,14},{8,0},{10,2},{12,4},{14,6},{16,24},{18,... | collective-permute-start | bytes 1007624 | tf_op jit(solution)/shard_map/ppermute | solution.py:213
  98.1 25.0 %collective-permute-start.19 = (s16[1824,128]{1,0:T(8,128)(2,1)}, s16[1824,128]{1,0:T(8,128)(2,1)}, u32[]{:S(2)}, u32[]{:S(2)}) collective-permute-start(s16[1824,128]{1,0:T(8,128)(2,1)} %get-tuple-element.95), channel_id=1, source_target_pairs={{0,4},{2,6},{4,0},{6,2},{8,12},{10,14},{12,8},{14,10},{16,20},{18,... | collective-permute-start | bytes 1400840 | tf_op jit(solution)/shard_map/ppermute | solution.py:213
  98.3 2.0 %copy-start.5 = (bf16[256,7168]{1,0:T(8,128)(2,1)S(1)}, bf16[256,7168]{1,0:T(8,128)(2,1)}, u32[]{:S(2)}) copy-start(bf16[256,7168]{1,0:T(8,128)(2,1)} %refs_2_.11) | copy-start | bytes 11010052
  100.3 2.3 %copy-start.20 = (f32[2048,128]{1,0:T(8,128)S(1)}, f32[2048,128]{1,0:T(8,128)}, u32[]{:S(2)}) copy-start(f32[2048,128]{1,0:T(8,128)} %copy-done.18) | copy-start | bytes 3145732
  102.6 4.1 %copy-start.15 = (f32[2560,128]{1,0:T(8,128)S(1)}, f32[2560,128]{1,0:T(8,128)}, u32[]{:S(2)}) copy-start(f32[2560,128]{1,0:T(8,128)} %copy-done.14) | copy-start | bytes 3932164
  104.1 17.7 %collective-permute-start.20 = (s16[1040,128]{1,0:T(8,128)(2,1)S(1)}, s16[1040,128]{1,0:T(8,128)(2,1)S(1)}, u32[]{:S(2)}, u32[]{:S(2)}) collective-permute-start(s16[1040,128]{1,0:T(8,128)(2,1)S(1)} %get-tuple-element.96), channel_id=1, source_target_pairs={{0,16},{2,18},{4,20},{6,22},{8,24},{10,26},{12,28},{14,30},{16,0},... | collective-permute-start | bytes 798728 | tf_op jit(solution)/shard_map/ppermute | solution.py:213
  104.5 22.4 %collective-permute-start.22 = (s16[1568,128]{1,0:T(8,128)(2,1)S(1)}, s16[1568,128]{1,0:T(8,128)(2,1)S(1)}, u32[]{:S(2)}, u32[]{:S(2)}) collective-permute-start(s16[1568,128]{1,0:T(8,128)(2,1)S(1)} %get-tuple-element.100), channel_id=1, source_target_pairs={{0,4},{2,6},{4,0},{6,2},{8,12},{10,14},{12,8},{14,10},{16,20},{18,... | collective-permute-start | bytes 1204232 | tf_op jit(solution)/shard_map/ppermute | solution.py:213
  108.2 14.9 %copy-start.25 = (f32[1792,128]{1,0:T(8,128)S(1)}, f32[1792,128]{1,0:T(8,128)}, u32[]{:S(2)}) copy-start(f32[1792,128]{1,0:T(8,128)} %copy-done.24) | copy-start | bytes 2752516
  110.2 14.5 %collective-permute-start.18 = (s16[656,128]{1,0:T(8,128)(2,1)S(1)}, s16[656,128]{1,0:T(8,128)(2,1)S(1)}, u32[]{:S(2)}, u32[]{:S(2)}) collective-permute-start(s16[656,128]{1,0:T(8,128)(2,1)S(1)} %get-tuple-element.94), channel_id=1, source_target_pairs={{0,16},{2,18},{4,20},{6,22},{8,24},{10,26},{12,28},{14,30},{16,0},... | collective-permute-start | bytes 503816 | tf_op jit(solution)/shard_map/ppermute | solution.py:213
  112.3 16.1 %collective-permute-start.25 = (s16[1312,128]{1,0:T(8,128)(2,1)S(1)}, s16[1312,128]{1,0:T(8,128)(2,1)S(1)}, u32[]{:S(2)}, u32[]{:S(2)}) collective-permute-start(s16[1312,128]{1,0:T(8,128)(2,1)S(1)} %get-tuple-element.104), channel_id=1, source_target_pairs={{0,8},{2,10},{4,12},{6,14},{8,0},{10,2},{12,4},{14,6},{16,24},{18,... | collective-permute-start | bytes 1007624 | tf_op jit(solution)/shard_map/ppermute | solution.py:213
  121.9 5.0 %collective-permute-start.15 = (s16[528,128]{1,0:T(8,128)(2,1)S(1)}, s16[528,128]{1,0:T(8,128)(2,1)S(1)}, u32[]{:S(2)}, u32[]{:S(2)}) collective-permute-start(s16[528,128]{1,0:T(8,128)(2,1)S(1)} %get-tuple-element.89), channel_id=1, source_target_pairs={{0,2},{2,0},{4,6},{6,4},{8,10},{10,8},{12,14},{14,12},{16,18},{18,... | collective-permute-start | bytes 405512 | tf_op jit(solution)/shard_map/ppermute | solution.py:213
  124.6 12.6 %collective-permute-start.24 = (s16[912,128]{1,0:T(8,128)(2,1)S(1)}, s16[912,128]{1,0:T(8,128)(2,1)S(1)}, u32[]{:S(2)}, u32[]{:S(2)}) collective-permute-start(s16[912,128]{1,0:T(8,128)(2,1)S(1)} %get-tuple-element.103), channel_id=1, source_target_pairs={{0,16},{2,18},{4,20},{6,22},{8,24},{10,26},{12,28},{14,30},{16,0},... | collective-permute-start | bytes 700424 | tf_op jit(solution)/shard_map/ppermute | solution.py:213
  127.2 10.1 %collective-permute-start.23 = (s16[784,128]{1,0:T(8,128)(2,1)S(1)}, s16[784,128]{1,0:T(8,128)(2,1)S(1)}, u32[]{:S(2)}, u32[]{:S(2)}) collective-permute-start(s16[784,128]{1,0:T(8,128)(2,1)S(1)} %get-tuple-element.102), channel_id=1, source_target_pairs={{0,8},{2,10},{4,12},{6,14},{8,0},{10,2},{12,4},{14,6},{16,24},{18,... | collective-permute-start | bytes 602120 | tf_op jit(solution)/shard_map/ppermute | solution.py:213
  127.3 10.3 %collective-permute-start.21 = (s16[528,128]{1,0:T(8,128)(2,1)S(1)}, s16[528,128]{1,0:T(8,128)(2,1)S(1)}, u32[]{:S(2)}, u32[]{:S(2)}) collective-permute-start(s16[528,128]{1,0:T(8,128)(2,1)S(1)} %get-tuple-element.99), channel_id=1, source_target_pairs={{0,2},{2,0},{4,6},{6,4},{8,10},{10,8},{12,14},{14,12},{16,18},{18,... | collective-permute-start | bytes 405512 | tf_op jit(solution)/shard_map/ppermute | solution.py:213
  128.7 10.3 %collective-permute-start.26 = (s16[656,128]{1,0:T(8,128)(2,1)S(1)}, s16[656,128]{1,0:T(8,128)(2,1)S(1)}, u32[]{:S(2)}, u32[]{:S(2)}) collective-permute-start(s16[656,128]{1,0:T(8,128)(2,1)S(1)} %get-tuple-element.107), channel_id=1, source_target_pairs={{0,16},{2,18},{4,20},{6,22},{8,24},{10,26},{12,28},{14,30},{16,0},... | collective-permute-start | bytes 503816 | tf_op jit(solution)/shard_map/ppermute | solution.py:213
  137.5 6.2 %collective-permute-start.27 = (s16[400,128]{1,0:T(8,128)(2,1)S(1)}, s16[400,128]{1,0:T(8,128)(2,1)S(1)}, u32[]{:S(2)}, u32[]{:S(2)}) collective-permute-start(s16[400,128]{1,0:T(8,128)(2,1)S(1)} %get-tuple-element.108), channel_id=1, source_target_pairs={{0,16},{2,18},{4,20},{6,22},{8,24},{10,26},{12,28},{14,30},{16,0},... | collective-permute-start | bytes 307208 | tf_op jit(solution)/shard_map/ppermute | solution.py:213
  139.1 4.6 %copy-start.29 = (f32[56,64,128]{2,1,0:T(8,128)}, f32[56,64,128]{2,1,0:T(8,128)S(1)}, u32[]{:S(2)}) copy-start(f32[56,64,128]{2,1,0:T(8,128)S(1)} %constant_dynamic-update-slice_fusion.7) | copy-start | bytes 5505028

commit v8 on v7

--- a/solution.py
+++ b/solution.py
@@ -87,7 +87,7 @@
             for mask in masks:
                 piece = (me[0] ^ mask) // 2
                 entry, part = piece // per_block, piece % per_block
-                block = picks[c, entry] ^ me[1]
+                block = picks[begins[0] + c, entry] ^ me[1]
                 starts.append((mask & 1, pl.multiple_of(block * height + part * rows, rows)))
             total = None
             for t, grad in enumerate(grads):
@@ -214,9 +214,9 @@
 
     def fetch(after):
         chunks = messages[len(near_g)]
-        whole, after = lax.optimization_barrier((out_grad, after))
-        piece = whole[:, starts[chunks[0]] * BLOCK : (starts[chunks[-1]] + widths[chunks[-1]]) * BLOCK]
+        piece = out_grad[:, starts[chunks[0]] * BLOCK : (starts[chunks[-1]] + widths[chunks[-1]]) * BLOCK]
         piece = jnp.pad(piece, ((0, PAD), (0, 0)))
+        piece, after = lax.optimization_barrier((piece, after))
         near_g.append(swap(piece, 0))
         return after
 
@@ -275,7 +275,7 @@
             scratch_shapes=[scale(width, n)],
             compiler_params=params(),
             name="multiply",
-        )(place, row_blocks[starts[i] : starts[i] + width], *lefts, *grads, last)
+        )(place, row_blocks, *lefts, *grads, last)
 
     def combine(sources, n, encoded, last):
         width = sum(w for w, *_ in sources)

time: 145 us -> 132 us (0.910)
  local copies, waits for them, and re-layouts: 31.1 us -> 7.21 us
  waiting for transfers between devices: 37.2 us -> 60.5 us
  Pallas kernels: 44.4 us -> 26.1 us
  starting transfers between devices: 31.2 us -> 38 us
    ppermute x25, waiting for transfers between devices: 37.2 us -> 60.5 us  [swap(): return lax.ppermute(sent, 'dp', [(o, o ^ 1 << bit) for o in range(owners)])]
    unnamed x74 -> x23, local copies, waits for them, and re-layouts: 23.2 us -> 0.33 us
    pallas_call x20, Pallas kernels: 18.8 us -> 5.41 us  [combine(): pl.pallas_call(functools.partial(combine_kernel, shapes, rows, n, encoded...]
    ppermute x25, starting transfers between devices: 30.7 us -> 37.4 us  [swap(): return lax.ppermute(sent, 'dp', [(o, o ^ 1 << bit) for o in range(owners)])]
    pallas_call x6, Pallas kernels: 22.6 us -> 18.5 us  [multiply(): pl.pallas_call(functools.partial(multiply_kernel, width, rows, height, or...]
    pad x4, local copies, waits for them, and re-layouts: 3.64 us -> 1.11 us  [fetch(): piece = jnp.pad(piece, ((0, PAD), (0, 0)))]
    slice x12 -> x5, local copies, waits for them, and re-layouts: 0.31 us -> 2.73 us  [fetch(): out_grad[:, starts[chunks[0]] * BLOCK:(starts[chunks[-1]] + widths[chunks...]
  transfers between devices with their start and end apart: 28 -> 28, of which waited for: 8 -> 15; matrix products, arithmetic and copies ran while one was open for 7% -> 2% of each run, Pallas kernels for 29% -> 18%
where the time goes in v8:
time: 132 us
  waiting for transfers between devices  60.5 us (46%)
  starting transfers between devices  38 us (29%)
  Pallas kernels  26.1 us (20%)
  local copies, waits for them, and re-layouts  7.21 us (5%)
    ppermute x25, waiting for transfers between devices, swap(): return lax.ppermute(sent, 'dp', [(o, o ^ 1 << bit) for o in range(owners)])  60.5 us
    ppermute x25, starting transfers between devices, swap(): return lax.ppermute(sent, 'dp', [(o, o ^ 1 << bit) for o in range(owners)])  37.4 us
    pallas_call x6, Pallas kernels, multiply(): pl.pallas_call(functools.partial(multiply_kernel, width, rows, height, or...  18.5 us
    pallas_call x20, Pallas kernels, combine(): pl.pallas_call(functools.partial(combine_kernel, shapes, rows, n, encoded...  5.41 us
    slice x5, local copies, waits for them, and re-layouts, fetch(): out_grad[:, starts[chunks[0]] * BLOCK:(starts[chunks[-1]] + widths[chunks...  2.73 us
  transfers between devices with their start and end apart: 28, of which 15 were waited for; matrix products, arithmetic and copies ran while one was open for 2% of the time, Pallas kernels for 18%

profile of v8, /device:TPU:0, one launch (start us, length us, event | category | flops | bytes accessed | tf_op | source)
XLA Modules:
  0.0 132.3 jit_solution(8633426992471013747)
XLA Ops:
  0.0 2.6 %fusion = (bf16[256,1280]{1,0:T(8,128)(2,1)}, bf16[256,1280]{1,0:T(8,128)(2,1)}) fusion(bf16[256,7168]{1,0:T(8,128)(2,1)} %refs_2_.11), kind=kLoop, calls=%fused_computation.13 | loop fusion | bytes 2621440 | tf_op jit(solution)/shard_map/slice | solution.py:217
  2.7 1.0 pad.16
  3.7 2.2 %prepare.1 = (bf16[1024,256]{1,0:T(8,128)(2,1)S(1)}, bf16[1024,256]{1,0:T(8,128)(2,1)S(1)}) custom-call(s32[2]{0:T(128)S(1)} %pad_add_fusion.me.refs_3_, s32[1,4]{1,0:T(1,128)S(1)} %copy-done.2, bf16[256,2048]{1,0:T(8,128)(2,1)S(1)} %copy-done.1), custom_call_target="tpu_custom_call" | custom-call | tf_op jit(solution)/shard_map/prepare/pallas_call | solution.py:227
  6.0 0.5 collective-permute-start
  6.6 2.9 %collective-permute-start.3 = (bf16[1024,256]{1,0:T(8,128)(2,1)S(1)}, bf16[1024,256]{1,0:T(8,128)(2,1)S(1)}, u32[]{:S(2)}, u32[]{:S(2)}) collective-permute-start(bf16[1024,256]{1,0:T(8,128)(2,1)S(1)} %get-tuple-element.60), channel_id=1, source_target_pairs={{0,2},{2,0},{4,6},{6,4},{8,10},{10,8},{12,14},{14,12},{16,18},{18,... | collective-permute-start | bytes 1572872 | tf_op jit(solution)/shard_map/ppermute | solution.py:213
  9.7 1.2 constant_dynamic-update-slice_fusion.refs_0_
  10.9 1.1 constant_dynamic-update-slice_fusion.2.refs_1_
  12.0 2.9 %multiply.6 = (f32[4096,128]{1,0:T(8,128)S(1)}, s16[4160,128]{1,0:T(8,128)(2,1)S(1)}) custom-call(s32[2]{0:T(128)S(1)} %pad_add_fusion.me.refs_3_, s32[56,8]{1,0:T(8,128)S(1)} %copy.5.picks, bf16[2048,256]{1,0:T(8,128)(2,1)S(1)} %constant_dynamic-update-slice_fusion.refs_0_, bf16[2048,256]{1,0:T(8,128)(2,1)S(1)} %constant_dynamic-update-slice_fusion.2.refs_1_, ...), custom_call_target="tpu_custom_call" | custom-call | tf_op jit(solution)/shard_map/multiply/pallas_call | solution.py:270
  15.0 2.2 %collective-permute-start.2 = (s16[4160,128]{1,0:T(8,128)(2,1)S(1)}, s16[4160,128]{1,0:T(8,128)(2,1)S(1)}, u32[]{:S(2)}, u32[]{:S(2)}) collective-permute-start(s16[4160,128]{1,0:T(8,128)(2,1)S(1)} %get-tuple-element.62), channel_id=1, source_target_pairs={{0,8},{2,10},{4,12},{6,14},{8,0},{10,2},{12,4},{14,6},{16,24},{18,... | collective-permute-start | bytes 3194888 | tf_op jit(solution)/shard_map/ppermute | solution.py:213
  17.1 2.9 %multiply.7 = (f32[4096,128]{1,0:T(8,128)S(1)}, s16[4160,128]{1,0:T(8,128)(2,1)S(1)}) custom-call(s32[2]{0:T(128)S(1)} %pad_add_fusion.me.refs_3_, s32[56,8]{1,0:T(8,128)S(1)} %copy.5.picks, bf16[2048,256]{1,0:T(8,128)(2,1)S(1)} %constant_dynamic-update-slice_fusion.refs_0_, bf16[2048,256]{1,0:T(8,128)(2,1)S(1)} %constant_dynamic-update-slice_fusion.2.refs_1_, ...), custom_call_target="tpu_custom_call" | custom-call | tf_op jit(solution)/shard_map/multiply/pallas_call | solution.py:270
  20.0 2.2 %collective-permute-done.3 = bf16[1024,256]{1,0:T(8,128)(2,1)S(1)} collective-permute-done((bf16[1024,256]{1,0:T(8,128)(2,1)S(1)}, bf16[1024,256]{1,0:T(8,128)(2,1)S(1)}, u32[]{:S(2)}, u32[]{:S(2)}) %collective-permute-start.3) | collective-permute-done | bytes 524320 | tf_op jit(solution)/shard_map/ppermute | solution.py:213
  22.2 2.1 %collective-permute-start.9 = (s16[4160,128]{1,0:T(8,128)(2,1)S(1)}, s16[4160,128]{1,0:T(8,128)(2,1)S(1)}, u32[]{:S(2)}, u32[]{:S(2)}) collective-permute-start(s16[4160,128]{1,0:T(8,128)(2,1)S(1)} %get-tuple-element.74), channel_id=1, source_target_pairs={{0,4},{2,6},{4,0},{6,2},{8,12},{10,14},{12,8},{14,10},{16,20},{18,... | collective-permute-start | bytes 3194888 | tf_op jit(solution)/shard_map/ppermute | solution.py:213
  24.3 1.5 %collective-permute-start.7 = (bf16[264,1280]{1,0:T(8,128)(2,1)S(1)}, bf16[264,1280]{1,0:T(8,128)(2,1)S(1)}, u32[]{:S(2)}, u32[]{:S(2)}) collective-permute-start(bf16[264,1280]{1,0:T(8,128)(2,1)S(1)} %pad.15), channel_id=1, source_target_pairs={{0,2},{2,0},{4,6},{6,4},{8,10},{10,8},{12,14},{14,12},{16,18},{18,... | collective-permute-start | bytes 2027528 | tf_op jit(solution)/shard_map/ppermute | solution.py:213
  25.9 16.6 %collective-permute-done.5.refs_3_ = bf16[264,1792]{1,0:T(8,128)(2,1)S(1)} collective-permute-done((bf16[264,1792]{1,0:T(8,128)(2,1)}, bf16[264,1792]{1,0:T(8,128)(2,1)S(1)}, u32[]{:S(2)}, u32[]{:S(2)}) %collective-permute-start.5) | collective-permute-done | bytes 946208 | tf_op jit(solution)/shard_map/ppermute | solution.py:213
  42.5 4.1 %multiply.8 = (f32[3584,128]{1,0:T(8,128)S(1)}, s16[3648,128]{1,0:T(8,128)(2,1)S(1)}) custom-call(s32[2]{0:T(128)S(1)} %pad_add_fusion.me.refs_3_, s32[56,8]{1,0:T(8,128)S(1)} %copy.5.picks, bf16[2048,256]{1,0:T(8,128)(2,1)S(1)} %constant_dynamic-update-slice_fusion.refs_0_, bf16[2048,256]{1,0:T(8,128)(2,1)S(1)} %constant_dynamic-update-slice_fusion.4.refs_1_, ...), custom_call_target="tpu_custom_call" | custom-call | tf_op jit(solution)/shard_map/multiply/pallas_call | solution.py:270
  46.6 2.2 %collective-permute-start.13 = (s16[3648,128]{1,0:T(8,128)(2,1)S(1)}, s16[3648,128]{1,0:T(8,128)(2,1)S(1)}, u32[]{:S(2)}, u32[]{:S(2)}) collective-permute-start(s16[3648,128]{1,0:T(8,128)(2,1)S(1)} %get-tuple-element.81), channel_id=1, source_target_pairs={{0,8},{2,10},{4,12},{6,14},{8,0},{10,2},{12,4},{14,6},{16,24},{18,... | collective-permute-start | bytes 2801672 | tf_op jit(solution)/shard_map/ppermute | solution.py:213
  48.8 1.5 %collective-permute-start.14 = (bf16[264,1280]{1,0:T(8,128)(2,1)S(1)}, bf16[264,1280]{1,0:T(8,128)(2,1)S(1)}, u32[]{:S(2)}, u32[]{:S(2)}) collective-permute-start(bf16[264,1280]{1,0:T(8,128)(2,1)S(1)} %pad.18), channel_id=1, source_target_pairs={{0,2},{2,0},{4,6},{6,4},{8,10},{10,8},{12,14},{14,12},{16,18},{18,... | collective-permute-start | bytes 2027528 | tf_op jit(solution)/shard_map/ppermute | solution.py:213
  50.4 0.6 combine.20
  50.9 1.6 %collective-permute-start.6 = (s16[2080,128]{1,0:T(8,128)(2,1)S(1)}, s16[2080,128]{1,0:T(8,128)(2,1)S(1)}, u32[]{:S(2)}, u32[]{:S(2)}) collective-permute-start(s16[2080,128]{1,0:T(8,128)(2,1)S(1)} %get-tuple-element.68), channel_id=1, source_target_pairs={{0,4},{2,6},{4,0},{6,2},{8,12},{10,14},{12,8},{14,10},{16,20},{18,... | collective-permute-start | bytes 1597448 | tf_op jit(solution)/shard_map/ppermute | solution.py:213
  52.5 4.4 %collective-permute-done.7.refs_3_ = bf16[264,1280]{1,0:T(8,128)(2,1)S(1)} collective-permute-done((bf16[264,1280]{1,0:T(8,128)(2,1)S(1)}, bf16[264,1280]{1,0:T(8,128)(2,1)S(1)}, u32[]{:S(2)}, u32[]{:S(2)}) %collective-permute-start.7) | collective-permute-done | bytes 675872 | tf_op jit(solution)/shard_map/ppermute | solution.py:213
  57.0 3.2 %multiply.9 = (f32[2560,128]{1,0:T(8,128)S(1)}, s16[2608,128]{1,0:T(8,128)(2,1)S(1)}) custom-call(s32[2]{0:T(128)S(1)} %pad_add_fusion.me.refs_3_, s32[56,8]{1,0:T(8,128)S(1)} %copy.5.picks, bf16[2048,256]{1,0:T(8,128)(2,1)S(1)} %constant_dynamic-update-slice_fusion.refs_0_, bf16[2048,256]{1,0:T(8,128)(2,1)S(1)} %constant_dynamic-update-slice_fusion.4.refs_1_, ...), custom_call_target="tpu_custom_call" | custom-call | tf_op jit(solution)/shard_map/multiply/pallas_call | solution.py:270
  60.2 2.2 %collective-permute-start.12 = (s16[2608,128]{1,0:T(8,128)(2,1)S(1)}, s16[2608,128]{1,0:T(8,128)(2,1)S(1)}, u32[]{:S(2)}, u32[]{:S(2)}) collective-permute-start(s16[2608,128]{1,0:T(8,128)(2,1)S(1)} %get-tuple-element.79), channel_id=1, source_target_pairs={{0,4},{2,6},{4,0},{6,2},{8,12},{10,14},{12,8},{14,10},{16,20},{18,... | collective-permute-start | bytes 2002952 | tf_op jit(solution)/shard_map/ppermute | solution.py:213
  62.3 1.4 %collective-permute-done.6.refs_1_ = s16[2080,128]{1,0:T(8,128)(2,1)S(1)} collective-permute-done((s16[2080,128]{1,0:T(8,128)(2,1)S(1)}, s16[2080,128]{1,0:T(8,128)(2,1)S(1)}, u32[]{:S(2)}, u32[]{:S(2)}) %collective-permute-start.6) | collective-permute-done | bytes 532512 | tf_op jit(solution)/shard_map/ppermute | solution.py:213
  63.7 0.3 combine.21
  64.1 0.6 combine.22
  64.6 0.3 collective-permute-start.10
  64.9 0.1 slice-done.1
  65.1 1.4 %collective-permute-start.11 = (bf16[264,768]{1,0:T(8,128)(2,1)S(1)}, bf16[264,768]{1,0:T(8,128)(2,1)S(1)}, u32[]{:S(2)}, u32[]{:S(2)}) collective-permute-start(bf16[264,768]{1,0:T(8,128)(2,1)S(1)} %pad.17), channel_id=1, source_target_pairs={{0,2},{2,0},{4,6},{6,4},{8,10},{10,8},{12,14},{14,12},{16,18},{18,... | collective-permute-start | bytes 1216520 | tf_op jit(solution)/shard_map/ppermute | solution.py:213
  66.5 4.9 %collective-permute-done.14.refs_3_ = bf16[264,1280]{1,0:T(8,128)(2,1)S(1)} collective-permute-done((bf16[264,1280]{1,0:T(8,128)(2,1)S(1)}, bf16[264,1280]{1,0:T(8,128)(2,1)S(1)}, u32[]{:S(2)}, u32[]{:S(2)}) %collective-permute-start.14) | collective-permute-done | bytes 675872 | tf_op jit(solution)/shard_map/ppermute | solution.py:213
  71.4 3.2 %multiply.10 = (f32[2560,128]{1,0:T(8,128)S(1)}, s16[2608,128]{1,0:T(8,128)(2,1)S(1)}) custom-call(s32[2]{0:T(128)S(1)} %pad_add_fusion.me.refs_3_, s32[56,8]{1,0:T(8,128)S(1)} %copy.5.picks, bf16[2048,256]{1,0:T(8,128)(2,1)S(1)} %constant_dynamic-update-slice_fusion.refs_0_, bf16[2048,256]{1,0:T(8,128)(2,1)S(1)} %constant_dynamic-update-slice_fusion.4.refs_1_, ...), custom_call_target="tpu_custom_call" | custom-call | tf_op jit(solution)/shard_map/multiply/pallas_call | solution.py:270
  74.6 2.2 %collective-permute-start.17 = (s16[2608,128]{1,0:T(8,128)(2,1)S(1)}, s16[2608,128]{1,0:T(8,128)(2,1)S(1)}, u32[]{:S(2)}, u32[]{:S(2)}) collective-permute-start(s16[2608,128]{1,0:T(8,128)(2,1)S(1)} %get-tuple-element.91), channel_id=1, source_target_pairs={{0,4},{2,6},{4,0},{6,2},{8,12},{10,14},{12,8},{14,10},{16,20},{18,... | collective-permute-start | bytes 2002952 | tf_op jit(solution)/shard_map/ppermute | solution.py:213
  76.8 2.6 %collective-permute-start.8 = (s16[1040,128]{1,0:T(8,128)(2,1)S(1)}, s16[1040,128]{1,0:T(8,128)(2,1)S(1)}, u32[]{:S(2)}, u32[]{:S(2)}) collective-permute-start(s16[1040,128]{1,0:T(8,128)(2,1)S(1)} %get-tuple-element.72), channel_id=1, source_target_pairs={{0,16},{2,18},{4,20},{6,22},{8,24},{10,26},{12,28},{14,30},{16,0},... | collective-permute-start | bytes 798728 | tf_op jit(solution)/shard_map/ppermute | solution.py:213
  79.4 0.6 combine.23
  80.0 0.4 combine.24
  80.4 1.7 %collective-permute-start.16 = (s16[1312,128]{1,0:T(8,128)(2,1)S(1)}, s16[1312,128]{1,0:T(8,128)(2,1)S(1)}, u32[]{:S(2)}, u32[]{:S(2)}) collective-permute-start(s16[1312,128]{1,0:T(8,128)(2,1)S(1)} %get-tuple-element.90), channel_id=1, source_target_pairs={{0,8},{2,10},{4,12},{6,14},{8,0},{10,2},{12,4},{14,6},{16,24},{18,... | collective-permute-start | bytes 1007624 | tf_op jit(solution)/shard_map/ppermute | solution.py:213
  82.0 0.5 collective-permute-start.19
  82.6 2.2 %multiply.11 = (f32[1536,128]{1,0:T(8,128)S(1)}, s16[1568,128]{1,0:T(8,128)(2,1)S(1)}) custom-call(s32[2]{0:T(128)S(1)} %pad_add_fusion.me.refs_3_, s32[56,8]{1,0:T(8,128)S(1)} %copy.5.picks, bf16[2048,256]{1,0:T(8,128)(2,1)S(1)} %constant_dynamic-update-slice_fusion.refs_0_, bf16[2048,256]{1,0:T(8,128)(2,1)S(1)} %constant_dynamic-update-slice_fusion.4.refs_1_, ...), custom_call_target="tpu_custom_call" | custom-call | tf_op jit(solution)/shard_map/multiply/pallas_call | solution.py:270
  84.7 0.3 combine.25
  85.1 1.5 %collective-permute-start.20 = (s16[1040,128]{1,0:T(8,128)(2,1)S(1)}, s16[1040,128]{1,0:T(8,128)(2,1)S(1)}, u32[]{:S(2)}, u32[]{:S(2)}) collective-permute-start(s16[1040,128]{1,0:T(8,128)(2,1)S(1)} %get-tuple-element.96), channel_id=1, source_target_pairs={{0,16},{2,18},{4,20},{6,22},{8,24},{10,26},{12,28},{14,30},{16,0},... | collective-permute-start | bytes 798728 | tf_op jit(solution)/shard_map/ppermute | solution.py:213
  86.5 5.2 %collective-permute-done.8.refs_1_ = s16[1040,128]{1,0:T(8,128)(2,1)S(1)} collective-permute-done((s16[1040,128]{1,0:T(8,128)(2,1)S(1)}, s16[1040,128]{1,0:T(8,128)(2,1)S(1)}, u32[]{:S(2)}, u32[]{:S(2)}) %collective-permute-start.8) | collective-permute-done | bytes 266272 | tf_op jit(solution)/shard_map/ppermute | solution.py:213
  91.8 0.2 combine.26
  92.0 0.7 collective-permute-done.17.refs_1_
  92.7 0.4 combine.27
  93.1 4.2 %collective-permute-done.16.refs_1_ = s16[1312,128]{1,0:T(8,128)(2,1)S(1)} collective-permute-done((s16[1312,128]{1,0:T(8,128)(2,1)S(1)}, s16[1312,128]{1,0:T(8,128)(2,1)S(1)}, u32[]{:S(2)}, u32[]{:S(2)}) %collective-permute-start.16) | collective-permute-done | bytes 335904 | tf_op jit(solution)/shard_map/ppermute | solution.py:213
  97.3 0.3 combine.28
  97.7 1.9 %collective-permute-start.25 = (s16[1312,128]{1,0:T(8,128)(2,1)S(1)}, s16[1312,128]{1,0:T(8,128)(2,1)S(1)}, u32[]{:S(2)}, u32[]{:S(2)}) collective-permute-start(s16[1312,128]{1,0:T(8,128)(2,1)S(1)} %get-tuple-element.104), channel_id=1, source_target_pairs={{0,8},{2,10},{4,12},{6,14},{8,0},{10,2},{12,4},{14,6},{16,24},{18,... | collective-permute-start | bytes 1007624 | tf_op jit(solution)/shard_map/ppermute | solution.py:213
  99.6 6.2 %collective-permute-done.20.refs_1_ = s16[1040,128]{1,0:T(8,128)(2,1)S(1)} collective-permute-done((s16[1040,128]{1,0:T(8,128)(2,1)S(1)}, s16[1040,128]{1,0:T(8,128)(2,1)S(1)}, u32[]{:S(2)}, u32[]{:S(2)}) %collective-permute-start.20) | collective-permute-done | bytes 266272 | tf_op jit(solution)/shard_map/ppermute | solution.py:213
  105.8 1.4 %collective-permute-start.15 = (s16[528,128]{1,0:T(8,128)(2,1)S(1)}, s16[528,128]{1,0:T(8,128)(2,1)S(1)}, u32[]{:S(2)}, u32[]{:S(2)}) collective-permute-start(s16[528,128]{1,0:T(8,128)(2,1)S(1)} %get-tuple-element.89), channel_id=1, source_target_pairs={{0,2},{2,0},{4,6},{6,4},{8,10},{10,8},{12,14},{14,12},{16,18},{18,... | collective-permute-start | bytes 405512 | tf_op jit(solution)/shard_map/ppermute | solution.py:213
  107.1 0.2 combine.29
  107.4 0.4 combine.30
  107.8 1.6 %collective-permute-done.18.refs_1_ = s16[656,128]{1,0:T(8,128)(2,1)S(1)} collective-permute-done((s16[656,128]{1,0:T(8,128)(2,1)S(1)}, s16[656,128]{1,0:T(8,128)(2,1)S(1)}, u32[]{:S(2)}, u32[]{:S(2)}) %collective-permute-start.18) | collective-permute-done | bytes 167968 | tf_op jit(solution)/shard_map/ppermute | solution.py:213
  109.6 1.2 collective-permute-done.15.refs_1_
  110.9 0.2 combine.33
  111.1 1.8 %collective-permute-start.23 = (s16[784,128]{1,0:T(8,128)(2,1)S(1)}, s16[784,128]{1,0:T(8,128)(2,1)S(1)}, u32[]{:S(2)}, u32[]{:S(2)}) collective-permute-start(s16[784,128]{1,0:T(8,128)(2,1)S(1)} %get-tuple-element.102), channel_id=1, source_target_pairs={{0,8},{2,10},{4,12},{6,14},{8,0},{10,2},{12,4},{14,6},{16,24},{18,... | collective-permute-start | bytes 602120 | tf_op jit(solution)/shard_map/ppermute | solution.py:213
  112.9 0.8 collective-permute-start.21
  113.7 0.4 collective-permute-done.25.refs_1_
  114.1 0.3 combine.34
  114.3 5.0 %collective-permute-start.26 = (s16[656,128]{1,0:T(8,128)(2,1)S(1)}, s16[656,128]{1,0:T(8,128)(2,1)S(1)}, u32[]{:S(2)}, u32[]{:S(2)}) collective-permute-start(s16[656,128]{1,0:T(8,128)(2,1)S(1)} %get-tuple-element.107), channel_id=1, source_target_pairs={{0,16},{2,18},{4,20},{6,22},{8,24},{10,26},{12,28},{14,30},{16,0},... | collective-permute-start | bytes 503816 | tf_op jit(solution)/shard_map/ppermute | solution.py:213
  119.3 5.9 %collective-permute-done.24.refs_1_ = s16[912,128]{1,0:T(8,128)(2,1)S(1)} collective-permute-done((s16[912,128]{1,0:T(8,128)(2,1)S(1)}, s16[912,128]{1,0:T(8,128)(2,1)S(1)}, u32[]{:S(2)}, u32[]{:S(2)}) %collective-permute-start.24) | collective-permute-done | bytes 233504 | tf_op jit(solution)/shard_map/ppermute | solution.py:213
  125.3 0.1 combine.35.refs_2_
  125.4 0.1 combine.36
  125.8 2.2 %collective-permute-done.26.refs_1_ = s16[656,128]{1,0:T(8,128)(2,1)S(1)} collective-permute-done((s16[656,128]{1,0:T(8,128)(2,1)S(1)}, s16[656,128]{1,0:T(8,128)(2,1)S(1)}, u32[]{:S(2)}, u32[]{:S(2)}) %collective-permute-start.26) | collective-permute-done | bytes 167968 | tf_op jit(solution)/shard_map/ppermute | solution.py:213
  128.1 3.4 %collective-permute-done.27.refs_1_ = s16[400,128]{1,0:T(8,128)(2,1)S(1)} collective-permute-done((s16[400,128]{1,0:T(8,128)(2,1)S(1)}, s16[400,128]{1,0:T(8,128)(2,1)S(1)}, u32[]{:S(2)}, u32[]{:S(2)}) %collective-permute-start.27) | collective-permute-done | bytes 102432 | tf_op jit(solution)/shard_map/ppermute | solution.py:213
  131.6 0.7 constant_dynamic-update-slice_fusion.6
  (56 shorter events, 1.3 us)
Async XLA Ops:
  0.0 2.7 %slice-start = ((bf16[256,7168]{1,0:T(8,128)(2,1)}), bf16[256,1792]{1,0:T(8,128)(2,1)S(1)}, s32[]{:S(2)}) async-start(bf16[256,7168]{1,0:T(8,128)(2,1)} %refs_2_.11), calls=%async_computation | async-start | bytes 1835008 | tf_op jit(solution)/shard_map/slice | solution.py:217
  0.0 3.7 %copy-start.1 = (bf16[256,2048]{1,0:T(8,128)(2,1)S(1)}, bf16[256,2048]{1,0:T(8,128)(2,1)}, u32[]{:S(2)}) copy-start(bf16[256,2048]{1,0:T(8,128)(2,1)} %activations.1) | copy-start | bytes 3145732
  0.0 3.7 %copy-start.2 = (s32[1,4]{1,0:T(1,128)S(1)}, s32[1,4]{1,0:T(1,128)}, u32[]{:S(2)}) copy-start(s32[1,4]{1,0:T(1,128)} %lengths.1) | copy-start | bytes 52
  2.6 3.3 %copy-start.4 = (bf16[256,1280]{1,0:T(8,128)(2,1)S(1)}, bf16[256,1280]{1,0:T(8,128)(2,1)}, u32[]{:S(2)}) copy-start(bf16[256,1280]{1,0:T(8,128)(2,1)} %get-tuple-element.110) | copy-start | bytes 1966084
  2.7 6.8 %copy-start.6 = (s32[56,8]{0,1:T(8,128)S(1)}, s32[56,8]{0,1:T(8,128)}, u32[]{:S(2)}) copy-start(s32[56,8]{0,1:T(8,128)} %param.6) | copy-start | bytes 5380
  6.0 3.7 %collective-permute-start = (bf16[1024,256]{1,0:T(8,128)(2,1)S(1)}, bf16[1024,256]{1,0:T(8,128)(2,1)}, u32[]{:S(2)}, u32[]{:S(2)}) collective-permute-start(bf16[1024,256]{1,0:T(8,128)(2,1)S(1)} %get-tuple-element.59), channel_id=1, source_target_pairs={{0,1},{1,0},{2,3},{3,2},{4,5},{5,4},{6,7},{7,6},{8,9},{9,8},{10,11... | collective-permute-start | bytes 1572872 | tf_op jit(solution)/shard_map/ppermute | solution.py:243
  6.5 4.4 %collective-permute-start.1 = (bf16[1024,256]{1,0:T(8,128)(2,1)S(1)}, bf16[1024,256]{1,0:T(8,128)(2,1)}, u32[]{:S(2)}, u32[]{:S(2)}) collective-permute-start(bf16[1024,256]{1,0:T(8,128)(2,1)S(1)} %get-tuple-element.60), channel_id=1, source_target_pairs={{0,1},{1,0},{2,3},{3,2},{4,5},{5,4},{6,7},{7,6},{8,9},{9,8},{10,11... | collective-permute-start | bytes 1572872 | tf_op jit(solution)/shard_map/ppermute | solution.py:243
  6.6 15.6 %collective-permute-start.3 = (bf16[1024,256]{1,0:T(8,128)(2,1)S(1)}, bf16[1024,256]{1,0:T(8,128)(2,1)S(1)}, u32[]{:S(2)}, u32[]{:S(2)}) collective-permute-start(bf16[1024,256]{1,0:T(8,128)(2,1)S(1)} %get-tuple-element.60), channel_id=1, source_target_pairs={{0,2},{2,0},{4,6},{6,4},{8,10},{10,8},{12,14},{14,12},{16,18},{18,... | collective-permute-start | bytes 1572872 | tf_op jit(solution)/shard_map/ppermute | solution.py:213
  9.5 33.0 %collective-permute-start.5 = (bf16[264,1792]{1,0:T(8,128)(2,1)}, bf16[264,1792]{1,0:T(8,128)(2,1)S(1)}, u32[]{:S(2)}, u32[]{:S(2)}) collective-permute-start(bf16[264,1792]{1,0:T(8,128)(2,1)} %pad.16), channel_id=1, source_target_pairs={{0,2},{2,0},{4,6},{6,4},{8,10},{10,8},{12,14},{14,12},{16,18},{18,... | collective-permute-start | bytes 2838536 | tf_op jit(solution)/shard_map/ppermute | solution.py:213
  9.6 2.4 %copy-start = (bf16[256,7168]{1,0:T(8,128)(2,1)S(1)}, bf16[256,7168]{1,0:T(8,128)(2,1)}, u32[]{:S(2)}) copy-start(bf16[256,7168]{1,0:T(8,128)(2,1)} %refs_2_.11) | copy-start | bytes 11010052
  15.0 35.4 %collective-permute-start.2 = (s16[4160,128]{1,0:T(8,128)(2,1)S(1)}, s16[4160,128]{1,0:T(8,128)(2,1)S(1)}, u32[]{:S(2)}, u32[]{:S(2)}) collective-permute-start(s16[4160,128]{1,0:T(8,128)(2,1)S(1)} %get-tuple-element.62), channel_id=1, source_target_pairs={{0,8},{2,10},{4,12},{6,14},{8,0},{10,2},{12,4},{14,6},{16,24},{18,... | collective-permute-start | bytes 3194888 | tf_op jit(solution)/shard_map/ppermute | solution.py:213
  22.2 3.6 %collective-permute-start.4 = (bf16[1024,256]{1,0:T(8,128)(2,1)S(1)}, bf16[1024,256]{1,0:T(8,128)(2,1)S(1)}, u32[]{:S(2)}, u32[]{:S(2)}) collective-permute-start(bf16[1024,256]{1,0:T(8,128)(2,1)S(1)} %collective-permute-done.3), channel_id=1, source_target_pairs={{0,1},{1,0},{2,3},{3,2},{4,5},{5,4},{6,7},{7,6},{8,9},{9,8},{10,11... | collective-permute-start | bytes 1572872 | tf_op jit(solution)/shard_map/ppermute | solution.py:243
  22.2 41.8 %collective-permute-start.9 = (s16[4160,128]{1,0:T(8,128)(2,1)S(1)}, s16[4160,128]{1,0:T(8,128)(2,1)S(1)}, u32[]{:S(2)}, u32[]{:S(2)}) collective-permute-start(s16[4160,128]{1,0:T(8,128)(2,1)S(1)} %get-tuple-element.74), channel_id=1, source_target_pairs={{0,4},{2,6},{4,0},{6,2},{8,12},{10,14},{12,8},{14,10},{16,20},{18,... | collective-permute-start | bytes 3194888 | tf_op jit(solution)/shard_map/ppermute | solution.py:213
  24.3 32.7 %collective-permute-start.7 = (bf16[264,1280]{1,0:T(8,128)(2,1)S(1)}, bf16[264,1280]{1,0:T(8,128)(2,1)S(1)}, u32[]{:S(2)}, u32[]{:S(2)}) collective-permute-start(bf16[264,1280]{1,0:T(8,128)(2,1)S(1)} %pad.15), channel_id=1, source_target_pairs={{0,2},{2,0},{4,6},{6,4},{8,10},{10,8},{12,14},{14,12},{16,18},{18,... | collective-permute-start | bytes 2027528 | tf_op jit(solution)/shard_map/ppermute | solution.py:213
  25.9 22.9 %copy-start.3 = (bf16[256,1280]{1,0:T(8,128)(2,1)S(1)}, bf16[256,1280]{1,0:T(8,128)(2,1)}, u32[]{:S(2)}) copy-start(bf16[256,1280]{1,0:T(8,128)(2,1)} %get-tuple-element.109) | copy-start | bytes 1966084
  46.6 30.3 %collective-permute-start.13 = (s16[3648,128]{1,0:T(8,128)(2,1)S(1)}, s16[3648,128]{1,0:T(8,128)(2,1)S(1)}, u32[]{:S(2)}, u32[]{:S(2)}) collective-permute-start(s16[3648,128]{1,0:T(8,128)(2,1)S(1)} %get-tuple-element.81), channel_id=1, source_target_pairs={{0,8},{2,10},{4,12},{6,14},{8,0},{10,2},{12,4},{14,6},{16,24},{18,... | collective-permute-start | bytes 2801672 | tf_op jit(solution)/shard_map/ppermute | solution.py:213
  48.8 22.6 %collective-permute-start.14 = (bf16[264,1280]{1,0:T(8,128)(2,1)S(1)}, bf16[264,1280]{1,0:T(8,128)(2,1)S(1)}, u32[]{:S(2)}, u32[]{:S(2)}) collective-permute-start(bf16[264,1280]{1,0:T(8,128)(2,1)S(1)} %pad.18), channel_id=1, source_target_pairs={{0,2},{2,0},{4,6},{6,4},{8,10},{10,8},{12,14},{14,12},{16,18},{18,... | collective-permute-start | bytes 2027528 | tf_op jit(solution)/shard_map/ppermute | solution.py:213
  50.9 12.8 %collective-permute-start.6 = (s16[2080,128]{1,0:T(8,128)(2,1)S(1)}, s16[2080,128]{1,0:T(8,128)(2,1)S(1)}, u32[]{:S(2)}, u32[]{:S(2)}) collective-permute-start(s16[2080,128]{1,0:T(8,128)(2,1)S(1)} %get-tuple-element.68), channel_id=1, source_target_pairs={{0,4},{2,6},{4,0},{6,2},{8,12},{10,14},{12,8},{14,10},{16,20},{18,... | collective-permute-start | bytes 1597448 | tf_op jit(solution)/shard_map/ppermute | solution.py:213
  60.2 19.8 %collective-permute-start.12 = (s16[2608,128]{1,0:T(8,128)(2,1)S(1)}, s16[2608,128]{1,0:T(8,128)(2,1)S(1)}, u32[]{:S(2)}, u32[]{:S(2)}) collective-permute-start(s16[2608,128]{1,0:T(8,128)(2,1)S(1)} %get-tuple-element.79), channel_id=1, source_target_pairs={{0,4},{2,6},{4,0},{6,2},{8,12},{10,14},{12,8},{14,10},{16,20},{18,... | collective-permute-start | bytes 2002952 | tf_op jit(solution)/shard_map/ppermute | solution.py:213
  64.0 1.0 slice-start.1
  64.6 20.1 %collective-permute-start.10 = (s16[2080,128]{1,0:T(8,128)(2,1)S(1)}, s16[2080,128]{1,0:T(8,128)(2,1)S(1)}, u32[]{:S(2)}, u32[]{:S(2)}) collective-permute-start(s16[2080,128]{1,0:T(8,128)(2,1)S(1)} %get-tuple-element.76), channel_id=1, source_target_pairs={{0,8},{2,10},{4,12},{6,14},{8,0},{10,2},{12,4},{14,6},{16,24},{18,... | collective-permute-start | bytes 1597448 | tf_op jit(solution)/shard_map/ppermute | solution.py:213
  65.1 17.0 %collective-permute-start.11 = (bf16[264,768]{1,0:T(8,128)(2,1)S(1)}, bf16[264,768]{1,0:T(8,128)(2,1)S(1)}, u32[]{:S(2)}, u32[]{:S(2)}) collective-permute-start(bf16[264,768]{1,0:T(8,128)(2,1)S(1)} %pad.17), channel_id=1, source_target_pairs={{0,2},{2,0},{4,6},{6,4},{8,10},{10,8},{12,14},{14,12},{16,18},{18,... | collective-permute-start | bytes 1216520 | tf_op jit(solution)/shard_map/ppermute | solution.py:213
  74.6 18.1 %collective-permute-start.17 = (s16[2608,128]{1,0:T(8,128)(2,1)S(1)}, s16[2608,128]{1,0:T(8,128)(2,1)S(1)}, u32[]{:S(2)}, u32[]{:S(2)}) collective-permute-start(s16[2608,128]{1,0:T(8,128)(2,1)S(1)} %get-tuple-element.91), channel_id=1, source_target_pairs={{0,4},{2,6},{4,0},{6,2},{8,12},{10,14},{12,8},{14,10},{16,20},{18,... | collective-permute-start | bytes 2002952 | tf_op jit(solution)/shard_map/ppermute | solution.py:213
  76.8 15.0 %collective-permute-start.8 = (s16[1040,128]{1,0:T(8,128)(2,1)S(1)}, s16[1040,128]{1,0:T(8,128)(2,1)S(1)}, u32[]{:S(2)}, u32[]{:S(2)}) collective-permute-start(s16[1040,128]{1,0:T(8,128)(2,1)S(1)} %get-tuple-element.72), channel_id=1, source_target_pairs={{0,16},{2,18},{4,20},{6,22},{8,24},{10,26},{12,28},{14,30},{16,0},... | collective-permute-start | bytes 798728 | tf_op jit(solution)/shard_map/ppermute | solution.py:213
  80.4 16.9 %collective-permute-start.16 = (s16[1312,128]{1,0:T(8,128)(2,1)S(1)}, s16[1312,128]{1,0:T(8,128)(2,1)S(1)}, u32[]{:S(2)}, u32[]{:S(2)}) collective-permute-start(s16[1312,128]{1,0:T(8,128)(2,1)S(1)} %get-tuple-element.90), channel_id=1, source_target_pairs={{0,8},{2,10},{4,12},{6,14},{8,0},{10,2},{12,4},{14,6},{16,24},{18,... | collective-permute-start | bytes 1007624 | tf_op jit(solution)/shard_map/ppermute | solution.py:213
  82.0 25.3 %collective-permute-start.19 = (s16[1824,128]{1,0:T(8,128)(2,1)S(1)}, s16[1824,128]{1,0:T(8,128)(2,1)S(1)}, u32[]{:S(2)}, u32[]{:S(2)}) collective-permute-start(s16[1824,128]{1,0:T(8,128)(2,1)S(1)} %get-tuple-element.95), channel_id=1, source_target_pairs={{0,4},{2,6},{4,0},{6,2},{8,12},{10,14},{12,8},{14,10},{16,20},{18,... | collective-permute-start | bytes 1400840 | tf_op jit(solution)/shard_map/ppermute | solution.py:213
  85.1 20.7 %collective-permute-start.20 = (s16[1040,128]{1,0:T(8,128)(2,1)S(1)}, s16[1040,128]{1,0:T(8,128)(2,1)S(1)}, u32[]{:S(2)}, u32[]{:S(2)}) collective-permute-start(s16[1040,128]{1,0:T(8,128)(2,1)S(1)} %get-tuple-element.96), channel_id=1, source_target_pairs={{0,16},{2,18},{4,20},{6,22},{8,24},{10,26},{12,28},{14,30},{16,0},... | collective-permute-start | bytes 798728 | tf_op jit(solution)/shard_map/ppermute | solution.py:213
  91.8 19.1 %collective-permute-start.22 = (s16[1568,128]{1,0:T(8,128)(2,1)S(1)}, s16[1568,128]{1,0:T(8,128)(2,1)S(1)}, u32[]{:S(2)}, u32[]{:S(2)}) collective-permute-start(s16[1568,128]{1,0:T(8,128)(2,1)S(1)} %get-tuple-element.100), channel_id=1, source_target_pairs={{0,4},{2,6},{4,0},{6,2},{8,12},{10,14},{12,8},{14,10},{16,20},{18,... | collective-permute-start | bytes 1204232 | tf_op jit(solution)/shard_map/ppermute | solution.py:213
  97.6 11.9 %collective-permute-start.18 = (s16[656,128]{1,0:T(8,128)(2,1)S(1)}, s16[656,128]{1,0:T(8,128)(2,1)S(1)}, u32[]{:S(2)}, u32[]{:S(2)}) collective-permute-start(s16[656,128]{1,0:T(8,128)(2,1)S(1)} %get-tuple-element.94), channel_id=1, source_target_pairs={{0,16},{2,18},{4,20},{6,22},{8,24},{10,26},{12,28},{14,30},{16,0},... | collective-permute-start | bytes 503816 | tf_op jit(solution)/shard_map/ppermute | solution.py:213
  97.7 16.4 %collective-permute-start.25 = (s16[1312,128]{1,0:T(8,128)(2,1)S(1)}, s16[1312,128]{1,0:T(8,128)(2,1)S(1)}, u32[]{:S(2)}, u32[]{:S(2)}) collective-permute-start(s16[1312,128]{1,0:T(8,128)(2,1)S(1)} %get-tuple-element.104), channel_id=1, source_target_pairs={{0,8},{2,10},{4,12},{6,14},{8,0},{10,2},{12,4},{14,6},{16,24},{18,... | collective-permute-start | bytes 1007624 | tf_op jit(solution)/shard_map/ppermute | solution.py:213
  105.8 5.0 %collective-permute-start.15 = (s16[528,128]{1,0:T(8,128)(2,1)S(1)}, s16[528,128]{1,0:T(8,128)(2,1)S(1)}, u32[]{:S(2)}, u32[]{:S(2)}) collective-permute-start(s16[528,128]{1,0:T(8,128)(2,1)S(1)} %get-tuple-element.89), channel_id=1, source_target_pairs={{0,2},{2,0},{4,6},{6,4},{8,10},{10,8},{12,14},{14,12},{16,18},{18,... | collective-permute-start | bytes 405512 | tf_op jit(solution)/shard_map/ppermute | solution.py:213
  107.8 17.5 %collective-permute-start.24 = (s16[912,128]{1,0:T(8,128)(2,1)S(1)}, s16[912,128]{1,0:T(8,128)(2,1)S(1)}, u32[]{:S(2)}, u32[]{:S(2)}) collective-permute-start(s16[912,128]{1,0:T(8,128)(2,1)S(1)} %get-tuple-element.103), channel_id=1, source_target_pairs={{0,16},{2,18},{4,20},{6,22},{8,24},{10,26},{12,28},{14,30},{16,0},... | collective-permute-start | bytes 700424 | tf_op jit(solution)/shard_map/ppermute | solution.py:213
  111.1 14.3 %collective-permute-start.23 = (s16[784,128]{1,0:T(8,128)(2,1)S(1)}, s16[784,128]{1,0:T(8,128)(2,1)S(1)}, u32[]{:S(2)}, u32[]{:S(2)}) collective-permute-start(s16[784,128]{1,0:T(8,128)(2,1)S(1)} %get-tuple-element.102), channel_id=1, source_target_pairs={{0,8},{2,10},{4,12},{6,14},{8,0},{10,2},{12,4},{14,6},{16,24},{18,... | collective-permute-start | bytes 602120 | tf_op jit(solution)/shard_map/ppermute | solution.py:213
  112.9 12.7 %collective-permute-start.21 = (s16[528,128]{1,0:T(8,128)(2,1)S(1)}, s16[528,128]{1,0:T(8,128)(2,1)S(1)}, u32[]{:S(2)}, u32[]{:S(2)}) collective-permute-start(s16[528,128]{1,0:T(8,128)(2,1)S(1)} %get-tuple-element.99), channel_id=1, source_target_pairs={{0,2},{2,0},{4,6},{6,4},{8,10},{10,8},{12,14},{14,12},{16,18},{18,... | collective-permute-start | bytes 405512 | tf_op jit(solution)/shard_map/ppermute | solution.py:213
  114.3 13.7 %collective-permute-start.26 = (s16[656,128]{1,0:T(8,128)(2,1)S(1)}, s16[656,128]{1,0:T(8,128)(2,1)S(1)}, u32[]{:S(2)}, u32[]{:S(2)}) collective-permute-start(s16[656,128]{1,0:T(8,128)(2,1)S(1)} %get-tuple-element.107), channel_id=1, source_target_pairs={{0,16},{2,18},{4,20},{6,22},{8,24},{10,26},{12,28},{14,30},{16,0},... | collective-permute-start | bytes 503816 | tf_op jit(solution)/shard_map/ppermute | solution.py:213
  125.5 6.0 %collective-permute-start.27 = (s16[400,128]{1,0:T(8,128)(2,1)S(1)}, s16[400,128]{1,0:T(8,128)(2,1)S(1)}, u32[]{:S(2)}, u32[]{:S(2)}) collective-permute-start(s16[400,128]{1,0:T(8,128)(2,1)S(1)} %get-tuple-element.108), channel_id=1, source_target_pairs={{0,16},{2,18},{4,20},{6,22},{8,24},{10,26},{12,28},{14,30},{16,0},... | collective-permute-start | bytes 307208 | tf_op jit(solution)/shard_map/ppermute | solution.py:213
  128.1 3.4 %copy-start.5 = (f32[56,64,128]{2,1,0:T(8,128)}, f32[56,64,128]{2,1,0:T(8,128)S(1)}, u32[]{:S(2)}) copy-start(f32[56,64,128]{2,1,0:T(8,128)S(1)} %constant_dynamic-update-slice_fusion.7) | copy-start | bytes 5505028

commit v9 on v6

--- a/solution.py
+++ b/solution.py
@@ -153,8 +153,8 @@
 def plan_of(columns, depth):
     if depth != 4 or columns % 56 != 0:
         return [columns], [list(range(1, depth))], [[0]], [("multiply", 0)] + [("step", 0)] * (depth - 1)
-    widths = [8, 8, 14, 10, 10, 6]
-    paths = [[2, 1, 3, 0], [1, 2, 3, 0], [2, 1, 3], [1, 2, 3], [1, 2, 3], [1, 2, 3]]
+    widths = [8, 8, 10, 10, 10, 10]
+    paths = [[1, 2, 3, 0], [2, 1, 3, 0], [1, 2, 3], [1, 2, 3], [2, 1, 3], [1, 2, 3]]
     messages = [[2], [3], [4], [5]]
     work = [
         ("multiply", 0),
@@ -162,25 +162,25 @@
         ("multiply", 2),
         ("step", 0),
         ("multiply", 3),
+        ("step", 1),
+        ("step", 2),
         ("step", 0),
-        ("step", 1),
         ("multiply", 4),
-        ("step", 2),
-        ("step", 3),
-        ("multiply", 5),
         ("step", 1),
         ("step", 0),
-        ("step", 4),
+        ("step", 2),
+        ("multiply", 5),
         ("step", 3),
-        ("step", 1),
-        ("step", 2),
-        ("step", 3),
-        ("step", 0),
-        ("step", 5),
         ("step", 4),
         ("step", 2),
         ("step", 5),
+        ("step", 3),
         ("step", 1),
+        ("step", 4),
+        ("step", 1),
+        ("step", 3),
+        ("step", 5),
+        ("step", 0),
         ("step", 4),
         ("step", 5),
     ]

time: 130 us -> 134 us (1.031); the launches traced: 130 us -> 132 us
  starting transfers between devices: 41.4 us -> 46.9 us
  waiting for transfers between devices: 54.7 us -> 49.7 us
  local copies, waits for them, and re-layouts: 7.29 us -> 8.71 us
    ppermute x25, starting transfers between devices: 40.8 us -> 46.3 us  [swap(): return lax.ppermute(sent, 'dp', [(o, o ^ 1 << bit) for o in range(owners)])]
    ppermute x25, waiting for transfers between devices: 54.7 us -> 49.7 us  [swap(): return lax.ppermute(sent, 'dp', [(o, o ^ 1 << bit) for o in range(owners)])]
    slice x5 -> x1, local copies, waits for them, and re-layouts: 2.62 us -> 2.73 us  [fetch(): out_grad[:, starts[chunks[0]] * BLOCK:(starts[chunks[-1]] + widths[chunks...]
  transfers between devices with their start and end apart: 28 -> 28, of which waited for: 14 -> 13; matrix products, arithmetic and copies ran while one was open for 2% -> 3% of each run, Pallas kernels for 18% -> 18%
where the time goes in v9:
time: 134 us; the launch traced here: 132 us
  waiting for transfers between devices  49.7 us (37%)
  starting transfers between devices  46.9 us (35%)
  Pallas kernels  26.2 us (20%)
  local copies, waits for them, and re-layouts  8.71 us (7%)
    ppermute x25, waiting for transfers between devices, swap(): return lax.ppermute(sent, 'dp', [(o, o ^ 1 << bit) for o in range(owners)])  49.7 us
    ppermute x25, starting transfers between devices, swap(): return lax.ppermute(sent, 'dp', [(o, o ^ 1 << bit) for o in range(owners)])  46.3 us
    pallas_call x6, Pallas kernels, multiply(): pl.pallas_call(functools.partial(multiply_kernel, width, rows, height, or...  18.6 us
    pallas_call x20, Pallas kernels, combine(): pl.pallas_call(functools.partial(combine_kernel, shapes, rows, n, encoded...  5.37 us
    slice x1, local copies, waits for them, and re-layouts, fetch(): out_grad[:, starts[chunks[0]] * BLOCK:(starts[chunks[-1]] + widths[chunks...  2.73 us
  transfers between devices with their start and end apart: 28, of which 13 were waited for; matrix products, arithmetic and copies ran while one was open for 3% of the time, Pallas kernels for 18%

profile of v9, /device:TPU:0, one launch (start us, length us, event | category | flops | bytes accessed | tf_op | source)
XLA Modules:
  0.0 132.0 jit_solution(2278266913148871301)
XLA Ops:
  0.0 2.7 %fusion = (bf16[256,1280]{1,0:T(8,128)(2,1)S(1)}, bf16[256,1280]{1,0:T(8,128)(2,1)S(1)}, bf16[256,1280]{1,0:T(8,128)(2,1)S(1)}, bf16[256,1280]{1,0:T(8,128)(2,1)}) fusion(bf16[256,7168]{1,0:T(8,128)(2,1)} %refs_2_.11), kind=kLoop, calls=%fused_computation.13 | loop fusion | bytes 5242880 | tf_op jit(solution)/shard_map/slice | solution.py:217
  2.8 0.9 pad.14
  3.7 0.5 copy-done.1
  4.2 2.2 %prepare.1 = (bf16[1024,256]{1,0:T(8,128)(2,1)S(1)}, bf16[1024,256]{1,0:T(8,128)(2,1)S(1)}) custom-call(s32[2]{0:T(128)S(1)} %pad_add_fusion.me.refs_3_, s32[1,4]{1,0:T(1,128)S(1)} %copy-done.2, bf16[256,2048]{1,0:T(8,128)(2,1)S(1)} %copy-done.1), custom_call_target="tpu_custom_call" | custom-call | tf_op jit(solution)/shard_map/prepare/pallas_call | solution.py:227
  6.5 0.5 collective-permute-start
  7.1 2.9 %collective-permute-start.3 = (bf16[1024,256]{1,0:T(8,128)(2,1)S(1)}, bf16[1024,256]{1,0:T(8,128)(2,1)}, u32[]{:S(2)}, u32[]{:S(2)}) collective-permute-start(bf16[1024,256]{1,0:T(8,128)(2,1)S(1)} %get-tuple-element.58), channel_id=1, source_target_pairs={{0,2},{2,0},{4,6},{6,4},{8,10},{10,8},{12,14},{14,12},{16,18},{18,... | collective-permute-start | bytes 1572872 | tf_op jit(solution)/shard_map/ppermute | solution.py:213
  10.2 1.2 constant_dynamic-update-slice_fusion.refs_0_
  11.4 1.1 constant_dynamic-update-slice_fusion.2.refs_1_
  12.5 2.9 %multiply.6 = (f32[4096,128]{1,0:T(8,128)S(1)}, s16[4160,128]{1,0:T(8,128)(2,1)S(1)}) custom-call(s32[2]{0:T(128)S(1)} %pad_add_fusion.me.refs_3_, s32[56,8]{1,0:T(8,128)S(1)} %copy.5.picks, bf16[2048,256]{1,0:T(8,128)(2,1)S(1)} %constant_dynamic-update-slice_fusion.refs_0_, bf16[2048,256]{1,0:T(8,128)(2,1)S(1)} %constant_dynamic-update-slice_fusion.2.refs_1_, ...), custom_call_target="tpu_custom_call" | custom-call | tf_op jit(solution)/shard_map/multiply/pallas_call | solution.py:269
  15.4 1.6 %collective-permute-start.2 = (s16[4160,128]{1,0:T(8,128)(2,1)S(1)}, s16[4160,128]{1,0:T(8,128)(2,1)S(1)}, u32[]{:S(2)}, u32[]{:S(2)}) collective-permute-start(s16[4160,128]{1,0:T(8,128)(2,1)S(1)} %get-tuple-element.60), channel_id=1, source_target_pairs={{0,4},{2,6},{4,0},{6,2},{8,12},{10,14},{12,8},{14,10},{16,20},{18,... | collective-permute-start | bytes 3194888 | tf_op jit(solution)/shard_map/ppermute | solution.py:213
  17.0 1.4 %collective-permute-start.5 = (bf16[264,1280]{1,0:T(8,128)(2,1)S(1)}, bf16[264,1280]{1,0:T(8,128)(2,1)S(1)}, u32[]{:S(2)}, u32[]{:S(2)}) collective-permute-start(bf16[264,1280]{1,0:T(8,128)(2,1)S(1)} %copy-done.4), channel_id=1, source_target_pairs={{0,2},{2,0},{4,6},{6,4},{8,10},{10,8},{12,14},{14,12},{16,18},{18,... | collective-permute-start | bytes 2027528 | tf_op jit(solution)/shard_map/ppermute | solution.py:213
  18.4 4.4 %collective-permute-done.3 = bf16[1024,256]{1,0:T(8,128)(2,1)} collective-permute-done((bf16[1024,256]{1,0:T(8,128)(2,1)S(1)}, bf16[1024,256]{1,0:T(8,128)(2,1)}, u32[]{:S(2)}, u32[]{:S(2)}) %collective-permute-start.3) | collective-permute-done | bytes 524320 | tf_op jit(solution)/shard_map/ppermute | solution.py:213
  22.8 2.9 %multiply.7 = (f32[4096,128]{1,0:T(8,128)S(1)}, s16[4160,128]{1,0:T(8,128)(2,1)S(1)}) custom-call(s32[2]{0:T(128)S(1)} %pad_add_fusion.me.refs_3_, s32[56,8]{1,0:T(8,128)S(1)} %copy.5.picks, bf16[2048,256]{1,0:T(8,128)(2,1)S(1)} %constant_dynamic-update-slice_fusion.refs_0_, bf16[2048,256]{1,0:T(8,128)(2,1)S(1)} %constant_dynamic-update-slice_fusion.2.refs_1_, ...), custom_call_target="tpu_custom_call" | custom-call | tf_op jit(solution)/shard_map/multiply/pallas_call | solution.py:269
  25.7 2.2 %collective-permute-start.8 = (s16[4160,128]{1,0:T(8,128)(2,1)S(1)}, s16[4160,128]{1,0:T(8,128)(2,1)S(1)}, u32[]{:S(2)}, u32[]{:S(2)}) collective-permute-start(s16[4160,128]{1,0:T(8,128)(2,1)S(1)} %get-tuple-element.68), channel_id=1, source_target_pairs={{0,8},{2,10},{4,12},{6,14},{8,0},{10,2},{12,4},{14,6},{16,24},{18,... | collective-permute-start | bytes 3194888 | tf_op jit(solution)/shard_map/ppermute | solution.py:213
  28.0 1.5 %collective-permute-start.9 = (bf16[264,1280]{1,0:T(8,128)(2,1)S(1)}, bf16[264,1280]{1,0:T(8,128)(2,1)S(1)}, u32[]{:S(2)}, u32[]{:S(2)}) collective-permute-start(bf16[264,1280]{1,0:T(8,128)(2,1)S(1)} %pad.13), channel_id=1, source_target_pairs={{0,2},{2,0},{4,6},{6,4},{8,10},{10,8},{12,14},{14,12},{16,18},{18,... | collective-permute-start | bytes 2027528 | tf_op jit(solution)/shard_map/ppermute | solution.py:213
  29.4 1.1 constant_dynamic-update-slice_fusion.5
  30.6 6.6 %collective-permute-done.5.refs_3_ = bf16[264,1280]{1,0:T(8,128)(2,1)S(1)} collective-permute-done((bf16[264,1280]{1,0:T(8,128)(2,1)S(1)}, bf16[264,1280]{1,0:T(8,128)(2,1)S(1)}, u32[]{:S(2)}, u32[]{:S(2)}) %collective-permute-start.5) | collective-permute-done | bytes 675872 | tf_op jit(solution)/shard_map/ppermute | solution.py:213
  37.2 3.2 %multiply.8 = (f32[2560,128]{1,0:T(8,128)S(1)}, s16[2608,128]{1,0:T(8,128)(2,1)S(1)}) custom-call(s32[2]{0:T(128)S(1)} %pad_add_fusion.me.refs_3_, s32[56,8]{1,0:T(8,128)S(1)} %copy.5.picks, bf16[2048,256]{1,0:T(8,128)(2,1)S(1)} %constant_dynamic-update-slice_fusion.refs_0_, bf16[2048,256]{1,0:T(8,128)(2,1)S(1)} %constant_dynamic-update-slice_fusion.4.refs_1_, ...), custom_call_target="tpu_custom_call" | custom-call | tf_op jit(solution)/shard_map/multiply/pallas_call | solution.py:269
  40.4 2.2 %collective-permute-start.7 = (s16[2608,128]{1,0:T(8,128)(2,1)S(1)}, s16[2608,128]{1,0:T(8,128)(2,1)S(1)}, u32[]{:S(2)}, u32[]{:S(2)}) collective-permute-start(s16[2608,128]{1,0:T(8,128)(2,1)S(1)} %get-tuple-element.67), channel_id=1, source_target_pairs={{0,4},{2,6},{4,0},{6,2},{8,12},{10,14},{12,8},{14,10},{16,20},{18,... | collective-permute-start | bytes 2002952 | tf_op jit(solution)/shard_map/ppermute | solution.py:213
  42.6 1.5 %collective-permute-start.12 = (bf16[264,1280]{1,0:T(8,128)(2,1)S(1)}, bf16[264,1280]{1,0:T(8,128)(2,1)S(1)}, u32[]{:S(2)}, u32[]{:S(2)}) collective-permute-start(bf16[264,1280]{1,0:T(8,128)(2,1)S(1)} %pad.15), channel_id=1, source_target_pairs={{0,2},{2,0},{4,6},{6,4},{8,10},{10,8},{12,14},{14,12},{16,18},{18,... | collective-permute-start | bytes 2027528 | tf_op jit(solution)/shard_map/ppermute | solution.py:213
  44.2 0.6 combine.20
  44.7 1.6 %collective-permute-start.6 = (s16[2080,128]{1,0:T(8,128)(2,1)S(1)}, s16[2080,128]{1,0:T(8,128)(2,1)S(1)}, u32[]{:S(2)}, u32[]{:S(2)}) collective-permute-start(s16[2080,128]{1,0:T(8,128)(2,1)S(1)} %get-tuple-element.65), channel_id=1, source_target_pairs={{0,8},{2,10},{4,12},{6,14},{8,0},{10,2},{12,4},{14,6},{16,24},{18,... | collective-permute-start | bytes 1597448 | tf_op jit(solution)/shard_map/ppermute | solution.py:213
  46.4 5.3 %collective-permute-done.9.refs_3_ = bf16[264,1280]{1,0:T(8,128)(2,1)S(1)} collective-permute-done((bf16[264,1280]{1,0:T(8,128)(2,1)S(1)}, bf16[264,1280]{1,0:T(8,128)(2,1)S(1)}, u32[]{:S(2)}, u32[]{:S(2)}) %collective-permute-start.9) | collective-permute-done | bytes 675872 | tf_op jit(solution)/shard_map/ppermute | solution.py:213
  51.7 3.2 %multiply.9 = (f32[2560,128]{1,0:T(8,128)S(1)}, s16[2608,128]{1,0:T(8,128)(2,1)S(1)}) custom-call(s32[2]{0:T(128)S(1)} %pad_add_fusion.me.refs_3_, s32[56,8]{1,0:T(8,128)S(1)} %copy.5.picks, bf16[2048,256]{1,0:T(8,128)(2,1)S(1)} %constant_dynamic-update-slice_fusion.refs_0_, bf16[2048,256]{1,0:T(8,128)(2,1)S(1)} %constant_dynamic-update-slice_fusion.4.refs_1_, ...), custom_call_target="tpu_custom_call" | custom-call | tf_op jit(solution)/shard_map/multiply/pallas_call | solution.py:269
  54.9 2.1 %collective-permute-start.14 = (bf16[264,1280]{1,0:T(8,128)(2,1)S(1)}, bf16[264,1280]{1,0:T(8,128)(2,1)S(1)}, u32[]{:S(2)}, u32[]{:S(2)}) collective-permute-start(bf16[264,1280]{1,0:T(8,128)(2,1)S(1)} %pad.16), channel_id=1, source_target_pairs={{0,2},{2,0},{4,6},{6,4},{8,10},{10,8},{12,14},{14,12},{16,18},{18,... | collective-permute-start | bytes 2027528 | tf_op jit(solution)/shard_map/ppermute | solution.py:213
  57.0 0.6 combine.21
  57.6 1.6 %collective-permute-start.11 = (s16[2080,128]{1,0:T(8,128)(2,1)S(1)}, s16[2080,128]{1,0:T(8,128)(2,1)S(1)}, u32[]{:S(2)}, u32[]{:S(2)}) collective-permute-start(s16[2080,128]{1,0:T(8,128)(2,1)S(1)} %get-tuple-element.75), channel_id=1, source_target_pairs={{0,4},{2,6},{4,0},{6,2},{8,12},{10,14},{12,8},{14,10},{16,20},{18,... | collective-permute-start | bytes 1597448 | tf_op jit(solution)/shard_map/ppermute | solution.py:213
  59.2 0.4 combine.22
  59.6 1.6 %collective-permute-start.15 = (s16[1312,128]{1,0:T(8,128)(2,1)S(1)}, s16[1312,128]{1,0:T(8,128)(2,1)S(1)}, u32[]{:S(2)}, u32[]{:S(2)}) collective-permute-start(s16[1312,128]{1,0:T(8,128)(2,1)S(1)} %get-tuple-element.82), channel_id=1, source_target_pairs={{0,8},{2,10},{4,12},{6,14},{8,0},{10,2},{12,4},{14,6},{16,24},{18,... | collective-permute-start | bytes 1007624 | tf_op jit(solution)/shard_map/ppermute | solution.py:213
  61.2 2.5 %collective-permute-done.6.refs_1_ = s16[2080,128]{1,0:T(8,128)(2,1)S(1)} collective-permute-done((s16[2080,128]{1,0:T(8,128)(2,1)S(1)}, s16[2080,128]{1,0:T(8,128)(2,1)S(1)}, u32[]{:S(2)}, u32[]{:S(2)}) %collective-permute-start.6) | collective-permute-done | bytes 532512 | tf_op jit(solution)/shard_map/ppermute | solution.py:213
  63.7 0.3 combine.23
  64.1 3.0 %collective-permute-start.10 = (s16[1040,128]{1,0:T(8,128)(2,1)S(1)}, s16[1040,128]{1,0:T(8,128)(2,1)S(1)}, u32[]{:S(2)}, u32[]{:S(2)}) collective-permute-start(s16[1040,128]{1,0:T(8,128)(2,1)S(1)} %get-tuple-element.74), channel_id=1, source_target_pairs={{0,16},{2,18},{4,20},{6,22},{8,24},{10,26},{12,28},{14,30},{16,0},... | collective-permute-start | bytes 798728 | tf_op jit(solution)/shard_map/ppermute | solution.py:213
  67.1 1.5 %collective-permute-start.19 = (s16[2608,128]{1,0:T(8,128)(2,1)S(1)}, s16[2608,128]{1,0:T(8,128)(2,1)S(1)}, u32[]{:S(2)}, u32[]{:S(2)}) collective-permute-start(s16[2608,128]{1,0:T(8,128)(2,1)S(1)} %get-tuple-element.89), channel_id=1, source_target_pairs={{0,4},{2,6},{4,0},{6,2},{8,12},{10,14},{12,8},{14,10},{16,20},{18,... | collective-permute-start | bytes 2002952 | tf_op jit(solution)/shard_map/ppermute | solution.py:213
  68.6 3.2 %multiply.10 = (f32[2560,128]{1,0:T(8,128)S(1)}, s16[2608,128]{1,0:T(8,128)(2,1)S(1)}) custom-call(s32[2]{0:T(128)S(1)} %pad_add_fusion.me.refs_3_, s32[56,8]{1,0:T(8,128)S(1)} %copy.5.picks, bf16[2048,256]{1,0:T(8,128)(2,1)S(1)} %constant_dynamic-update-slice_fusion.refs_0_, bf16[2048,256]{1,0:T(8,128)(2,1)S(1)} %constant_dynamic-update-slice_fusion.4.refs_1_, ...), custom_call_target="tpu_custom_call" | custom-call | tf_op jit(solution)/shard_map/multiply/pallas_call | solution.py:269
  71.8 1.6 %collective-permute-start.18 = (s16[2608,128]{1,0:T(8,128)(2,1)S(1)}, s16[2608,128]{1,0:T(8,128)(2,1)S(1)}, u32[]{:S(2)}, u32[]{:S(2)}) collective-permute-start(s16[2608,128]{1,0:T(8,128)(2,1)S(1)} %get-tuple-element.87), channel_id=1, source_target_pairs={{0,8},{2,10},{4,12},{6,14},{8,0},{10,2},{12,4},{14,6},{16,24},{18,... | collective-permute-start | bytes 2002952 | tf_op jit(solution)/shard_map/ppermute | solution.py:213
  73.5 0.3 combine.24
  73.8 4.8 %collective-permute-done.10.refs_1_ = s16[1040,128]{1,0:T(8,128)(2,1)S(1)} collective-permute-done((s16[1040,128]{1,0:T(8,128)(2,1)S(1)}, s16[1040,128]{1,0:T(8,128)(2,1)S(1)}, u32[]{:S(2)}, u32[]{:S(2)}) %collective-permute-start.10) | collective-permute-done | bytes 266272 | tf_op jit(solution)/shard_map/ppermute | solution.py:213
  78.8 0.3 combine.26
  79.1 1.0 collective-permute-done.14.refs_3_
  80.1 3.2 %multiply.11 = (f32[2560,128]{1,0:T(8,128)S(1)}, s16[2608,128]{1,0:T(8,128)(2,1)S(1)}) custom-call(s32[2]{0:T(128)S(1)} %pad_add_fusion.me.refs_3_, s32[56,8]{1,0:T(8,128)S(1)} %copy.5.picks, bf16[2048,256]{1,0:T(8,128)(2,1)S(1)} %constant_dynamic-update-slice_fusion.refs_0_, bf16[2048,256]{1,0:T(8,128)(2,1)S(1)} %constant_dynamic-update-slice_fusion.4.refs_1_, ...), custom_call_target="tpu_custom_call" | custom-call | tf_op jit(solution)/shard_map/multiply/pallas_call | solution.py:269
  83.3 1.8 %collective-permute-start.16 = (s16[2608,128]{1,0:T(8,128)(2,1)S(1)}, s16[2608,128]{1,0:T(8,128)(2,1)S(1)}, u32[]{:S(2)}, u32[]{:S(2)}) collective-permute-start(s16[2608,128]{1,0:T(8,128)(2,1)S(1)} %get-tuple-element.85), channel_id=1, source_target_pairs={{0,4},{2,6},{4,0},{6,2},{8,12},{10,14},{12,8},{14,10},{16,20},{18,... | collective-permute-start | bytes 2002952 | tf_op jit(solution)/shard_map/ppermute | solution.py:213
  85.1 2.6 %collective-permute-start.17 = (s16[656,128]{1,0:T(8,128)(2,1)S(1)}, s16[656,128]{1,0:T(8,128)(2,1)S(1)}, u32[]{:S(2)}, u32[]{:S(2)}) collective-permute-start(s16[656,128]{1,0:T(8,128)(2,1)S(1)} %get-tuple-element.86), channel_id=1, source_target_pairs={{0,16},{2,18},{4,20},{6,22},{8,24},{10,26},{12,28},{14,30},{16,0},... | collective-permute-start | bytes 503816 | tf_op jit(solution)/shard_map/ppermute | solution.py:213
  87.7 0.4 combine.27
  88.1 1.6 %collective-permute-start.21 = (s16[1312,128]{1,0:T(8,128)(2,1)S(1)}, s16[1312,128]{1,0:T(8,128)(2,1)S(1)}, u32[]{:S(2)}, u32[]{:S(2)}) collective-permute-start(s16[1312,128]{1,0:T(8,128)(2,1)S(1)} %get-tuple-element.94), channel_id=1, source_target_pairs={{0,8},{2,10},{4,12},{6,14},{8,0},{10,2},{12,4},{14,6},{16,24},{18,... | collective-permute-start | bytes 1007624 | tf_op jit(solution)/shard_map/ppermute | solution.py:213
  89.8 0.3 collective-permute-start.23
  90.1 5.8 %collective-permute-done.18.refs_1_ = s16[2608,128]{1,0:T(8,128)(2,1)S(1)} collective-permute-done((s16[2608,128]{1,0:T(8,128)(2,1)S(1)}, s16[2608,128]{1,0:T(8,128)(2,1)S(1)}, u32[]{:S(2)}, u32[]{:S(2)}) %collective-permute-start.18) | collective-permute-done | bytes 667680 | tf_op jit(solution)/shard_map/ppermute | solution.py:213
  96.0 0.4 combine.28
  96.4 6.2 %collective-permute-start.25 = (s16[1312,128]{1,0:T(8,128)(2,1)S(1)}, s16[1312,128]{1,0:T(8,128)(2,1)S(1)}, u32[]{:S(2)}, u32[]{:S(2)}) collective-permute-start(s16[1312,128]{1,0:T(8,128)(2,1)S(1)} %get-tuple-element.100), channel_id=1, source_target_pairs={{0,4},{2,6},{4,0},{6,2},{8,12},{10,14},{12,8},{14,10},{16,20},{18,... | collective-permute-start | bytes 1007624 | tf_op jit(solution)/shard_map/ppermute | solution.py:213
  102.7 0.4 combine.30
  103.1 0.5 collective-permute-start.20
  103.6 3.8 %collective-permute-done.21.refs_1_ = s16[1312,128]{1,0:T(8,128)(2,1)S(1)} collective-permute-done((s16[1312,128]{1,0:T(8,128)(2,1)S(1)}, s16[1312,128]{1,0:T(8,128)(2,1)S(1)}, u32[]{:S(2)}, u32[]{:S(2)}) %collective-permute-start.21) | collective-permute-done | bytes 335904 | tf_op jit(solution)/shard_map/ppermute | solution.py:213
  107.4 0.3 combine.31
  107.7 2.7 %collective-permute-start.22 = (s16[656,128]{1,0:T(8,128)(2,1)S(1)}, s16[656,128]{1,0:T(8,128)(2,1)S(1)}, u32[]{:S(2)}, u32[]{:S(2)}) collective-permute-start(s16[656,128]{1,0:T(8,128)(2,1)S(1)} %get-tuple-element.96), channel_id=1, source_target_pairs={{0,16},{2,18},{4,20},{6,22},{8,24},{10,26},{12,28},{14,30},{16,0},... | collective-permute-start | bytes 503816 | tf_op jit(solution)/shard_map/ppermute | solution.py:213
  110.7 1.4 %collective-permute-start.24 = (s16[528,128]{1,0:T(8,128)(2,1)S(1)}, s16[528,128]{1,0:T(8,128)(2,1)S(1)}, u32[]{:S(2)}, u32[]{:S(2)}) collective-permute-start(s16[528,128]{1,0:T(8,128)(2,1)S(1)} %get-tuple-element.99), channel_id=1, source_target_pairs={{0,2},{2,0},{4,6},{6,4},{8,10},{10,8},{12,14},{14,12},{16,18},{18,... | collective-permute-start | bytes 405512 | tf_op jit(solution)/shard_map/ppermute | solution.py:213
  112.1 0.7 collective-permute-start.13
  113.1 0.3 collective-permute-start.26
  113.4 2.4 %collective-permute-done.24.refs_1_ = s16[528,128]{1,0:T(8,128)(2,1)S(1)} collective-permute-done((s16[528,128]{1,0:T(8,128)(2,1)S(1)}, s16[528,128]{1,0:T(8,128)(2,1)S(1)}, u32[]{:S(2)}, u32[]{:S(2)}) %collective-permute-start.24) | collective-permute-done | bytes 135200 | tf_op jit(solution)/shard_map/ppermute | solution.py:213
  115.9 2.0 %collective-permute-done.22.refs_1_ = s16[656,128]{1,0:T(8,128)(2,1)S(1)} collective-permute-done((s16[656,128]{1,0:T(8,128)(2,1)S(1)}, s16[656,128]{1,0:T(8,128)(2,1)S(1)}, u32[]{:S(2)}, u32[]{:S(2)}) %collective-permute-start.22) | collective-permute-done | bytes 167968 | tf_op jit(solution)/shard_map/ppermute | solution.py:213
  117.9 2.0 %collective-permute-done.20.refs_1_ = s16[1312,128]{1,0:T(8,128)(2,1)S(1)} collective-permute-done((s16[1312,128]{1,0:T(8,128)(2,1)S(1)}, s16[1312,128]{1,0:T(8,128)(2,1)S(1)}, u32[]{:S(2)}, u32[]{:S(2)}) %collective-permute-start.20) | collective-permute-done | bytes 335904 | tf_op jit(solution)/shard_map/ppermute | solution.py:213
  120.0 0.3 combine.36
  120.2 1.5 %collective-permute-start.27 = (s16[656,128]{1,0:T(8,128)(2,1)S(1)}, s16[656,128]{1,0:T(8,128)(2,1)S(1)}, u32[]{:S(2)}, u32[]{:S(2)}) collective-permute-start(s16[656,128]{1,0:T(8,128)(2,1)S(1)} %get-tuple-element.104), channel_id=1, source_target_pairs={{0,16},{2,18},{4,20},{6,22},{8,24},{10,26},{12,28},{14,30},{16,0},... | collective-permute-start | bytes 503816 | tf_op jit(solution)/shard_map/ppermute | solution.py:213
  121.9 7.3 %collective-permute-done.26.refs_1_ = s16[656,128]{1,0:T(8,128)(2,1)S(1)} collective-permute-done((s16[656,128]{1,0:T(8,128)(2,1)S(1)}, s16[656,128]{1,0:T(8,128)(2,1)S(1)}, u32[]{:S(2)}, u32[]{:S(2)}) %collective-permute-start.26) | collective-permute-done | bytes 167968 | tf_op jit(solution)/shard_map/ppermute | solution.py:213
  129.4 1.8 %collective-permute-done.27.refs_1_ = s16[656,128]{1,0:T(8,128)(2,1)S(1)} collective-permute-done((s16[656,128]{1,0:T(8,128)(2,1)S(1)}, s16[656,128]{1,0:T(8,128)(2,1)S(1)}, u32[]{:S(2)}, u32[]{:S(2)}) %collective-permute-start.27) | collective-permute-done | bytes 167968 | tf_op jit(solution)/shard_map/ppermute | solution.py:213
  131.2 0.8 constant_dynamic-update-slice_fusion.6
  (52 shorter events, 1.9 us)
Async XLA Ops:
  0.0 3.7 %copy-start.2 = (s32[1,4]{1,0:T(1,128)S(1)}, s32[1,4]{1,0:T(1,128)}, u32[]{:S(2)}) copy-start(s32[1,4]{1,0:T(1,128)} %lengths.1) | copy-start | bytes 52
  2.7 1.5 %copy-start.1 = (bf16[256,2048]{1,0:T(8,128)(2,1)S(1)}, bf16[256,2048]{1,0:T(8,128)(2,1)}, u32[]{:S(2)}) copy-start(bf16[256,2048]{1,0:T(8,128)(2,1)} %activations.1) | copy-start | bytes 3145732
  2.7 3.7 %copy-start.3 = (bf16[256,1280]{1,0:T(8,128)(2,1)S(1)}, bf16[256,1280]{1,0:T(8,128)(2,1)}, u32[]{:S(2)}) copy-start(bf16[256,1280]{1,0:T(8,128)(2,1)} %get-tuple-element.108) | copy-start | bytes 1966084
  2.8 7.2 %copy-start.6 = (s32[56,8]{0,1:T(8,128)S(1)}, s32[56,8]{0,1:T(8,128)}, u32[]{:S(2)}) copy-start(s32[56,8]{0,1:T(8,128)} %param.6) | copy-start | bytes 5380
  6.5 3.7 %collective-permute-start = (bf16[1024,256]{1,0:T(8,128)(2,1)S(1)}, bf16[1024,256]{1,0:T(8,128)(2,1)}, u32[]{:S(2)}, u32[]{:S(2)}) collective-permute-start(bf16[1024,256]{1,0:T(8,128)(2,1)S(1)} %get-tuple-element.57), channel_id=1, source_target_pairs={{0,1},{1,0},{2,3},{3,2},{4,5},{5,4},{6,7},{7,6},{8,9},{9,8},{10,11... | collective-permute-start | bytes 1572872 | tf_op jit(solution)/shard_map/ppermute | solution.py:243
  7.0 4.4 %collective-permute-start.1 = (bf16[1024,256]{1,0:T(8,128)(2,1)S(1)}, bf16[1024,256]{1,0:T(8,128)(2,1)}, u32[]{:S(2)}, u32[]{:S(2)}) collective-permute-start(bf16[1024,256]{1,0:T(8,128)(2,1)S(1)} %get-tuple-element.58), channel_id=1, source_target_pairs={{0,1},{1,0},{2,3},{3,2},{4,5},{5,4},{6,7},{7,6},{8,9},{9,8},{10,11... | collective-permute-start | bytes 1572872 | tf_op jit(solution)/shard_map/ppermute | solution.py:243
  7.1 15.7 %collective-permute-start.3 = (bf16[1024,256]{1,0:T(8,128)(2,1)S(1)}, bf16[1024,256]{1,0:T(8,128)(2,1)}, u32[]{:S(2)}, u32[]{:S(2)}) collective-permute-start(bf16[1024,256]{1,0:T(8,128)(2,1)S(1)} %get-tuple-element.58), channel_id=1, source_target_pairs={{0,2},{2,0},{4,6},{6,4},{8,10},{10,8},{12,14},{14,12},{16,18},{18,... | collective-permute-start | bytes 1572872 | tf_op jit(solution)/shard_map/ppermute | solution.py:213
  10.1 2.4 %copy-start = (bf16[256,7168]{1,0:T(8,128)(2,1)S(1)}, bf16[256,7168]{1,0:T(8,128)(2,1)}, u32[]{:S(2)}) copy-start(bf16[256,7168]{1,0:T(8,128)(2,1)} %refs_2_.11) | copy-start | bytes 11010052
  12.5 4.5 %copy-start.4 = (bf16[264,1280]{1,0:T(8,128)(2,1)S(1)}, bf16[264,1280]{1,0:T(8,128)(2,1)}, u32[]{:S(2)}) copy-start(bf16[264,1280]{1,0:T(8,128)(2,1)} %pad.14) | copy-start | bytes 2027524
  15.4 28.7 %collective-permute-start.2 = (s16[4160,128]{1,0:T(8,128)(2,1)S(1)}, s16[4160,128]{1,0:T(8,128)(2,1)S(1)}, u32[]{:S(2)}, u32[]{:S(2)}) collective-permute-start(s16[4160,128]{1,0:T(8,128)(2,1)S(1)} %get-tuple-element.60), channel_id=1, source_target_pairs={{0,4},{2,6},{4,0},{6,2},{8,12},{10,14},{12,8},{14,10},{16,20},{18,... | collective-permute-start | bytes 3194888 | tf_op jit(solution)/shard_map/ppermute | solution.py:213
  17.0 20.2 %collective-permute-start.5 = (bf16[264,1280]{1,0:T(8,128)(2,1)S(1)}, bf16[264,1280]{1,0:T(8,128)(2,1)S(1)}, u32[]{:S(2)}, u32[]{:S(2)}) collective-permute-start(bf16[264,1280]{1,0:T(8,128)(2,1)S(1)} %copy-done.4), channel_id=1, source_target_pairs={{0,2},{2,0},{4,6},{6,4},{8,10},{10,8},{12,14},{14,12},{16,18},{18,... | collective-permute-start | bytes 2027528 | tf_op jit(solution)/shard_map/ppermute | solution.py:213
  22.8 7.7 %collective-permute-start.4 = (bf16[1024,256]{1,0:T(8,128)(2,1)}, bf16[1024,256]{1,0:T(8,128)(2,1)S(1)}, u32[]{:S(2)}, u32[]{:S(2)}) collective-permute-start(bf16[1024,256]{1,0:T(8,128)(2,1)} %collective-permute-done.3), channel_id=1, source_target_pairs={{0,1},{1,0},{2,3},{3,2},{4,5},{5,4},{6,7},{7,6},{8,9},{9,8},{10,11... | collective-permute-start | bytes 1572872 | tf_op jit(solution)/shard_map/ppermute | solution.py:243
  25.7 31.3 %collective-permute-start.8 = (s16[4160,128]{1,0:T(8,128)(2,1)S(1)}, s16[4160,128]{1,0:T(8,128)(2,1)S(1)}, u32[]{:S(2)}, u32[]{:S(2)}) collective-permute-start(s16[4160,128]{1,0:T(8,128)(2,1)S(1)} %get-tuple-element.68), channel_id=1, source_target_pairs={{0,8},{2,10},{4,12},{6,14},{8,0},{10,2},{12,4},{14,6},{16,24},{18,... | collective-permute-start | bytes 3194888 | tf_op jit(solution)/shard_map/ppermute | solution.py:213
  28.0 23.7 %collective-permute-start.9 = (bf16[264,1280]{1,0:T(8,128)(2,1)S(1)}, bf16[264,1280]{1,0:T(8,128)(2,1)S(1)}, u32[]{:S(2)}, u32[]{:S(2)}) collective-permute-start(bf16[264,1280]{1,0:T(8,128)(2,1)S(1)} %pad.13), channel_id=1, source_target_pairs={{0,2},{2,0},{4,6},{6,4},{8,10},{10,8},{12,14},{14,12},{16,18},{18,... | collective-permute-start | bytes 2027528 | tf_op jit(solution)/shard_map/ppermute | solution.py:213
  40.4 18.8 %collective-permute-start.7 = (s16[2608,128]{1,0:T(8,128)(2,1)S(1)}, s16[2608,128]{1,0:T(8,128)(2,1)S(1)}, u32[]{:S(2)}, u32[]{:S(2)}) collective-permute-start(s16[2608,128]{1,0:T(8,128)(2,1)S(1)} %get-tuple-element.67), channel_id=1, source_target_pairs={{0,4},{2,6},{4,0},{6,2},{8,12},{10,14},{12,8},{14,10},{16,20},{18,... | collective-permute-start | bytes 2002952 | tf_op jit(solution)/shard_map/ppermute | solution.py:213
  42.6 24.5 %collective-permute-start.12 = (bf16[264,1280]{1,0:T(8,128)(2,1)S(1)}, bf16[264,1280]{1,0:T(8,128)(2,1)S(1)}, u32[]{:S(2)}, u32[]{:S(2)}) collective-permute-start(bf16[264,1280]{1,0:T(8,128)(2,1)S(1)} %pad.15), channel_id=1, source_target_pairs={{0,2},{2,0},{4,6},{6,4},{8,10},{10,8},{12,14},{14,12},{16,18},{18,... | collective-permute-start | bytes 2027528 | tf_op jit(solution)/shard_map/ppermute | solution.py:213
  44.7 19.0 %collective-permute-start.6 = (s16[2080,128]{1,0:T(8,128)(2,1)S(1)}, s16[2080,128]{1,0:T(8,128)(2,1)S(1)}, u32[]{:S(2)}, u32[]{:S(2)}) collective-permute-start(s16[2080,128]{1,0:T(8,128)(2,1)S(1)} %get-tuple-element.65), channel_id=1, source_target_pairs={{0,8},{2,10},{4,12},{6,14},{8,0},{10,2},{12,4},{14,6},{16,24},{18,... | collective-permute-start | bytes 1597448 | tf_op jit(solution)/shard_map/ppermute | solution.py:213
  54.9 25.2 %collective-permute-start.14 = (bf16[264,1280]{1,0:T(8,128)(2,1)S(1)}, bf16[264,1280]{1,0:T(8,128)(2,1)S(1)}, u32[]{:S(2)}, u32[]{:S(2)}) collective-permute-start(bf16[264,1280]{1,0:T(8,128)(2,1)S(1)} %pad.16), channel_id=1, source_target_pairs={{0,2},{2,0},{4,6},{6,4},{8,10},{10,8},{12,14},{14,12},{16,18},{18,... | collective-permute-start | bytes 2027528 | tf_op jit(solution)/shard_map/ppermute | solution.py:213
  57.6 14.2 %collective-permute-start.11 = (s16[2080,128]{1,0:T(8,128)(2,1)S(1)}, s16[2080,128]{1,0:T(8,128)(2,1)S(1)}, u32[]{:S(2)}, u32[]{:S(2)}) collective-permute-start(s16[2080,128]{1,0:T(8,128)(2,1)S(1)} %get-tuple-element.75), channel_id=1, source_target_pairs={{0,4},{2,6},{4,0},{6,2},{8,12},{10,14},{12,8},{14,10},{16,20},{18,... | collective-permute-start | bytes 1597448 | tf_op jit(solution)/shard_map/ppermute | solution.py:213
  59.6 19.2 %collective-permute-start.15 = (s16[1312,128]{1,0:T(8,128)(2,1)S(1)}, s16[1312,128]{1,0:T(8,128)(2,1)S(1)}, u32[]{:S(2)}, u32[]{:S(2)}) collective-permute-start(s16[1312,128]{1,0:T(8,128)(2,1)S(1)} %get-tuple-element.82), channel_id=1, source_target_pairs={{0,8},{2,10},{4,12},{6,14},{8,0},{10,2},{12,4},{14,6},{16,24},{18,... | collective-permute-start | bytes 1007624 | tf_op jit(solution)/shard_map/ppermute | solution.py:213
  64.1 14.5 %collective-permute-start.10 = (s16[1040,128]{1,0:T(8,128)(2,1)S(1)}, s16[1040,128]{1,0:T(8,128)(2,1)S(1)}, u32[]{:S(2)}, u32[]{:S(2)}) collective-permute-start(s16[1040,128]{1,0:T(8,128)(2,1)S(1)} %get-tuple-element.74), channel_id=1, source_target_pairs={{0,16},{2,18},{4,20},{6,22},{8,24},{10,26},{12,28},{14,30},{16,0},... | collective-permute-start | bytes 798728 | tf_op jit(solution)/shard_map/ppermute | solution.py:213
  67.1 20.7 %collective-permute-start.19 = (s16[2608,128]{1,0:T(8,128)(2,1)S(1)}, s16[2608,128]{1,0:T(8,128)(2,1)S(1)}, u32[]{:S(2)}, u32[]{:S(2)}) collective-permute-start(s16[2608,128]{1,0:T(8,128)(2,1)S(1)} %get-tuple-element.89), channel_id=1, source_target_pairs={{0,4},{2,6},{4,0},{6,2},{8,12},{10,14},{12,8},{14,10},{16,20},{18,... | collective-permute-start | bytes 2002952 | tf_op jit(solution)/shard_map/ppermute | solution.py:213
  71.8 24.1 %collective-permute-start.18 = (s16[2608,128]{1,0:T(8,128)(2,1)S(1)}, s16[2608,128]{1,0:T(8,128)(2,1)S(1)}, u32[]{:S(2)}, u32[]{:S(2)}) collective-permute-start(s16[2608,128]{1,0:T(8,128)(2,1)S(1)} %get-tuple-element.87), channel_id=1, source_target_pairs={{0,8},{2,10},{4,12},{6,14},{8,0},{10,2},{12,4},{14,6},{16,24},{18,... | collective-permute-start | bytes 2002952 | tf_op jit(solution)/shard_map/ppermute | solution.py:213
  83.3 19.4 %collective-permute-start.16 = (s16[2608,128]{1,0:T(8,128)(2,1)S(1)}, s16[2608,128]{1,0:T(8,128)(2,1)S(1)}, u32[]{:S(2)}, u32[]{:S(2)}) collective-permute-start(s16[2608,128]{1,0:T(8,128)(2,1)S(1)} %get-tuple-element.85), channel_id=1, source_target_pairs={{0,4},{2,6},{4,0},{6,2},{8,12},{10,14},{12,8},{14,10},{16,20},{18,... | collective-permute-start | bytes 2002952 | tf_op jit(solution)/shard_map/ppermute | solution.py:213
  85.1 17.4 %collective-permute-start.17 = (s16[656,128]{1,0:T(8,128)(2,1)S(1)}, s16[656,128]{1,0:T(8,128)(2,1)S(1)}, u32[]{:S(2)}, u32[]{:S(2)}) collective-permute-start(s16[656,128]{1,0:T(8,128)(2,1)S(1)} %get-tuple-element.86), channel_id=1, source_target_pairs={{0,16},{2,18},{4,20},{6,22},{8,24},{10,26},{12,28},{14,30},{16,0},... | collective-permute-start | bytes 503816 | tf_op jit(solution)/shard_map/ppermute | solution.py:213
  88.1 19.3 %collective-permute-start.21 = (s16[1312,128]{1,0:T(8,128)(2,1)S(1)}, s16[1312,128]{1,0:T(8,128)(2,1)S(1)}, u32[]{:S(2)}, u32[]{:S(2)}) collective-permute-start(s16[1312,128]{1,0:T(8,128)(2,1)S(1)} %get-tuple-element.94), channel_id=1, source_target_pairs={{0,8},{2,10},{4,12},{6,14},{8,0},{10,2},{12,4},{14,6},{16,24},{18,... | collective-permute-start | bytes 1007624 | tf_op jit(solution)/shard_map/ppermute | solution.py:213
  89.8 20.7 %collective-permute-start.23 = (s16[1040,128]{1,0:T(8,128)(2,1)S(1)}, s16[1040,128]{1,0:T(8,128)(2,1)S(1)}, u32[]{:S(2)}, u32[]{:S(2)}) collective-permute-start(s16[1040,128]{1,0:T(8,128)(2,1)S(1)} %get-tuple-element.97), channel_id=1, source_target_pairs={{0,16},{2,18},{4,20},{6,22},{8,24},{10,26},{12,28},{14,30},{16,0},... | collective-permute-start | bytes 798728 | tf_op jit(solution)/shard_map/ppermute | solution.py:213
  96.4 16.4 %collective-permute-start.25 = (s16[1312,128]{1,0:T(8,128)(2,1)S(1)}, s16[1312,128]{1,0:T(8,128)(2,1)S(1)}, u32[]{:S(2)}, u32[]{:S(2)}) collective-permute-start(s16[1312,128]{1,0:T(8,128)(2,1)S(1)} %get-tuple-element.100), channel_id=1, source_target_pairs={{0,4},{2,6},{4,0},{6,2},{8,12},{10,14},{12,8},{14,10},{16,20},{18,... | collective-permute-start | bytes 1007624 | tf_op jit(solution)/shard_map/ppermute | solution.py:213
  103.1 16.9 %collective-permute-start.20 = (s16[1312,128]{1,0:T(8,128)(2,1)S(1)}, s16[1312,128]{1,0:T(8,128)(2,1)S(1)}, u32[]{:S(2)}, u32[]{:S(2)}) collective-permute-start(s16[1312,128]{1,0:T(8,128)(2,1)S(1)} %get-tuple-element.93), channel_id=1, source_target_pairs={{0,8},{2,10},{4,12},{6,14},{8,0},{10,2},{12,4},{14,6},{16,24},{18,... | collective-permute-start | bytes 1007624 | tf_op jit(solution)/shard_map/ppermute | solution.py:213
  107.7 10.1 %collective-permute-start.22 = (s16[656,128]{1,0:T(8,128)(2,1)S(1)}, s16[656,128]{1,0:T(8,128)(2,1)S(1)}, u32[]{:S(2)}, u32[]{:S(2)}) collective-permute-start(s16[656,128]{1,0:T(8,128)(2,1)S(1)} %get-tuple-element.96), channel_id=1, source_target_pairs={{0,16},{2,18},{4,20},{6,22},{8,24},{10,26},{12,28},{14,30},{16,0},... | collective-permute-start | bytes 503816 | tf_op jit(solution)/shard_map/ppermute | solution.py:213
  110.7 5.1 %collective-permute-start.24 = (s16[528,128]{1,0:T(8,128)(2,1)S(1)}, s16[528,128]{1,0:T(8,128)(2,1)S(1)}, u32[]{:S(2)}, u32[]{:S(2)}) collective-permute-start(s16[528,128]{1,0:T(8,128)(2,1)S(1)} %get-tuple-element.99), channel_id=1, source_target_pairs={{0,2},{2,0},{4,6},{6,4},{8,10},{10,8},{12,14},{14,12},{16,18},{18,... | collective-permute-start | bytes 405512 | tf_op jit(solution)/shard_map/ppermute | solution.py:213
  112.1 9.7 %collective-permute-start.13 = (s16[528,128]{1,0:T(8,128)(2,1)S(1)}, s16[528,128]{1,0:T(8,128)(2,1)S(1)}, u32[]{:S(2)}, u32[]{:S(2)}) collective-permute-start(s16[528,128]{1,0:T(8,128)(2,1)S(1)} %get-tuple-element.80), channel_id=1, source_target_pairs={{0,2},{2,0},{4,6},{6,4},{8,10},{10,8},{12,14},{14,12},{16,18},{18,... | collective-permute-start | bytes 405512 | tf_op jit(solution)/shard_map/ppermute | solution.py:213
  113.1 16.2 %collective-permute-start.26 = (s16[656,128]{1,0:T(8,128)(2,1)S(1)}, s16[656,128]{1,0:T(8,128)(2,1)S(1)}, u32[]{:S(2)}, u32[]{:S(2)}) collective-permute-start(s16[656,128]{1,0:T(8,128)(2,1)S(1)} %get-tuple-element.103), channel_id=1, source_target_pairs={{0,16},{2,18},{4,20},{6,22},{8,24},{10,26},{12,28},{14,30},{16,0},... | collective-permute-start | bytes 503816 | tf_op jit(solution)/shard_map/ppermute | solution.py:213
  120.2 10.9 %collective-permute-start.27 = (s16[656,128]{1,0:T(8,128)(2,1)S(1)}, s16[656,128]{1,0:T(8,128)(2,1)S(1)}, u32[]{:S(2)}, u32[]{:S(2)}) collective-permute-start(s16[656,128]{1,0:T(8,128)(2,1)S(1)} %get-tuple-element.104), channel_id=1, source_target_pairs={{0,16},{2,18},{4,20},{6,22},{8,24},{10,26},{12,28},{14,30},{16,0},... | collective-permute-start | bytes 503816 | tf_op jit(solution)/shard_map/ppermute | solution.py:213
  129.4 1.9 %copy-start.5 = (f32[56,64,128]{2,1,0:T(8,128)}, f32[56,64,128]{2,1,0:T(8,128)S(1)}, u32[]{:S(2)}) copy-start(f32[56,64,128]{2,1,0:T(8,128)S(1)} %constant_dynamic-update-slice_fusion.7) | copy-start | bytes 5505028

commit v10 on v6

--- a/solution.py
+++ b/solution.py
@@ -87,7 +87,7 @@
             for mask in masks:
                 piece = (me[0] ^ mask) // 2
                 entry, part = piece // per_block, piece % per_block
-                block = picks[begins[0] + c, entry] ^ me[1]
+                block = picks[c, entry] ^ me[1]
                 starts.append((mask & 1, pl.multiple_of(block * height + part * rows, rows)))
             total = None
             for t, grad in enumerate(grads):
@@ -274,7 +274,7 @@
             scratch_shapes=[scale(width, n)],
             compiler_params=params(),
             name="multiply",
-        )(place, row_blocks, *lefts, *grads, last)
+        )(place, row_blocks[starts[i] : starts[i] + width], *lefts, *grads, last)
 
     def combine(sources, n, encoded, last):
         width = sum(w for w, *_ in sources)

time: 130 us -> 148 us (1.14); the launches traced: 130 us -> 147 us
  Pallas kernels: 26.1 us -> 46 us
  local copies, waits for them, and re-layouts: 7.29 us -> 26.8 us
  waiting for transfers between devices: 54.7 us -> 42.5 us
  starting transfers between devices: 41.4 us -> 30.7 us
    unnamed x23 -> x76, local copies, waits for them, and re-layouts: 0.53 us -> 18.6 us
    pallas_call x20, Pallas kernels: 5.41 us -> 20 us  [combine(): pl.pallas_call(functools.partial(combine_kernel, shapes, rows, n, encoded...]
    ppermute x25, waiting for transfers between devices: 54.7 us -> 42.5 us  [swap(): return lax.ppermute(sent, 'dp', [(o, o ^ 1 << bit) for o in range(owners)])]
    ppermute x25, starting transfers between devices: 40.8 us -> 30.2 us  [swap(): return lax.ppermute(sent, 'dp', [(o, o ^ 1 << bit) for o in range(owners)])]
    pallas_call x6, Pallas kernels: 18.5 us -> 23 us  [multiply(): pl.pallas_call(functools.partial(multiply_kernel, width, rows, height, or...]
    pad x4, local copies, waits for them, and re-layouts: 1.11 us -> 3.65 us  [fetch(): piece = jnp.pad(piece, ((0, PAD), (0, 0)))]
  transfers between devices with their start and end apart: 28 -> 28, of which waited for: 14 -> 8; matrix products, arithmetic and copies ran while one was open for 2% -> 4% of each run, Pallas kernels for 18% -> 29%
where the time goes in v10:
time: 148 us; the launch traced here: 147 us
  Pallas kernels  46 us (31%)
  waiting for transfers between devices  42.5 us (29%)
  starting transfers between devices  30.7 us (21%)
  local copies, waits for them, and re-layouts  26.8 us (18%)
    ppermute x25, waiting for transfers between devices, swap(): return lax.ppermute(sent, 'dp', [(o, o ^ 1 << bit) for o in range(owners)])  42.5 us
    ppermute x25, starting transfers between devices, swap(): return lax.ppermute(sent, 'dp', [(o, o ^ 1 << bit) for o in range(owners)])  30.2 us
    pallas_call x6, Pallas kernels, multiply(): pl.pallas_call(functools.partial(multiply_kernel, width, rows, height, or...  23 us
    pallas_call x20, Pallas kernels, combine(): pl.pallas_call(functools.partial(combine_kernel, shapes, rows, n, encoded...  20 us
    unnamed x76, local copies, waits for them, and re-layouts  18.6 us
    pad x4, local copies, waits for them, and re-layouts, fetch(): piece = jnp.pad(piece, ((0, PAD), (0, 0)))  3.65 us
    pallas_call x1, Pallas kernels, shards(): pl.pallas_call(functools.partial(prepare_kernel, rows), out_shape=[jax.Sh...  3 us
  transfers between devices with their start and end apart: 28, of which 8 were waited for; matrix products, arithmetic and copies ran while one was open for 4% of the time, Pallas kernels for 29%

profile of v10, /device:TPU:0, one launch (start us, length us, event | category | flops | bytes accessed | tf_op | source)
XLA Modules:
  0.0 146.5 jit_solution(17113155753662018767)
XLA Ops:
  0.0 2.4 %fusion = (bf16[256,1280]{1,0:T(8,128)(2,1)}, bf16[256,1280]{1,0:T(8,128)(2,1)S(1)}) fusion(bf16[256,7168]{1,0:T(8,128)(2,1)} %refs_2_.11), kind=kLoop, calls=%fused_computation.13 | loop fusion | bytes 2621440 | tf_op jit(solution)/shard_map/slice | solution.py:217
  2.5 1.0 pad.16
  3.5 3.0 %prepare.1 = (bf16[1024,256]{1,0:T(8,128)(2,1)S(1)}, bf16[1024,256]{1,0:T(8,128)(2,1)}) custom-call(s32[2]{0:T(128)S(1)} %pad_add_fusion.me.refs_3_, s32[1,4]{1,0:T(1,128)S(1)} %copy-done.27, bf16[256,2048]{1,0:T(8,128)(2,1)S(1)} %copy-done.26), custom_call_target="tpu_custom_call" | custom-call | tf_op jit(solution)/shard_map/prepare/pallas_call | solution.py:227
  6.5 0.9 pad.15
  7.4 0.5 collective-permute-start
  7.9 2.9 %collective-permute-start.3 = (bf16[1024,256]{1,0:T(8,128)(2,1)}, bf16[1024,256]{1,0:T(8,128)(2,1)}, u32[]{:S(2)}, u32[]{:S(2)}) collective-permute-start(bf16[1024,256]{1,0:T(8,128)(2,1)} %get-tuple-element.58), channel_id=1, source_target_pairs={{0,2},{2,0},{4,6},{6,4},{8,10},{10,8},{12,14},{14,12},{16,18},{18,... | collective-permute-start | bytes 1572872 | tf_op jit(solution)/shard_map/ppermute | solution.py:213
  11.1 1.2 constant_dynamic-update-slice_fusion.3
  12.4 0.8 copy-done
  13.2 3.6 %multiply.6 = (f32[4096,128]{1,0:T(8,128)S(1)}, s16[4160,128]{1,0:T(8,128)(2,1)}) custom-call(s32[2]{0:T(128)S(1)} %pad_add_fusion.me.refs_3_, s32[8,8]{1,0:T(8,128)S(1)} %copy.11.picks, bf16[2048,256]{1,0:T(8,128)(2,1)S(1)} %constant_dynamic-update-slice_fusion.refs_0_, bf16[2048,256]{1,0:T(8,128)(2,1)S(1)} %constant_dynamic-update-slice_fusion.2.refs_1_, ...), custom_call_target="tpu_custom_call" | custom-call | tf_op jit(solution)/shard_map/multiply/pallas_call | solution.py:269
  16.8 2.1 %collective-permute-start.2 = (s16[4160,128]{1,0:T(8,128)(2,1)}, s16[4160,128]{1,0:T(8,128)(2,1)}, u32[]{:S(2)}, u32[]{:S(2)}) collective-permute-start(s16[4160,128]{1,0:T(8,128)(2,1)} %get-tuple-element.60), channel_id=1, source_target_pairs={{0,8},{2,10},{4,12},{6,14},{8,0},{10,2},{12,4},{14,6},{16,24},{18,... | collective-permute-start | bytes 3194888 | tf_op jit(solution)/shard_map/ppermute | solution.py:213
  18.9 5.0 %collective-permute-done.3 = bf16[1024,256]{1,0:T(8,128)(2,1)} collective-permute-done((bf16[1024,256]{1,0:T(8,128)(2,1)}, bf16[1024,256]{1,0:T(8,128)(2,1)}, u32[]{:S(2)}, u32[]{:S(2)}) %collective-permute-start.3) | collective-permute-done | bytes 524320 | tf_op jit(solution)/shard_map/ppermute | solution.py:213
  24.0 2.0 %copy-done.1 = bf16[256,7168]{1,0:T(8,128)(2,1)S(1)} copy-done((bf16[256,7168]{1,0:T(8,128)(2,1)S(1)}, bf16[256,7168]{1,0:T(8,128)(2,1)}, u32[]{:S(2)}) %copy-start.1) | copy-done | bytes 3670040
  26.0 1.2 copy-done.14
  27.2 3.5 %multiply.7 = (f32[4096,128]{1,0:T(8,128)S(1)}, s16[4160,128]{1,0:T(8,128)(2,1)}) custom-call(s32[2]{0:T(128)S(1)} %pad_add_fusion.me.refs_3_, s32[8,8]{1,0:T(8,128)S(1)} %copy.13.picks, bf16[2048,256]{1,0:T(8,128)(2,1)S(1)} %constant_dynamic-update-slice_fusion.refs_0_, bf16[2048,256]{1,0:T(8,128)(2,1)S(1)} %copy-done.14, bf16[256,7168]{1,0:T(8,128)(2,1)S(1)} %copy-done.1, ...), custom_call_target="tpu_custom_call" | custom-call | tf_op jit(solution)/shard_map/multiply/pallas_call | solution.py:269
  30.7 1.3 copy-done.8
  32.0 2.1 %collective-permute-start.9 = (s16[4160,128]{1,0:T(8,128)(2,1)}, s16[4160,128]{1,0:T(8,128)(2,1)}, u32[]{:S(2)}, u32[]{:S(2)}) collective-permute-start(s16[4160,128]{1,0:T(8,128)(2,1)} %get-tuple-element.70), channel_id=1, source_target_pairs={{0,4},{2,6},{4,0},{6,2},{8,12},{10,14},{12,8},{14,10},{16,20},{18,... | collective-permute-start | bytes 3194888 | tf_op jit(solution)/shard_map/ppermute | solution.py:213
  34.1 1.5 %collective-permute-start.7 = (bf16[264,1280]{1,0:T(8,128)(2,1)}, bf16[264,1280]{1,0:T(8,128)(2,1)}, u32[]{:S(2)}, u32[]{:S(2)}) collective-permute-start(bf16[264,1280]{1,0:T(8,128)(2,1)} %pad.15), channel_id=1, source_target_pairs={{0,2},{2,0},{4,6},{6,4},{8,10},{10,8},{12,14},{14,12},{16,18},{18,... | collective-permute-start | bytes 2027528 | tf_op jit(solution)/shard_map/ppermute | solution.py:213
  35.8 1.2 constant_dynamic-update-slice_fusion.5
  37.0 1.1 constant_dynamic-update-slice_fusion.4.refs_1_
  38.1 6.1 %collective-permute-done.5.refs_3_ = bf16[264,1792]{1,0:T(8,128)(2,1)} collective-permute-done((bf16[264,1792]{1,0:T(8,128)(2,1)}, bf16[264,1792]{1,0:T(8,128)(2,1)}, u32[]{:S(2)}, u32[]{:S(2)}) %collective-permute-start.5) | collective-permute-done | bytes 946208 | tf_op jit(solution)/shard_map/ppermute | solution.py:213
  44.2 2.0 %copy-done.2 = bf16[256,7168]{1,0:T(8,128)(2,1)S(1)} copy-done((bf16[256,7168]{1,0:T(8,128)(2,1)S(1)}, bf16[256,7168]{1,0:T(8,128)(2,1)}, u32[]{:S(2)}) %copy-start.2) | copy-done | bytes 3670040
  46.2 5.3 %multiply.8 = (f32[3584,128]{1,0:T(8,128)S(1)}, s16[3648,128]{1,0:T(8,128)(2,1)}) custom-call(s32[2]{0:T(128)S(1)} %pad_add_fusion.me.refs_3_, s32[14,8]{1,0:T(8,128)S(1)} %copy.12.picks, bf16[2048,256]{1,0:T(8,128)(2,1)S(1)} %constant_dynamic-update-slice_fusion.refs_0_, bf16[2048,256]{1,0:T(8,128)(2,1)S(1)} %constant_dynamic-update-slice_fusion.4.refs_1_, ...), custom_call_target="tpu_custom_call" | custom-call | tf_op jit(solution)/shard_map/multiply/pallas_call | solution.py:269
  51.6 2.2 %collective-permute-start.13 = (s16[3648,128]{1,0:T(8,128)(2,1)}, s16[3648,128]{1,0:T(8,128)(2,1)}, u32[]{:S(2)}, u32[]{:S(2)}) collective-permute-start(s16[3648,128]{1,0:T(8,128)(2,1)} %get-tuple-element.77), channel_id=1, source_target_pairs={{0,8},{2,10},{4,12},{6,14},{8,0},{10,2},{12,4},{14,6},{16,24},{18,... | collective-permute-start | bytes 2801672 | tf_op jit(solution)/shard_map/ppermute | solution.py:213
  53.7 0.9 pad.18
  54.6 1.5 %collective-permute-start.14 = (bf16[264,1280]{1,0:T(8,128)(2,1)}, bf16[264,1280]{1,0:T(8,128)(2,1)}, u32[]{:S(2)}, u32[]{:S(2)}) collective-permute-start(bf16[264,1280]{1,0:T(8,128)(2,1)} %pad.18), channel_id=1, source_target_pairs={{0,2},{2,0},{4,6},{6,4},{8,10},{10,8},{12,14},{14,12},{16,18},{18,... | collective-permute-start | bytes 2027528 | tf_op jit(solution)/shard_map/ppermute | solution.py:213
  56.1 2.7 %combine.20 = (f32[2048,128]{1,0:T(8,128)S(1)}, s16[2080,128]{1,0:T(8,128)(2,1)}) custom-call(f32[4096,128]{1,0:T(8,128)S(1)} %copy-done.7, s16[4160,128]{1,0:T(8,128)(2,1)} %collective-permute-done.2.refs_1_, f32[3584,128]{1,0:T(8,128)S(1)} %get-tuple-element.76.refs_2_.refs_0_), custom_call_target="tpu_custom_call" | custom-call | tf_op jit(solution)/shard_map/combine/pallas_call | solution.py:291
  58.8 1.5 %collective-permute-start.6 = (s16[2080,128]{1,0:T(8,128)(2,1)}, s16[2080,128]{1,0:T(8,128)(2,1)}, u32[]{:S(2)}, u32[]{:S(2)}) collective-permute-start(s16[2080,128]{1,0:T(8,128)(2,1)} %get-tuple-element.65), channel_id=1, source_target_pairs={{0,4},{2,6},{4,0},{6,2},{8,12},{10,14},{12,8},{14,10},{16,20},{18,... | collective-permute-start | bytes 1597448 | tf_op jit(solution)/shard_map/ppermute | solution.py:213
  60.5 2.0 %copy-done.3 = bf16[256,7168]{1,0:T(8,128)(2,1)S(1)} copy-done((bf16[256,7168]{1,0:T(8,128)(2,1)S(1)}, bf16[256,7168]{1,0:T(8,128)(2,1)}, u32[]{:S(2)}) %copy-start.3) | copy-done | bytes 3670040
  62.5 4.2 %multiply.9 = (f32[2560,128]{1,0:T(8,128)S(1)}, s16[2608,128]{1,0:T(8,128)(2,1)}) custom-call(s32[2]{0:T(128)S(1)} %pad_add_fusion.me.refs_3_, s32[10,8]{1,0:T(8,128)S(1)} %copy.14.picks, bf16[2048,256]{1,0:T(8,128)(2,1)S(1)} %constant_dynamic-update-slice_fusion.refs_0_, bf16[2048,256]{1,0:T(8,128)(2,1)S(1)} %constant_dynamic-update-slice_fusion.4.refs_1_, ...), custom_call_target="tpu_custom_call" | custom-call | tf_op jit(solution)/shard_map/multiply/pallas_call | solution.py:269
  66.7 0.5 collective-permute-start.12
  67.2 7.0 %collective-permute-done.6.refs_1_ = s16[2080,128]{1,0:T(8,128)(2,1)} collective-permute-done((s16[2080,128]{1,0:T(8,128)(2,1)}, s16[2080,128]{1,0:T(8,128)(2,1)}, u32[]{:S(2)}, u32[]{:S(2)}) %collective-permute-start.6) | collective-permute-done | bytes 532512 | tf_op jit(solution)/shard_map/ppermute | solution.py:213
  74.1 2.1 %combine.21 = (f32[1024,128]{1,0:T(8,128)S(1)}, s16[1040,128]{1,0:T(8,128)(2,1)}) custom-call(f32[2048,128]{1,0:T(8,128)S(1)} %get-tuple-element.64.refs_4_.refs_0_, s16[2080,128]{1,0:T(8,128)(2,1)} %collective-permute-done.6.refs_1_, f32[2560,128]{1,0:T(8,128)S(1)} %get-tuple-element.74.refs_2_.refs_0_), custom_call_target="tpu_custom_call" | custom-call | tf_op jit(solution)/shard_map/combine/pallas_call | solution.py:291
  76.3 2.8 %combine.22 = (f32[2048,128]{1,0:T(8,128)S(1)}, s16[2080,128]{1,0:T(8,128)(2,1)}) custom-call(f32[4096,128]{1,0:T(8,128)S(1)} %copy-done.10, s16[4160,128]{1,0:T(8,128)(2,1)} %collective-permute-done.9.refs_1_, f32[1024,128]{1,0:T(8,128)S(1)} %get-tuple-element.68.refs_2_.refs_0_), custom_call_target="tpu_custom_call" | custom-call | tf_op jit(solution)/shard_map/combine/pallas_call | solution.py:291
  79.1 0.6 collective-permute-start.10
  79.6 0.8 pad.17
  80.5 2.0 %copy-done.4 = bf16[256,7168]{1,0:T(8,128)(2,1)S(1)} copy-done((bf16[256,7168]{1,0:T(8,128)(2,1)S(1)}, bf16[256,7168]{1,0:T(8,128)(2,1)}, u32[]{:S(2)}) %copy-start.4) | copy-done | bytes 3670040
  82.6 4.3 %multiply.10 = (f32[2560,128]{1,0:T(8,128)S(1)}, s16[2608,128]{1,0:T(8,128)(2,1)}) custom-call(s32[2]{0:T(128)S(1)} %pad_add_fusion.me.refs_3_, s32[10,8]{1,0:T(8,128)S(1)} %copy.16.picks, bf16[2048,256]{1,0:T(8,128)(2,1)S(1)} %constant_dynamic-update-slice_fusion.refs_0_, bf16[2048,256]{1,0:T(8,128)(2,1)S(1)} %constant_dynamic-update-slice_fusion.4.refs_1_, ...), custom_call_target="tpu_custom_call" | custom-call | tf_op jit(solution)/shard_map/multiply/pallas_call | solution.py:269
  86.9 2.0 %collective-permute-start.17 = (s16[2608,128]{1,0:T(8,128)(2,1)}, s16[2608,128]{1,0:T(8,128)(2,1)}, u32[]{:S(2)}, u32[]{:S(2)}) collective-permute-start(s16[2608,128]{1,0:T(8,128)(2,1)} %get-tuple-element.87), channel_id=1, source_target_pairs={{0,4},{2,6},{4,0},{6,2},{8,12},{10,14},{12,8},{14,10},{16,20},{18,... | collective-permute-start | bytes 2002952 | tf_op jit(solution)/shard_map/ppermute | solution.py:213
  88.9 2.6 %collective-permute-start.8 = (s16[1040,128]{1,0:T(8,128)(2,1)}, s16[1040,128]{1,0:T(8,128)(2,1)}, u32[]{:S(2)}, u32[]{:S(2)}) collective-permute-start(s16[1040,128]{1,0:T(8,128)(2,1)} %get-tuple-element.69), channel_id=1, source_target_pairs={{0,16},{2,18},{4,20},{6,22},{8,24},{10,26},{12,28},{14,30},{16,0},... | collective-permute-start | bytes 798728 | tf_op jit(solution)/shard_map/ppermute | solution.py:213
  91.5 2.7 %combine.23 = (f32[1792,128]{1,0:T(8,128)S(1)}, s16[1824,128]{1,0:T(8,128)(2,1)}) custom-call(f32[3584,128]{1,0:T(8,128)S(1)} %copy-done.12, s16[3648,128]{1,0:T(8,128)(2,1)} %collective-permute-done.13.refs_1_, f32[2560,128]{1,0:T(8,128)S(1)} %get-tuple-element.79.refs_2_.refs_0_), custom_call_target="tpu_custom_call" | custom-call | tf_op jit(solution)/shard_map/combine/pallas_call | solution.py:291
  94.1 2.6 %combine.24 = (f32[1280,128]{1,0:T(8,128)S(1)}, s16[1312,128]{1,0:T(8,128)(2,1)}) custom-call(f32[2560,128]{1,0:T(8,128)S(1)} %copy-done.18, s16[2608,128]{1,0:T(8,128)(2,1)} %collective-permute-done.12.refs_1_, f32[1792,128]{1,0:T(8,128)S(1)} %get-tuple-element.80.refs_2_.refs_0_), custom_call_target="tpu_custom_call" | custom-call | tf_op jit(solution)/shard_map/combine/pallas_call | solution.py:291
  96.7 0.8 copy-done.21
  97.5 1.5 %collective-permute-start.16 = (s16[1312,128]{1,0:T(8,128)(2,1)}, s16[1312,128]{1,0:T(8,128)(2,1)S(1)}, u32[]{:S(2)}, u32[]{:S(2)}) collective-permute-start(s16[1312,128]{1,0:T(8,128)(2,1)} %get-tuple-element.86), channel_id=1, source_target_pairs={{0,8},{2,10},{4,12},{6,14},{8,0},{10,2},{12,4},{14,6},{16,24},{18,... | collective-permute-start | bytes 1007624 | tf_op jit(solution)/shard_map/ppermute | solution.py:213
  99.0 0.5 collective-permute-start.19
  99.7 2.0 %copy-done.5 = bf16[256,7168]{1,0:T(8,128)(2,1)S(1)} copy-done((bf16[256,7168]{1,0:T(8,128)(2,1)S(1)}, bf16[256,7168]{1,0:T(8,128)(2,1)}, u32[]{:S(2)}) %copy-start.5) | copy-done | bytes 3670040
  101.7 1.1 copy-done.22
  102.8 2.2 %multiply.11 = (f32[1536,128]{1,0:T(8,128)S(1)}, s16[1568,128]{1,0:T(8,128)(2,1)S(1)}) custom-call(s32[2]{0:T(128)S(1)} %pad_add_fusion.me.refs_3_, s32[6,8]{1,0:T(8,128)S(1)} %copy.15.picks, bf16[2048,256]{1,0:T(8,128)(2,1)S(1)} %constant_dynamic-update-slice_fusion.refs_0_, bf16[2048,256]{1,0:T(8,128)(2,1)S(1)} %constant_dynamic-update-slice_fusion.4.refs_1_, ...), custom_call_target="tpu_custom_call" | custom-call | tf_op jit(solution)/shard_map/multiply/pallas_call | solution.py:269
  105.0 1.5 %combine.25 = (f32[1024,128]{1,0:T(8,128)S(1)}, s16[1040,128]{1,0:T(8,128)(2,1)S(1)}) custom-call(f32[2048,128]{1,0:T(8,128)S(1)} %get-tuple-element.71.refs_4_.refs_0_, s16[2080,128]{1,0:T(8,128)(2,1)} %collective-permute-done.10.refs_1_, f32[1536,128]{1,0:T(8,128)S(1)} %get-tuple-element.82.refs_2_.refs_0_), custom_call_target="tpu_custom_call" | custom-call | tf_op jit(solution)/shard_map/combine/pallas_call | solution.py:291
  106.5 0.4 collective-permute-start.20
  106.9 1.5 %collective-permute-start.22 = (s16[1568,128]{1,0:T(8,128)(2,1)S(1)}, s16[1568,128]{1,0:T(8,128)(2,1)S(1)}, u32[]{:S(2)}, u32[]{:S(2)}) collective-permute-start(s16[1568,128]{1,0:T(8,128)(2,1)S(1)} %get-tuple-element.96), channel_id=1, source_target_pairs={{0,4},{2,6},{4,0},{6,2},{8,12},{10,14},{12,8},{14,10},{16,20},{18,... | collective-permute-start | bytes 1204232 | tf_op jit(solution)/shard_map/ppermute | solution.py:213
  108.5 1.2 combine.26
  109.7 1.5 %combine.27 = (f32[1280,128]{1,0:T(8,128)S(1)}, s16[1312,128]{1,0:T(8,128)(2,1)S(1)}) custom-call(f32[2560,128]{1,0:T(8,128)S(1)} %copy-done.16, s16[2608,128]{1,0:T(8,128)(2,1)} %collective-permute-done.17.refs_1_, f32[512,128]{1,0:T(8,128)S(1)} %get-tuple-element.84.refs_2_.refs_0_), custom_call_target="tpu_custom_call" | custom-call | tf_op jit(solution)/shard_map/combine/pallas_call | solution.py:291
  111.2 0.3 combine.28
  111.5 2.7 %collective-permute-start.18 = (s16[656,128]{1,0:T(8,128)(2,1)S(1)}, s16[656,128]{1,0:T(8,128)(2,1)S(1)}, u32[]{:S(2)}, u32[]{:S(2)}) collective-permute-start(s16[656,128]{1,0:T(8,128)(2,1)S(1)} %get-tuple-element.90), channel_id=1, source_target_pairs={{0,16},{2,18},{4,20},{6,22},{8,24},{10,26},{12,28},{14,30},{16,0},... | collective-permute-start | bytes 503816 | tf_op jit(solution)/shard_map/ppermute | solution.py:213
  114.2 0.5 collective-permute-start.25
  114.7 9.3 %collective-permute-done.20.refs_1_ = s16[1040,128]{1,0:T(8,128)(2,1)S(1)} collective-permute-done((s16[1040,128]{1,0:T(8,128)(2,1)S(1)}, s16[1040,128]{1,0:T(8,128)(2,1)S(1)}, u32[]{:S(2)}, u32[]{:S(2)}) %collective-permute-start.20) | collective-permute-done | bytes 266272 | tf_op jit(solution)/shard_map/ppermute | solution.py:213
  124.0 0.4 collective-permute-start.15
  124.6 1.4 combine.30
  126.1 3.4 %collective-permute-done.18.refs_1_ = s16[656,128]{1,0:T(8,128)(2,1)S(1)} collective-permute-done((s16[656,128]{1,0:T(8,128)(2,1)S(1)}, s16[656,128]{1,0:T(8,128)(2,1)S(1)}, u32[]{:S(2)}, u32[]{:S(2)}) %collective-permute-start.18) | collective-permute-done | bytes 167968 | tf_op jit(solution)/shard_map/ppermute | solution.py:213
  130.6 2.8 %collective-permute-start.26 = (s16[656,128]{1,0:T(8,128)(2,1)S(1)}, s16[656,128]{1,0:T(8,128)(2,1)S(1)}, u32[]{:S(2)}, u32[]{:S(2)}) collective-permute-start(s16[656,128]{1,0:T(8,128)(2,1)S(1)} %get-tuple-element.103), channel_id=1, source_target_pairs={{0,16},{2,18},{4,20},{6,22},{8,24},{10,26},{12,28},{14,30},{16,0},... | collective-permute-start | bytes 503816 | tf_op jit(solution)/shard_map/ppermute | solution.py:213
  133.4 6.5 %collective-permute-done.24.refs_1_ = s16[912,128]{1,0:T(8,128)(2,1)S(1)} collective-permute-done((s16[912,128]{1,0:T(8,128)(2,1)S(1)}, s16[912,128]{1,0:T(8,128)(2,1)S(1)}, u32[]{:S(2)}, u32[]{:S(2)}) %collective-permute-start.24) | collective-permute-done | bytes 233504 | tf_op jit(solution)/shard_map/ppermute | solution.py:213
  140.4 1.3 collective-permute-done.26.refs_1_
  141.8 4.0 %collective-permute-done.27.refs_1_ = s16[400,128]{1,0:T(8,128)(2,1)S(1)} collective-permute-done((s16[400,128]{1,0:T(8,128)(2,1)S(1)}, s16[400,128]{1,0:T(8,128)(2,1)S(1)}, u32[]{:S(2)}, u32[]{:S(2)}) %collective-permute-start.27) | collective-permute-done | bytes 102432 | tf_op jit(solution)/shard_map/ppermute | solution.py:213
  145.8 0.7 constant_dynamic-update-slice_fusion.6
  (113 shorter events, 3.2 us)
Async XLA Ops:
  0.0 2.5 %slice-start = ((bf16[256,7168]{1,0:T(8,128)(2,1)}), bf16[256,1792]{1,0:T(8,128)(2,1)S(1)}, s32[]{:S(2)}) async-start(bf16[256,7168]{1,0:T(8,128)(2,1)} %refs_2_.11), calls=%async_computation | async-start | bytes 1835008 | tf_op jit(solution)/shard_map/slice | solution.py:217
  0.0 3.5 %copy-start.26 = (bf16[256,2048]{1,0:T(8,128)(2,1)S(1)}, bf16[256,2048]{1,0:T(8,128)(2,1)}, u32[]{:S(2)}) copy-start(bf16[256,2048]{1,0:T(8,128)(2,1)} %activations.1) | copy-start | bytes 3145732
  0.0 3.5 %copy-start.27 = (s32[1,4]{1,0:T(1,128)S(1)}, s32[1,4]{1,0:T(1,128)}, u32[]{:S(2)}) copy-start(s32[1,4]{1,0:T(1,128)} %lengths.1) | copy-start | bytes 52
  2.5 8.4 %copy-start.29 = (s32[56,8]{0,1:T(8,128)S(1)}, s32[56,8]{0,1:T(8,128)}, u32[]{:S(2)}) copy-start(s32[56,8]{0,1:T(8,128)} %param.6) | copy-start | bytes 5380
  7.4 4.9 %collective-permute-start = (bf16[1024,256]{1,0:T(8,128)(2,1)S(1)}, bf16[1024,256]{1,0:T(8,128)(2,1)S(1)}, u32[]{:S(2)}, u32[]{:S(2)}) collective-permute-start(bf16[1024,256]{1,0:T(8,128)(2,1)S(1)} %get-tuple-element.57), channel_id=1, source_target_pairs={{0,1},{1,0},{2,3},{3,2},{4,5},{5,4},{6,7},{7,6},{8,9},{9,8},{10,11... | collective-permute-start | bytes 1572872 | tf_op jit(solution)/shard_map/ppermute | solution.py:243
  7.9 4.5 %collective-permute-start.1 = (bf16[1024,256]{1,0:T(8,128)(2,1)}, bf16[1024,256]{1,0:T(8,128)(2,1)S(1)}, u32[]{:S(2)}, u32[]{:S(2)}) collective-permute-start(bf16[1024,256]{1,0:T(8,128)(2,1)} %get-tuple-element.58), channel_id=1, source_target_pairs={{0,1},{1,0},{2,3},{3,2},{4,5},{5,4},{6,7},{7,6},{8,9},{9,8},{10,11... | collective-permute-start | bytes 1572872 | tf_op jit(solution)/shard_map/ppermute | solution.py:243
  7.9 16.0 %collective-permute-start.3 = (bf16[1024,256]{1,0:T(8,128)(2,1)}, bf16[1024,256]{1,0:T(8,128)(2,1)}, u32[]{:S(2)}, u32[]{:S(2)}) collective-permute-start(bf16[1024,256]{1,0:T(8,128)(2,1)} %get-tuple-element.58), channel_id=1, source_target_pairs={{0,2},{2,0},{4,6},{6,4},{8,10},{10,8},{12,14},{14,12},{16,18},{18,... | collective-permute-start | bytes 1572872 | tf_op jit(solution)/shard_map/ppermute | solution.py:213
  10.9 33.3 %collective-permute-start.5 = (bf16[264,1792]{1,0:T(8,128)(2,1)}, bf16[264,1792]{1,0:T(8,128)(2,1)}, u32[]{:S(2)}, u32[]{:S(2)}) collective-permute-start(bf16[264,1792]{1,0:T(8,128)(2,1)} %pad.16), channel_id=1, source_target_pairs={{0,2},{2,0},{4,6},{6,4},{8,10},{10,8},{12,14},{14,12},{16,18},{18,... | collective-permute-start | bytes 2838536 | tf_op jit(solution)/shard_map/ppermute | solution.py:213
  11.0 2.2 %copy-start = (bf16[256,7168]{1,0:T(8,128)(2,1)S(1)}, bf16[256,7168]{1,0:T(8,128)(2,1)}, u32[]{:S(2)}) copy-start(bf16[256,7168]{1,0:T(8,128)(2,1)} %refs_2_.11) | copy-start | bytes 11010052
  13.2 3.6 %copy-start.13 = (bf16[2048,256]{1,0:T(8,128)(2,1)}, bf16[2048,256]{1,0:T(8,128)(2,1)S(1)}, u32[]{:S(2)}) copy-start(bf16[2048,256]{1,0:T(8,128)(2,1)S(1)} %constant_dynamic-update-slice_fusion.2.refs_1_) | copy-start | bytes 3145732
  16.8 13.9 %copy-start.6 = (f32[4096,128]{1,0:T(8,128)}, f32[4096,128]{1,0:T(8,128)S(1)}, u32[]{:S(2)}) copy-start(f32[4096,128]{1,0:T(8,128)S(1)} %get-tuple-element.59.refs_3_.refs_0_) | copy-start | bytes 6291460
  16.8 39.3 %collective-permute-start.2 = (s16[4160,128]{1,0:T(8,128)(2,1)}, s16[4160,128]{1,0:T(8,128)(2,1)}, u32[]{:S(2)}, u32[]{:S(2)}) collective-permute-start(s16[4160,128]{1,0:T(8,128)(2,1)} %get-tuple-element.60), channel_id=1, source_target_pairs={{0,8},{2,10},{4,12},{6,14},{8,0},{10,2},{12,4},{14,6},{16,24},{18,... | collective-permute-start | bytes 3194888 | tf_op jit(solution)/shard_map/ppermute | solution.py:213
  23.9 13.1 %collective-permute-start.4 = (bf16[1024,256]{1,0:T(8,128)(2,1)}, bf16[1024,256]{1,0:T(8,128)(2,1)}, u32[]{:S(2)}, u32[]{:S(2)}) collective-permute-start(bf16[1024,256]{1,0:T(8,128)(2,1)} %collective-permute-done.3), channel_id=1, source_target_pairs={{0,1},{1,0},{2,3},{3,2},{4,5},{5,4},{6,7},{7,6},{8,9},{9,8},{10,11... | collective-permute-start | bytes 1572872 | tf_op jit(solution)/shard_map/ppermute | solution.py:243
  24.0 2.0 %copy-start.1 = (bf16[256,7168]{1,0:T(8,128)(2,1)S(1)}, bf16[256,7168]{1,0:T(8,128)(2,1)}, u32[]{:S(2)}) copy-start(bf16[256,7168]{1,0:T(8,128)(2,1)} %refs_2_.11) | copy-start | bytes 11010052
  26.0 1.2 copy-start.14
  30.7 1.3 copy-start.8
  32.0 44.2 %collective-permute-start.9 = (s16[4160,128]{1,0:T(8,128)(2,1)}, s16[4160,128]{1,0:T(8,128)(2,1)}, u32[]{:S(2)}, u32[]{:S(2)}) collective-permute-start(s16[4160,128]{1,0:T(8,128)(2,1)} %get-tuple-element.70), channel_id=1, source_target_pairs={{0,4},{2,6},{4,0},{6,2},{8,12},{10,14},{12,8},{14,10},{16,20},{18,... | collective-permute-start | bytes 3194888 | tf_op jit(solution)/shard_map/ppermute | solution.py:213
  34.1 26.3 %collective-permute-start.7 = (bf16[264,1280]{1,0:T(8,128)(2,1)}, bf16[264,1280]{1,0:T(8,128)(2,1)}, u32[]{:S(2)}, u32[]{:S(2)}) collective-permute-start(bf16[264,1280]{1,0:T(8,128)(2,1)} %pad.15), channel_id=1, source_target_pairs={{0,2},{2,0},{4,6},{6,4},{8,10},{10,8},{12,14},{14,12},{16,18},{18,... | collective-permute-start | bytes 2027528 | tf_op jit(solution)/shard_map/ppermute | solution.py:213
  35.8 8.4 %copy-start.9 = (f32[4096,128]{1,0:T(8,128)S(1)}, f32[4096,128]{1,0:T(8,128)}, u32[]{:S(2)}) copy-start(f32[4096,128]{1,0:T(8,128)} %copy-done.8) | copy-start | bytes 6291460
  44.2 2.0 %copy-start.2 = (bf16[256,7168]{1,0:T(8,128)(2,1)S(1)}, bf16[256,7168]{1,0:T(8,128)(2,1)}, u32[]{:S(2)}) copy-start(bf16[256,7168]{1,0:T(8,128)(2,1)} %refs_2_.11) | copy-start | bytes 11010052
  46.2 7.5 %copy-start.28 = (bf16[256,1280]{1,0:T(8,128)(2,1)S(1)}, bf16[256,1280]{1,0:T(8,128)(2,1)}, u32[]{:S(2)}) copy-start(bf16[256,1280]{1,0:T(8,128)(2,1)} %get-tuple-element.105) | copy-start | bytes 1966084
  46.2 9.9 %copy-start.7 = (f32[4096,128]{1,0:T(8,128)S(1)}, f32[4096,128]{1,0:T(8,128)}, u32[]{:S(2)}) copy-start(f32[4096,128]{1,0:T(8,128)} %copy-done.6) | copy-start | bytes 6291460
  51.6 7.2 %copy-start.11 = (f32[3584,128]{1,0:T(8,128)}, f32[3584,128]{1,0:T(8,128)S(1)}, u32[]{:S(2)}) copy-start(f32[3584,128]{1,0:T(8,128)S(1)} %get-tuple-element.76.refs_2_.refs_0_) | copy-start | bytes 5505028
  51.6 37.3 %collective-permute-start.13 = (s16[3648,128]{1,0:T(8,128)(2,1)}, s16[3648,128]{1,0:T(8,128)(2,1)}, u32[]{:S(2)}, u32[]{:S(2)}) collective-permute-start(s16[3648,128]{1,0:T(8,128)(2,1)} %get-tuple-element.77), channel_id=1, source_target_pairs={{0,8},{2,10},{4,12},{6,14},{8,0},{10,2},{12,4},{14,6},{16,24},{18,... | collective-permute-start | bytes 2801672 | tf_op jit(solution)/shard_map/ppermute | solution.py:213
  54.6 25.9 %collective-permute-start.14 = (bf16[264,1280]{1,0:T(8,128)(2,1)}, bf16[264,1280]{1,0:T(8,128)(2,1)}, u32[]{:S(2)}, u32[]{:S(2)}) collective-permute-start(bf16[264,1280]{1,0:T(8,128)(2,1)} %pad.18), channel_id=1, source_target_pairs={{0,2},{2,0},{4,6},{6,4},{8,10},{10,8},{12,14},{14,12},{16,18},{18,... | collective-permute-start | bytes 2027528 | tf_op jit(solution)/shard_map/ppermute | solution.py:213
  58.8 15.4 %collective-permute-start.6 = (s16[2080,128]{1,0:T(8,128)(2,1)}, s16[2080,128]{1,0:T(8,128)(2,1)}, u32[]{:S(2)}, u32[]{:S(2)}) collective-permute-start(s16[2080,128]{1,0:T(8,128)(2,1)} %get-tuple-element.65), channel_id=1, source_target_pairs={{0,4},{2,6},{4,0},{6,2},{8,12},{10,14},{12,8},{14,10},{16,20},{18,... | collective-permute-start | bytes 1597448 | tf_op jit(solution)/shard_map/ppermute | solution.py:213
  60.5 2.0 %copy-start.3 = (bf16[256,7168]{1,0:T(8,128)(2,1)S(1)}, bf16[256,7168]{1,0:T(8,128)(2,1)}, u32[]{:S(2)}) copy-start(bf16[256,7168]{1,0:T(8,128)(2,1)} %refs_2_.11) | copy-start | bytes 11010052
  66.7 9.6 %copy-start.17 = (f32[2560,128]{1,0:T(8,128)}, f32[2560,128]{1,0:T(8,128)S(1)}, u32[]{:S(2)}) copy-start(f32[2560,128]{1,0:T(8,128)S(1)} %get-tuple-element.74.refs_2_.refs_0_) | copy-start | bytes 3932164
  66.7 9.6 %copy-start.10 = (f32[4096,128]{1,0:T(8,128)S(1)}, f32[4096,128]{1,0:T(8,128)}, u32[]{:S(2)}) copy-start(f32[4096,128]{1,0:T(8,128)} %copy-done.8) | copy-start | bytes 6291460
  66.7 27.5 %collective-permute-start.12 = (s16[2608,128]{1,0:T(8,128)(2,1)}, s16[2608,128]{1,0:T(8,128)(2,1)}, u32[]{:S(2)}, u32[]{:S(2)}) collective-permute-start(s16[2608,128]{1,0:T(8,128)(2,1)} %get-tuple-element.75), channel_id=1, source_target_pairs={{0,4},{2,6},{4,0},{6,2},{8,12},{10,14},{12,8},{14,10},{16,20},{18,... | collective-permute-start | bytes 2002952 | tf_op jit(solution)/shard_map/ppermute | solution.py:213
  76.2 2.8 %copy-start.24 = (f32[1024,128]{1,0:T(8,128)}, f32[1024,128]{1,0:T(8,128)S(1)}, u32[]{:S(2)}) copy-start(f32[1024,128]{1,0:T(8,128)S(1)} %get-tuple-element.68.refs_2_.refs_0_) | copy-start | bytes 1572868
  76.2 3.4 %slice-start.1 = ((bf16[256,7168]{1,0:T(8,128)(2,1)}), bf16[256,768]{1,0:T(8,128)(2,1)S(1)}, s32[]{:S(2)}) async-start(bf16[256,7168]{1,0:T(8,128)(2,1)} %refs_2_.11), calls=%async_computation.1 | async-start | bytes 786432 | tf_op jit(solution)/shard_map/slice | solution.py:217
  79.1 25.9 %collective-permute-start.10 = (s16[2080,128]{1,0:T(8,128)(2,1)}, s16[2080,128]{1,0:T(8,128)(2,1)}, u32[]{:S(2)}, u32[]{:S(2)}) collective-permute-start(s16[2080,128]{1,0:T(8,128)(2,1)} %get-tuple-element.72), channel_id=1, source_target_pairs={{0,8},{2,10},{4,12},{6,14},{8,0},{10,2},{12,4},{14,6},{16,24},{18,... | collective-permute-start | bytes 1597448 | tf_op jit(solution)/shard_map/ppermute | solution.py:213
  80.4 18.6 %collective-permute-start.11 = (bf16[264,768]{1,0:T(8,128)(2,1)}, bf16[264,768]{1,0:T(8,128)(2,1)}, u32[]{:S(2)}, u32[]{:S(2)}) collective-permute-start(bf16[264,768]{1,0:T(8,128)(2,1)} %pad.17), channel_id=1, source_target_pairs={{0,2},{2,0},{4,6},{6,4},{8,10},{10,8},{12,14},{14,12},{16,18},{18,... | collective-permute-start | bytes 1216520 | tf_op jit(solution)/shard_map/ppermute | solution.py:213
  80.5 2.0 %copy-start.4 = (bf16[256,7168]{1,0:T(8,128)(2,1)S(1)}, bf16[256,7168]{1,0:T(8,128)(2,1)}, u32[]{:S(2)}) copy-start(bf16[256,7168]{1,0:T(8,128)(2,1)} %refs_2_.11) | copy-start | bytes 11010052
  82.6 8.9 %copy-start.12 = (f32[3584,128]{1,0:T(8,128)S(1)}, f32[3584,128]{1,0:T(8,128)}, u32[]{:S(2)}) copy-start(f32[3584,128]{1,0:T(8,128)} %copy-done.11) | copy-start | bytes 5505028
  86.9 7.3 %copy-start.15 = (f32[2560,128]{1,0:T(8,128)}, f32[2560,128]{1,0:T(8,128)S(1)}, u32[]{:S(2)}) copy-start(f32[2560,128]{1,0:T(8,128)S(1)} %get-tuple-element.79.refs_2_.refs_0_) | copy-start | bytes 3932164
  86.9 22.8 %collective-permute-start.17 = (s16[2608,128]{1,0:T(8,128)(2,1)}, s16[2608,128]{1,0:T(8,128)(2,1)}, u32[]{:S(2)}, u32[]{:S(2)}) collective-permute-start(s16[2608,128]{1,0:T(8,128)(2,1)} %get-tuple-element.87), channel_id=1, source_target_pairs={{0,4},{2,6},{4,0},{6,2},{8,12},{10,14},{12,8},{14,10},{16,20},{18,... | collective-permute-start | bytes 2002952 | tf_op jit(solution)/shard_map/ppermute | solution.py:213
  88.9 18.1 %collective-permute-start.8 = (s16[1040,128]{1,0:T(8,128)(2,1)}, s16[1040,128]{1,0:T(8,128)(2,1)}, u32[]{:S(2)}, u32[]{:S(2)}) collective-permute-start(s16[1040,128]{1,0:T(8,128)(2,1)} %get-tuple-element.69), channel_id=1, source_target_pairs={{0,16},{2,18},{4,20},{6,22},{8,24},{10,26},{12,28},{14,30},{16,0},... | collective-permute-start | bytes 798728 | tf_op jit(solution)/shard_map/ppermute | solution.py:213
  91.5 2.7 %copy-start.18 = (f32[2560,128]{1,0:T(8,128)S(1)}, f32[2560,128]{1,0:T(8,128)}, u32[]{:S(2)}) copy-start(f32[2560,128]{1,0:T(8,128)} %copy-done.17) | copy-start | bytes 3932164
  94.1 2.6 %copy-start.19 = (f32[1792,128]{1,0:T(8,128)}, f32[1792,128]{1,0:T(8,128)S(1)}, u32[]{:S(2)}) copy-start(f32[1792,128]{1,0:T(8,128)S(1)} %get-tuple-element.80.refs_2_.refs_0_) | copy-start | bytes 2752516
  96.7 0.8 copy-start.21
  97.5 13.6 %collective-permute-start.16 = (s16[1312,128]{1,0:T(8,128)(2,1)}, s16[1312,128]{1,0:T(8,128)(2,1)S(1)}, u32[]{:S(2)}, u32[]{:S(2)}) collective-permute-start(s16[1312,128]{1,0:T(8,128)(2,1)} %get-tuple-element.86), channel_id=1, source_target_pairs={{0,8},{2,10},{4,12},{6,14},{8,0},{10,2},{12,4},{14,6},{16,24},{18,... | collective-permute-start | bytes 1007624 | tf_op jit(solution)/shard_map/ppermute | solution.py:213
  99.0 25.6 %collective-permute-start.19 = (s16[1824,128]{1,0:T(8,128)(2,1)}, s16[1824,128]{1,0:T(8,128)(2,1)}, u32[]{:S(2)}, u32[]{:S(2)}) collective-permute-start(s16[1824,128]{1,0:T(8,128)(2,1)} %get-tuple-element.91), channel_id=1, source_target_pairs={{0,4},{2,6},{4,0},{6,2},{8,12},{10,14},{12,8},{14,10},{16,20},{18,... | collective-permute-start | bytes 1400840 | tf_op jit(solution)/shard_map/ppermute | solution.py:213
  99.7 2.0 %copy-start.5 = (bf16[256,7168]{1,0:T(8,128)(2,1)S(1)}, bf16[256,7168]{1,0:T(8,128)(2,1)}, u32[]{:S(2)}) copy-start(bf16[256,7168]{1,0:T(8,128)(2,1)} %refs_2_.11) | copy-start | bytes 11010052
  101.7 1.1 copy-start.22
  105.0 3.5 %copy-start.25 = (f32[1024,128]{1,0:T(8,128)S(1)}, f32[1024,128]{1,0:T(8,128)}, u32[]{:S(2)}) copy-start(f32[1024,128]{1,0:T(8,128)} %copy-done.24) | copy-start | bytes 1572868
  105.0 4.7 %copy-start.16 = (f32[2560,128]{1,0:T(8,128)S(1)}, f32[2560,128]{1,0:T(8,128)}, u32[]{:S(2)}) copy-start(f32[2560,128]{1,0:T(8,128)} %copy-done.15) | copy-start | bytes 3932164
  106.5 4.7 %copy-start.23 = (f32[1280,128]{1,0:T(8,128)S(1)}, f32[1280,128]{1,0:T(8,128)}, u32[]{:S(2)}) copy-start(f32[1280,128]{1,0:T(8,128)} %copy-done.21) | copy-start | bytes 1966084
  106.5 17.5 %collective-permute-start.20 = (s16[1040,128]{1,0:T(8,128)(2,1)S(1)}, s16[1040,128]{1,0:T(8,128)(2,1)S(1)}, u32[]{:S(2)}, u32[]{:S(2)}) collective-permute-start(s16[1040,128]{1,0:T(8,128)(2,1)S(1)} %get-tuple-element.92), channel_id=1, source_target_pairs={{0,16},{2,18},{4,20},{6,22},{8,24},{10,26},{12,28},{14,30},{16,0},... | collective-permute-start | bytes 798728 | tf_op jit(solution)/shard_map/ppermute | solution.py:213
  106.9 22.8 %collective-permute-start.22 = (s16[1568,128]{1,0:T(8,128)(2,1)S(1)}, s16[1568,128]{1,0:T(8,128)(2,1)S(1)}, u32[]{:S(2)}, u32[]{:S(2)}) collective-permute-start(s16[1568,128]{1,0:T(8,128)(2,1)S(1)} %get-tuple-element.96), channel_id=1, source_target_pairs={{0,4},{2,6},{4,0},{6,2},{8,12},{10,14},{12,8},{14,10},{16,20},{18,... | collective-permute-start | bytes 1204232 | tf_op jit(solution)/shard_map/ppermute | solution.py:213
  111.2 13.4 %copy-start.20 = (f32[1792,128]{1,0:T(8,128)S(1)}, f32[1792,128]{1,0:T(8,128)}, u32[]{:S(2)}) copy-start(f32[1792,128]{1,0:T(8,128)} %copy-done.19) | copy-start | bytes 2752516
  111.5 18.0 %collective-permute-start.18 = (s16[656,128]{1,0:T(8,128)(2,1)S(1)}, s16[656,128]{1,0:T(8,128)(2,1)S(1)}, u32[]{:S(2)}, u32[]{:S(2)}) collective-permute-start(s16[656,128]{1,0:T(8,128)(2,1)S(1)} %get-tuple-element.90), channel_id=1, source_target_pairs={{0,16},{2,18},{4,20},{6,22},{8,24},{10,26},{12,28},{14,30},{16,0},... | collective-permute-start | bytes 503816 | tf_op jit(solution)/shard_map/ppermute | solution.py:213
  114.2 16.1 %collective-permute-start.25 = (s16[1312,128]{1,0:T(8,128)(2,1)S(1)}, s16[1312,128]{1,0:T(8,128)(2,1)S(1)}, u32[]{:S(2)}, u32[]{:S(2)}) collective-permute-start(s16[1312,128]{1,0:T(8,128)(2,1)S(1)} %get-tuple-element.100), channel_id=1, source_target_pairs={{0,8},{2,10},{4,12},{6,14},{8,0},{10,2},{12,4},{14,6},{16,24},{18,... | collective-permute-start | bytes 1007624 | tf_op jit(solution)/shard_map/ppermute | solution.py:213
  124.0 5.6 %collective-permute-start.15 = (s16[528,128]{1,0:T(8,128)(2,1)S(1)}, s16[528,128]{1,0:T(8,128)(2,1)S(1)}, u32[]{:S(2)}, u32[]{:S(2)}) collective-permute-start(s16[528,128]{1,0:T(8,128)(2,1)S(1)} %get-tuple-element.85), channel_id=1, source_target_pairs={{0,2},{2,0},{4,6},{6,4},{8,10},{10,8},{12,14},{14,12},{16,18},{18,... | collective-permute-start | bytes 405512 | tf_op jit(solution)/shard_map/ppermute | solution.py:213
  126.0 13.8 %collective-permute-start.24 = (s16[912,128]{1,0:T(8,128)(2,1)S(1)}, s16[912,128]{1,0:T(8,128)(2,1)S(1)}, u32[]{:S(2)}, u32[]{:S(2)}) collective-permute-start(s16[912,128]{1,0:T(8,128)(2,1)S(1)} %get-tuple-element.99), channel_id=1, source_target_pairs={{0,16},{2,18},{4,20},{6,22},{8,24},{10,26},{12,28},{14,30},{16,0},... | collective-permute-start | bytes 700424 | tf_op jit(solution)/shard_map/ppermute | solution.py:213
  129.9 10.0 %collective-permute-start.23 = (s16[784,128]{1,0:T(8,128)(2,1)S(1)}, s16[784,128]{1,0:T(8,128)(2,1)S(1)}, u32[]{:S(2)}, u32[]{:S(2)}) collective-permute-start(s16[784,128]{1,0:T(8,128)(2,1)S(1)} %get-tuple-element.98), channel_id=1, source_target_pairs={{0,8},{2,10},{4,12},{6,14},{8,0},{10,2},{12,4},{14,6},{16,24},{18,... | collective-permute-start | bytes 602120 | tf_op jit(solution)/shard_map/ppermute | solution.py:213
  130.0 10.2 %collective-permute-start.21 = (s16[528,128]{1,0:T(8,128)(2,1)S(1)}, s16[528,128]{1,0:T(8,128)(2,1)S(1)}, u32[]{:S(2)}, u32[]{:S(2)}) collective-permute-start(s16[528,128]{1,0:T(8,128)(2,1)S(1)} %get-tuple-element.95), channel_id=1, source_target_pairs={{0,2},{2,0},{4,6},{6,4},{8,10},{10,8},{12,14},{14,12},{16,18},{18,... | collective-permute-start | bytes 405512 | tf_op jit(solution)/shard_map/ppermute | solution.py:213
  130.6 11.1 %collective-permute-start.26 = (s16[656,128]{1,0:T(8,128)(2,1)S(1)}, s16[656,128]{1,0:T(8,128)(2,1)S(1)}, u32[]{:S(2)}, u32[]{:S(2)}) collective-permute-start(s16[656,128]{1,0:T(8,128)(2,1)S(1)} %get-tuple-element.103), channel_id=1, source_target_pairs={{0,16},{2,18},{4,20},{6,22},{8,24},{10,26},{12,28},{14,30},{16,0},... | collective-permute-start | bytes 503816 | tf_op jit(solution)/shard_map/ppermute | solution.py:213
  140.1 5.6 %collective-permute-start.27 = (s16[400,128]{1,0:T(8,128)(2,1)S(1)}, s16[400,128]{1,0:T(8,128)(2,1)S(1)}, u32[]{:S(2)}, u32[]{:S(2)}) collective-permute-start(s16[400,128]{1,0:T(8,128)(2,1)S(1)} %get-tuple-element.104), channel_id=1, source_target_pairs={{0,16},{2,18},{4,20},{6,22},{8,24},{10,26},{12,28},{14,30},{16,0},... | collective-permute-start | bytes 307208 | tf_op jit(solution)/shard_map/ppermute | solution.py:213
  141.8 4.0 %copy-start.30 = (f32[56,64,128]{2,1,0:T(8,128)}, f32[56,64,128]{2,1,0:T(8,128)S(1)}, u32[]{:S(2)}) copy-start(f32[56,64,128]{2,1,0:T(8,128)S(1)} %constant_dynamic-update-slice_fusion.7) | copy-start | bytes 5505028

commit v11 on v6

--- a/solution.py
+++ b/solution.py
@@ -214,9 +214,9 @@
 
     def fetch(after):
         chunks = messages[len(near_g)]
-        piece = out_grad[:, starts[chunks[0]] * BLOCK : (starts[chunks[-1]] + widths[chunks[-1]]) * BLOCK]
+        whole, after = lax.optimization_barrier((out_grad, after))
+        piece = whole[:, starts[chunks[0]] * BLOCK : (starts[chunks[-1]] + widths[chunks[-1]]) * BLOCK]
         piece = jnp.pad(piece, ((0, PAD), (0, 0)))
-        piece, after = lax.optimization_barrier((piece, after))
         near_g.append(swap(piece, 0))
         return after
 

time: 130 us -> 128 us (0.985)
  local copies, waits for them, and re-layouts: 7.29 us -> 5.69 us
    slice x5 -> x8, local copies, waits for them, and re-layouts: 2.62 us -> 0.02 us  [fetch(): whole[:, starts[chunks[0]] * BLOCK:(starts[chunks[-1]] + widths[chunks[-1...]
    unnamed x23 -> x19, local copies, waits for them, and re-layouts: 0.53 us -> 2.46 us
  transfers between devices with their start and end apart: 28 -> 28, of which waited for: 14 -> 15; matrix products, arithmetic and copies ran while one was open for 2% -> 2% of each run, Pallas kernels for 18% -> 19%
where the time goes in v11:
time: 128 us
  waiting for transfers between devices  54.6 us (43%)
  starting transfers between devices  41.5 us (32%)
  Pallas kernels  26.1 us (20%)
  local copies, waits for them, and re-layouts  5.69 us (4%)
    ppermute x25, waiting for transfers between devices, swap(): return lax.ppermute(sent, 'dp', [(o, o ^ 1 << bit) for o in range(owners)])  54.6 us
    ppermute x25, starting transfers between devices, swap(): return lax.ppermute(sent, 'dp', [(o, o ^ 1 << bit) for o in range(owners)])  40.8 us
    pallas_call x6, Pallas kernels, multiply(): pl.pallas_call(functools.partial(multiply_kernel, width, rows, height, or...  18.5 us
    pallas_call x20, Pallas kernels, combine(): pl.pallas_call(functools.partial(combine_kernel, shapes, rows, n, encoded...  5.41 us
  transfers between devices with their start and end apart: 28, of which 15 were waited for; matrix products, arithmetic and copies ran while one was open for 2% of the time, Pallas kernels for 19%

profile of v11, /device:TPU:0, one launch (start us, length us, event | category | flops | bytes accessed | tf_op | source)
XLA Modules:
  0.0 128.3 jit_solution(6009457015319726807)
XLA Ops:
  0.1 1.3 %copy-done.1 = bf16[256,2048]{1,0:T(8,128)(2,1)S(1)} copy-done((bf16[256,2048]{1,0:T(8,128)(2,1)S(1)}, bf16[256,2048]{1,0:T(8,128)(2,1)}, u32[]{:S(2)}) %copy-start.1) | copy-done | bytes 1048600
  1.4 0.7 copy-done.2
  2.0 2.2 %prepare.1 = (bf16[1024,256]{1,0:T(8,128)(2,1)S(1)}, bf16[1024,256]{1,0:T(8,128)(2,1)S(1)}) custom-call(s32[2]{0:T(128)S(1)} %pad_add_fusion.me.refs_3_, s32[1,4]{1,0:T(1,128)S(1)} %copy-done.2, bf16[256,2048]{1,0:T(8,128)(2,1)S(1)} %copy-done.1), custom_call_target="tpu_custom_call" | custom-call | tf_op jit(solution)/shard_map/prepare/pallas_call | solution.py:227
  4.2 0.5 collective-permute-start
  4.8 2.9 %collective-permute-start.3 = (bf16[1024,256]{1,0:T(8,128)(2,1)S(1)}, bf16[1024,256]{1,0:T(8,128)(2,1)S(1)}, u32[]{:S(2)}, u32[]{:S(2)}) collective-permute-start(bf16[1024,256]{1,0:T(8,128)(2,1)S(1)} %get-tuple-element.58), channel_id=1, source_target_pairs={{0,2},{2,0},{4,6},{6,4},{8,10},{10,8},{12,14},{14,12},{16,18},{18,... | collective-permute-start | bytes 1572872 | tf_op jit(solution)/shard_map/ppermute | solution.py:213
  8.1 1.2 constant_dynamic-update-slice_fusion.refs_0_
  9.3 1.1 constant_dynamic-update-slice_fusion.2.refs_1_
  10.4 2.9 %multiply.6 = (f32[4096,128]{1,0:T(8,128)S(1)}, s16[4160,128]{1,0:T(8,128)(2,1)S(1)}) custom-call(s32[2]{0:T(128)S(1)} %pad_add_fusion.me.refs_3_, s32[56,8]{1,0:T(8,128)S(1)} %copy.5.picks, bf16[2048,256]{1,0:T(8,128)(2,1)S(1)} %constant_dynamic-update-slice_fusion.refs_0_, bf16[2048,256]{1,0:T(8,128)(2,1)S(1)} %constant_dynamic-update-slice_fusion.2.refs_1_, ...), custom_call_target="tpu_custom_call" | custom-call | tf_op jit(solution)/shard_map/multiply/pallas_call | solution.py:269
  13.3 2.2 %collective-permute-start.2 = (s16[4160,128]{1,0:T(8,128)(2,1)S(1)}, s16[4160,128]{1,0:T(8,128)(2,1)S(1)}, u32[]{:S(2)}, u32[]{:S(2)}) collective-permute-start(s16[4160,128]{1,0:T(8,128)(2,1)S(1)} %get-tuple-element.60), channel_id=1, source_target_pairs={{0,8},{2,10},{4,12},{6,14},{8,0},{10,2},{12,4},{14,6},{16,24},{18,... | collective-permute-start | bytes 3194888 | tf_op jit(solution)/shard_map/ppermute | solution.py:213
  15.5 5.0 %collective-permute-done.3 = bf16[1024,256]{1,0:T(8,128)(2,1)S(1)} collective-permute-done((bf16[1024,256]{1,0:T(8,128)(2,1)S(1)}, bf16[1024,256]{1,0:T(8,128)(2,1)S(1)}, u32[]{:S(2)}, u32[]{:S(2)}) %collective-permute-start.3) | collective-permute-done | bytes 524320 | tf_op jit(solution)/shard_map/ppermute | solution.py:213
  20.5 2.9 %multiply.7 = (f32[4096,128]{1,0:T(8,128)S(1)}, s16[4160,128]{1,0:T(8,128)(2,1)S(1)}) custom-call(s32[2]{0:T(128)S(1)} %pad_add_fusion.me.refs_3_, s32[56,8]{1,0:T(8,128)S(1)} %copy.5.picks, bf16[2048,256]{1,0:T(8,128)(2,1)S(1)} %constant_dynamic-update-slice_fusion.refs_0_, bf16[2048,256]{1,0:T(8,128)(2,1)S(1)} %constant_dynamic-update-slice_fusion.2.refs_1_, ...), custom_call_target="tpu_custom_call" | custom-call | tf_op jit(solution)/shard_map/multiply/pallas_call | solution.py:269
  23.4 2.2 %collective-permute-start.9 = (s16[4160,128]{1,0:T(8,128)(2,1)S(1)}, s16[4160,128]{1,0:T(8,128)(2,1)S(1)}, u32[]{:S(2)}, u32[]{:S(2)}) collective-permute-start(s16[4160,128]{1,0:T(8,128)(2,1)S(1)} %get-tuple-element.70), channel_id=1, source_target_pairs={{0,4},{2,6},{4,0},{6,2},{8,12},{10,14},{12,8},{14,10},{16,20},{18,... | collective-permute-start | bytes 3194888 | tf_op jit(solution)/shard_map/ppermute | solution.py:213
  25.6 1.5 %collective-permute-start.7 = (bf16[264,1280]{1,0:T(8,128)(2,1)S(1)}, bf16[264,1280]{1,0:T(8,128)(2,1)S(1)}, u32[]{:S(2)}, u32[]{:S(2)}) collective-permute-start(bf16[264,1280]{1,0:T(8,128)(2,1)S(1)} %pad.16), channel_id=1, source_target_pairs={{0,2},{2,0},{4,6},{6,4},{8,10},{10,8},{12,14},{14,12},{16,18},{18,... | collective-permute-start | bytes 2027528 | tf_op jit(solution)/shard_map/ppermute | solution.py:213
  27.2 13.5 %collective-permute-done.5.refs_3_ = bf16[264,1792]{1,0:T(8,128)(2,1)S(1)} collective-permute-done((bf16[264,1792]{1,0:T(8,128)(2,1)S(1)}, bf16[264,1792]{1,0:T(8,128)(2,1)S(1)}, u32[]{:S(2)}, u32[]{:S(2)}) %collective-permute-start.5) | collective-permute-done | bytes 946208 | tf_op jit(solution)/shard_map/ppermute | solution.py:213
  40.7 4.1 %multiply.8 = (f32[3584,128]{1,0:T(8,128)S(1)}, s16[3648,128]{1,0:T(8,128)(2,1)S(1)}) custom-call(s32[2]{0:T(128)S(1)} %pad_add_fusion.me.refs_3_, s32[56,8]{1,0:T(8,128)S(1)} %copy.5.picks, bf16[2048,256]{1,0:T(8,128)(2,1)S(1)} %constant_dynamic-update-slice_fusion.refs_0_, bf16[2048,256]{1,0:T(8,128)(2,1)S(1)} %constant_dynamic-update-slice_fusion.4.refs_1_, ...), custom_call_target="tpu_custom_call" | custom-call | tf_op jit(solution)/shard_map/multiply/pallas_call | solution.py:269
  44.8 2.2 %collective-permute-start.13 = (s16[3648,128]{1,0:T(8,128)(2,1)S(1)}, s16[3648,128]{1,0:T(8,128)(2,1)S(1)}, u32[]{:S(2)}, u32[]{:S(2)}) collective-permute-start(s16[3648,128]{1,0:T(8,128)(2,1)S(1)} %get-tuple-element.77), channel_id=1, source_target_pairs={{0,8},{2,10},{4,12},{6,14},{8,0},{10,2},{12,4},{14,6},{16,24},{18,... | collective-permute-start | bytes 2801672 | tf_op jit(solution)/shard_map/ppermute | solution.py:213
  47.1 1.6 %collective-permute-start.14 = (bf16[264,1280]{1,0:T(8,128)(2,1)S(1)}, bf16[264,1280]{1,0:T(8,128)(2,1)S(1)}, u32[]{:S(2)}, u32[]{:S(2)}) collective-permute-start(bf16[264,1280]{1,0:T(8,128)(2,1)S(1)} %pad.18), channel_id=1, source_target_pairs={{0,2},{2,0},{4,6},{6,4},{8,10},{10,8},{12,14},{14,12},{16,18},{18,... | collective-permute-start | bytes 2027528 | tf_op jit(solution)/shard_map/ppermute | solution.py:213
  48.6 0.6 combine.20
  49.2 1.6 %collective-permute-start.6 = (s16[2080,128]{1,0:T(8,128)(2,1)S(1)}, s16[2080,128]{1,0:T(8,128)(2,1)S(1)}, u32[]{:S(2)}, u32[]{:S(2)}) collective-permute-start(s16[2080,128]{1,0:T(8,128)(2,1)S(1)} %get-tuple-element.65), channel_id=1, source_target_pairs={{0,4},{2,6},{4,0},{6,2},{8,12},{10,14},{12,8},{14,10},{16,20},{18,... | collective-permute-start | bytes 1597448 | tf_op jit(solution)/shard_map/ppermute | solution.py:213
  50.8 4.4 %collective-permute-done.7.refs_3_ = bf16[264,1280]{1,0:T(8,128)(2,1)S(1)} collective-permute-done((bf16[264,1280]{1,0:T(8,128)(2,1)S(1)}, bf16[264,1280]{1,0:T(8,128)(2,1)S(1)}, u32[]{:S(2)}, u32[]{:S(2)}) %collective-permute-start.7) | collective-permute-done | bytes 675872 | tf_op jit(solution)/shard_map/ppermute | solution.py:213
  55.2 3.2 %multiply.9 = (f32[2560,128]{1,0:T(8,128)S(1)}, s16[2608,128]{1,0:T(8,128)(2,1)S(1)}) custom-call(s32[2]{0:T(128)S(1)} %pad_add_fusion.me.refs_3_, s32[56,8]{1,0:T(8,128)S(1)} %copy.5.picks, bf16[2048,256]{1,0:T(8,128)(2,1)S(1)} %constant_dynamic-update-slice_fusion.refs_0_, bf16[2048,256]{1,0:T(8,128)(2,1)S(1)} %constant_dynamic-update-slice_fusion.4.refs_1_, ...), custom_call_target="tpu_custom_call" | custom-call | tf_op jit(solution)/shard_map/multiply/pallas_call | solution.py:269
  58.4 2.2 %collective-permute-start.12 = (s16[2608,128]{1,0:T(8,128)(2,1)S(1)}, s16[2608,128]{1,0:T(8,128)(2,1)S(1)}, u32[]{:S(2)}, u32[]{:S(2)}) collective-permute-start(s16[2608,128]{1,0:T(8,128)(2,1)S(1)} %get-tuple-element.75), channel_id=1, source_target_pairs={{0,4},{2,6},{4,0},{6,2},{8,12},{10,14},{12,8},{14,10},{16,20},{18,... | collective-permute-start | bytes 2002952 | tf_op jit(solution)/shard_map/ppermute | solution.py:213
  60.6 1.5 %collective-permute-done.6.refs_1_ = s16[2080,128]{1,0:T(8,128)(2,1)S(1)} collective-permute-done((s16[2080,128]{1,0:T(8,128)(2,1)S(1)}, s16[2080,128]{1,0:T(8,128)(2,1)S(1)}, u32[]{:S(2)}, u32[]{:S(2)}) %collective-permute-start.6) | collective-permute-done | bytes 532512 | tf_op jit(solution)/shard_map/ppermute | solution.py:213
  62.1 0.3 combine.21
  62.4 0.6 combine.22
  63.0 2.1 %collective-permute-start.10 = (s16[2080,128]{1,0:T(8,128)(2,1)S(1)}, s16[2080,128]{1,0:T(8,128)(2,1)S(1)}, u32[]{:S(2)}, u32[]{:S(2)}) collective-permute-start(s16[2080,128]{1,0:T(8,128)(2,1)S(1)} %get-tuple-element.72), channel_id=1, source_target_pairs={{0,8},{2,10},{4,12},{6,14},{8,0},{10,2},{12,4},{14,6},{16,24},{18,... | collective-permute-start | bytes 1597448 | tf_op jit(solution)/shard_map/ppermute | solution.py:213
  65.2 0.8 collective-permute-start.11
  66.0 3.7 %collective-permute-done.14.refs_3_ = bf16[264,1280]{1,0:T(8,128)(2,1)S(1)} collective-permute-done((bf16[264,1280]{1,0:T(8,128)(2,1)S(1)}, bf16[264,1280]{1,0:T(8,128)(2,1)S(1)}, u32[]{:S(2)}, u32[]{:S(2)}) %collective-permute-start.14) | collective-permute-done | bytes 675872 | tf_op jit(solution)/shard_map/ppermute | solution.py:213
  69.7 3.2 %multiply.10 = (f32[2560,128]{1,0:T(8,128)S(1)}, s16[2608,128]{1,0:T(8,128)(2,1)S(1)}) custom-call(s32[2]{0:T(128)S(1)} %pad_add_fusion.me.refs_3_, s32[56,8]{1,0:T(8,128)S(1)} %copy.5.picks, bf16[2048,256]{1,0:T(8,128)(2,1)S(1)} %constant_dynamic-update-slice_fusion.refs_0_, bf16[2048,256]{1,0:T(8,128)(2,1)S(1)} %constant_dynamic-update-slice_fusion.4.refs_1_, ...), custom_call_target="tpu_custom_call" | custom-call | tf_op jit(solution)/shard_map/multiply/pallas_call | solution.py:269
  72.9 2.2 %collective-permute-start.17 = (s16[2608,128]{1,0:T(8,128)(2,1)S(1)}, s16[2608,128]{1,0:T(8,128)(2,1)S(1)}, u32[]{:S(2)}, u32[]{:S(2)}) collective-permute-start(s16[2608,128]{1,0:T(8,128)(2,1)S(1)} %get-tuple-element.87), channel_id=1, source_target_pairs={{0,4},{2,6},{4,0},{6,2},{8,12},{10,14},{12,8},{14,10},{16,20},{18,... | collective-permute-start | bytes 2002952 | tf_op jit(solution)/shard_map/ppermute | solution.py:213
  75.1 2.6 %collective-permute-start.8 = (s16[1040,128]{1,0:T(8,128)(2,1)S(1)}, s16[1040,128]{1,0:T(8,128)(2,1)S(1)}, u32[]{:S(2)}, u32[]{:S(2)}) collective-permute-start(s16[1040,128]{1,0:T(8,128)(2,1)S(1)} %get-tuple-element.69), channel_id=1, source_target_pairs={{0,16},{2,18},{4,20},{6,22},{8,24},{10,26},{12,28},{14,30},{16,0},... | collective-permute-start | bytes 798728 | tf_op jit(solution)/shard_map/ppermute | solution.py:213
  77.7 0.6 combine.23
  78.2 0.4 combine.24
  78.7 1.6 %collective-permute-start.16 = (s16[1312,128]{1,0:T(8,128)(2,1)S(1)}, s16[1312,128]{1,0:T(8,128)(2,1)S(1)}, u32[]{:S(2)}, u32[]{:S(2)}) collective-permute-start(s16[1312,128]{1,0:T(8,128)(2,1)S(1)} %get-tuple-element.86), channel_id=1, source_target_pairs={{0,8},{2,10},{4,12},{6,14},{8,0},{10,2},{12,4},{14,6},{16,24},{18,... | collective-permute-start | bytes 1007624 | tf_op jit(solution)/shard_map/ppermute | solution.py:213
  80.3 0.5 collective-permute-start.19
  80.8 2.2 %multiply.11 = (f32[1536,128]{1,0:T(8,128)S(1)}, s16[1568,128]{1,0:T(8,128)(2,1)S(1)}) custom-call(s32[2]{0:T(128)S(1)} %pad_add_fusion.me.refs_3_, s32[56,8]{1,0:T(8,128)S(1)} %copy.5.picks, bf16[2048,256]{1,0:T(8,128)(2,1)S(1)} %constant_dynamic-update-slice_fusion.refs_0_, bf16[2048,256]{1,0:T(8,128)(2,1)S(1)} %constant_dynamic-update-slice_fusion.4.refs_1_, ...), custom_call_target="tpu_custom_call" | custom-call | tf_op jit(solution)/shard_map/multiply/pallas_call | solution.py:269
  83.0 0.3 combine.25
  83.3 2.2 %collective-permute-start.20 = (s16[1040,128]{1,0:T(8,128)(2,1)S(1)}, s16[1040,128]{1,0:T(8,128)(2,1)S(1)}, u32[]{:S(2)}, u32[]{:S(2)}) collective-permute-start(s16[1040,128]{1,0:T(8,128)(2,1)S(1)} %get-tuple-element.92), channel_id=1, source_target_pairs={{0,16},{2,18},{4,20},{6,22},{8,24},{10,26},{12,28},{14,30},{16,0},... | collective-permute-start | bytes 798728 | tf_op jit(solution)/shard_map/ppermute | solution.py:213
  85.5 4.6 %collective-permute-done.8.refs_1_ = s16[1040,128]{1,0:T(8,128)(2,1)S(1)} collective-permute-done((s16[1040,128]{1,0:T(8,128)(2,1)S(1)}, s16[1040,128]{1,0:T(8,128)(2,1)S(1)}, u32[]{:S(2)}, u32[]{:S(2)}) %collective-permute-start.8) | collective-permute-done | bytes 266272 | tf_op jit(solution)/shard_map/ppermute | solution.py:213
  90.1 0.2 combine.26
  90.3 0.7 collective-permute-done.17.refs_1_
  91.0 0.4 combine.27
  91.4 4.2 %collective-permute-done.16.refs_1_ = s16[1312,128]{1,0:T(8,128)(2,1)S(1)} collective-permute-done((s16[1312,128]{1,0:T(8,128)(2,1)S(1)}, s16[1312,128]{1,0:T(8,128)(2,1)S(1)}, u32[]{:S(2)}, u32[]{:S(2)}) %collective-permute-start.16) | collective-permute-done | bytes 335904 | tf_op jit(solution)/shard_map/ppermute | solution.py:213
  95.6 0.3 combine.28
  96.0 1.9 %collective-permute-start.25 = (s16[1312,128]{1,0:T(8,128)(2,1)S(1)}, s16[1312,128]{1,0:T(8,128)(2,1)S(1)}, u32[]{:S(2)}, u32[]{:S(2)}) collective-permute-start(s16[1312,128]{1,0:T(8,128)(2,1)S(1)} %get-tuple-element.100), channel_id=1, source_target_pairs={{0,8},{2,10},{4,12},{6,14},{8,0},{10,2},{12,4},{14,6},{16,24},{18,... | collective-permute-start | bytes 1007624 | tf_op jit(solution)/shard_map/ppermute | solution.py:213
  97.9 5.9 %collective-permute-done.20.refs_1_ = s16[1040,128]{1,0:T(8,128)(2,1)S(1)} collective-permute-done((s16[1040,128]{1,0:T(8,128)(2,1)S(1)}, s16[1040,128]{1,0:T(8,128)(2,1)S(1)}, u32[]{:S(2)}, u32[]{:S(2)}) %collective-permute-start.20) | collective-permute-done | bytes 266272 | tf_op jit(solution)/shard_map/ppermute | solution.py:213
  103.7 1.5 %collective-permute-start.15 = (s16[528,128]{1,0:T(8,128)(2,1)S(1)}, s16[528,128]{1,0:T(8,128)(2,1)S(1)}, u32[]{:S(2)}, u32[]{:S(2)}) collective-permute-start(s16[528,128]{1,0:T(8,128)(2,1)S(1)} %get-tuple-element.85), channel_id=1, source_target_pairs={{0,2},{2,0},{4,6},{6,4},{8,10},{10,8},{12,14},{14,12},{16,18},{18,... | collective-permute-start | bytes 405512 | tf_op jit(solution)/shard_map/ppermute | solution.py:213
  105.3 0.2 combine.29
  105.5 0.4 combine.30
  106.0 1.8 %collective-permute-done.18.refs_1_ = s16[656,128]{1,0:T(8,128)(2,1)S(1)} collective-permute-done((s16[656,128]{1,0:T(8,128)(2,1)S(1)}, s16[656,128]{1,0:T(8,128)(2,1)S(1)}, u32[]{:S(2)}, u32[]{:S(2)}) %collective-permute-start.18) | collective-permute-done | bytes 167968 | tf_op jit(solution)/shard_map/ppermute | solution.py:213
  107.8 0.9 collective-permute-done.15.refs_1_
  108.8 0.2 combine.33
  109.1 2.1 %collective-permute-start.23 = (s16[784,128]{1,0:T(8,128)(2,1)S(1)}, s16[784,128]{1,0:T(8,128)(2,1)S(1)}, u32[]{:S(2)}, u32[]{:S(2)}) collective-permute-start(s16[784,128]{1,0:T(8,128)(2,1)S(1)} %get-tuple-element.98), channel_id=1, source_target_pairs={{0,8},{2,10},{4,12},{6,14},{8,0},{10,2},{12,4},{14,6},{16,24},{18,... | collective-permute-start | bytes 602120 | tf_op jit(solution)/shard_map/ppermute | solution.py:213
  111.2 0.8 collective-permute-start.21
  112.1 0.3 combine.34
  112.3 5.2 %collective-permute-start.26 = (s16[656,128]{1,0:T(8,128)(2,1)S(1)}, s16[656,128]{1,0:T(8,128)(2,1)S(1)}, u32[]{:S(2)}, u32[]{:S(2)}) collective-permute-start(s16[656,128]{1,0:T(8,128)(2,1)S(1)} %get-tuple-element.103), channel_id=1, source_target_pairs={{0,16},{2,18},{4,20},{6,22},{8,24},{10,26},{12,28},{14,30},{16,0},... | collective-permute-start | bytes 503816 | tf_op jit(solution)/shard_map/ppermute | solution.py:213
  117.6 2.6 %collective-permute-done.24.refs_1_ = s16[912,128]{1,0:T(8,128)(2,1)S(1)} collective-permute-done((s16[912,128]{1,0:T(8,128)(2,1)S(1)}, s16[912,128]{1,0:T(8,128)(2,1)S(1)}, u32[]{:S(2)}, u32[]{:S(2)}) %collective-permute-start.24) | collective-permute-done | bytes 233504 | tf_op jit(solution)/shard_map/ppermute | solution.py:213
  120.2 0.1 combine.35.refs_2_
  120.4 0.1 combine.36
  120.5 0.8 collective-permute-start.27
  121.5 4.8 %collective-permute-done.26.refs_1_ = s16[656,128]{1,0:T(8,128)(2,1)S(1)} collective-permute-done((s16[656,128]{1,0:T(8,128)(2,1)S(1)}, s16[656,128]{1,0:T(8,128)(2,1)S(1)}, u32[]{:S(2)}, u32[]{:S(2)}) %collective-permute-start.26) | collective-permute-done | bytes 167968 | tf_op jit(solution)/shard_map/ppermute | solution.py:213
  126.4 1.0 collective-permute-done.27.refs_1_
  127.4 0.2 copy-done.3
  127.6 0.7 constant_dynamic-update-slice_fusion.6
  (55 shorter events, 1.4 us)
Async XLA Ops:
  0.0 7.7 %slice-start = ((bf16[256,7168]{1,0:T(8,128)(2,1)}), bf16[256,1792]{1,0:T(8,128)(2,1)S(1)}, s32[]{:S(2)}) async-start(bf16[256,7168]{1,0:T(8,128)(2,1)} %refs_2_.11), calls=%async_computation | async-start | bytes 1835008 | tf_op jit(solution)/shard_map/slice | solution.py:218
  0.1 1.3 %copy-start.1 = (bf16[256,2048]{1,0:T(8,128)(2,1)S(1)}, bf16[256,2048]{1,0:T(8,128)(2,1)}, u32[]{:S(2)}) copy-start(bf16[256,2048]{1,0:T(8,128)(2,1)} %activations.1) | copy-start | bytes 3145732
  1.4 0.7 copy-start.2
  4.2 3.8 %collective-permute-start = (bf16[1024,256]{1,0:T(8,128)(2,1)S(1)}, bf16[1024,256]{1,0:T(8,128)(2,1)}, u32[]{:S(2)}, u32[]{:S(2)}) collective-permute-start(bf16[1024,256]{1,0:T(8,128)(2,1)S(1)} %get-tuple-element.57), channel_id=1, source_target_pairs={{0,1},{1,0},{2,3},{3,2},{4,5},{5,4},{6,7},{7,6},{8,9},{9,8},{10,11... | collective-permute-start | bytes 1572872 | tf_op jit(solution)/shard_map/ppermute | solution.py:243
  4.8 3.1 %copy-start.4 = (s32[56,8]{0,1:T(8,128)S(1)}, s32[56,8]{0,1:T(8,128)}, u32[]{:S(2)}) copy-start(s32[56,8]{0,1:T(8,128)} %param.6) | copy-start | bytes 5380
  4.8 4.6 %collective-permute-start.1 = (bf16[1024,256]{1,0:T(8,128)(2,1)S(1)}, bf16[1024,256]{1,0:T(8,128)(2,1)}, u32[]{:S(2)}, u32[]{:S(2)}) collective-permute-start(bf16[1024,256]{1,0:T(8,128)(2,1)S(1)} %get-tuple-element.58), channel_id=1, source_target_pairs={{0,1},{1,0},{2,3},{3,2},{4,5},{5,4},{6,7},{7,6},{8,9},{9,8},{10,11... | collective-permute-start | bytes 1572872 | tf_op jit(solution)/shard_map/ppermute | solution.py:243
  4.8 15.6 %collective-permute-start.3 = (bf16[1024,256]{1,0:T(8,128)(2,1)S(1)}, bf16[1024,256]{1,0:T(8,128)(2,1)S(1)}, u32[]{:S(2)}, u32[]{:S(2)}) collective-permute-start(bf16[1024,256]{1,0:T(8,128)(2,1)S(1)} %get-tuple-element.58), channel_id=1, source_target_pairs={{0,2},{2,0},{4,6},{6,4},{8,10},{10,8},{12,14},{14,12},{16,18},{18,... | collective-permute-start | bytes 1572872 | tf_op jit(solution)/shard_map/ppermute | solution.py:213
  7.8 32.9 %collective-permute-start.5 = (bf16[264,1792]{1,0:T(8,128)(2,1)S(1)}, bf16[264,1792]{1,0:T(8,128)(2,1)S(1)}, u32[]{:S(2)}, u32[]{:S(2)}) collective-permute-start(bf16[264,1792]{1,0:T(8,128)(2,1)S(1)} %pad.15), channel_id=1, source_target_pairs={{0,2},{2,0},{4,6},{6,4},{8,10},{10,8},{12,14},{14,12},{16,18},{18,... | collective-permute-start | bytes 2838536 | tf_op jit(solution)/shard_map/ppermute | solution.py:213
  8.0 2.4 %copy-start = (bf16[256,7168]{1,0:T(8,128)(2,1)S(1)}, bf16[256,7168]{1,0:T(8,128)(2,1)}, u32[]{:S(2)}) copy-start(bf16[256,7168]{1,0:T(8,128)(2,1)} %refs_2_.11) | copy-start | bytes 11010052
  13.3 35.3 %collective-permute-start.2 = (s16[4160,128]{1,0:T(8,128)(2,1)S(1)}, s16[4160,128]{1,0:T(8,128)(2,1)S(1)}, u32[]{:S(2)}, u32[]{:S(2)}) collective-permute-start(s16[4160,128]{1,0:T(8,128)(2,1)S(1)} %get-tuple-element.60), channel_id=1, source_target_pairs={{0,8},{2,10},{4,12},{6,14},{8,0},{10,2},{12,4},{14,6},{16,24},{18,... | collective-permute-start | bytes 3194888 | tf_op jit(solution)/shard_map/ppermute | solution.py:213
  20.5 6.7 %collective-permute-start.4 = (bf16[1024,256]{1,0:T(8,128)(2,1)S(1)}, bf16[1024,256]{1,0:T(8,128)(2,1)S(1)}, u32[]{:S(2)}, u32[]{:S(2)}) collective-permute-start(bf16[1024,256]{1,0:T(8,128)(2,1)S(1)} %collective-permute-done.3), channel_id=1, source_target_pairs={{0,1},{1,0},{2,3},{3,2},{4,5},{5,4},{6,7},{7,6},{8,9},{9,8},{10,11... | collective-permute-start | bytes 1572872 | tf_op jit(solution)/shard_map/ppermute | solution.py:243
  20.5 5.1 %slice-start.1 = ((bf16[256,7168]{1,0:T(8,128)(2,1)}), bf16[256,1280]{1,0:T(8,128)(2,1)S(1)}, s32[]{:S(2)}) async-start(bf16[256,7168]{1,0:T(8,128)(2,1)} %refs_2_.11), calls=%async_computation.1 | async-start | bytes 1310720 | tf_op jit(solution)/shard_map/slice | solution.py:218
  23.4 39.0 %collective-permute-start.9 = (s16[4160,128]{1,0:T(8,128)(2,1)S(1)}, s16[4160,128]{1,0:T(8,128)(2,1)S(1)}, u32[]{:S(2)}, u32[]{:S(2)}) collective-permute-start(s16[4160,128]{1,0:T(8,128)(2,1)S(1)} %get-tuple-element.70), channel_id=1, source_target_pairs={{0,4},{2,6},{4,0},{6,2},{8,12},{10,14},{12,8},{14,10},{16,20},{18,... | collective-permute-start | bytes 3194888 | tf_op jit(solution)/shard_map/ppermute | solution.py:213
  25.6 29.6 %collective-permute-start.7 = (bf16[264,1280]{1,0:T(8,128)(2,1)S(1)}, bf16[264,1280]{1,0:T(8,128)(2,1)S(1)}, u32[]{:S(2)}, u32[]{:S(2)}) collective-permute-start(bf16[264,1280]{1,0:T(8,128)(2,1)S(1)} %pad.16), channel_id=1, source_target_pairs={{0,2},{2,0},{4,6},{6,4},{8,10},{10,8},{12,14},{14,12},{16,18},{18,... | collective-permute-start | bytes 2027528 | tf_op jit(solution)/shard_map/ppermute | solution.py:213
  40.7 6.3 %slice-start.2 = ((bf16[256,7168]{1,0:T(8,128)(2,1)}), bf16[256,1280]{1,0:T(8,128)(2,1)S(1)}, s32[]{:S(2)}) async-start(bf16[256,7168]{1,0:T(8,128)(2,1)} %refs_2_.11), calls=%async_computation.2 | async-start | bytes 1310720 | tf_op jit(solution)/shard_map/slice | solution.py:218
  44.8 30.3 %collective-permute-start.13 = (s16[3648,128]{1,0:T(8,128)(2,1)S(1)}, s16[3648,128]{1,0:T(8,128)(2,1)S(1)}, u32[]{:S(2)}, u32[]{:S(2)}) collective-permute-start(s16[3648,128]{1,0:T(8,128)(2,1)S(1)} %get-tuple-element.77), channel_id=1, source_target_pairs={{0,8},{2,10},{4,12},{6,14},{8,0},{10,2},{12,4},{14,6},{16,24},{18,... | collective-permute-start | bytes 2801672 | tf_op jit(solution)/shard_map/ppermute | solution.py:213
  47.1 22.6 %collective-permute-start.14 = (bf16[264,1280]{1,0:T(8,128)(2,1)S(1)}, bf16[264,1280]{1,0:T(8,128)(2,1)S(1)}, u32[]{:S(2)}, u32[]{:S(2)}) collective-permute-start(bf16[264,1280]{1,0:T(8,128)(2,1)S(1)} %pad.18), channel_id=1, source_target_pairs={{0,2},{2,0},{4,6},{6,4},{8,10},{10,8},{12,14},{14,12},{16,18},{18,... | collective-permute-start | bytes 2027528 | tf_op jit(solution)/shard_map/ppermute | solution.py:213
  49.2 12.9 %collective-permute-start.6 = (s16[2080,128]{1,0:T(8,128)(2,1)S(1)}, s16[2080,128]{1,0:T(8,128)(2,1)S(1)}, u32[]{:S(2)}, u32[]{:S(2)}) collective-permute-start(s16[2080,128]{1,0:T(8,128)(2,1)S(1)} %get-tuple-element.65), channel_id=1, source_target_pairs={{0,4},{2,6},{4,0},{6,2},{8,12},{10,14},{12,8},{14,10},{16,20},{18,... | collective-permute-start | bytes 1597448 | tf_op jit(solution)/shard_map/ppermute | solution.py:213
  58.4 19.8 %collective-permute-start.12 = (s16[2608,128]{1,0:T(8,128)(2,1)S(1)}, s16[2608,128]{1,0:T(8,128)(2,1)S(1)}, u32[]{:S(2)}, u32[]{:S(2)}) collective-permute-start(s16[2608,128]{1,0:T(8,128)(2,1)S(1)} %get-tuple-element.75), channel_id=1, source_target_pairs={{0,4},{2,6},{4,0},{6,2},{8,12},{10,14},{12,8},{14,10},{16,20},{18,... | collective-permute-start | bytes 2002952 | tf_op jit(solution)/shard_map/ppermute | solution.py:213
  62.4 2.8 %slice-start.3 = ((bf16[256,7168]{1,0:T(8,128)(2,1)}), bf16[256,768]{1,0:T(8,128)(2,1)S(1)}, s32[]{:S(2)}) async-start(bf16[256,7168]{1,0:T(8,128)(2,1)} %refs_2_.11), calls=%async_computation.3 | async-start | bytes 786432 | tf_op jit(solution)/shard_map/slice | solution.py:218
  63.0 19.9 %collective-permute-start.10 = (s16[2080,128]{1,0:T(8,128)(2,1)S(1)}, s16[2080,128]{1,0:T(8,128)(2,1)S(1)}, u32[]{:S(2)}, u32[]{:S(2)}) collective-permute-start(s16[2080,128]{1,0:T(8,128)(2,1)S(1)} %get-tuple-element.72), channel_id=1, source_target_pairs={{0,8},{2,10},{4,12},{6,14},{8,0},{10,2},{12,4},{14,6},{16,24},{18,... | collective-permute-start | bytes 1597448 | tf_op jit(solution)/shard_map/ppermute | solution.py:213
  65.2 15.1 %collective-permute-start.11 = (bf16[264,768]{1,0:T(8,128)(2,1)S(1)}, bf16[264,768]{1,0:T(8,128)(2,1)S(1)}, u32[]{:S(2)}, u32[]{:S(2)}) collective-permute-start(bf16[264,768]{1,0:T(8,128)(2,1)S(1)} %pad.17), channel_id=1, source_target_pairs={{0,2},{2,0},{4,6},{6,4},{8,10},{10,8},{12,14},{14,12},{16,18},{18,... | collective-permute-start | bytes 1216520 | tf_op jit(solution)/shard_map/ppermute | solution.py:213
  72.9 18.1 %collective-permute-start.17 = (s16[2608,128]{1,0:T(8,128)(2,1)S(1)}, s16[2608,128]{1,0:T(8,128)(2,1)S(1)}, u32[]{:S(2)}, u32[]{:S(2)}) collective-permute-start(s16[2608,128]{1,0:T(8,128)(2,1)S(1)} %get-tuple-element.87), channel_id=1, source_target_pairs={{0,4},{2,6},{4,0},{6,2},{8,12},{10,14},{12,8},{14,10},{16,20},{18,... | collective-permute-start | bytes 2002952 | tf_op jit(solution)/shard_map/ppermute | solution.py:213
  75.1 15.0 %collective-permute-start.8 = (s16[1040,128]{1,0:T(8,128)(2,1)S(1)}, s16[1040,128]{1,0:T(8,128)(2,1)S(1)}, u32[]{:S(2)}, u32[]{:S(2)}) collective-permute-start(s16[1040,128]{1,0:T(8,128)(2,1)S(1)} %get-tuple-element.69), channel_id=1, source_target_pairs={{0,16},{2,18},{4,20},{6,22},{8,24},{10,26},{12,28},{14,30},{16,0},... | collective-permute-start | bytes 798728 | tf_op jit(solution)/shard_map/ppermute | solution.py:213
  78.7 17.0 %collective-permute-start.16 = (s16[1312,128]{1,0:T(8,128)(2,1)S(1)}, s16[1312,128]{1,0:T(8,128)(2,1)S(1)}, u32[]{:S(2)}, u32[]{:S(2)}) collective-permute-start(s16[1312,128]{1,0:T(8,128)(2,1)S(1)} %get-tuple-element.86), channel_id=1, source_target_pairs={{0,8},{2,10},{4,12},{6,14},{8,0},{10,2},{12,4},{14,6},{16,24},{18,... | collective-permute-start | bytes 1007624 | tf_op jit(solution)/shard_map/ppermute | solution.py:213
  80.3 25.2 %collective-permute-start.19 = (s16[1824,128]{1,0:T(8,128)(2,1)S(1)}, s16[1824,128]{1,0:T(8,128)(2,1)S(1)}, u32[]{:S(2)}, u32[]{:S(2)}) collective-permute-start(s16[1824,128]{1,0:T(8,128)(2,1)S(1)} %get-tuple-element.91), channel_id=1, source_target_pairs={{0,4},{2,6},{4,0},{6,2},{8,12},{10,14},{12,8},{14,10},{16,20},{18,... | collective-permute-start | bytes 1400840 | tf_op jit(solution)/shard_map/ppermute | solution.py:213
  83.3 20.4 %collective-permute-start.20 = (s16[1040,128]{1,0:T(8,128)(2,1)S(1)}, s16[1040,128]{1,0:T(8,128)(2,1)S(1)}, u32[]{:S(2)}, u32[]{:S(2)}) collective-permute-start(s16[1040,128]{1,0:T(8,128)(2,1)S(1)} %get-tuple-element.92), channel_id=1, source_target_pairs={{0,16},{2,18},{4,20},{6,22},{8,24},{10,26},{12,28},{14,30},{16,0},... | collective-permute-start | bytes 798728 | tf_op jit(solution)/shard_map/ppermute | solution.py:213
  90.1 18.8 %collective-permute-start.22 = (s16[1568,128]{1,0:T(8,128)(2,1)S(1)}, s16[1568,128]{1,0:T(8,128)(2,1)S(1)}, u32[]{:S(2)}, u32[]{:S(2)}) collective-permute-start(s16[1568,128]{1,0:T(8,128)(2,1)S(1)} %get-tuple-element.96), channel_id=1, source_target_pairs={{0,4},{2,6},{4,0},{6,2},{8,12},{10,14},{12,8},{14,10},{16,20},{18,... | collective-permute-start | bytes 1204232 | tf_op jit(solution)/shard_map/ppermute | solution.py:213
  95.9 11.9 %collective-permute-start.18 = (s16[656,128]{1,0:T(8,128)(2,1)S(1)}, s16[656,128]{1,0:T(8,128)(2,1)S(1)}, u32[]{:S(2)}, u32[]{:S(2)}) collective-permute-start(s16[656,128]{1,0:T(8,128)(2,1)S(1)} %get-tuple-element.90), channel_id=1, source_target_pairs={{0,16},{2,18},{4,20},{6,22},{8,24},{10,26},{12,28},{14,30},{16,0},... | collective-permute-start | bytes 503816 | tf_op jit(solution)/shard_map/ppermute | solution.py:213
  96.0 16.1 %collective-permute-start.25 = (s16[1312,128]{1,0:T(8,128)(2,1)S(1)}, s16[1312,128]{1,0:T(8,128)(2,1)S(1)}, u32[]{:S(2)}, u32[]{:S(2)}) collective-permute-start(s16[1312,128]{1,0:T(8,128)(2,1)S(1)} %get-tuple-element.100), channel_id=1, source_target_pairs={{0,8},{2,10},{4,12},{6,14},{8,0},{10,2},{12,4},{14,6},{16,24},{18,... | collective-permute-start | bytes 1007624 | tf_op jit(solution)/shard_map/ppermute | solution.py:213
  103.7 5.0 %collective-permute-start.15 = (s16[528,128]{1,0:T(8,128)(2,1)S(1)}, s16[528,128]{1,0:T(8,128)(2,1)S(1)}, u32[]{:S(2)}, u32[]{:S(2)}) collective-permute-start(s16[528,128]{1,0:T(8,128)(2,1)S(1)} %get-tuple-element.85), channel_id=1, source_target_pairs={{0,2},{2,0},{4,6},{6,4},{8,10},{10,8},{12,14},{14,12},{16,18},{18,... | collective-permute-start | bytes 405512 | tf_op jit(solution)/shard_map/ppermute | solution.py:213
  105.9 14.3 %collective-permute-start.24 = (s16[912,128]{1,0:T(8,128)(2,1)S(1)}, s16[912,128]{1,0:T(8,128)(2,1)S(1)}, u32[]{:S(2)}, u32[]{:S(2)}) collective-permute-start(s16[912,128]{1,0:T(8,128)(2,1)S(1)} %get-tuple-element.99), channel_id=1, source_target_pairs={{0,16},{2,18},{4,20},{6,22},{8,24},{10,26},{12,28},{14,30},{16,0},... | collective-permute-start | bytes 700424 | tf_op jit(solution)/shard_map/ppermute | solution.py:213
  109.1 11.3 %collective-permute-start.23 = (s16[784,128]{1,0:T(8,128)(2,1)S(1)}, s16[784,128]{1,0:T(8,128)(2,1)S(1)}, u32[]{:S(2)}, u32[]{:S(2)}) collective-permute-start(s16[784,128]{1,0:T(8,128)(2,1)S(1)} %get-tuple-element.98), channel_id=1, source_target_pairs={{0,8},{2,10},{4,12},{6,14},{8,0},{10,2},{12,4},{14,6},{16,24},{18,... | collective-permute-start | bytes 602120 | tf_op jit(solution)/shard_map/ppermute | solution.py:213
  111.2 10.1 %collective-permute-start.21 = (s16[528,128]{1,0:T(8,128)(2,1)S(1)}, s16[528,128]{1,0:T(8,128)(2,1)S(1)}, u32[]{:S(2)}, u32[]{:S(2)}) collective-permute-start(s16[528,128]{1,0:T(8,128)(2,1)S(1)} %get-tuple-element.95), channel_id=1, source_target_pairs={{0,2},{2,0},{4,6},{6,4},{8,10},{10,8},{12,14},{14,12},{16,18},{18,... | collective-permute-start | bytes 405512 | tf_op jit(solution)/shard_map/ppermute | solution.py:213
  112.3 13.9 %collective-permute-start.26 = (s16[656,128]{1,0:T(8,128)(2,1)S(1)}, s16[656,128]{1,0:T(8,128)(2,1)S(1)}, u32[]{:S(2)}, u32[]{:S(2)}) collective-permute-start(s16[656,128]{1,0:T(8,128)(2,1)S(1)} %get-tuple-element.103), channel_id=1, source_target_pairs={{0,16},{2,18},{4,20},{6,22},{8,24},{10,26},{12,28},{14,30},{16,0},... | collective-permute-start | bytes 503816 | tf_op jit(solution)/shard_map/ppermute | solution.py:213
  120.5 6.9 %collective-permute-start.27 = (s16[400,128]{1,0:T(8,128)(2,1)S(1)}, s16[400,128]{1,0:T(8,128)(2,1)S(1)}, u32[]{:S(2)}, u32[]{:S(2)}) collective-permute-start(s16[400,128]{1,0:T(8,128)(2,1)S(1)} %get-tuple-element.104), channel_id=1, source_target_pairs={{0,16},{2,18},{4,20},{6,22},{8,24},{10,26},{12,28},{14,30},{16,0},... | collective-permute-start | bytes 307208 | tf_op jit(solution)/shard_map/ppermute | solution.py:213
  126.4 1.2 copy-start.3
